TPU v7x, 512 devices: a whole 4x8x8 slice. The times are simulated.
512 devices in a mesh: seq: 32 (over z_lo, y), rep: 16 (over z_hi, x, core).
Axes of the slice: x: 4, y: 8, z: 8 (z_hi: 2, z_lo: 4; z = z_hi * 4 + z_lo), core: 2. Of those that a mesh axis runs over, the one named last changes fastest.
Arguments:
- hidden: bfloat16 [16, 4096, 4096], P('rep', 'seq'), may hold values from -6 to 6
- queries: bfloat16 [16, 4096, 4096], P('rep', 'seq'), may hold values from -110 to 110, as said below
- weight_copies: bfloat16 [16, 4096, 1024], P('rep', 'seq'), may hold values from -0.09375 to 0.09375
- segment_ids: int32 [16, 4096], P('rep'), may hold values from 0 to 5, never falling along the last dimension, each value on 1 to 2048 neighbouring positions
- owner: int32 [1], replicated, may hold values from 0 to 1048575
Outputs:
- attended: bfloat16 [16, 4096, 4096], P('rep', 'seq')
Inputs may be any that keep to these rules, and one draw needn't show every extreme that they name: `queries`: query features of each token and head.
All inputs are finite; a program needn't handle non-finite values.
Results may differ from a plain program's by a relative error of at most 0.007.
The roundings to bfloat16 on the way count: a program that leaves them out, or rounds other values in their place, can miss the bound.
Values may be sent and summed in bfloat16 or wider, within the bound.
No kernel may reach another device: no remote copies, remote signals or barrier semaphores. Data moves between devices by JAX's collectives and lax.ppermute only.
A program may use at most 64 MiB of HBM per device.

v0:
```python
import jax
import jax.numpy as jnp
from jax import lax
from jax.sharding import PartitionSpec as P

HEADS = 32
KV_HEADS = 4
HEAD_DIM = 128


THETA = 1000000.0


def broadcast(value, axis, source):
    kept = jnp.where(lax.axis_index(axis) == source, value, 0).astype(value.dtype)
    return lax.psum(kept, axis)


def rotary(tensor, positions):
    half_dim = tensor.shape[-1] // 2
    freqs = THETA ** (-(jnp.arange(half_dim, dtype=jnp.float32) * 2.0) / tensor.shape[-1])
    angles = positions.astype(jnp.float32)[:, None] * freqs[None, :]
    cosine = jnp.cos(angles)[:, None, :]
    sine = jnp.sin(angles)[:, None, :]
    first_half = tensor[..., :half_dim]
    second_half = tensor[..., half_dim:]
    return jnp.concatenate(
        [first_half * cosine - second_half * sine, second_half * cosine + first_half * sine],
        axis=-1,
    )


def doc_starts(segment_row, own_segments):
    return jnp.sum((segment_row[None, :] < own_segments[:, None]).astype(jnp.int32), axis=1)


def attend(query_all, key_all, value_all, segment_row):
    length = query_all.shape[0]
    block_rows = min(length, max(512, length // 8))
    score_scale = 1.0 / query_all.shape[-1] ** 0.5
    outputs = []
    for row_begin in range(0, length, block_rows):
        row_end = row_begin + block_rows
        scores = (
            jnp.einsum(
                "qhd,khd->hqk",
                query_all[row_begin:row_end],
                key_all[:row_end],
                preferred_element_type=jnp.float32,
            )
            * score_scale
        )
        query_index = jnp.arange(row_begin, row_end, dtype=jnp.int32)[:, None]
        key_index = jnp.arange(row_end, dtype=jnp.int32)[None, :]
        allowed = (key_index <= query_index) & (
            segment_row[row_begin:row_end][:, None] == segment_row[:row_end][None, :]
        )
        masked = jnp.where(allowed[None], scores, -1e30)
        row_max = jnp.max(masked, axis=-1, keepdims=True)
        exponent = jnp.exp(masked - row_max)
        totals = jnp.sum(exponent, axis=-1, keepdims=True)
        weights = exponent.astype(jnp.bfloat16)
        mixed = jnp.einsum(
            "hqk,khd->qhd", weights, value_all[:row_end], preferred_element_type=jnp.float32
        )
        mixed = mixed / jnp.transpose(totals, (1, 0, 2))
        outputs.append(mixed.astype(jnp.bfloat16))
    return jnp.concatenate(outputs, axis=0)


def on_device(hidden, queries, weight_copies, segment_ids, owner):
    tok_rows = hidden.shape[1]
    hidden_rows = hidden[0]
    kv_width = KV_HEADS * HEAD_DIM
    root_index = owner[0] % lax.axis_size("rep")
    fresh_part = broadcast(weight_copies[0], "rep", root_index)
    fresh = lax.all_gather(fresh_part, "seq", axis=0, tiled=True)
    projected = jnp.dot(hidden_rows, fresh, preferred_element_type=jnp.float32)
    segment_row = segment_ids[0]
    first_row = lax.axis_index("seq") * tok_rows
    own_segments = lax.dynamic_slice_in_dim(segment_row, first_row, tok_rows)
    positions = (
        first_row + jnp.arange(tok_rows, dtype=jnp.int32) - doc_starts(segment_row, own_segments)
    )
    keys = rotary(projected[:, :kv_width].reshape(tok_rows, KV_HEADS, HEAD_DIM), positions).astype(
        jnp.bfloat16
    )
    values = projected[:, kv_width:].reshape(tok_rows, KV_HEADS, HEAD_DIM).astype(jnp.bfloat16)
    rotated = rotary(
        queries[0].astype(jnp.float32).reshape(tok_rows, HEADS, HEAD_DIM), positions
    ).astype(jnp.bfloat16)
    shards = lax.axis_size("seq")
    local_heads = HEADS // shards
    group_size = HEADS // KV_HEADS

    def arrange(tensor):
        return tensor.reshape(tok_rows, shards, local_heads, HEAD_DIM)

    key_heads = jnp.repeat(keys, group_size, axis=1)
    value_heads = jnp.repeat(values, group_size, axis=1)
    query_part = lax.all_to_all(arrange(rotated), "seq", split_axis=1, concat_axis=0, tiled=True)
    key_part = lax.all_to_all(arrange(key_heads), "seq", split_axis=1, concat_axis=0, tiled=True)
    value_part = lax.all_to_all(
        arrange(value_heads), "seq", split_axis=1, concat_axis=0, tiled=True
    )
    result = attend(query_part[:, 0], key_part[:, 0], value_part[:, 0], segment_row)
    mixed = result[:, None]
    returned = lax.all_to_all(mixed, "seq", split_axis=0, concat_axis=1, tiled=True)
    return returned.reshape(1, tok_rows, HEADS * HEAD_DIM)


def solution(mesh):
    placed = (
        P("rep", "seq", None),
        P("rep", "seq", None),
        P("rep", "seq", None),
        P("rep", None),
        P(),
    )
    return jax.shard_map(
        on_device, mesh=mesh, in_specs=placed, out_specs=P("rep", "seq", None), check_vma=False
    )
```

profile of v0, /device:TPU:56, one launch (start us, length us, event | category | flops | bytes accessed | tf_op | source)
XLA Modules:
  0.0 528.8 jit_solution(274618214669984020)
XLA Ops:
  7.3 0.7 select_bitcast_fusion
  8.1 188.5 %all-reduce.2.cloned.1.call-done = bf16[128,1024]{1,0:T(8,128)(2,1)} async-done(((bf16[128,1024]{1,0:T(8,128)(2,1)}), bf16[128,1024]{1,0:T(8,128)(2,1)}) %all-reduce.2.cloned.1.call-update) | async-done | bytes 262160 | tf_op jit(solution)/shard_map/psum | solution.py:16
  196.7 2.3 copy.50
  198.9 1.5 convert.23
  201.3 1.1 maximum_bitcast_fusion
  202.4 9.7 %all-to-all-start.1 = ((bf16[128,32,1,128]{0,3,2,1:T(8,128)(2,1)}), bf16[128,32,1,128]{0,3,2,1:T(8,128)(2,1)S(1)}, u32[]{:S(2)}, u32[]{:S(2)}) async-start(bf16[128,32,1,128]{0,3,2,1:T(8,128)(2,1)} %maximum_bitcast_fusion), calls=%async_computation.1 | async-start | bytes 2097152 | tf_op jit(solution)/shard_map/all_to_all | solution.py:101
  212.1 160.1 %all-gather.2.cloned.1.call-done = bf16[4096,1024]{1,0:T(8,128)(2,1)} async-done(((bf16[128,1024]{1,0:T(8,128)(2,1)}), bf16[4096,1024]{1,0:T(8,128)(2,1)}) %all-gather.2.cloned.1.call-update) | async-done | bytes 8388624 | tf_op jit(solution)/shard_map/all_gather | solution.py:77
  372.2 5.7 %convolution_bitcast_fusion = f32[128,1024]{0,1:T(8,128)S(1)} fusion(bf16[4096,1024]{1,0:T(8,128)(2,1)} %all-gather.2.cloned.1.call-done, bf16[1,128,4096]{2,1,0:T(8,128)(2,1)S(1)} %copy-done), kind=kOutput, calls=%fused_computation.58 | convolution fusion | flops 1073741824 | bytes 9961472 | tf_op jit(solution)/shard_map/dot_general | solution.py:78
  378.1 1.2 broadcast_in_dim.38
  379.4 14.9 %all-to-all-start = ((bf16[128,32,1,128]{3,0,2,1:T(8,128)(2,1)}), bf16[128,32,1,128]{3,0,2,1:T(8,128)(2,1)S(1)}, u32[]{:S(2)}, u32[]{:S(2)}) async-start(bf16[128,32,1,128]{3,0,2,1:T(8,128)(2,1)} %bitcast.5), calls=%async_computation | async-start | bytes 2097152 | tf_op jit(solution)/shard_map/all_to_all | solution.py:103
  394.5 24.1 %all-to-all-done = bf16[128,32,1,128]{3,0,2,1:T(8,128)(2,1)S(1)} async-done(((bf16[128,32,1,128]{3,0,2,1:T(8,128)(2,1)}), bf16[128,32,1,128]{3,0,2,1:T(8,128)(2,1)S(1)}, u32[]{:S(2)}, u32[]{:S(2)}) %all-to-all-start) | async-done | bytes 1048608 | tf_op jit(solution)/shard_map/all_to_all | solution.py:103
  418.6 1.2 broadcast_in_dim.39
  419.8 8.5 %all-to-all-start.2 = ((bf16[128,32,1,128]{3,0,2,1:T(8,128)(2,1)}), bf16[128,32,1,128]{3,0,2,1:T(8,128)(2,1)S(1)}, u32[]{:S(2)}, u32[]{:S(2)}) async-start(bf16[128,32,1,128]{3,0,2,1:T(8,128)(2,1)} %bitcast.234), calls=%async_computation.2 | async-start | bytes 2097152 | tf_op jit(solution)/shard_map/all_to_all | solution.py:102
  436.6 1.3 copy.52
  437.9 2.1 fusion.149
  440.6 0.7 slice.215
  441.3 3.6 all-to-all-done.2
  445.0 0.8 slice.218
  445.8 0.9 slice.221
  446.7 0.9 slice.224
  447.7 1.0 slice.227
  448.8 1.0 slice.230
  450.5 1.0 fusion.138
  451.5 0.8 fusion.152
  452.3 1.3 fusion.35
  453.7 1.0 fusion.153
  455.4 1.3 fusion.154
  457.4 1.6 fusion.155
  459.1 0.8 fusion.10
  459.9 1.9 fusion.156
  461.9 1.0 fusion.7
  462.9 2.4 fusion.157
  465.4 1.1 fusion.4
  466.5 2.5 fusion.158
  469.1 1.3 fusion.1
  470.4 3.1 fusion.134
  473.4 2.6 fusion.104
  476.0 1.6 fusion.116
  477.6 1.8 fusion.110
  479.4 2.0 fusion.122
  481.4 2.2 fusion.128
  483.6 2.3 fusion.98
  486.5 2.6 reduce.38
  490.1 23.5 %all_to_all.60 = bf16[32,2,8192]{2,1,0:T(2,128)(2,1)} all-to-all(bf16[32,2,8192]{2,1,0:T(2,128)(2,1)S(1)} %reshape.481), channel_id=1, replica_groups=mesh['seq'=32,'rep'=16] {'seq'}, dimensions={0} | all-to-all | bytes 2097152 | tf_op jit(solution)/shard_map/all_to_all | solution.py:108
  513.5 4.4 reshape.482
  517.9 1.1 copy.57
  519.0 1.6 copy.55
  520.7 1.3 copy.56
  (131 shorter events, 14.1 us)
Async XLA Ops:
  6.5 365.7 %copy-start = (bf16[1,128,4096]{2,1,0:T(8,128)(2,1)S(1)}, bf16[1,128,4096]{2,1,0:T(8,128)(2,1)}, u32[]{:S(2)}) copy-start(bf16[1,128,4096]{2,1,0:T(8,128)(2,1)} %param.5) | copy-start | bytes 3145732
  6.5 193.9 %copy-start.10 = (s32[1,4096]{1,0:T(1,128)S(1)}, s32[1,4096]{1,0:T(1,128)}, u32[]{:S(2)}) copy-start(s32[1,4096]{1,0:T(1,128)} %param.8) | copy-start | bytes 49156
  6.5 190.1 %all-reduce.2.cloned.1.call-start = ((), (), s32[]{:S(2)}) async-start(), calls=%async_computation.4 | async-start | bytes 524288 | tf_op jit(solution)/shard_map/psum | solution.py:16
  8.1 364.2 %all-gather.2.cloned.1.call-start = ((), (), s32[]{:S(2)}) async-start(), calls=%async_computation.5 | async-start | bytes 8650752 | tf_op jit(solution)/shard_map/all_gather | solution.py:77
  202.4 175.7 %all-to-all-start.1 = ((bf16[128,32,1,128]{0,3,2,1:T(8,128)(2,1)}), bf16[128,32,1,128]{0,3,2,1:T(8,128)(2,1)S(1)}, u32[]{:S(2)}, u32[]{:S(2)}) async-start(bf16[128,32,1,128]{0,3,2,1:T(8,128)(2,1)} %maximum_bitcast_fusion), calls=%async_computation.1 | async-start | bytes 2097152 | tf_op jit(solution)/shard_map/all_to_all | solution.py:101
  379.4 39.2 %all-to-all-start = ((bf16[128,32,1,128]{3,0,2,1:T(8,128)(2,1)}), bf16[128,32,1,128]{3,0,2,1:T(8,128)(2,1)S(1)}, u32[]{:S(2)}, u32[]{:S(2)}) async-start(bf16[128,32,1,128]{3,0,2,1:T(8,128)(2,1)} %bitcast.5), calls=%async_computation | async-start | bytes 2097152 | tf_op jit(solution)/shard_map/all_to_all | solution.py:103
  419.8 25.2 %all-to-all-start.2 = ((bf16[128,32,1,128]{3,0,2,1:T(8,128)(2,1)}), bf16[128,32,1,128]{3,0,2,1:T(8,128)(2,1)S(1)}, u32[]{:S(2)}, u32[]{:S(2)}) async-start(bf16[128,32,1,128]{3,0,2,1:T(8,128)(2,1)} %bitcast.234), calls=%async_computation.2 | async-start | bytes 2097152 | tf_op jit(solution)/shard_map/all_to_all | solution.py:102
  447.6 2.3 copy-start.12
  447.7 2.3 copy-start.29
  448.7 1.9 copy-start.13
  448.8 2.8 copy-start.11
  448.8 2.8 copy-start.21
  448.8 2.7 copy-start.28
  448.8 2.7 copy-start.36
  450.3 3.4 copy-start.19
  450.3 3.4 copy-start.27
  450.3 3.3 copy-start.35
  452.3 1.4 copy-start.8
  452.3 2.4 copy-start.37
  453.7 1.6 copy-start.20
  453.7 1.6 copy-start.26
  453.7 1.6 copy-start.34
  454.7 2.0 copy-start.3
  454.7 2.0 copy-start.17
  455.3 2.1 copy-start.16
  455.3 2.1 copy-start.25
  455.3 2.1 copy-start.33
  459.0 2.8 copy-start.2
  459.1 0.9 copy-start.15
  459.1 0.9 copy-start.24
  459.1 0.9 copy-start.32
  461.9 1.0 copy-start.14
  461.9 1.0 copy-start.23
  461.9 1.0 copy-start.31
  465.3 1.1 copy-start.22
  465.3 1.1 copy-start.30
  469.0 1.3 copy-start.38
  469.0 1.3 copy-start.39
  469.0 4.4 copy-start.4
  469.0 4.4 copy-start.18
  470.3 5.7 %copy-start.9 = (bf16[16,128,1,1,128]{4,1,0,3,2:T(8,128)(2,1)S(1)}, bf16[16,128,1,1,128]{4,1,0,3,2:T(8,128)(2,1)}, u32[]{:S(2)}) copy-start(bf16[16,128,1,1,128]{4,1,0,3,2:T(8,128)(2,1)} %slice.221) | copy-start | bytes 1572868
  470.4 7.3 %slice-start = ((s8[5242880]{0:T(1024)(128)(4,1)}), s8[4194304]{0:T(1024)(128)(4,1)S(1)}, s32[]{:S(2)}) async-start(s8[5242880]{0:T(1024)(128)(4,1)} %bitcast.230), calls=%async_computation.6 | async-start | bytes 8388608
  473.4 4.2 slice-start.1
  473.4 4.2 copy-start.7
  477.6 1.8 copy-start.6
  479.4 2.0 copy-start.5
  513.5 8.4 %copy-start.1 = (bf16[1,128,4096]{2,1,0:T(8,128)(2,1)S(1)}, bf16[1,128,4096]{2,1,0:T(8,128)(2,1)}, u32[]{:S(2)}) copy-start(bf16[1,128,4096]{2,1,0:T(8,128)(2,1)} %param.5) | copy-start | bytes 3145732
Sparse Core Ops, SparseCore 0:
  10.3 186.3 all-reduce.1
  198.9 173.2 all-gather.1
where the time goes:
time: 536 us; the launch traced here: 529 us
  waiting for transfers between devices  376 us (70%)
  matrix products  34.2 us (6%)
  starting transfers between devices  33.1 us (6%)
  local copies, waits for them, and re-layouts  29 us (5%)
  blocking collectives  23.5 us (4%)
  other arithmetic  17.7 us (3%)
  between operations  14.8 us (3%)
    psum x1, waiting for transfers between devices, broadcast(): return lax.psum(kept, axis)  189 us
    all_gather x1, waiting for transfers between devices, on_device(): fresh = lax.all_gather(fresh_part, 'seq', axis=0, tiled=True)  160 us
    all_to_all x1, waiting for transfers between devices, on_device(): lax.all_to_all(arrange(value_heads), 'seq', split_axis=1, concat_axis=0,...  24.1 us
    all_to_all x1, blocking collectives, on_device(): lax.all_to_all(mixed, 'seq', split_axis=0, concat_axis=1, tiled=True)  23.5 us
    dot_general x8, matrix products, attend(): jnp.einsum('hqk,khd->qhd', weights, value_all[:row_end], preferred_elemen...  16.5 us
    all_to_all x1, starting transfers between devices, on_device(): lax.all_to_all(arrange(value_heads), 'seq', split_axis=1, concat_axis=0,...  14.9 us
    dot_general x8, matrix products, attend(): jnp.einsum('qhd,khd->hqk', query_all[row_begin:row_end], key_all[:row_end...  11.9 us
  transfers between devices with their start and end apart: 5, of which 4 were waited for; matrix products, arithmetic and copies ran while one was open for 5% of the time, Pallas kernels for 0%

commit v1 on v0

v1 whole, which is shorter than its diff:
```python
import math

import jax
import jax.numpy as jnp
from jax import lax
from jax.experimental import pallas as pl
from jax.experimental.pallas import tpu as pltpu
from jax.sharding import Mesh
from jax.sharding import PartitionSpec as P

HEADS = 32
KV_HEADS = 4
HEAD_DIM = 128
GROUP = HEADS // KV_HEADS
THETA = 1000000.0
BLOCK = 128
LOW = -1e30
DOCS = 6

AXES = ("z1", "z0", "y1", "y0", "zh", "x", "c")
SIZES = (2, 2, 4, 2, 2, 4, 2)
SEQ = ("z1", "z0", "y1", "y0")
REP = ("zh", "x", "c")
Y = ("y1", "y0")
Z = ("z1", "z0")


def ring(size, shift):
    return [(i, (i + shift) % size) for i in range(size)]


def exchange(value, axes):
    return lax.all_to_all(value, axes, split_axis=0, concat_axis=0, tiled=True)


def spread(value, axes, members):
    return exchange(jnp.broadcast_to(value[None], (members,) + value.shape), axes)


def angles_of(positions):
    half = HEAD_DIM // 2
    freqs = THETA ** (-(jnp.arange(half, dtype=jnp.float32) * 2.0) / HEAD_DIM)
    return positions.astype(jnp.float32)[..., None] * freqs


def starts_of(segment_row, segments):
    first = jnp.zeros(segments.shape, jnp.int32)
    for doc in range(1, DOCS):
        begin = jnp.sum((segment_row < doc).astype(jnp.int32))
        first = jnp.where(segments >= doc, begin, first)
    return first


def turn_kernel(q_ref, cos_ref, sin_ref, out_ref):
    half = HEAD_DIM // 2

    @pl.loop(0, 4)
    def _(z):
        cosine, sine = cos_ref[z], sin_ref[z]
        for h in range(GROUP):
            cols = slice(h * HEAD_DIM, (h + 1) * HEAD_DIM)
            t = q_ref[z, :, cols].astype(jnp.float32).T
            a, b = t[:half], t[half:]
            out_ref[z, :half, cols] = (a * cosine - b * sine).astype(jnp.bfloat16)
            out_ref[z, half:, cols] = (b * cosine + a * sine).astype(jnp.bfloat16)


def turn_queries(q, cosine, sine):
    vm = pl.BlockSpec(memory_space=pltpu.VMEM)
    return pl.pallas_call(
        turn_kernel,
        out_shape=jax.ShapeDtypeStruct((4, HEAD_DIM, GROUP * BLOCK), jnp.bfloat16),
        in_specs=[vm] * 3,
        out_specs=vm,
        compiler_params=pltpu.CompilerParams(vmem_limit_bytes=32 * 2**20),
        cost_estimate=pl.CostEstimate(flops=4 * 2**20, bytes_accessed=2 * 2**20, transcendentals=0),
    )(q, cosine, sine)


def attend_kernel(where_ref, q_ref, start_ref, kv_ref, out_ref, acc, top, total):
    factor = math.log2(math.e) / math.sqrt(HEAD_DIM)
    wide = 2 * BLOCK
    y = where_ref[0]

    @pl.loop(0, 4)
    def _(z):
        block = z * 8 + y
        last = block // 2
        first = where_ref[1 + z]
        top[...] = jnp.full(top.shape, LOW, jnp.float32)
        total[...] = jnp.zeros(total.shape, jnp.float32)
        acc[...] = jnp.zeros(acc.shape, jnp.float32)
        start = start_ref[z]

        def pair_step(step, carry):
            pair = last - step
            zz = pair // 4
            y0 = (pair % 4) * 2
            r0, r1 = (y - y0) & 7, (y - y0 - 1) & 7
            key = jnp.concatenate([kv_ref[r0, zz, 0], kv_ref[r1, zz, 0]], axis=0)
            val = jnp.concatenate([kv_ref[r0, zz, 1], kv_ref[r1, zz, 1]], axis=1)
            key_at = pair * wide + lax.broadcasted_iota(jnp.int32, (wide, BLOCK), 0)
            row_at = block * BLOCK + lax.broadcasted_iota(jnp.int32, (wide, BLOCK), 1)
            allowed = (key_at >= start) & (key_at <= row_at)
            for h in range(GROUP):
                cols = slice(h * BLOCK, (h + 1) * BLOCK)
                s = jnp.dot(key, q_ref[z, :, cols], preferred_element_type=jnp.float32)
                s = jnp.where(allowed, s, LOW)
                old = top[:, cols]
                new = jnp.maximum(old, jnp.max(s, axis=0, keepdims=True))
                p = jnp.exp2((s - new) * factor)
                scale = jnp.exp2((old - new) * factor)
                top[:, cols] = new
                total[:, cols] = total[:, cols] * scale + jnp.sum(p, axis=0, keepdims=True)
                acc[:, cols] = acc[:, cols] * scale + jnp.dot(
                    val, p.astype(jnp.bfloat16), preferred_element_type=jnp.float32
                )
            return carry

        lax.fori_loop(0, last - first + 1, pair_step, 0)
        for h in range(GROUP):
            cols = slice(h * BLOCK, (h + 1) * BLOCK)
            mixed = acc[:, cols] / total[:, cols]
            out_ref[z, :, cols] = mixed.T.astype(jnp.bfloat16)


def attend(where, q, start, kv):
    vm = pl.BlockSpec(memory_space=pltpu.VMEM)
    rows = GROUP * BLOCK
    return pl.pallas_call(
        attend_kernel,
        out_shape=jax.ShapeDtypeStruct((4, BLOCK, rows), jnp.bfloat16),
        in_specs=[pl.BlockSpec(memory_space=pltpu.SMEM), vm, vm, vm],
        out_specs=vm,
        scratch_shapes=[
            pltpu.VMEM((HEAD_DIM, rows), jnp.float32),
            pltpu.VMEM((1, rows), jnp.float32),
            pltpu.VMEM((1, rows), jnp.float32),
        ],
        compiler_params=pltpu.CompilerParams(vmem_limit_bytes=32 * 2**20),
        cost_estimate=pl.CostEstimate(
            flops=2 * 2**30, bytes_accessed=4 * 2**20, transcendentals=4 * 2**20
        ),
    )(where, q, start, kv)


def on_device(hidden, queries, weight_copies, segment_ids, owner):
    y, z = lax.axis_index(Y), lax.axis_index(Z)
    x, c = lax.axis_index("x"), lax.axis_index("c")
    half = HEAD_DIM // 2

    pieces = weight_copies[0].reshape(2, 64, 2, 4, 128).transpose(0, 3, 2, 1, 4)
    got = exchange(pieces.reshape(16, 64, 128), REP)
    piece = lax.dynamic_index_in_dim(got, owner[0] % 16, 0, keepdims=False)
    part = spread(piece, ("zh", "z1", "y1"), 16).reshape(16 * 64, 128)
    part = spread(part, ("z0", "y0"), 4)
    mine = part.reshape(2, 2, 2, 2, 4, 64, 128).transpose(3, 0, 4, 1, 2, 5, 6).reshape(4096, 128)
    other = lax.ppermute(mine, "c", ring(2, 1))

    own = hidden[0]
    left = lax.ppermute(own, "x", ring(4, 1))
    right = lax.ppermute(own, "x", ring(4, -1))
    far0 = lax.ppermute(left[:64], "x", ring(4, 1))
    far1 = lax.ppermute(right[64:], "x", ring(4, -1))
    rows = jnp.concatenate([own, left, far0, far1, right], axis=0)

    split = queries[0].reshape(BLOCK, 4, GROUP * HEAD_DIM).transpose(1, 0, 2)
    q_part = exchange(split, Z)

    segment_row = segment_ids[0]
    blocks = segment_row.reshape(4, 8, BLOCK)
    mine_segments = lax.dynamic_index_in_dim(blocks, y, 1, keepdims=False)
    start = starts_of(segment_row, mine_segments)
    token = (jnp.arange(4)[:, None] * 8 + y) * BLOCK + jnp.arange(BLOCK)[None]
    positions = (token - start).astype(jnp.int32)
    q_angles = jnp.swapaxes(angles_of(positions), 1, 2)
    q_turned = turn_queries(q_part, jnp.cos(q_angles), jnp.sin(q_angles))
    own_positions = lax.dynamic_index_in_dim(positions, z, 0, keepdims=False)
    k_angles = angles_of(lax.all_gather(own_positions, "x", axis=0))

    first = jnp.dot(rows, mine, preferred_element_type=jnp.float32)
    second = jnp.dot(rows, other, preferred_element_type=jnp.float32)
    order = (x - jnp.arange(4)) % 4
    first = first.reshape(4, BLOCK, HEAD_DIM)[order]
    second = second.reshape(4, BLOCK, HEAD_DIM)[order]
    key = jnp.where(c == 0, first, second)
    value = jnp.where(c == 0, second, first).astype(jnp.bfloat16)
    cosine, sine = jnp.cos(k_angles), jnp.sin(k_angles)
    a, b = key[..., :half], key[..., half:]
    key = jnp.concatenate([a * cosine - b * sine, b * cosine + a * sine], axis=-1)
    both = jnp.stack([key.astype(jnp.bfloat16), jnp.swapaxes(value, 1, 2)], axis=1)
    kv = exchange(exchange(both, "x"), Z)

    up1 = lax.ppermute(kv, Y, ring(8, 1))
    down1 = lax.ppermute(kv, Y, ring(8, -1))
    up2 = lax.ppermute(up1, Y, ring(8, 1))
    down2 = lax.ppermute(down1, Y, ring(8, -1))
    up3 = lax.ppermute(up2, Y, ring(8, 1))
    down3 = lax.ppermute(down2, Y, ring(8, -1))
    up4 = lax.ppermute(up3, Y, ring(8, 1))
    kv_all = jnp.stack([kv, up1, up2, up3, up4, down3, down2, down1])

    where = jnp.concatenate([y[None], start[:, 0] // (2 * BLOCK)]).astype(jnp.int32)
    mixed = attend(where, q_turned, start[:, None, :], kv_all)
    back = exchange(mixed, Z)
    return back.transpose(1, 0, 2).reshape(1, BLOCK, HEADS * HEAD_DIM)


def solution(mesh):
    fine = Mesh(mesh.devices.reshape(SIZES), AXES)
    placed = (
        P(REP, SEQ, None),
        P(REP, SEQ, None),
        P(REP, SEQ, None),
        P(REP, None),
        P(),
    )
    return jax.shard_map(
        on_device, mesh=fine, in_specs=placed, out_specs=P(REP, SEQ, None), check_vma=False
    )
```

time: 536 us -> 212 us (0.40)
  waiting for transfers between devices: 376 us -> 44.8 us
  starting transfers between devices: 33.1 us -> 72.9 us
  blocking collectives: 23.5 us -> 52 us
  matrix products: 34.2 us -> 6.88 us
  between operations: 14.8 us -> 1.08 us
  other arithmetic: 17.7 us -> 5.23 us
  local copies, waits for them, and re-layouts: 29 us -> 18.4 us
  Pallas kernels: 0 us -> 7.68 us
    psum x1 -> x0, waiting for transfers between devices: 189 us -> none  [broadcast(): return lax.psum(kept, axis)]
    all_gather x1 -> x0, waiting for transfers between devices: 160 us -> none  [on_device(): fresh = lax.all_gather(fresh_part, 'seq', axis=0, tiled=True)]
    ppermute x0 -> x12, starting transfers between devices: none -> 35.6 us  [the longest x1 5.38 us: on_device(): up4 = lax.ppermute(up3, Y, ring(8, 1))]
    dot_general x17 -> x2, matrix products: 34.2 us -> 6.88 us  [the longest x1 3.44 us: on_device(): second = jnp.dot(rows, other, preferred_element_type=jnp.float32)]
    ppermute x0 -> x12, waiting for transfers between devices: none -> 22.4 us  [the longest x1 6.54 us: on_device(): up1 = lax.ppermute(kv, Y, ring(8, 1))]
    all_gather x0 -> x1, blocking collectives: none -> 15.6 us  [on_device(): k_angles = angles_of(lax.all_gather(own_positions, 'x', axis=0))]
    all_to_all x1 -> x2, blocking collectives: 23.5 us -> 36.3 us  [exchange(): return lax.all_to_all(value, axes, split_axis=0, concat_axis=0, tiled=True)]
    slice x24 -> x3, local copies, waits for them, and re-layouts: 12.6 us -> 1.77 us  [the longest x1 0.83 us: on_device(): far1 = lax.ppermute(right[64:], 'x', ring(4, -1))]
  transfers between devices with their start and end apart: 5 -> 17, of which waited for: 4 -> 9; matrix products, arithmetic and copies ran while one was open for 5% -> 10% of each run, Pallas kernels for 0% -> 0%
where the time goes in v1:
time: 212 us; the launch traced here: 209 us
  starting transfers between devices  72.9 us (34%)
  blocking collectives  52 us (25%)
  waiting for transfers between devices  44.8 us (21%)
  local copies, waits for them, and re-layouts  18.4 us (9%)
  Pallas kernels  7.68 us (4%)
  matrix products  6.88 us (3%)
  other arithmetic  5.23 us (2%)
    all_to_all x5, starting transfers between devices, exchange(): return lax.all_to_all(value, axes, split_axis=0, concat_axis=0, tiled=True)  37.2 us
    all_to_all x2, blocking collectives, exchange(): return lax.all_to_all(value, axes, split_axis=0, concat_axis=0, tiled=True)  36.3 us
    all_to_all x5, waiting for transfers between devices, exchange(): return lax.all_to_all(value, axes, split_axis=0, concat_axis=0, tiled=True)  22.4 us
    all_gather x1, blocking collectives, on_device(): k_angles = angles_of(lax.all_gather(own_positions, 'x', axis=0))  15.6 us
    pallas_call x1, Pallas kernels, attend(): pl.pallas_call(attend_kernel, out_shape=jax.ShapeDtypeStruct((4, BLOCK, r...  7.02 us
    unnamed x19, local copies, waits for them, and re-layouts  6.81 us
    ppermute x1, waiting for transfers between devices, on_device(): up1 = lax.ppermute(kv, Y, ring(8, 1))  6.54 us
    ppermute x1, waiting for transfers between devices, on_device(): far1 = lax.ppermute(right[64:], 'x', ring(4, -1))  6.32 us
  transfers between devices with their start and end apart: 17, of which 9 were waited for; matrix products, arithmetic and copies ran while one was open for 10% of the time, Pallas kernels for 0%

profile of v1, /device:TPU:56, one launch (start us, length us, event | category | flops | bytes accessed | tf_op | source)
XLA Modules:
  0.0 208.9 jit_solution(7930182556941167616)
XLA Ops:
  0.0 1.2 reshape_squeeze.11
  1.2 0.8 copy.30
  2.0 12.8 %all-to-all-start.1 = ((bf16[16,64,128]{2,1,0:T(8,128)(2,1)}), bf16[16,64,128]{2,1,0:T(8,128)(2,1)S(1)}, u32[]{:S(2)}, u32[]{:S(2)}) async-start(bf16[16,64,128]{2,1,0:T(8,128)(2,1)} %bitcast.8), calls=%async_computation.1 | async-start | bytes 524288 | tf_op jit(solution)/shard_map/all_to_all | solution.py:33
  14.8 3.8 %collective-permute-start = (bf16[128,4096]{1,0:T(8,128)(2,1)}, bf16[128,4096]{1,0:T(8,128)(2,1)S(1)}, u32[]{:S(2)}, u32[]{:S(2)}) collective-permute-start(bf16[128,4096]{1,0:T(8,128)(2,1)} %bitcast.69), channel_id=1, source_target_pairs={{0,2},{2,4},{4,6},{6,0},{1,3},{3,5},{5,7},{7,1},{8,10},{10,12},{12... | collective-permute-start | bytes 3145736 | tf_op jit(solution)/shard_map/ppermute | solution.py:161
  18.7 3.2 %collective-permute-start.2 = (bf16[128,4096]{1,0:T(8,128)(2,1)}, bf16[128,4096]{1,0:T(8,128)(2,1)S(1)}, u32[]{:S(2)}, u32[]{:S(2)}) collective-permute-start(bf16[128,4096]{1,0:T(8,128)(2,1)} %bitcast.70), channel_id=1, source_target_pairs={{0,6},{2,0},{4,2},{6,4},{1,7},{3,1},{5,3},{7,5},{8,14},{10,8},{12,... | collective-permute-start | bytes 3145736 | tf_op jit(solution)/shard_map/ppermute | solution.py:162
  22.6 4.3 %all-to-all-done.1 = bf16[16,64,128]{2,1,0:T(8,128)(2,1)S(1)} async-done(((bf16[16,64,128]{2,1,0:T(8,128)(2,1)}), bf16[16,64,128]{2,1,0:T(8,128)(2,1)S(1)}, u32[]{:S(2)}, u32[]{:S(2)}) %all-to-all-start.1) | async-done | bytes 262176 | tf_op jit(solution)/shard_map/all_to_all | solution.py:33
  26.9 0.8 broadcast_in_dim.60
  27.7 11.5 %all-to-all-start.2 = ((bf16[16,64,128]{2,1,0:T(8,128)(2,1)}), bf16[16,64,128]{2,1,0:T(8,128)(2,1)S(1)}, u32[]{:S(2)}, u32[]{:S(2)}) async-start(bf16[16,64,128]{2,1,0:T(8,128)(2,1)} %broadcast_in_dim.60), calls=%async_computation.2 | async-start | bytes 524288 | tf_op jit(solution)/shard_map/all_to_all | solution.py:33
  39.2 1.0 constant_dynamic-update-slice_fusion.4
  40.3 0.8 fusion.13
  41.0 9.7 %all-to-all-done.2 = bf16[16,64,128]{2,1,0:T(8,128)(2,1)S(1)} async-done(((bf16[16,64,128]{2,1,0:T(8,128)(2,1)}), bf16[16,64,128]{2,1,0:T(8,128)(2,1)S(1)}, u32[]{:S(2)}, u32[]{:S(2)}) %all-to-all-start.2) | async-done | bytes 262176 | tf_op jit(solution)/shard_map/all_to_all | solution.py:33
  50.8 1.1 broadcast_in_dim.62
  51.9 5.5 %all-to-all-start.3 = ((bf16[4,1024,128]{2,1,0:T(8,128)(2,1)}), bf16[4,1024,128]{2,1,0:T(8,128)(2,1)S(1)}, u32[]{:S(2)}, u32[]{:S(2)}) async-start(bf16[4,1024,128]{2,1,0:T(8,128)(2,1)} %broadcast_in_dim.62), calls=%async_computation.3 | async-start | bytes 2097152 | tf_op jit(solution)/shard_map/all_to_all | solution.py:33
  57.4 3.1 %compare_select_fusion.4.start_ref = s32[4,1,128]{2,1,0:T(1,128)S(1)} fusion(s32[4,8,128]{2,1,0:T(8,128)S(1)} %bitcast.73, s32[]{:T(128)S(6)} %select_n.112, s32[]{:T(128)} %get-tuple-element.7, s32[]{:T(128)} %get-tuple-element.6, s32[]{:T(128)} %get-tuple-element.8, s32[]{:T(128)} %get-tuple-element.9, s32[]{:T(128)} %get-tuple-element.5), kind=kLoop, calls=%fused_computation.49 | loop fusion | flops 5120 | bytes 4120 | tf_op jit(solution)/shard_map/jit(_where)/select_n | solution.py:50
  60.5 0.8 slice.24
  61.4 1.9 collective-permute-start.1
  63.3 15.6 %all-gather = s32[4,1,128]{2,1,0:T(1,128)S(1)} all-gather(s32[1,1,128]{2,1,0:T(1,128)S(1)} %fusion.16), channel_id=1, replica_groups=mesh['z1'=2,'z0'=2,'y1'=4,'y0'=2,'zh'=2,'x'=4,'c'=2] {'x'}, dimensions={0}, use_global_device_ids=true | all-gather | bytes 2560 | tf_op jit(solution)/shard_map/all_gather | solution.py:179
  78.9 0.8 slice.25
  79.8 1.9 collective-permute-start.3
  81.7 1.1 constant_dynamic-update-slice_fusion.3
  82.8 1.9 constant_dynamic-update-slice_fusion.2
  84.7 1.9 collective-permute-start.4
  86.7 6.3 %collective-permute-done.3 = bf16[64,4096]{1,0:T(8,128)(2,1)} collective-permute-done((bf16[64,4096]{1,0:T(8,128)(2,1)}, bf16[64,4096]{1,0:T(8,128)(2,1)}, u32[]{:S(2)}, u32[]{:S(2)}) %collective-permute-start.3) | collective-permute-done | bytes 524320 | tf_op jit(solution)/shard_map/ppermute | solution.py:164
  93.0 1.9 constant_dynamic-update-slice_fusion.1
  94.9 1.1 constant_dynamic-update-slice_fusion
  95.9 3.4 %fusion.20 = f32[4,128,128]{2,1,0:T(8,128)S(1)} fusion(bf16[4,128,4096]{2,1,0:T(8,128)(2,1)} %bitcast.61, bf16[4096,128,1]{1,0,2:T(8,128)(2,1)S(1)} %bitcast.67), kind=kOutput, calls=%fused_computation.69 | convolution fusion | flops 536870912 | bytes 5505024 | tf_op jit(solution)/shard_map/dot_general | solution.py:181
  100.1 3.4 %fusion.21 = f32[512,128]{1,0:T(8,128)S(1)} fusion(bf16[512,4096]{1,0:T(8,128)(2,1)} %constant_dynamic-update-slice_fusion, bf16[4096,128]{1,0:T(8,128)(2,1)S(1)} %collective-permute-done.4), kind=kOutput, calls=%fused_computation.70 | convolution fusion | flops 536870912 | bytes 5505024 | tf_op jit(solution)/shard_map/dot_general | solution.py:182
  105.1 9.7 %all_to_all.35 = bf16[4,2,128,128]{3,2,1,0:T(8,128)(2,1)} all-to-all(bf16[4,2,128,128]{3,2,1,0:T(8,128)(2,1)S(1)} %pad_maximum_fusion), channel_id=1, replica_groups=mesh['z1'=2,'z0'=2,'y1'=4,'y0'=2,'zh'=2,'x'=4,'c'=2] {'x'}, dimensions={0} | all-to-all | bytes 524288 | tf_op jit(solution)/shard_map/all_to_all | solution.py:33
  114.8 3.9 %all-to-all-start.5 = ((bf16[4,2,128,128]{3,2,1,0:T(8,128)(2,1)}), bf16[4,2,128,128]{3,2,1,0:T(8,128)(2,1)S(1)}, u32[]{:S(2)}, u32[]{:S(2)}) async-start(bf16[4,2,128,128]{3,2,1,0:T(8,128)(2,1)} %all_to_all.35), calls=%async_computation.5 | async-start | bytes 524288 | tf_op jit(solution)/shard_map/all_to_all | solution.py:33
  118.7 0.7 copy.28
  119.4 1.3 copy.29
  120.7 4.8 %all-to-all-done.5 = bf16[4,2,128,128]{3,2,1,0:T(8,128)(2,1)S(1)} async-done(((bf16[4,2,128,128]{3,2,1,0:T(8,128)(2,1)}), bf16[4,2,128,128]{3,2,1,0:T(8,128)(2,1)S(1)}, u32[]{:S(2)}, u32[]{:S(2)}) %all-to-all-start.5) | async-done | bytes 262176 | tf_op jit(solution)/shard_map/all_to_all | solution.py:33
  125.5 3.5 %all-to-all-start = ((bf16[4,128,1024]{2,1,0:T(8,128)(2,1)}), bf16[4,128,1024]{2,1,0:T(8,128)(2,1)S(1)}, u32[]{:S(2)}, u32[]{:S(2)}) async-start(bf16[4,128,1024]{2,1,0:T(8,128)(2,1)} %bitcast.4), calls=%async_computation | async-start | bytes 2097152 | tf_op jit(solution)/shard_map/all_to_all | solution.py:33
  129.0 3.6 %collective-permute-start.5 = (bf16[4,2,128,128]{3,2,1,0:T(8,128)(2,1)S(1)}, bf16[4,2,128,128]{3,2,1,0:T(8,128)(2,1)S(1)}, u32[]{:S(2)}, u32[]{:S(2)}) collective-permute-start(bf16[4,2,128,128]{3,2,1,0:T(8,128)(2,1)S(1)} %all-to-all-done.5), channel_id=1, source_target_pairs={{0,16},{16,32},{32,48},{48,64},{64,80},{80,96},{96,112},{112,0},{1... | collective-permute-start | bytes 786440 | tf_op jit(solution)/shard_map/ppermute | solution.py:194
  133.3 6.5 %collective-permute-done.5 = bf16[4,2,128,128]{3,2,1,0:T(8,128)(2,1)S(1)} collective-permute-done((bf16[4,2,128,128]{3,2,1,0:T(8,128)(2,1)S(1)}, bf16[4,2,128,128]{3,2,1,0:T(8,128)(2,1)S(1)}, u32[]{:S(2)}, u32[]{:S(2)}) %collective-permute-start.5) | collective-permute-done | bytes 262176 | tf_op jit(solution)/shard_map/ppermute | solution.py:194
  139.8 2.9 %collective-permute-start.6 = (bf16[4,2,128,128]{3,2,1,0:T(8,128)(2,1)S(1)}, bf16[4,2,128,128]{3,2,1,0:T(8,128)(2,1)S(1)}, u32[]{:S(2)}, u32[]{:S(2)}) collective-permute-start(bf16[4,2,128,128]{3,2,1,0:T(8,128)(2,1)S(1)} %collective-permute-done.5), channel_id=1, source_target_pairs={{0,16},{16,32},{32,48},{48,64},{64,80},{80,96},{96,112},{112,0},{1... | collective-permute-start | bytes 786440 | tf_op jit(solution)/shard_map/ppermute | solution.py:196
  142.8 2.9 %collective-permute-start.9 = (bf16[4,2,128,128]{3,2,1,0:T(8,128)(2,1)S(1)}, bf16[4,2,128,128]{3,2,1,0:T(8,128)(2,1)S(1)}, u32[]{:S(2)}, u32[]{:S(2)}) collective-permute-start(bf16[4,2,128,128]{3,2,1,0:T(8,128)(2,1)S(1)} %all-to-all-done.5), channel_id=1, source_target_pairs={{0,112},{16,0},{32,16},{48,32},{64,48},{80,64},{96,80},{112,96},{1... | collective-permute-start | bytes 786440 | tf_op jit(solution)/shard_map/ppermute | solution.py:195
  145.8 3.6 %all-to-all-done.q_ref = bf16[4,128,1024]{2,1,0:T(8,128)(2,1)S(1)} async-done(((bf16[4,128,1024]{2,1,0:T(8,128)(2,1)}), bf16[4,128,1024]{2,1,0:T(8,128)(2,1)S(1)}, u32[]{:S(2)}, u32[]{:S(2)}) %all-to-all-start) | async-done | bytes 1048608 | tf_op jit(solution)/shard_map/all_to_all | solution.py:33
  150.0 4.2 %collective-permute-start.7 = (bf16[4,2,128,128]{3,2,1,0:T(8,128)(2,1)S(1)}, bf16[4,2,128,128]{3,2,1,0:T(8,128)(2,1)S(1)}, u32[]{:S(2)}, u32[]{:S(2)}) collective-permute-start(bf16[4,2,128,128]{3,2,1,0:T(8,128)(2,1)S(1)} %collective-permute-done.6), channel_id=1, source_target_pairs={{0,16},{16,32},{32,48},{48,64},{64,80},{80,96},{96,112},{112,0},{1... | collective-permute-start | bytes 786440 | tf_op jit(solution)/shard_map/ppermute | solution.py:198
  154.2 1.9 collective-permute-start.10
  156.2 2.1 collective-permute-done.7
  158.3 5.4 %collective-permute-start.8 = (bf16[4,2,128,128]{3,2,1,0:T(8,128)(2,1)S(1)}, bf16[4,2,128,128]{3,2,1,0:T(8,128)(2,1)S(1)}, u32[]{:S(2)}, u32[]{:S(2)}) collective-permute-start(bf16[4,2,128,128]{3,2,1,0:T(8,128)(2,1)S(1)} %collective-permute-done.7), channel_id=1, source_target_pairs={{0,16},{16,32},{32,48},{48,64},{64,80},{80,96},{96,112},{112,0},{1... | collective-permute-start | bytes 786440 | tf_op jit(solution)/shard_map/ppermute | solution.py:200
  163.7 1.9 collective-permute-start.11
  165.7 1.8 collective-permute-done.8
  167.6 5.6 %collective-permute-done.11 = bf16[4,2,128,128]{3,2,1,0:T(8,128)(2,1)S(1)} collective-permute-done((bf16[4,2,128,128]{3,2,1,0:T(8,128)(2,1)S(1)}, bf16[4,2,128,128]{3,2,1,0:T(8,128)(2,1)S(1)}, u32[]{:S(2)}, u32[]{:S(2)}) %collective-permute-start.11) | collective-permute-done | bytes 262176 | tf_op jit(solution)/shard_map/ppermute | solution.py:199
  173.3 7.0 %shard_map.56 = bf16[4,128,1024]{2,1,0:T(8,128)(2,1)S(1)} custom-call(s32[5]{0:T(128)S(1)} %pad_add_fusion.where_ref, bf16[4,128,1024]{2,1,0:T(8,128)(2,1)S(1)} %shard_map.55.q_ref, s32[4,1,128]{2,1,0:T(1,128)S(1)} %compare_select_fusion.4.start_ref, bf16[8,4,2,128,128]{4,3,2,1,0:T(8,128)(2,1)S(1)} %bitcast_dynamic-update-slice_fusion.kv_ref), custom_call_target="tpu_custom_call" | custom-call | flops 2147483648 | bytes 4194304 | tf_op jit(solution)/shard_map/pallas_call | solution.py:130
  180.3 26.6 %all_to_all.36 = bf16[4,128,1024]{2,1,0:T(8,128)(2,1)S(1)} all-to-all(bf16[4,128,1024]{2,1,0:T(8,128)(2,1)S(1)} %shard_map.56), channel_id=1, replica_groups=mesh['z1'=2,'z0'=2,'y1'=4,'y0'=2,'zh'=2,'x'=4,'c'=2] {'z1','z0'}, dimensions={0} | all-to-all | bytes 2097152 | tf_op jit(solution)/shard_map/all_to_all | solution.py:33
  207.6 1.3 copy.38
  (47 shorter events, 4.8 us)
Async XLA Ops:
  0.0 39.2 %copy-start = (bf16[1,128,4096]{2,1,0:T(8,128)(2,1)S(1)}, bf16[1,128,4096]{2,1,0:T(8,128)(2,1)}, u32[]{:S(2)}) copy-start(bf16[1,128,4096]{2,1,0:T(8,128)(2,1)} %param.5) | copy-start | bytes 3145732
  1.2 39.0 %copy-start.2 = (s32[1,4096]{1,0:T(1,128)S(1)}, s32[1,4096]{1,0:T(1,128)}, u32[]{:S(2)}) copy-start(s32[1,4096]{1,0:T(1,128)} %param.8) | copy-start | bytes 49156
  2.0 24.9 %all-to-all-start.1 = ((bf16[16,64,128]{2,1,0:T(8,128)(2,1)}), bf16[16,64,128]{2,1,0:T(8,128)(2,1)S(1)}, u32[]{:S(2)}, u32[]{:S(2)}) async-start(bf16[16,64,128]{2,1,0:T(8,128)(2,1)} %bitcast.8), calls=%async_computation.1 | async-start | bytes 524288 | tf_op jit(solution)/shard_map/all_to_all | solution.py:33
  14.8 45.7 %collective-permute-start = (bf16[128,4096]{1,0:T(8,128)(2,1)}, bf16[128,4096]{1,0:T(8,128)(2,1)S(1)}, u32[]{:S(2)}, u32[]{:S(2)}) collective-permute-start(bf16[128,4096]{1,0:T(8,128)(2,1)} %bitcast.69), channel_id=1, source_target_pairs={{0,2},{2,4},{4,6},{6,0},{1,3},{3,5},{5,7},{7,1},{8,10},{10,12},{12... | collective-permute-start | bytes 3145736 | tf_op jit(solution)/shard_map/ppermute | solution.py:161
  18.7 60.3 %collective-permute-start.2 = (bf16[128,4096]{1,0:T(8,128)(2,1)}, bf16[128,4096]{1,0:T(8,128)(2,1)S(1)}, u32[]{:S(2)}, u32[]{:S(2)}) collective-permute-start(bf16[128,4096]{1,0:T(8,128)(2,1)} %bitcast.70), channel_id=1, source_target_pairs={{0,6},{2,0},{4,2},{6,4},{1,7},{3,1},{5,3},{7,5},{8,14},{10,8},{12,... | collective-permute-start | bytes 3145736 | tf_op jit(solution)/shard_map/ppermute | solution.py:162
  27.7 23.1 %all-to-all-start.2 = ((bf16[16,64,128]{2,1,0:T(8,128)(2,1)}), bf16[16,64,128]{2,1,0:T(8,128)(2,1)S(1)}, u32[]{:S(2)}, u32[]{:S(2)}) async-start(bf16[16,64,128]{2,1,0:T(8,128)(2,1)} %broadcast_in_dim.60), calls=%async_computation.2 | async-start | bytes 524288 | tf_op jit(solution)/shard_map/all_to_all | solution.py:33
  51.9 32.8 %all-to-all-start.3 = ((bf16[4,1024,128]{2,1,0:T(8,128)(2,1)}), bf16[4,1024,128]{2,1,0:T(8,128)(2,1)S(1)}, u32[]{:S(2)}, u32[]{:S(2)}) async-start(bf16[4,1024,128]{2,1,0:T(8,128)(2,1)} %broadcast_in_dim.62), calls=%async_computation.3 | async-start | bytes 2097152 | tf_op jit(solution)/shard_map/all_to_all | solution.py:33
  61.4 21.4 %collective-permute-start.1 = (bf16[64,4096]{1,0:T(8,128)(2,1)}, bf16[64,4096]{1,0:T(8,128)(2,1)}, u32[]{:S(2)}, u32[]{:S(2)}) collective-permute-start(bf16[64,4096]{1,0:T(8,128)(2,1)} %slice.24), channel_id=1, source_target_pairs={{0,2},{2,4},{4,6},{6,0},{1,3},{3,5},{5,7},{7,1},{8,10},{10,12},{12... | collective-permute-start | bytes 1572872 | tf_op jit(solution)/shard_map/ppermute | solution.py:163
  79.8 13.2 %collective-permute-start.3 = (bf16[64,4096]{1,0:T(8,128)(2,1)}, bf16[64,4096]{1,0:T(8,128)(2,1)}, u32[]{:S(2)}, u32[]{:S(2)}) collective-permute-start(bf16[64,4096]{1,0:T(8,128)(2,1)} %slice.25), channel_id=1, source_target_pairs={{0,6},{2,0},{4,2},{6,4},{1,7},{3,1},{5,3},{7,5},{8,14},{10,8},{12,... | collective-permute-start | bytes 1572872 | tf_op jit(solution)/shard_map/ppermute | solution.py:164
  84.7 15.4 %collective-permute-start.4 = (bf16[4096,128]{1,0:T(8,128)(2,1)S(1)}, bf16[4096,128]{1,0:T(8,128)(2,1)S(1)}, u32[]{:S(2)}, u32[]{:S(2)}) collective-permute-start(bf16[4096,128]{1,0:T(8,128)(2,1)S(1)} %bitcast.66), channel_id=1, source_target_pairs={{0,1},{1,0},{2,3},{3,2},{4,5},{5,4},{6,7},{7,6},{8,9},{9,8},{10,11... | collective-permute-start | bytes 3145736 | tf_op jit(solution)/shard_map/ppermute | solution.py:158
  104.3 14.5 %copy-start.1 = (bf16[1,128,4096]{2,1,0:T(8,128)(2,1)S(1)}, bf16[1,128,4096]{2,1,0:T(8,128)(2,1)}, u32[]{:S(2)}) copy-start(bf16[1,128,4096]{2,1,0:T(8,128)(2,1)} %param.6) | copy-start | bytes 3145732
  114.8 10.7 %all-to-all-start.5 = ((bf16[4,2,128,128]{3,2,1,0:T(8,128)(2,1)}), bf16[4,2,128,128]{3,2,1,0:T(8,128)(2,1)S(1)}, u32[]{:S(2)}, u32[]{:S(2)}) async-start(bf16[4,2,128,128]{3,2,1,0:T(8,128)(2,1)} %all_to_all.35), calls=%async_computation.5 | async-start | bytes 524288 | tf_op jit(solution)/shard_map/all_to_all | solution.py:33
  125.5 23.8 %all-to-all-start = ((bf16[4,128,1024]{2,1,0:T(8,128)(2,1)}), bf16[4,128,1024]{2,1,0:T(8,128)(2,1)S(1)}, u32[]{:S(2)}, u32[]{:S(2)}) async-start(bf16[4,128,1024]{2,1,0:T(8,128)(2,1)} %bitcast.4), calls=%async_computation | async-start | bytes 2097152 | tf_op jit(solution)/shard_map/all_to_all | solution.py:33
  129.0 10.8 %collective-permute-start.5 = (bf16[4,2,128,128]{3,2,1,0:T(8,128)(2,1)S(1)}, bf16[4,2,128,128]{3,2,1,0:T(8,128)(2,1)S(1)}, u32[]{:S(2)}, u32[]{:S(2)}) collective-permute-start(bf16[4,2,128,128]{3,2,1,0:T(8,128)(2,1)S(1)} %all-to-all-done.5), channel_id=1, source_target_pairs={{0,16},{16,32},{32,48},{48,64},{64,80},{80,96},{96,112},{112,0},{1... | collective-permute-start | bytes 786440 | tf_op jit(solution)/shard_map/ppermute | solution.py:194
  139.8 10.2 %collective-permute-start.6 = (bf16[4,2,128,128]{3,2,1,0:T(8,128)(2,1)S(1)}, bf16[4,2,128,128]{3,2,1,0:T(8,128)(2,1)S(1)}, u32[]{:S(2)}, u32[]{:S(2)}) collective-permute-start(bf16[4,2,128,128]{3,2,1,0:T(8,128)(2,1)S(1)} %collective-permute-done.5), channel_id=1, source_target_pairs={{0,16},{16,32},{32,48},{48,64},{64,80},{80,96},{96,112},{112,0},{1... | collective-permute-start | bytes 786440 | tf_op jit(solution)/shard_map/ppermute | solution.py:196
  142.8 11.5 %collective-permute-start.9 = (bf16[4,2,128,128]{3,2,1,0:T(8,128)(2,1)S(1)}, bf16[4,2,128,128]{3,2,1,0:T(8,128)(2,1)S(1)}, u32[]{:S(2)}, u32[]{:S(2)}) collective-permute-start(bf16[4,2,128,128]{3,2,1,0:T(8,128)(2,1)S(1)} %all-to-all-done.5), channel_id=1, source_target_pairs={{0,112},{16,0},{32,16},{48,32},{64,48},{80,64},{96,80},{112,96},{1... | collective-permute-start | bytes 786440 | tf_op jit(solution)/shard_map/ppermute | solution.py:195
  150.0 8.3 %collective-permute-start.7 = (bf16[4,2,128,128]{3,2,1,0:T(8,128)(2,1)S(1)}, bf16[4,2,128,128]{3,2,1,0:T(8,128)(2,1)S(1)}, u32[]{:S(2)}, u32[]{:S(2)}) collective-permute-start(bf16[4,2,128,128]{3,2,1,0:T(8,128)(2,1)S(1)} %collective-permute-done.6), channel_id=1, source_target_pairs={{0,16},{16,32},{32,48},{48,64},{64,80},{80,96},{96,112},{112,0},{1... | collective-permute-start | bytes 786440 | tf_op jit(solution)/shard_map/ppermute | solution.py:198
  154.2 9.5 %collective-permute-start.10 = (bf16[4,2,128,128]{3,2,1,0:T(8,128)(2,1)S(1)}, bf16[4,2,128,128]{3,2,1,0:T(8,128)(2,1)S(1)}, u32[]{:S(2)}, u32[]{:S(2)}) collective-permute-start(bf16[4,2,128,128]{3,2,1,0:T(8,128)(2,1)S(1)} %collective-permute-done.9), channel_id=1, source_target_pairs={{0,112},{16,0},{32,16},{48,32},{64,48},{80,64},{96,80},{112,96},{1... | collective-permute-start | bytes 786440 | tf_op jit(solution)/shard_map/ppermute | solution.py:197
  158.3 9.3 %collective-permute-start.8 = (bf16[4,2,128,128]{3,2,1,0:T(8,128)(2,1)S(1)}, bf16[4,2,128,128]{3,2,1,0:T(8,128)(2,1)S(1)}, u32[]{:S(2)}, u32[]{:S(2)}) collective-permute-start(bf16[4,2,128,128]{3,2,1,0:T(8,128)(2,1)S(1)} %collective-permute-done.7), channel_id=1, source_target_pairs={{0,16},{16,32},{32,48},{48,64},{64,80},{80,96},{96,112},{112,0},{1... | collective-permute-start | bytes 786440 | tf_op jit(solution)/shard_map/ppermute | solution.py:200
  163.7 9.5 %collective-permute-start.11 = (bf16[4,2,128,128]{3,2,1,0:T(8,128)(2,1)S(1)}, bf16[4,2,128,128]{3,2,1,0:T(8,128)(2,1)S(1)}, u32[]{:S(2)}, u32[]{:S(2)}) collective-permute-start(bf16[4,2,128,128]{3,2,1,0:T(8,128)(2,1)S(1)} %collective-permute-done.10), channel_id=1, source_target_pairs={{0,112},{16,0},{32,16},{48,32},{64,48},{80,64},{96,80},{112,96},{1... | collective-permute-start | bytes 786440 | tf_op jit(solution)/shard_map/ppermute | solution.py:199

commit v2 on v1

v2 whole, which is shorter than its diff:
```python
import functools
import math

import jax
import jax.numpy as jnp
from jax import lax
from jax.experimental import pallas as pl
from jax.experimental.pallas import tpu as pltpu
from jax.sharding import Mesh
from jax.sharding import PartitionSpec as P

HEADS = 32
KV_HEADS = 4
HEAD_DIM = 128
GROUP = HEADS // KV_HEADS
THETA = 1000000.0
BLOCK = 128
LOW = -1e30
DOCS = 6

AXES = ("z1", "z0", "y1", "y0", "zh", "x", "c")
SIZES = (2, 2, 4, 2, 2, 4, 2)
SEQ = ("z1", "z0", "y1", "y0")
REP = ("zh", "x", "c")
Y = ("y1", "y0")
Z = ("z1", "z0")


def ring(size, shift):
    return [(i, (i + shift) % size) for i in range(size)]


def pick(value, index, axis=0):
    return lax.dynamic_index_in_dim(value, index, axis, keepdims=False)


def exchange(value, axes):
    return lax.all_to_all(value, axes, split_axis=0, concat_axis=0, tiled=True)


def spread(value, axes, members):
    return exchange(jnp.broadcast_to(value[None], (members,) + value.shape), axes)


def angles_of(positions):
    half = HEAD_DIM // 2
    freqs = THETA ** (-(jnp.arange(half, dtype=jnp.float32) * 2.0) / HEAD_DIM)
    return positions.astype(jnp.float32)[..., None] * freqs


def starts_of(segment_row, segments):
    first = jnp.zeros(segments.shape, jnp.int32)
    for doc in range(1, DOCS):
        begin = jnp.sum((segment_row < doc).astype(jnp.int32))
        first = jnp.where(segments >= doc, begin, first)
    return first


VMEM = pl.BlockSpec(memory_space=pltpu.VMEM)
SMEM = pl.BlockSpec(memory_space=pltpu.SMEM)


def call(kernel, out_shape, specs, cost, scratch=()):
    flops, moved = cost
    return pl.pallas_call(
        kernel,
        out_shape=out_shape,
        in_specs=specs,
        out_specs=jax.tree.map(lambda _: VMEM, out_shape),
        scratch_shapes=list(scratch),
        compiler_params=pltpu.CompilerParams(vmem_limit_bytes=32 * 2**20),
        cost_estimate=pl.CostEstimate(flops=flops, bytes_accessed=moved, transcendentals=0),
    )


def turn_kernel(where_ref, *refs):
    parts, (cos_ref, sin_ref, out_ref) = refs[:4], refs[4:]
    half = HEAD_DIM // 2
    for d in range(4):
        z = (where_ref[0] - d) & 3
        cosine, sine = cos_ref[z], sin_ref[z]
        for h in range(GROUP):
            cols = slice(h * HEAD_DIM, (h + 1) * HEAD_DIM)
            t = parts[d][:, cols].astype(jnp.float32).T
            a, b = t[:half], t[half:]
            out_ref[z, :half, cols] = (a * cosine - b * sine).astype(jnp.bfloat16)
            out_ref[z, half:, cols] = (b * cosine + a * sine).astype(jnp.bfloat16)


def turn_queries(where, parts, cosine, sine):
    return call(
        turn_kernel,
        jax.ShapeDtypeStruct((4, HEAD_DIM, GROUP * BLOCK), jnp.bfloat16),
        [SMEM] + [VMEM] * 6,
        (4 * 2**20, 2 * 2**20),
    )(where, *parts, cosine, sine)


def multiply(hidden_refs, weight_ref, out_ref):
    for row, hidden_ref in enumerate(hidden_refs):
        at = (0, 128, 256, 320, 384)[row]
        total = None
        for block in range(0, 32, 2):
            z1, z0, y1 = block // 16, block // 8 % 2, block // 2 % 4
            low = z0 * 16 + z1 * 4 + y1
            weight = jnp.concatenate([weight_ref[low], weight_ref[low + 8]], axis=0)
            term = jnp.dot(
                hidden_ref[:, block * 128 : block * 128 + 256],
                weight,
                preferred_element_type=jnp.float32,
            )
            total = term if total is None else total + term
        out_ref[at : at + hidden_ref.shape[0]] = total


def project_first_kernel(*refs):
    multiply(refs[:5], refs[5], refs[6])


def project_first(hidden, weight):
    return call(
        project_first_kernel,
        jax.ShapeDtypeStruct((4 * BLOCK, HEAD_DIM), jnp.float32),
        [VMEM] * 6,
        (2**29, 5 * 2**20),
    )(*hidden, weight)


def project_second_kernel(*refs):
    where_ref, first_ref, cos_ref, sin_ref, out_ref, second = (refs[0],) + refs[7:]
    half = HEAD_DIM // 2
    multiply(refs[1:6], refs[6], second)
    x, keys_first = where_ref[0], where_ref[1] == 0
    for d in range(4):
        pack = (x - d) & 3
        one, two = first_ref[d * BLOCK : (d + 1) * BLOCK], second[d * BLOCK : (d + 1) * BLOCK]
        key = jnp.where(keys_first, one, two)
        value = jnp.where(keys_first, two, one)
        a, b = key[:, :half], key[:, half:]
        cosine, sine = cos_ref[pack], sin_ref[pack]
        turned = jnp.concatenate([a * cosine - b * sine, b * cosine + a * sine], axis=1)
        out_ref[pack, 0] = turned.astype(jnp.bfloat16)
        out_ref[pack, 1] = value.T.astype(jnp.bfloat16)


def project_second(where, hidden, weight, first, cosine, sine):
    return call(
        project_second_kernel,
        jax.ShapeDtypeStruct((4, 2, BLOCK, HEAD_DIM), jnp.bfloat16),
        [SMEM] + [VMEM] * 9,
        (2**29, 5 * 2**20),
        [pltpu.VMEM((4 * BLOCK, HEAD_DIM), jnp.float32)],
    )(where, *hidden, weight, first, cosine, sine)


def attend_kernel(tiles, opening, closing, where_ref, q_ref, start_ref, *refs):
    factor = math.log2(math.e) / math.sqrt(HEAD_DIM)
    y = where_ref[0]
    shifts = [shift for tile in tiles for shift in tile]
    kv, rest = dict(zip(shifts, refs)), refs[len(shifts) :]
    if not opening:
        given, rest = rest[:3], rest[3:]
    if closing:
        out_ref, acc, top, total = rest
    else:
        acc, top, total = rest

    @pl.loop(0, 4)
    def _(z):
        block = z * 8 + y
        slot = 0 if closing else z
        start = start_ref[z]
        row_at = block * BLOCK + lax.broadcasted_iota(jnp.int32, (BLOCK, BLOCK), 1)
        if opening:
            top[slot] = jnp.full(top.shape[1:], LOW, jnp.float32)
            total[slot] = jnp.zeros(total.shape[1:], jnp.float32)
            acc[slot] = jnp.zeros(acc.shape[1:], jnp.float32)
        else:
            for ref, source in zip((acc, top, total), given):
                ref[slot] = source[z]

        def turn(step, carry):
            zz = z - step
            for tile in tiles:
                places = [zz * 8 + ((y - shift) & 7) for shift in tile]
                needed = [
                    (place <= block) & ((place + 1) * BLOCK > where_ref[1 + z])
                    for place in places
                ]

                @pl.when(functools.reduce(jnp.logical_or, needed))
                def _():
                    key = jnp.concatenate([kv[shift][zz, 0] for shift in tile], axis=0)
                    val = jnp.concatenate([kv[shift][zz, 1] for shift in tile], axis=1)
                    allowed = []
                    for place in places:
                        at = place * BLOCK + lax.broadcasted_iota(jnp.int32, (BLOCK, BLOCK), 0)
                        allowed.append((at >= start) & (at <= row_at))
                    allowed = jnp.concatenate(allowed, axis=0)
                    for h in range(GROUP):
                        cols = slice(h * BLOCK, (h + 1) * BLOCK)
                        s = jnp.dot(key, q_ref[z, :, cols], preferred_element_type=jnp.float32)
                        s = jnp.where(allowed, s, LOW)
                        old = top[slot, :, cols]
                        new = jnp.maximum(old, jnp.max(s, axis=0, keepdims=True))
                        p = jnp.exp2((s - new) * factor)
                        scale = jnp.exp2((old - new) * factor)
                        top[slot, :, cols] = new
                        total[slot, :, cols] = total[slot, :, cols] * scale + jnp.sum(
                            p, axis=0, keepdims=True
                        )
                        acc[slot, :, cols] = acc[slot, :, cols] * scale + jnp.dot(
                            val, p.astype(jnp.bfloat16), preferred_element_type=jnp.float32
                        )

            return carry

        lax.fori_loop(0, z + 1, turn, 0)
        if closing:
            for h in range(GROUP):
                cols = slice(h * BLOCK, (h + 1) * BLOCK)
                mixed = acc[slot, :, cols] / total[slot, :, cols]
                out_ref[z, :, cols] = mixed.T.astype(jnp.bfloat16)


def attend(tiles, where, q, start, kv, state=None, closing=False):
    rows = GROUP * BLOCK
    slots = 1 if closing else 4
    shapes = [(slots, HEAD_DIM, rows), (slots, 1, rows), (slots, 1, rows)]
    held = [jax.ShapeDtypeStruct(shape, jnp.float32) for shape in shapes]
    given = [] if state is None else list(state)
    shifts = [shift for tile in tiles for shift in tile]
    out = jax.ShapeDtypeStruct((4, BLOCK, rows), jnp.bfloat16)
    return call(
        functools.partial(attend_kernel, tiles, state is None, closing),
        out if closing else held,
        [SMEM] + [VMEM] * (2 + len(shifts) + len(given)),
        (len(shifts) * 2**30, 4 * 2**20),
        [pltpu.VMEM(shape, jnp.float32) for shape in shapes] if closing else (),
    )(where, q, start, *[kv[shift] for shift in shifts], *given)


def on_device(hidden, queries, weight_copies, segment_ids, owner):
    y, z = lax.axis_index(Y), lax.axis_index(Z)
    x, c, zh = lax.axis_index("x"), lax.axis_index("c"), lax.axis_index("zh")
    segment_row = segment_ids[0]
    origin = owner[0] % 16

    pieces = weight_copies[0].reshape(BLOCK, 2, 4, 128).transpose(2, 1, 0, 3)
    row = segment_row.astype(jnp.bfloat16).reshape(1, 1, 32, 128)
    pieces = jnp.concatenate([pieces, jnp.broadcast_to(row, (4, 2, 32, 128))], axis=2)
    got = exchange(pieces.reshape(8, 160, 128), ("x", "c"))
    piece = pick(got[:, :BLOCK], origin % 8)
    rows_along = pick(got.reshape(4, 2, 160, 128)[:, :, BLOCK:], c, 1)
    piece = jnp.where(zh == origin // 8, piece, lax.ppermute(piece, "zh", ring(2, 1)))
    part = spread(piece, ("z1", "y1"), 8).reshape(8 * BLOCK, 128)
    mine = spread(part, ("z0", "y0"), 4).reshape(32, BLOCK, 128)
    other = lax.ppermute(mine, "c", ring(2, 1))

    own = hidden[0]
    left = lax.ppermute(own, "x", ring(4, 1))
    right = lax.ppermute(own, "x", ring(4, -1))
    far0 = lax.ppermute(left[:64], "x", ring(4, 1))
    far1 = lax.ppermute(right[64:], "x", ring(4, -1))
    rows = [own, left, far0, far1, right]

    after_part = lax.optimization_barrier((queries[0], part))[0].reshape(BLOCK, 4, -1)
    q_parts = []
    for d in range(4):
        chunk = pick(after_part, (z + d) % 4, 1)
        q_parts.append(lax.ppermute(chunk, Z, ring(4, d)) if d else chunk)

    blocks = segment_row.reshape(4, 8, BLOCK)
    start = starts_of(segment_row, pick(blocks, y, 1))
    token = (jnp.arange(4)[:, None] * 8 + y) * BLOCK + jnp.arange(BLOCK)[None]
    q_angles = jnp.swapaxes(angles_of(token - start), 1, 2)
    q_turned = turn_queries(
        z[None].astype(jnp.int32), q_parts, jnp.cos(q_angles), jnp.sin(q_angles)
    )

    rows_along = rows_along.astype(jnp.int32)
    along = pick(rows_along, z * 8 + y, 1)
    start_along = jax.vmap(starts_of)(rows_along, along)
    k_angles = angles_of((z * 8 + y) * BLOCK + jnp.arange(BLOCK)[None] - start_along)

    first = project_first(rows, mine)
    both = project_second(
        jnp.stack([x, c]).astype(jnp.int32), rows, other, first, jnp.cos(k_angles), jnp.sin(k_angles)
    )
    own_kv = exchange(exchange(both, "x"), Z)

    kv = {0: own_kv}
    for step in range(1, 5):
        kv[step] = lax.ppermute(kv[step - 1], Y, ring(8, 1))
        if step < 4:
            kv[-step] = lax.ppermute(kv[1 - step], Y, ring(8, -1))
    where = jnp.concatenate([y[None], start[:, 0]]).astype(jnp.int32)
    start = start[:, None, :]
    state = attend(((0,), (1, 2), (-1, -2)), where, q_turned, start, kv)
    mixed = attend(((-3,), (3, 4)), where, q_turned, start, kv, state, closing=True)
    back = exchange(mixed, Z)
    return back.transpose(1, 0, 2).reshape(1, BLOCK, HEADS * HEAD_DIM)


def solution(mesh):
    fine = Mesh(mesh.devices.reshape(SIZES), AXES)
    placed = (
        P(REP, SEQ, None),
        P(REP, SEQ, None),
        P(REP, SEQ, None),
        P(REP, None),
        P(),
    )
    return jax.shard_map(
        on_device, mesh=fine, in_specs=placed, out_specs=P(REP, SEQ, None), check_vma=False
    )
```

time: 212 us -> 203 us (0.958)
  Pallas kernels: 7.68 us -> 19.4 us
  local copies, waits for them, and re-layouts: 18.4 us -> 9.9 us
  matrix products: 6.88 us -> 0 us
  blocking collectives: 52 us -> 46.9 us
  waiting for transfers between devices: 44.8 us -> 42 us
  starting transfers between devices: 72.9 us -> 75.3 us
    all_to_all x5 -> x3, starting transfers between devices: 37.2 us -> 14.9 us  [exchange(): return lax.all_to_all(value, axes, split_axis=0, concat_axis=0, tiled=True)]
    ppermute x7 -> x11, starting transfers between devices: 22.8 us -> 44.5 us  [the longest x4 14.3 us: on_device(): kv[step] = lax.ppermute(kv[step - 1], Y, ring(8, 1))]
    all_gather x1 -> x0, blocking collectives: 15.6 us -> none  [on_device(): k_angles = angles_of(lax.all_gather(own_positions, 'x', axis=0))]
    ppermute x1, waiting for transfers between devices: 0.01 us -> 11.8 us  [on_device(): left = lax.ppermute(own, 'x', ring(4, 1))]
    pallas_call x2 -> x5, Pallas kernels: 7.68 us -> 19.4 us  [the longest x2 14.5 us: attend(): call(functools.partial(attend_kernel, tiles, state is None, closing), out...]
    all_to_all x2 -> x3, blocking collectives: 36.3 us -> 46.9 us  [exchange(): return lax.all_to_all(value, axes, split_axis=0, concat_axis=0, tiled=True)]
    all_to_all x5 -> x3, waiting for transfers between devices: 22.4 us -> 12.7 us  [exchange(): return lax.all_to_all(value, axes, split_axis=0, concat_axis=0, tiled=True)]
    dot_general x2 -> x0, matrix products: 6.88 us -> none  [the longest x1 3.44 us: on_device(): second = jnp.dot(rows, other, preferred_element_type=jnp.float32)]
  transfers between devices with their start and end apart: 17 -> 19, of which waited for: 9 -> 12; matrix products, arithmetic and copies ran while one was open for 10% -> 5% of each run, Pallas kernels for 0% -> 6%
where the time goes in v2:
time: 203 us; the launch traced here: 202 us
  starting transfers between devices  75.3 us (37%)
  blocking collectives  46.9 us (23%)
  waiting for transfers between devices  42 us (21%)
  Pallas kernels  19.4 us (10%)
  local copies, waits for them, and re-layouts  9.9 us (5%)
  other arithmetic  7.2 us (4%)
    all_to_all x3, blocking collectives, exchange(): return lax.all_to_all(value, axes, split_axis=0, concat_axis=0, tiled=True)  46.9 us
    all_to_all x3, starting transfers between devices, exchange(): return lax.all_to_all(value, axes, split_axis=0, concat_axis=0, tiled=True)  14.9 us
    pallas_call x2, Pallas kernels, attend(): call(functools.partial(attend_kernel, tiles, state is None, closing), out...  14.5 us
    ppermute x4, starting transfers between devices, on_device(): kv[step] = lax.ppermute(kv[step - 1], Y, ring(8, 1))  14.3 us
    all_to_all x3, waiting for transfers between devices, exchange(): return lax.all_to_all(value, axes, split_axis=0, concat_axis=0, tiled=True)  12.7 us
    ppermute x1, waiting for transfers between devices, on_device(): left = lax.ppermute(own, 'x', ring(4, 1))  11.8 us
    ppermute x3, starting transfers between devices, on_device(): q_parts.append(lax.ppermute(chunk, Z, ring(4, d)) if d else chunk)  11.6 us
    ppermute x1, starting transfers between devices, on_device(): lax.ppermute(piece, 'zh', ring(2, 1))  10.9 us
  transfers between devices with their start and end apart: 19, of which 12 were waited for; matrix products, arithmetic and copies ran while one was open for 5% of the time, Pallas kernels for 6%

profile of v2, /device:TPU:56, one launch (start us, length us, event | category | flops | bytes accessed | tf_op | source)
XLA Modules:
  0.0 201.9 jit_solution(4245653763480154898)
XLA Ops:
  0.0 0.8 convert_reduce_fusion.5
  0.9 1.1 copy.66
  2.2 0.9 copy.68
  3.1 4.3 %all-to-all-start = ((bf16[8,160,128]{2,1,0:T(8,128)(2,1)}), bf16[8,160,128]{2,1,0:T(8,128)(2,1)S(1)}, u32[]{:S(2)}, u32[]{:S(2)}) async-start(bf16[8,160,128]{2,1,0:T(8,128)(2,1)} %bitcast.15), calls=%async_computation | async-start | bytes 655360 | tf_op jit(solution)/shard_map/all_to_all | solution.py:38
  8.1 7.6 %all-to-all-done = bf16[8,160,128]{2,1,0:T(8,128)(2,1)S(1)} async-done(((bf16[8,160,128]{2,1,0:T(8,128)(2,1)}), bf16[8,160,128]{2,1,0:T(8,128)(2,1)S(1)}, u32[]{:S(2)}, u32[]{:S(2)}) %all-to-all-start) | async-done | bytes 327712 | tf_op jit(solution)/shard_map/all_to_all | solution.py:38
  15.7 10.9 %collective-permute-start.7 = (bf16[128,128]{1,0:T(8,128)(2,1)S(1)}, bf16[128,128]{1,0:T(8,128)(2,1)S(1)}, u32[]{:S(2)}, u32[]{:S(2)}) collective-permute-start(bf16[128,128]{1,0:T(8,128)(2,1)S(1)} %dynamic-slice_bitcast_fusion), channel_id=1, source_target_pairs={{0,8},{8,0},{1,9},{9,1},{2,10},{10,2},{3,11},{11,3},{4,12},{12,4},... | collective-permute-start | bytes 98312 | tf_op jit(solution)/shard_map/ppermute | solution.py:255
  26.7 1.9 collective-permute-done.7
  28.6 16.4 %all_to_all.30 = bf16[8,128,128]{2,1,0:T(8,128)(2,1)S(1)} all-to-all(bf16[8,128,128]{2,1,0:T(8,128)(2,1)S(1)} %broadcast_in_dim.88), channel_id=1, replica_groups=mesh['z1'=2,'z0'=2,'y1'=4,'y0'=2,'zh'=2,'x'=4,'c'=2] {'z1','y1'}, dimensions={0} | all-to-all | bytes 524288 | tf_op jit(solution)/shard_map/all_to_all | solution.py:38
  45.0 1.1 broadcast_in_dim.90
  46.1 6.0 %all-to-all-start.2 = ((bf16[4,1024,128]{2,1,0:T(8,128)(2,1)}), bf16[4,1024,128]{2,1,0:T(8,128)(2,1)}, u32[]{:S(2)}, u32[]{:S(2)}) async-start(bf16[4,1024,128]{2,1,0:T(8,128)(2,1)} %broadcast_in_dim.90), calls=%async_computation.2 | async-start | bytes 2097152 | tf_op jit(solution)/shard_map/all_to_all | solution.py:38
  52.1 2.5 %collective-permute-start.3 = (bf16[128,4096]{1,0:T(8,128)(2,1)S(1)}, bf16[128,4096]{1,0:T(8,128)(2,1)S(1)}, u32[]{:S(2)}, u32[]{:S(2)}) collective-permute-start(bf16[128,4096]{1,0:T(8,128)(2,1)S(1)} %bitcast.48), channel_id=1, source_target_pairs={{0,2},{2,4},{4,6},{6,0},{1,3},{3,5},{5,7},{7,1},{8,10},{10,12},{12... | collective-permute-start | bytes 3145736 | tf_op jit(solution)/shard_map/ppermute | solution.py:261
  54.6 4.6 %collective-permute-start.5 = (bf16[128,4096]{1,0:T(8,128)(2,1)S(1)}, bf16[128,4096]{1,0:T(8,128)(2,1)S(1)}, u32[]{:S(2)}, u32[]{:S(2)}) collective-permute-start(bf16[128,4096]{1,0:T(8,128)(2,1)S(1)} %bitcast.49), channel_id=1, source_target_pairs={{0,6},{2,0},{4,2},{6,4},{1,7},{3,1},{5,3},{7,5},{8,14},{10,8},{12,... | collective-permute-start | bytes 3145736 | tf_op jit(solution)/shard_map/ppermute | solution.py:262
  59.2 4.0 %all-to-all-done.2 = bf16[4,1024,128]{2,1,0:T(8,128)(2,1)} async-done(((bf16[4,1024,128]{2,1,0:T(8,128)(2,1)}), bf16[4,1024,128]{2,1,0:T(8,128)(2,1)}, u32[]{:S(2)}, u32[]{:S(2)}) %all-to-all-start.2) | async-done | bytes 1048608 | tf_op jit(solution)/shard_map/all_to_all | solution.py:38
  63.2 1.9 collective-permute-start.8
  65.7 11.8 %collective-permute-done.3.refs_1_.refs_2_ = bf16[128,4096]{1,0:T(8,128)(2,1)S(1)} collective-permute-done((bf16[128,4096]{1,0:T(8,128)(2,1)S(1)}, bf16[128,4096]{1,0:T(8,128)(2,1)S(1)}, u32[]{:S(2)}, u32[]{:S(2)}) %collective-permute-start.3) | collective-permute-done | bytes 1048608 | tf_op jit(solution)/shard_map/ppermute | solution.py:261
  77.5 1.9 collective-permute-start.4
  79.5 5.1 %collective-permute-start.6 = (bf16[64,4096]{1,0:T(8,128)(2,1)S(1)}, bf16[64,4096]{1,0:T(8,128)(2,1)S(1)}, u32[]{:S(2)}, u32[]{:S(2)}) collective-permute-start(bf16[64,4096]{1,0:T(8,128)(2,1)S(1)} %slice.21), channel_id=1, source_target_pairs={{0,6},{2,0},{4,2},{6,4},{1,7},{3,1},{5,3},{7,5},{8,14},{10,8},{12,... | collective-permute-start | bytes 1572872 | tf_op jit(solution)/shard_map/ppermute | solution.py:264
  84.7 1.0 multiply_sine_fusion
  85.7 5.0 %collective-permute-done.4.refs_2_.refs_3_ = bf16[64,4096]{1,0:T(8,128)(2,1)S(1)} collective-permute-done((bf16[64,4096]{1,0:T(8,128)(2,1)S(1)}, bf16[64,4096]{1,0:T(8,128)(2,1)S(1)}, u32[]{:S(2)}, u32[]{:S(2)}) %collective-permute-start.4) | collective-permute-done | bytes 524320 | tf_op jit(solution)/shard_map/ppermute | solution.py:263
  90.7 1.2 collective-permute-done.6.refs_3_.refs_4_
  91.9 2.5 %shard_map.56.refs_7_ = f32[512,128]{1,0:T(8,128)S(1)} custom-call(bf16[128,4096]{1,0:T(8,128)(2,1)S(1)} %bitcast.50, bf16[128,4096]{1,0:T(8,128)(2,1)S(1)} %collective-permute-done.3.refs_1_.refs_2_, bf16[64,4096]{1,0:T(8,128)(2,1)S(1)} %collective-permute-done.4.refs_2_.refs_3_, bf16[64,4096]{1,0:T(8,128)(2,1)S(1)} %collective-permute-done.6.refs_3_.refs_4_, ...), custom_call_target="tpu_custom_call" | custom-call | flops 536870912 | bytes 5242880 | tf_op jit(solution)/shard_map/pallas_call | solution.py:121
  94.4 2.0 shard_map.57
  96.4 11.5 %all_to_all.31 = bf16[4,2,128,128]{3,2,1,0:T(8,128)(2,1)} all-to-all(bf16[4,2,128,128]{3,2,1,0:T(8,128)(2,1)S(1)} %shard_map.57), channel_id=1, replica_groups=mesh['z1'=2,'z0'=2,'y1'=4,'y0'=2,'zh'=2,'x'=4,'c'=2] {'x'}, dimensions={0} | all-to-all | bytes 524288 | tf_op jit(solution)/shard_map/all_to_all | solution.py:38
  108.0 4.5 %all-to-all-start.4 = ((bf16[4,2,128,128]{3,2,1,0:T(8,128)(2,1)}), bf16[4,2,128,128]{3,2,1,0:T(8,128)(2,1)S(1)}, u32[]{:S(2)}, u32[]{:S(2)}) async-start(bf16[4,2,128,128]{3,2,1,0:T(8,128)(2,1)} %all_to_all.31), calls=%async_computation.4 | async-start | bytes 524288 | tf_op jit(solution)/shard_map/all_to_all | solution.py:38
  112.5 1.8 reshape.273
  114.4 2.2 %constant_dynamic-slice_fusion.1 = (bf16[128,1,1024]{2,1,0:T(2,128)(2,1)S(1)}, bf16[128,1,1024]{2,1,0:T(2,128)(2,1)S(1)}, bf16[128,1,1024]{2,1,0:T(2,128)(2,1)S(1)}, bf16[128,1,1024]{2,1,0:T(2,128)(2,1)S(1)}) fusion(bf16[128,4,1024]{2,1,0:T(4,128)(2,1)S(1)} %reshape.273, s32[]{:T(128)S(6)} %select_n.169, s32[]{:T(128)S(6)} %select_n.167, s32[]{:T(128)S(6)} %select_n.165, ...), kind=kLoop, calls=%fused_computation.42 | loop fusion | bytes 2097168 | tf_op jit(solution)/shard_map/jit(dynamic_index_in_dim)/dynamic_slice | solution.py:34
  116.7 3.9 %collective-permute-start = (bf16[128,1024]{1,0:T(8,128)(2,1)S(1)}, bf16[128,1024]{1,0:T(8,128)(2,1)S(1)}, u32[]{:S(2)}, u32[]{:S(2)}) collective-permute-start(bf16[128,1024]{1,0:T(8,128)(2,1)S(1)} %bitcast.61), channel_id=1, source_target_pairs={{0,128},{128,256},{256,384},{384,0},{1,129},{129,257},{257,385},{3... | collective-permute-start | bytes 786440 | tf_op jit(solution)/shard_map/ppermute | solution.py:271
  120.7 4.3 %collective-permute-start.1 = (bf16[128,1024]{1,0:T(8,128)(2,1)S(1)}, bf16[128,1024]{1,0:T(8,128)(2,1)S(1)}, u32[]{:S(2)}, u32[]{:S(2)}) collective-permute-start(bf16[128,1024]{1,0:T(8,128)(2,1)S(1)} %bitcast.62), channel_id=1, source_target_pairs={{0,256},{128,384},{256,0},{384,128},{1,257},{129,385},{257,1},{385... | collective-permute-start | bytes 786440 | tf_op jit(solution)/shard_map/ppermute | solution.py:271
  125.1 3.4 %collective-permute-start.2 = (bf16[128,1024]{1,0:T(8,128)(2,1)S(1)}, bf16[128,1024]{1,0:T(8,128)(2,1)S(1)}, u32[]{:S(2)}, u32[]{:S(2)}) collective-permute-start(bf16[128,1024]{1,0:T(8,128)(2,1)S(1)} %bitcast.63), channel_id=1, source_target_pairs={{0,384},{128,0},{256,128},{384,256},{1,385},{129,1},{257,129},{385... | collective-permute-start | bytes 786440 | tf_op jit(solution)/shard_map/ppermute | solution.py:271
  128.4 1.2 all-to-all-done.4.refs_0_
  129.6 1.9 collective-permute-start.12
  131.5 0.8 fusion.2
  132.3 3.2 %compare_select_fusion.4.start_ref = s32[4,1,128]{2,1,0:T(1,128)S(1)} fusion(s32[4,8,128]{2,1,0:T(8,128)S(1)} %bitcast.64, s32[]{:T(128)S(6)} %select_n.155, s32[]{:T(128)} %get-tuple-element.19, s32[]{:T(128)} %get-tuple-element.18, s32[]{:T(128)} %get-tuple-element.20, s32[]{:T(128)} %get-tuple-element.17, s32[]{:T(128)} %get-tuple-element.16), kind=kLoop, calls=%fused_computation.37 | loop fusion | flops 5120 | bytes 4120 | tf_op jit(solution)/shard_map/jit(_where)/select_n | solution.py:55
  135.6 3.9 %collective-permute-start.9 = (bf16[4,2,128,128]{3,2,1,0:T(8,128)(2,1)S(1)}, bf16[4,2,128,128]{3,2,1,0:T(8,128)(2,1)S(1)}, u32[]{:S(2)}, u32[]{:S(2)}) collective-permute-start(bf16[4,2,128,128]{3,2,1,0:T(8,128)(2,1)S(1)} %all-to-all-done.4.refs_0_), channel_id=1, source_target_pairs={{0,112},{16,0},{32,16},{48,32},{64,48},{80,64},{96,80},{112,96},{1... | collective-permute-start | bytes 786440 | tf_op jit(solution)/shard_map/ppermute | solution.py:296
  139.6 0.9 collective-permute-done.12.refs_1_
  140.4 2.3 %collective-permute-start.13 = (bf16[4,2,128,128]{3,2,1,0:T(8,128)(2,1)S(1)}, bf16[4,2,128,128]{3,2,1,0:T(8,128)(2,1)S(1)}, u32[]{:S(2)}, u32[]{:S(2)}) collective-permute-start(bf16[4,2,128,128]{3,2,1,0:T(8,128)(2,1)S(1)} %collective-permute-done.12.refs_1_), channel_id=1, source_target_pairs={{0,16},{16,32},{32,48},{48,64},{64,80},{80,96},{96,112},{112,0},{1... | collective-permute-start | bytes 786440 | tf_op jit(solution)/shard_map/ppermute | solution.py:294
  142.8 4.4 %collective-permute-done.9.refs_3_ = bf16[4,2,128,128]{3,2,1,0:T(8,128)(2,1)S(1)} collective-permute-done((bf16[4,2,128,128]{3,2,1,0:T(8,128)(2,1)S(1)}, bf16[4,2,128,128]{3,2,1,0:T(8,128)(2,1)S(1)}, u32[]{:S(2)}, u32[]{:S(2)}) %collective-permute-start.9) | collective-permute-done | bytes 262176 | tf_op jit(solution)/shard_map/ppermute | solution.py:296
  147.2 1.9 collective-permute-start.10
  149.1 1.5 collective-permute-done.13.refs_2_
  150.6 4.3 %collective-permute-start.14 = (bf16[4,2,128,128]{3,2,1,0:T(8,128)(2,1)S(1)}, bf16[4,2,128,128]{3,2,1,0:T(8,128)(2,1)S(1)}, u32[]{:S(2)}, u32[]{:S(2)}) collective-permute-start(bf16[4,2,128,128]{3,2,1,0:T(8,128)(2,1)S(1)} %collective-permute-done.13.refs_2_), channel_id=1, source_target_pairs={{0,16},{16,32},{32,48},{48,64},{64,80},{80,96},{96,112},{112,0},{1... | collective-permute-start | bytes 786440 | tf_op jit(solution)/shard_map/ppermute | solution.py:294
  156.1 1.8 collective-permute-done.10.refs_4_
  158.0 1.9 collective-permute-start.11
  159.9 0.8 collective-permute-done.14.refs_1_
  160.7 5.8 %collective-permute-start.15 = (bf16[4,2,128,128]{3,2,1,0:T(8,128)(2,1)S(1)}, bf16[4,2,128,128]{3,2,1,0:T(8,128)(2,1)S(1)}, u32[]{:S(2)}, u32[]{:S(2)}) collective-permute-start(bf16[4,2,128,128]{3,2,1,0:T(8,128)(2,1)S(1)} %collective-permute-done.14.refs_1_), channel_id=1, source_target_pairs={{0,16},{16,32},{32,48},{48,64},{64,80},{80,96},{96,112},{112,0},{1... | collective-permute-start | bytes 786440 | tf_op jit(solution)/shard_map/ppermute | solution.py:294
  166.5 8.4 %shard_map.58 = (f32[4,128,1024]{2,1,0:T(8,128)S(1)}, f32[4,1,1024]{2,1,0:T(1,128)S(1)}, f32[4,1,1024]{2,1,0:T(1,128)S(1)}) custom-call(s32[5]{0:T(128)S(1)} %pad_add_fusion.where_ref, bf16[4,128,1024]{2,1,0:T(8,128)(2,1)S(1)} %shard_map.55.q_ref, s32[4,1,128]{2,1,0:T(1,128)S(1)} %compare_select_fusion.4.start_ref, ...), custom_call_target="tpu_custom_call" | custom-call | flops 5368709120 | bytes 4194304 | tf_op jit(solution)/shard_map/pallas_call | solution.py:234
  174.9 6.0 %shard_map.59 = bf16[4,128,1024]{2,1,0:T(8,128)(2,1)S(1)} custom-call(s32[5]{0:T(128)S(1)} %pad_add_fusion.where_ref, bf16[4,128,1024]{2,1,0:T(8,128)(2,1)S(1)} %shard_map.55.q_ref, s32[4,1,128]{2,1,0:T(1,128)S(1)} %compare_select_fusion.4.start_ref, bf16[4,2,128,128]{3,2,1,0:T(8,128)(2,1)S(1)} %collective-permute-done.11.refs_0_, ...), custom_call_target="tpu_custom_call" | custom-call | flops 3221225472 | bytes 4194304 | tf_op jit(solution)/shard_map/pallas_call | solution.py:234
  181.0 19.0 %all_to_all.32 = bf16[4,128,1024]{2,1,0:T(8,128)(2,1)S(1)} all-to-all(bf16[4,128,1024]{2,1,0:T(8,128)(2,1)S(1)} %shard_map.59), channel_id=1, replica_groups=mesh['z1'=2,'z0'=2,'y1'=4,'y0'=2,'zh'=2,'x'=4,'c'=2] {'z1','z0'}, dimensions={0} | all-to-all | bytes 2097152 | tf_op jit(solution)/shard_map/all_to_all | solution.py:38
  200.6 1.3 copy.70
  (39 shorter events, 3.4 us)
Async XLA Ops:
  3.1 12.5 %all-to-all-start = ((bf16[8,160,128]{2,1,0:T(8,128)(2,1)}), bf16[8,160,128]{2,1,0:T(8,128)(2,1)S(1)}, u32[]{:S(2)}, u32[]{:S(2)}) async-start(bf16[8,160,128]{2,1,0:T(8,128)(2,1)} %bitcast.15), calls=%async_computation | async-start | bytes 655360 | tf_op jit(solution)/shard_map/all_to_all | solution.py:38
  15.7 12.8 %collective-permute-start.7 = (bf16[128,128]{1,0:T(8,128)(2,1)S(1)}, bf16[128,128]{1,0:T(8,128)(2,1)S(1)}, u32[]{:S(2)}, u32[]{:S(2)}) collective-permute-start(bf16[128,128]{1,0:T(8,128)(2,1)S(1)} %dynamic-slice_bitcast_fusion), channel_id=1, source_target_pairs={{0,8},{8,0},{1,9},{9,1},{2,10},{10,2},{3,11},{11,3},{4,12},{12,4},... | collective-permute-start | bytes 98312 | tf_op jit(solution)/shard_map/ppermute | solution.py:255
  28.5 23.6 %copy-start = (bf16[1,128,4096]{2,1,0:T(8,128)(2,1)S(1)}, bf16[1,128,4096]{2,1,0:T(8,128)(2,1)}, u32[]{:S(2)}) copy-start(bf16[1,128,4096]{2,1,0:T(8,128)(2,1)} %param.5) | copy-start | bytes 3145732
  46.1 17.1 %all-to-all-start.2 = ((bf16[4,1024,128]{2,1,0:T(8,128)(2,1)}), bf16[4,1024,128]{2,1,0:T(8,128)(2,1)}, u32[]{:S(2)}, u32[]{:S(2)}) async-start(bf16[4,1024,128]{2,1,0:T(8,128)(2,1)} %broadcast_in_dim.90), calls=%async_computation.2 | async-start | bytes 2097152 | tf_op jit(solution)/shard_map/all_to_all | solution.py:38
  52.1 25.4 %collective-permute-start.3 = (bf16[128,4096]{1,0:T(8,128)(2,1)S(1)}, bf16[128,4096]{1,0:T(8,128)(2,1)S(1)}, u32[]{:S(2)}, u32[]{:S(2)}) collective-permute-start(bf16[128,4096]{1,0:T(8,128)(2,1)S(1)} %bitcast.48), channel_id=1, source_target_pairs={{0,2},{2,4},{4,6},{6,0},{1,3},{3,5},{5,7},{7,1},{8,10},{10,12},{12... | collective-permute-start | bytes 3145736 | tf_op jit(solution)/shard_map/ppermute | solution.py:261
  54.6 24.9 %collective-permute-start.5 = (bf16[128,4096]{1,0:T(8,128)(2,1)S(1)}, bf16[128,4096]{1,0:T(8,128)(2,1)S(1)}, u32[]{:S(2)}, u32[]{:S(2)}) collective-permute-start(bf16[128,4096]{1,0:T(8,128)(2,1)S(1)} %bitcast.49), channel_id=1, source_target_pairs={{0,6},{2,0},{4,2},{6,4},{1,7},{3,1},{5,3},{7,5},{8,14},{10,8},{12,... | collective-permute-start | bytes 3145736 | tf_op jit(solution)/shard_map/ppermute | solution.py:262
  63.2 31.3 %collective-permute-start.8 = (bf16[32,128,128]{2,1,0:T(8,128)(2,1)}, bf16[32,128,128]{2,1,0:T(8,128)(2,1)S(1)}, u32[]{:S(2)}, u32[]{:S(2)}) collective-permute-start(bf16[32,128,128]{2,1,0:T(8,128)(2,1)} %bitcast.18.refs_5_), channel_id=1, source_target_pairs={{0,1},{1,0},{2,3},{3,2},{4,5},{5,4},{6,7},{7,6},{8,9},{9,8},{10,11... | collective-permute-start | bytes 3145736 | tf_op jit(solution)/shard_map/ppermute | solution.py:258
  77.5 13.2 %collective-permute-start.4 = (bf16[64,4096]{1,0:T(8,128)(2,1)S(1)}, bf16[64,4096]{1,0:T(8,128)(2,1)S(1)}, u32[]{:S(2)}, u32[]{:S(2)}) collective-permute-start(bf16[64,4096]{1,0:T(8,128)(2,1)S(1)} %slice.20), channel_id=1, source_target_pairs={{0,2},{2,4},{4,6},{6,0},{1,3},{3,5},{5,7},{7,1},{8,10},{10,12},{12... | collective-permute-start | bytes 1572872 | tf_op jit(solution)/shard_map/ppermute | solution.py:263
  79.5 12.5 %collective-permute-start.6 = (bf16[64,4096]{1,0:T(8,128)(2,1)S(1)}, bf16[64,4096]{1,0:T(8,128)(2,1)S(1)}, u32[]{:S(2)}, u32[]{:S(2)}) collective-permute-start(bf16[64,4096]{1,0:T(8,128)(2,1)S(1)} %slice.21), channel_id=1, source_target_pairs={{0,6},{2,0},{4,2},{6,4},{1,7},{3,1},{5,3},{7,5},{8,14},{10,8},{12,... | collective-permute-start | bytes 1572872 | tf_op jit(solution)/shard_map/ppermute | solution.py:264
  108.0 21.6 %all-to-all-start.4 = ((bf16[4,2,128,128]{3,2,1,0:T(8,128)(2,1)}), bf16[4,2,128,128]{3,2,1,0:T(8,128)(2,1)S(1)}, u32[]{:S(2)}, u32[]{:S(2)}) async-start(bf16[4,2,128,128]{3,2,1,0:T(8,128)(2,1)} %all_to_all.31), calls=%async_computation.4 | async-start | bytes 524288 | tf_op jit(solution)/shard_map/all_to_all | solution.py:38
  116.6 15.0 %copy-start.1 = (s32[1,4096]{1,0:T(1,128)S(1)}, s32[1,4096]{1,0:T(1,128)}, u32[]{:S(2)}) copy-start(s32[1,4096]{1,0:T(1,128)} %param.8) | copy-start | bytes 49156
  116.7 39.0 %collective-permute-start = (bf16[128,1024]{1,0:T(8,128)(2,1)S(1)}, bf16[128,1024]{1,0:T(8,128)(2,1)S(1)}, u32[]{:S(2)}, u32[]{:S(2)}) collective-permute-start(bf16[128,1024]{1,0:T(8,128)(2,1)S(1)} %bitcast.61), channel_id=1, source_target_pairs={{0,128},{128,256},{256,384},{384,0},{1,129},{129,257},{257,385},{3... | collective-permute-start | bytes 786440 | tf_op jit(solution)/shard_map/ppermute | solution.py:271
  120.7 34.9 %collective-permute-start.1 = (bf16[128,1024]{1,0:T(8,128)(2,1)S(1)}, bf16[128,1024]{1,0:T(8,128)(2,1)S(1)}, u32[]{:S(2)}, u32[]{:S(2)}) collective-permute-start(bf16[128,1024]{1,0:T(8,128)(2,1)S(1)} %bitcast.62), channel_id=1, source_target_pairs={{0,256},{128,384},{256,0},{384,128},{1,257},{129,385},{257,1},{385... | collective-permute-start | bytes 786440 | tf_op jit(solution)/shard_map/ppermute | solution.py:271
  125.1 30.6 %collective-permute-start.2 = (bf16[128,1024]{1,0:T(8,128)(2,1)S(1)}, bf16[128,1024]{1,0:T(8,128)(2,1)S(1)}, u32[]{:S(2)}, u32[]{:S(2)}) collective-permute-start(bf16[128,1024]{1,0:T(8,128)(2,1)S(1)} %bitcast.63), channel_id=1, source_target_pairs={{0,384},{128,0},{256,128},{384,256},{1,385},{129,1},{257,129},{385... | collective-permute-start | bytes 786440 | tf_op jit(solution)/shard_map/ppermute | solution.py:271
  129.6 10.8 %collective-permute-start.12 = (bf16[4,2,128,128]{3,2,1,0:T(8,128)(2,1)S(1)}, bf16[4,2,128,128]{3,2,1,0:T(8,128)(2,1)S(1)}, u32[]{:S(2)}, u32[]{:S(2)}) collective-permute-start(bf16[4,2,128,128]{3,2,1,0:T(8,128)(2,1)S(1)} %all-to-all-done.4.refs_0_), channel_id=1, source_target_pairs={{0,16},{16,32},{32,48},{48,64},{64,80},{80,96},{96,112},{112,0},{1... | collective-permute-start | bytes 786440 | tf_op jit(solution)/shard_map/ppermute | solution.py:294
  135.6 11.6 %collective-permute-start.9 = (bf16[4,2,128,128]{3,2,1,0:T(8,128)(2,1)S(1)}, bf16[4,2,128,128]{3,2,1,0:T(8,128)(2,1)S(1)}, u32[]{:S(2)}, u32[]{:S(2)}) collective-permute-start(bf16[4,2,128,128]{3,2,1,0:T(8,128)(2,1)S(1)} %all-to-all-done.4.refs_0_), channel_id=1, source_target_pairs={{0,112},{16,0},{32,16},{48,32},{64,48},{80,64},{96,80},{112,96},{1... | collective-permute-start | bytes 786440 | tf_op jit(solution)/shard_map/ppermute | solution.py:296
  140.4 10.2 %collective-permute-start.13 = (bf16[4,2,128,128]{3,2,1,0:T(8,128)(2,1)S(1)}, bf16[4,2,128,128]{3,2,1,0:T(8,128)(2,1)S(1)}, u32[]{:S(2)}, u32[]{:S(2)}) collective-permute-start(bf16[4,2,128,128]{3,2,1,0:T(8,128)(2,1)S(1)} %collective-permute-done.12.refs_1_), channel_id=1, source_target_pairs={{0,16},{16,32},{32,48},{48,64},{64,80},{80,96},{96,112},{112,0},{1... | collective-permute-start | bytes 786440 | tf_op jit(solution)/shard_map/ppermute | solution.py:294
  147.2 10.8 %collective-permute-start.10 = (bf16[4,2,128,128]{3,2,1,0:T(8,128)(2,1)S(1)}, bf16[4,2,128,128]{3,2,1,0:T(8,128)(2,1)S(1)}, u32[]{:S(2)}, u32[]{:S(2)}) collective-permute-start(bf16[4,2,128,128]{3,2,1,0:T(8,128)(2,1)S(1)} %collective-permute-done.9.refs_3_), channel_id=1, source_target_pairs={{0,112},{16,0},{32,16},{48,32},{64,48},{80,64},{96,80},{112,96},{1... | collective-permute-start | bytes 786440 | tf_op jit(solution)/shard_map/ppermute | solution.py:296
  150.6 10.1 %collective-permute-start.14 = (bf16[4,2,128,128]{3,2,1,0:T(8,128)(2,1)S(1)}, bf16[4,2,128,128]{3,2,1,0:T(8,128)(2,1)S(1)}, u32[]{:S(2)}, u32[]{:S(2)}) collective-permute-start(bf16[4,2,128,128]{3,2,1,0:T(8,128)(2,1)S(1)} %collective-permute-done.13.refs_2_), channel_id=1, source_target_pairs={{0,16},{16,32},{32,48},{48,64},{64,80},{80,96},{96,112},{112,0},{1... | collective-permute-start | bytes 786440 | tf_op jit(solution)/shard_map/ppermute | solution.py:294
  158.0 16.9 %collective-permute-start.11 = (bf16[4,2,128,128]{3,2,1,0:T(8,128)(2,1)S(1)}, bf16[4,2,128,128]{3,2,1,0:T(8,128)(2,1)S(1)}, u32[]{:S(2)}, u32[]{:S(2)}) collective-permute-start(bf16[4,2,128,128]{3,2,1,0:T(8,128)(2,1)S(1)} %collective-permute-done.10.refs_4_), channel_id=1, source_target_pairs={{0,112},{16,0},{32,16},{48,32},{64,48},{80,64},{96,80},{112,96},{1... | collective-permute-start | bytes 786440 | tf_op jit(solution)/shard_map/ppermute | solution.py:296
  160.7 14.2 %collective-permute-start.15 = (bf16[4,2,128,128]{3,2,1,0:T(8,128)(2,1)S(1)}, bf16[4,2,128,128]{3,2,1,0:T(8,128)(2,1)S(1)}, u32[]{:S(2)}, u32[]{:S(2)}) collective-permute-start(bf16[4,2,128,128]{3,2,1,0:T(8,128)(2,1)S(1)} %collective-permute-done.14.refs_1_), channel_id=1, source_target_pairs={{0,16},{16,32},{32,48},{48,64},{64,80},{80,96},{96,112},{112,0},{1... | collective-permute-start | bytes 786440 | tf_op jit(solution)/shard_map/ppermute | solution.py:294

commit v3 on v2

--- a/solution.py
+++ b/solution.py
@@ -97,8 +97,8 @@
 
 
 def multiply(hidden_refs, weight_ref, out_ref):
-    for row, hidden_ref in enumerate(hidden_refs):
-        at = (0, 128, 256, 320, 384)[row]
+    at = 0
+    for hidden_ref in hidden_refs:
         total = None
         for block in range(0, 32, 2):
             z1, z0, y1 = block // 16, block // 8 % 2, block // 2 % 4
@@ -111,25 +111,26 @@
             )
             total = term if total is None else total + term
         out_ref[at : at + hidden_ref.shape[0]] = total
+        at += hidden_ref.shape[0]
 
 
 def project_first_kernel(*refs):
-    multiply(refs[:5], refs[5], refs[6])
+    multiply(refs[:7], refs[7], refs[8])
 
 
 def project_first(hidden, weight):
     return call(
         project_first_kernel,
         jax.ShapeDtypeStruct((4 * BLOCK, HEAD_DIM), jnp.float32),
-        [VMEM] * 6,
+        [VMEM] * 8,
         (2**29, 5 * 2**20),
     )(*hidden, weight)
 
 
 def project_second_kernel(*refs):
-    where_ref, first_ref, cos_ref, sin_ref, out_ref, second = (refs[0],) + refs[7:]
+    where_ref, first_ref, cos_ref, sin_ref, out_ref, second = (refs[0],) + refs[9:]
     half = HEAD_DIM // 2
-    multiply(refs[1:6], refs[6], second)
+    multiply(refs[1:8], refs[8], second)
     x, keys_first = where_ref[0], where_ref[1] == 0
     for d in range(4):
         pack = (x - d) & 3
@@ -147,7 +148,7 @@
     return call(
         project_second_kernel,
         jax.ShapeDtypeStruct((4, 2, BLOCK, HEAD_DIM), jnp.bfloat16),
-        [SMEM] + [VMEM] * 9,
+        [SMEM] + [VMEM] * 11,
         (2**29, 5 * 2**20),
         [pltpu.VMEM((4 * BLOCK, HEAD_DIM), jnp.float32)],
     )(where, *hidden, weight, first, cosine, sine)
@@ -253,30 +254,35 @@
     piece = pick(got[:, :BLOCK], origin % 8)
     rows_along = pick(got.reshape(4, 2, 160, 128)[:, :, BLOCK:], c, 1)
     piece = jnp.where(zh == origin // 8, piece, lax.ppermute(piece, "zh", ring(2, 1)))
+
+    own = hidden[0]
+    low, high = own[:64], own[64:]
+    left_low = lax.ppermute(low, "x", ring(4, 1))
+    right_high = lax.ppermute(high, "x", ring(4, -1))
+    piece, left_low, right_high = lax.optimization_barrier((piece, left_low, right_high))
     part = spread(piece, ("z1", "y1"), 8).reshape(8 * BLOCK, 128)
+    left_high = lax.ppermute(high, "x", ring(4, 1))
+    right_low = lax.ppermute(low, "x", ring(4, -1))
+    far_low = lax.ppermute(left_low, "x", ring(4, 1))
+    far_high = lax.ppermute(right_high, "x", ring(4, -1))
+    part, left_high, right_low, far_low, far_high = lax.optimization_barrier(
+        (part, left_high, right_low, far_low, far_high)
+    )
     mine = spread(part, ("z0", "y0"), 4).reshape(32, BLOCK, 128)
+    rows = [own, left_low, left_high, far_low, far_high, right_low, right_high]
+
+    chunks = [
+        lax.dynamic_slice_in_dim(queries[0], (z + d) % 4 * GROUP * HEAD_DIM, GROUP * HEAD_DIM, 1)
+        for d in range(4)
+    ]
+    mine, *chunks = lax.optimization_barrier((mine, *chunks))
+    q_parts = [lax.ppermute(chunk, Z, ring(4, d)) if d else chunk for d, chunk in enumerate(chunks)]
     other = lax.ppermute(mine, "c", ring(2, 1))
-
-    own = hidden[0]
-    left = lax.ppermute(own, "x", ring(4, 1))
-    right = lax.ppermute(own, "x", ring(4, -1))
-    far0 = lax.ppermute(left[:64], "x", ring(4, 1))
-    far1 = lax.ppermute(right[64:], "x", ring(4, -1))
-    rows = [own, left, far0, far1, right]
-
-    after_part = lax.optimization_barrier((queries[0], part))[0].reshape(BLOCK, 4, -1)
-    q_parts = []
-    for d in range(4):
-        chunk = pick(after_part, (z + d) % 4, 1)
-        q_parts.append(lax.ppermute(chunk, Z, ring(4, d)) if d else chunk)
 
     blocks = segment_row.reshape(4, 8, BLOCK)
     start = starts_of(segment_row, pick(blocks, y, 1))
     token = (jnp.arange(4)[:, None] * 8 + y) * BLOCK + jnp.arange(BLOCK)[None]
     q_angles = jnp.swapaxes(angles_of(token - start), 1, 2)
-    q_turned = turn_queries(
-        z[None].astype(jnp.int32), q_parts, jnp.cos(q_angles), jnp.sin(q_angles)
-    )
 
     rows_along = rows_along.astype(jnp.int32)
     along = pick(rows_along, z * 8 + y, 1)
@@ -287,17 +293,24 @@
     both = project_second(
         jnp.stack([x, c]).astype(jnp.int32), rows, other, first, jnp.cos(k_angles), jnp.sin(k_angles)
     )
-    own_kv = exchange(exchange(both, "x"), Z)
-
+    near, *q_parts = lax.optimization_barrier((exchange(both, "x"), *q_parts))
+    q_turned = turn_queries(
+        z[None].astype(jnp.int32), q_parts, jnp.cos(q_angles), jnp.sin(q_angles)
+    )
+    own_kv = exchange(near, Z)
+
+    where = jnp.concatenate([y[None], start[:, 0]]).astype(jnp.int32)
+    start = start[:, None, :]
     kv = {0: own_kv}
     for step in range(1, 5):
+        if step == 4:
+            state = attend(((0,), (1, 2), (-1, -2)), where, q_turned, start, kv)
+            kv[3], kv[-3], *state = lax.optimization_barrier((kv[3], kv[-3], *state))
         kv[step] = lax.ppermute(kv[step - 1], Y, ring(8, 1))
         if step < 4:
             kv[-step] = lax.ppermute(kv[1 - step], Y, ring(8, -1))
-    where = jnp.concatenate([y[None], start[:, 0]]).astype(jnp.int32)
-    start = start[:, None, :]
-    state = attend(((0,), (1, 2), (-1, -2)), where, q_turned, start, kv)
-    mixed = attend(((-3,), (3, 4)), where, q_turned, start, kv, state, closing=True)
+    state = attend(((3,), (-3,)), where, q_turned, start, kv, state)
+    mixed = attend(((4,),), where, q_turned, start, kv, state, closing=True)
     back = exchange(mixed, Z)
     return back.transpose(1, 0, 2).reshape(1, BLOCK, HEADS * HEAD_DIM)
 

time: 203 us -> 199 us (0.980)
  the two profiles are of different devices: /device:TPU:56 before, /device:TPU:10 now
where the time goes in v3:
time: 199 us; the launch traced here: 198 us
  starting transfers between devices  88.3 us (44%)
  waiting for transfers between devices  36.5 us (18%)
  blocking collectives  32 us (16%)
  Pallas kernels  19.4 us (10%)
  local copies, waits for them, and re-layouts  12.9 us (6%)
  other arithmetic  7.21 us (4%)
    all_to_all x1, blocking collectives, exchange(): return lax.all_to_all(value, axes, split_axis=0, concat_axis=0, tiled=True)  32 us
    all_to_all x5, waiting for transfers between devices, exchange(): return lax.all_to_all(value, axes, split_axis=0, concat_axis=0, tiled=True)  30.2 us
    all_to_all x5, starting transfers between devices, exchange(): return lax.all_to_all(value, axes, split_axis=0, concat_axis=0, tiled=True)  27.2 us
    pallas_call x3, Pallas kernels, attend(): call(functools.partial(attend_kernel, tiles, state is None, closing), out...  11.8 us
    ppermute x4, starting transfers between devices, on_device(): kv[step] = lax.ppermute(kv[step - 1], Y, ring(8, 1))  11.2 us
    ppermute x1, starting transfers between devices, on_device(): lax.ppermute(piece, 'zh', ring(2, 1))  10.9 us
    ppermute x3, starting transfers between devices, on_device(): lax.ppermute(chunk, Z, ring(4, d))  9.56 us
    ppermute x3, starting transfers between devices, on_device(): kv[-step] = lax.ppermute(kv[1 - step], Y, ring(8, -1))  9.56 us
  transfers between devices with their start and end apart: 23, of which 6 were waited for; matrix products, arithmetic and copies ran while one was open for 6% of the time, Pallas kernels for 9%

profile of v3, /device:TPU:10, one launch (start us, length us, event | category | flops | bytes accessed | tf_op | source)
XLA Modules:
  0.0 197.5 jit_solution(7220399608194849218)
XLA Ops:
  0.0 0.9 convert_reduce_fusion.5
  1.0 1.1 copy.38
  2.3 0.9 copy.40
  3.2 4.8 %all-to-all-start = ((bf16[8,160,128]{2,1,0:T(8,128)(2,1)}), bf16[8,160,128]{2,1,0:T(8,128)(2,1)S(1)}, u32[]{:S(2)}, u32[]{:S(2)}) async-start(bf16[8,160,128]{2,1,0:T(8,128)(2,1)} %bitcast.10), calls=%async_computation | async-start | bytes 655360 | tf_op jit(solution)/shard_map/all_to_all | solution.py:38
  8.0 1.1 slice_bitcast_fusion
  9.1 3.4 %collective-permute-start.1 = (bf16[64,4096]{1,0:T(8,128)(2,1)}, bf16[64,4096]{1,0:T(8,128)(2,1)S(1)}, u32[]{:S(2)}, u32[]{:S(2)}) collective-permute-start(bf16[64,4096]{1,0:T(8,128)(2,1)} %get-tuple-element.78), channel_id=1, source_target_pairs={{0,2},{2,4},{4,6},{6,0},{1,3},{3,5},{5,7},{7,1},{8,10},{10,12},{12... | collective-permute-start | bytes 1572872 | tf_op jit(solution)/shard_map/ppermute | solution.py:260
  12.5 2.5 %collective-permute-start.2 = (bf16[64,4096]{1,0:T(8,128)(2,1)}, bf16[64,4096]{1,0:T(8,128)(2,1)S(1)}, u32[]{:S(2)}, u32[]{:S(2)}) collective-permute-start(bf16[64,4096]{1,0:T(8,128)(2,1)} %get-tuple-element.77), channel_id=1, source_target_pairs={{0,6},{2,0},{4,2},{6,4},{1,7},{3,1},{5,3},{7,5},{8,14},{10,8},{12,... | collective-permute-start | bytes 1572872 | tf_op jit(solution)/shard_map/ppermute | solution.py:261
  16.3 10.9 %collective-permute-start = (bf16[128,128]{1,0:T(8,128)(2,1)S(1)}, bf16[128,128]{1,0:T(8,128)(2,1)S(1)}, u32[]{:S(2)}, u32[]{:S(2)}) collective-permute-start(bf16[128,128]{1,0:T(8,128)(2,1)S(1)} %dynamic-slice_bitcast_fusion.4), channel_id=1, source_target_pairs={{0,8},{8,0},{1,9},{9,1},{2,10},{10,2},{3,11},{11,3},{4,12},{12,4},... | collective-permute-start | bytes 98312 | tf_op jit(solution)/shard_map/ppermute | solution.py:256
  27.3 3.4 %collective-permute-start.3 = (bf16[64,4096]{1,0:T(8,128)(2,1)}, bf16[64,4096]{1,0:T(8,128)(2,1)S(1)}, u32[]{:S(2)}, u32[]{:S(2)}) collective-permute-start(bf16[64,4096]{1,0:T(8,128)(2,1)} %get-tuple-element.77), channel_id=1, source_target_pairs={{0,2},{2,4},{4,6},{6,0},{1,3},{3,5},{5,7},{7,1},{8,10},{10,12},{12... | collective-permute-start | bytes 1572872 | tf_op jit(solution)/shard_map/ppermute | solution.py:264
  30.6 2.5 %collective-permute-start.4 = (bf16[64,4096]{1,0:T(8,128)(2,1)}, bf16[64,4096]{1,0:T(8,128)(2,1)S(1)}, u32[]{:S(2)}, u32[]{:S(2)}) collective-permute-start(bf16[64,4096]{1,0:T(8,128)(2,1)} %get-tuple-element.78), channel_id=1, source_target_pairs={{0,6},{2,0},{4,2},{6,4},{1,7},{3,1},{5,3},{7,5},{8,14},{10,8},{12,... | collective-permute-start | bytes 1572872 | tf_op jit(solution)/shard_map/ppermute | solution.py:265
  33.2 3.4 %collective-permute-start.5 = (bf16[64,4096]{1,0:T(8,128)(2,1)S(1)}, bf16[64,4096]{1,0:T(8,128)(2,1)}, u32[]{:S(2)}, u32[]{:S(2)}) collective-permute-start(bf16[64,4096]{1,0:T(8,128)(2,1)S(1)} %collective-permute-done.1.refs_1_.refs_2_), channel_id=1, source_target_pairs={{0,2},{2,4},{4,6},{6,0},{1,3},{3,5},{5,7},{7,1},{8,10},{10,12},{12... | collective-permute-start | bytes 1572872 | tf_op jit(solution)/shard_map/ppermute | solution.py:266
  36.6 2.9 %collective-permute-start.6 = (bf16[64,4096]{1,0:T(8,128)(2,1)S(1)}, bf16[64,4096]{1,0:T(8,128)(2,1)}, u32[]{:S(2)}, u32[]{:S(2)}) collective-permute-start(bf16[64,4096]{1,0:T(8,128)(2,1)S(1)} %collective-permute-done.2.refs_6_.refs_7_), channel_id=1, source_target_pairs={{0,6},{2,0},{4,2},{6,4},{1,7},{3,1},{5,3},{7,5},{8,14},{10,8},{12,... | collective-permute-start | bytes 1572872 | tf_op jit(solution)/shard_map/ppermute | solution.py:267
  40.2 8.0 %all-to-all-start.1 = ((bf16[8,128,128]{2,1,0:T(8,128)(2,1)}), bf16[8,128,128]{2,1,0:T(8,128)(2,1)S(1)}, u32[]{:S(2)}, u32[]{:S(2)}) async-start(bf16[8,128,128]{2,1,0:T(8,128)(2,1)} %broadcast_in_dim.85), calls=%async_computation.1 | async-start | bytes 524288 | tf_op jit(solution)/shard_map/all_to_all | solution.py:38
  48.3 12.5 %all-to-all-done.1 = bf16[8,128,128]{2,1,0:T(8,128)(2,1)S(1)} async-done(((bf16[8,128,128]{2,1,0:T(8,128)(2,1)}), bf16[8,128,128]{2,1,0:T(8,128)(2,1)S(1)}, u32[]{:S(2)}, u32[]{:S(2)}) %all-to-all-start.1) | async-done | bytes 262176 | tf_op jit(solution)/shard_map/all_to_all | solution.py:38
  60.8 1.1 broadcast_in_dim.86
  61.9 4.2 %all-to-all-start.2 = ((bf16[4,1024,128]{2,1,0:T(8,128)(2,1)}), bf16[4,1024,128]{2,1,0:T(8,128)(2,1)S(1)}, u32[]{:S(2)}, u32[]{:S(2)}) async-start(bf16[4,1024,128]{2,1,0:T(8,128)(2,1)} %broadcast_in_dim.86), calls=%async_computation.2 | async-start | bytes 2097152 | tf_op jit(solution)/shard_map/all_to_all | solution.py:38
  66.1 2.1 %dynamic-slice_bitcast_fusion = (bf16[128,1024]{1,0:T(8,128)(2,1)}, bf16[128,1024]{1,0:T(8,128)(2,1)}, bf16[128,1024]{1,0:T(8,128)(2,1)S(1)}, bf16[128,1024]{1,0:T(8,128)(2,1)}) fusion(bf16[1,128,4096]{2,1,0:T(8,128)(2,1)} %param.6, s32[]{:T(128)S(6)} %select_n.174, s32[]{:T(128)S(6)} %select_n.170, s32[]{:T(128)S(6)} %select_n.168, s32[]{:T(128)S(6)} %select_n.172), kind=kLoop, calls=%fused_computation.5 | loop fusion | bytes 2097168 | tf_op jit(solution)/shard_map/dynamic_slice | solution.py:275
  68.2 7.9 %all-to-all-done.2 = bf16[4,1024,128]{2,1,0:T(8,128)(2,1)S(1)} async-done(((bf16[4,1024,128]{2,1,0:T(8,128)(2,1)}), bf16[4,1024,128]{2,1,0:T(8,128)(2,1)S(1)}, u32[]{:S(2)}, u32[]{:S(2)}) %all-to-all-start.2) | async-done | bytes 1048608 | tf_op jit(solution)/shard_map/all_to_all | solution.py:38
  76.1 1.9 collective-permute-start.7
  78.1 0.8 slice.29
  79.5 1.0 multiply_sine_fusion
  80.5 2.5 %collective-permute-start.8 = (bf16[128,1024]{1,0:T(8,128)(2,1)}, bf16[128,1024]{1,0:T(8,128)(2,1)}, u32[]{:S(2)}, u32[]{:S(2)}) collective-permute-start(bf16[128,1024]{1,0:T(8,128)(2,1)} %get-tuple-element.44), channel_id=1, source_target_pairs={{0,128},{128,256},{256,384},{384,0},{1,129},{129,257},{257,385},{3... | collective-permute-start | bytes 786440 | tf_op jit(solution)/shard_map/ppermute | solution.py:279
  83.0 2.6 %collective-permute-start.9 = (bf16[128,1024]{1,0:T(8,128)(2,1)}, bf16[128,1024]{1,0:T(8,128)(2,1)}, u32[]{:S(2)}, u32[]{:S(2)}) collective-permute-start(bf16[128,1024]{1,0:T(8,128)(2,1)} %get-tuple-element.45), channel_id=1, source_target_pairs={{0,256},{128,384},{256,0},{384,128},{1,257},{129,385},{257,1},{385... | collective-permute-start | bytes 786440 | tf_op jit(solution)/shard_map/ppermute | solution.py:279
  85.7 4.4 %collective-permute-start.10 = (bf16[128,1024]{1,0:T(8,128)(2,1)}, bf16[128,1024]{1,0:T(8,128)(2,1)}, u32[]{:S(2)}, u32[]{:S(2)}) collective-permute-start(bf16[128,1024]{1,0:T(8,128)(2,1)} %get-tuple-element.46), channel_id=1, source_target_pairs={{0,384},{128,0},{256,128},{384,256},{1,385},{129,1},{257,129},{385... | collective-permute-start | bytes 786440 | tf_op jit(solution)/shard_map/ppermute | solution.py:279
  90.1 1.0 copy-done.2
  91.2 1.0 copy-done.4
  92.2 2.5 %shard_map.55.refs_9_ = f32[512,128]{1,0:T(8,128)S(1)} custom-call(bf16[128,4096]{1,0:T(8,128)(2,1)S(1)} %bitcast.47, bf16[64,4096]{1,0:T(8,128)(2,1)S(1)} %collective-permute-done.1.refs_1_.refs_2_, bf16[64,4096]{1,0:T(8,128)(2,1)S(1)} %copy-done.2, bf16[64,4096]{1,0:T(8,128)(2,1)} %collective-permute-done.5.refs_3_.refs_4_, ...), custom_call_target="tpu_custom_call" | custom-call | flops 536870912 | bytes 5242880 | tf_op jit(solution)/shard_map/pallas_call | solution.py:122
  94.7 3.4 %shard_map.56 = bf16[4,2,128,128]{3,2,1,0:T(8,128)(2,1)} custom-call(s32[2]{0:T(128)S(1)} %pad_add_fusion.1.refs_0_, bf16[128,4096]{1,0:T(8,128)(2,1)S(1)} %bitcast.48, bf16[64,4096]{1,0:T(8,128)(2,1)S(1)} %collective-permute-done.1.refs_1_.refs_2_, bf16[64,4096]{1,0:T(8,128)(2,1)S(1)} %copy-done.2, bf16[64,4096]{1,0:T(8,128)(2,1)} %collective-permute-done.5.refs_3_.refs_4_, ...), custom_call_target="tpu_custom_call" | custom-call | flops 536870912 | bytes 5242880 | tf_op jit(solution)/shard_map/pallas_call | solution.py:148
  98.2 6.8 %all-to-all-start.3 = ((bf16[4,2,128,128]{3,2,1,0:T(8,128)(2,1)}), bf16[4,2,128,128]{3,2,1,0:T(8,128)(2,1)}, u32[]{:S(2)}, u32[]{:S(2)}) async-start(bf16[4,2,128,128]{3,2,1,0:T(8,128)(2,1)} %shard_map.56), calls=%async_computation.3 | async-start | bytes 524288 | tf_op jit(solution)/shard_map/all_to_all | solution.py:38
  105.0 5.7 %all-to-all-done.3 = bf16[4,2,128,128]{3,2,1,0:T(8,128)(2,1)} async-done(((bf16[4,2,128,128]{3,2,1,0:T(8,128)(2,1)}), bf16[4,2,128,128]{3,2,1,0:T(8,128)(2,1)}, u32[]{:S(2)}, u32[]{:S(2)}) %all-to-all-start.3) | async-done | bytes 262176 | tf_op jit(solution)/shard_map/all_to_all | solution.py:38
  110.6 3.4 %all-to-all-start.4 = ((bf16[4,2,128,128]{3,2,1,0:T(8,128)(2,1)}), bf16[4,2,128,128]{3,2,1,0:T(8,128)(2,1)S(1)}, u32[]{:S(2)}, u32[]{:S(2)}) async-start(bf16[4,2,128,128]{3,2,1,0:T(8,128)(2,1)} %all-to-all-done.3), calls=%async_computation.4 | async-start | bytes 524288 | tf_op jit(solution)/shard_map/all_to_all | solution.py:38
  114.9 3.1 %compare_select_fusion.4.start_ref = s32[4,1,128]{2,1,0:T(1,128)S(1)} fusion(s32[4,8,128]{2,1,0:T(8,128)S(1)} %bitcast.58, s32[]{:T(128)S(6)} %select_n.154, s32[]{:T(128)} %get-tuple-element.71, s32[]{:T(128)} %get-tuple-element.70, s32[]{:T(128)} %get-tuple-element.72, s32[]{:T(128)} %get-tuple-element.69, s32[]{:T(128)} %get-tuple-element.68), kind=kLoop, calls=%fused_computation.39 | loop fusion | flops 5120 | bytes 4120 | tf_op jit(solution)/shard_map/jit(_where)/select_n | solution.py:55
  118.1 4.1 %all-to-all-done.4.refs_0_ = bf16[4,2,128,128]{3,2,1,0:T(8,128)(2,1)S(1)} async-done(((bf16[4,2,128,128]{3,2,1,0:T(8,128)(2,1)}), bf16[4,2,128,128]{3,2,1,0:T(8,128)(2,1)S(1)}, u32[]{:S(2)}, u32[]{:S(2)}) %all-to-all-start.4) | async-done | bytes 262176 | tf_op jit(solution)/shard_map/all_to_all | solution.py:38
  122.2 2.6 %collective-permute-start.11 = (bf16[4,2,128,128]{3,2,1,0:T(8,128)(2,1)S(1)}, bf16[4,2,128,128]{3,2,1,0:T(8,128)(2,1)S(1)}, u32[]{:S(2)}, u32[]{:S(2)}) collective-permute-start(bf16[4,2,128,128]{3,2,1,0:T(8,128)(2,1)S(1)} %all-to-all-done.4.refs_0_), channel_id=1, source_target_pairs={{0,16},{16,32},{32,48},{48,64},{64,80},{80,96},{96,112},{112,0},{1... | collective-permute-start | bytes 786440 | tf_op jit(solution)/shard_map/ppermute | solution.py:309
  124.8 3.2 %collective-permute-start.14 = (bf16[4,2,128,128]{3,2,1,0:T(8,128)(2,1)S(1)}, bf16[4,2,128,128]{3,2,1,0:T(8,128)(2,1)S(1)}, u32[]{:S(2)}, u32[]{:S(2)}) collective-permute-start(bf16[4,2,128,128]{3,2,1,0:T(8,128)(2,1)S(1)} %all-to-all-done.4.refs_0_), channel_id=1, source_target_pairs={{0,112},{16,0},{32,16},{48,32},{64,48},{80,64},{96,80},{112,96},{1... | collective-permute-start | bytes 786440 | tf_op jit(solution)/shard_map/ppermute | solution.py:311
  128.1 2.5 %collective-permute-done.11.refs_1_ = bf16[4,2,128,128]{3,2,1,0:T(8,128)(2,1)S(1)} collective-permute-done((bf16[4,2,128,128]{3,2,1,0:T(8,128)(2,1)S(1)}, bf16[4,2,128,128]{3,2,1,0:T(8,128)(2,1)S(1)}, u32[]{:S(2)}, u32[]{:S(2)}) %collective-permute-start.11) | collective-permute-done | bytes 262176 | tf_op jit(solution)/shard_map/ppermute | solution.py:309
  130.6 2.7 %collective-permute-start.12 = (bf16[4,2,128,128]{3,2,1,0:T(8,128)(2,1)S(1)}, bf16[4,2,128,128]{3,2,1,0:T(8,128)(2,1)S(1)}, u32[]{:S(2)}, u32[]{:S(2)}) collective-permute-start(bf16[4,2,128,128]{3,2,1,0:T(8,128)(2,1)S(1)} %collective-permute-done.11.refs_1_), channel_id=1, source_target_pairs={{0,16},{16,32},{32,48},{48,64},{64,80},{80,96},{96,112},{112,0},{1... | collective-permute-start | bytes 786440 | tf_op jit(solution)/shard_map/ppermute | solution.py:309
  133.4 3.3 %collective-permute-start.15 = (bf16[4,2,128,128]{3,2,1,0:T(8,128)(2,1)S(1)}, bf16[4,2,128,128]{3,2,1,0:T(8,128)(2,1)S(1)}, u32[]{:S(2)}, u32[]{:S(2)}) collective-permute-start(bf16[4,2,128,128]{3,2,1,0:T(8,128)(2,1)S(1)} %collective-permute-done.14.refs_3_), channel_id=1, source_target_pairs={{0,112},{16,0},{32,16},{48,32},{64,48},{80,64},{96,80},{112,96},{1... | collective-permute-start | bytes 786440 | tf_op jit(solution)/shard_map/ppermute | solution.py:311
  137.3 1.6 shard_map.57.q_ref
  138.9 3.7 %collective-permute-start.13 = (bf16[4,2,128,128]{3,2,1,0:T(8,128)(2,1)S(1)}, bf16[4,2,128,128]{3,2,1,0:T(8,128)(2,1)S(1)}, u32[]{:S(2)}, u32[]{:S(2)}) collective-permute-start(bf16[4,2,128,128]{3,2,1,0:T(8,128)(2,1)S(1)} %collective-permute-done.12.refs_2_), channel_id=1, source_target_pairs={{0,16},{16,32},{32,48},{48,64},{64,80},{80,96},{96,112},{112,0},{1... | collective-permute-start | bytes 786440 | tf_op jit(solution)/shard_map/ppermute | solution.py:309
  142.6 3.0 %collective-permute-start.16 = (bf16[4,2,128,128]{3,2,1,0:T(8,128)(2,1)S(1)}, bf16[4,2,128,128]{3,2,1,0:T(8,128)(2,1)S(1)}, u32[]{:S(2)}, u32[]{:S(2)}) collective-permute-start(bf16[4,2,128,128]{3,2,1,0:T(8,128)(2,1)S(1)} %collective-permute-done.15.refs_4_), channel_id=1, source_target_pairs={{0,112},{16,0},{32,16},{48,32},{64,48},{80,64},{96,80},{112,96},{1... | collective-permute-start | bytes 786440 | tf_op jit(solution)/shard_map/ppermute | solution.py:311
  145.6 7.7 %shard_map.58 = (f32[4,128,1024]{2,1,0:T(8,128)S(1)}, f32[4,1,1024]{2,1,0:T(1,128)S(1)}, f32[4,1,1024]{2,1,0:T(1,128)S(1)}) custom-call(s32[5]{0:T(128)S(1)} %pad_add_fusion.where_ref, bf16[4,128,1024]{2,1,0:T(8,128)(2,1)S(1)} %shard_map.57.q_ref, s32[4,1,128]{2,1,0:T(1,128)S(1)} %compare_select_fusion.4.start_ref, ...), custom_call_target="tpu_custom_call" | custom-call | flops 5368709120 | bytes 4194304 | tf_op jit(solution)/shard_map/pallas_call | solution.py:235
  153.4 2.2 %collective-permute-start.17 = (bf16[4,2,128,128]{3,2,1,0:T(8,128)(2,1)S(1)}, bf16[4,2,128,128]{3,2,1,0:T(8,128)(2,1)S(1)}, u32[]{:S(2)}, u32[]{:S(2)}) collective-permute-start(bf16[4,2,128,128]{3,2,1,0:T(8,128)(2,1)S(1)} %collective-permute-done.13.refs_0_), channel_id=1, source_target_pairs={{0,16},{16,32},{32,48},{48,64},{64,80},{80,96},{96,112},{112,0},{1... | collective-permute-start | bytes 786440 | tf_op jit(solution)/shard_map/ppermute | solution.py:309
  155.6 2.2 %shard_map.59 = (f32[4,128,1024]{2,1,0:T(8,128)S(1)}, f32[4,1,1024]{2,1,0:T(1,128)S(1)}, f32[4,1,1024]{2,1,0:T(1,128)S(1)}) custom-call(s32[5]{0:T(128)S(1)} %pad_add_fusion.where_ref, bf16[4,128,1024]{2,1,0:T(8,128)(2,1)S(1)} %shard_map.57.q_ref, s32[4,1,128]{2,1,0:T(1,128)S(1)} %compare_select_fusion.4.start_ref, ...), custom_call_target="tpu_custom_call" | custom-call | flops 2147483648 | bytes 4194304 | tf_op jit(solution)/shard_map/pallas_call | solution.py:235
  157.9 3.8 %collective-permute-done.17.refs_0_ = bf16[4,2,128,128]{3,2,1,0:T(8,128)(2,1)S(1)} collective-permute-done((bf16[4,2,128,128]{3,2,1,0:T(8,128)(2,1)S(1)}, bf16[4,2,128,128]{3,2,1,0:T(8,128)(2,1)S(1)}, u32[]{:S(2)}, u32[]{:S(2)}) %collective-permute-start.17) | collective-permute-done | bytes 262176 | tf_op jit(solution)/shard_map/ppermute | solution.py:309
  161.7 1.8 shard_map.60
  163.5 32.0 %all_to_all.30 = bf16[4,128,1024]{2,1,0:T(8,128)(2,1)S(1)} all-to-all(bf16[4,128,1024]{2,1,0:T(8,128)(2,1)S(1)} %shard_map.60), channel_id=1, replica_groups=mesh['z1'=2,'z0'=2,'y1'=4,'y0'=2,'zh'=2,'x'=4,'c'=2] {'z1','z0'}, dimensions={0} | all-to-all | bytes 2097152 | tf_op jit(solution)/shard_map/all_to_all | solution.py:38
  196.2 1.3 copy.42
  (50 shorter events, 4.7 us)
Async XLA Ops:
  0.0 8.0 %copy-start = (bf16[1,128,4096]{2,1,0:T(8,128)(2,1)S(1)}, bf16[1,128,4096]{2,1,0:T(8,128)(2,1)}, u32[]{:S(2)}) copy-start(bf16[1,128,4096]{2,1,0:T(8,128)(2,1)} %param.5) | copy-start | bytes 3145732
  3.2 12.4 %all-to-all-start = ((bf16[8,160,128]{2,1,0:T(8,128)(2,1)}), bf16[8,160,128]{2,1,0:T(8,128)(2,1)S(1)}, u32[]{:S(2)}, u32[]{:S(2)}) async-start(bf16[8,160,128]{2,1,0:T(8,128)(2,1)} %bitcast.10), calls=%async_computation | async-start | bytes 655360 | tf_op jit(solution)/shard_map/all_to_all | solution.py:38
  9.1 24.1 %collective-permute-start.1 = (bf16[64,4096]{1,0:T(8,128)(2,1)}, bf16[64,4096]{1,0:T(8,128)(2,1)S(1)}, u32[]{:S(2)}, u32[]{:S(2)}) collective-permute-start(bf16[64,4096]{1,0:T(8,128)(2,1)} %get-tuple-element.78), channel_id=1, source_target_pairs={{0,2},{2,4},{4,6},{6,0},{1,3},{3,5},{5,7},{7,1},{8,10},{10,12},{12... | collective-permute-start | bytes 1572872 | tf_op jit(solution)/shard_map/ppermute | solution.py:260
  12.5 20.7 %collective-permute-start.2 = (bf16[64,4096]{1,0:T(8,128)(2,1)}, bf16[64,4096]{1,0:T(8,128)(2,1)S(1)}, u32[]{:S(2)}, u32[]{:S(2)}) collective-permute-start(bf16[64,4096]{1,0:T(8,128)(2,1)} %get-tuple-element.77), channel_id=1, source_target_pairs={{0,6},{2,0},{4,2},{6,4},{1,7},{3,1},{5,3},{7,5},{8,14},{10,8},{12,... | collective-permute-start | bytes 1572872 | tf_op jit(solution)/shard_map/ppermute | solution.py:261
  15.6 0.7 copy-start.5
  16.3 16.8 %collective-permute-start = (bf16[128,128]{1,0:T(8,128)(2,1)S(1)}, bf16[128,128]{1,0:T(8,128)(2,1)S(1)}, u32[]{:S(2)}, u32[]{:S(2)}) collective-permute-start(bf16[128,128]{1,0:T(8,128)(2,1)S(1)} %dynamic-slice_bitcast_fusion.4), channel_id=1, source_target_pairs={{0,8},{8,0},{1,9},{9,1},{2,10},{10,2},{3,11},{11,3},{4,12},{12,4},... | collective-permute-start | bytes 98312 | tf_op jit(solution)/shard_map/ppermute | solution.py:256
  27.3 21.0 %collective-permute-start.3 = (bf16[64,4096]{1,0:T(8,128)(2,1)}, bf16[64,4096]{1,0:T(8,128)(2,1)S(1)}, u32[]{:S(2)}, u32[]{:S(2)}) collective-permute-start(bf16[64,4096]{1,0:T(8,128)(2,1)} %get-tuple-element.77), channel_id=1, source_target_pairs={{0,2},{2,4},{4,6},{6,0},{1,3},{3,5},{5,7},{7,1},{8,10},{10,12},{12... | collective-permute-start | bytes 1572872 | tf_op jit(solution)/shard_map/ppermute | solution.py:264
  30.6 17.6 %collective-permute-start.4 = (bf16[64,4096]{1,0:T(8,128)(2,1)}, bf16[64,4096]{1,0:T(8,128)(2,1)S(1)}, u32[]{:S(2)}, u32[]{:S(2)}) collective-permute-start(bf16[64,4096]{1,0:T(8,128)(2,1)} %get-tuple-element.78), channel_id=1, source_target_pairs={{0,6},{2,0},{4,2},{6,4},{1,7},{3,1},{5,3},{7,5},{8,14},{10,8},{12,... | collective-permute-start | bytes 1572872 | tf_op jit(solution)/shard_map/ppermute | solution.py:265
  33.2 27.6 %collective-permute-start.5 = (bf16[64,4096]{1,0:T(8,128)(2,1)S(1)}, bf16[64,4096]{1,0:T(8,128)(2,1)}, u32[]{:S(2)}, u32[]{:S(2)}) collective-permute-start(bf16[64,4096]{1,0:T(8,128)(2,1)S(1)} %collective-permute-done.1.refs_1_.refs_2_), channel_id=1, source_target_pairs={{0,2},{2,4},{4,6},{6,0},{1,3},{3,5},{5,7},{7,1},{8,10},{10,12},{12... | collective-permute-start | bytes 1572872 | tf_op jit(solution)/shard_map/ppermute | solution.py:266
  36.6 24.2 %collective-permute-start.6 = (bf16[64,4096]{1,0:T(8,128)(2,1)S(1)}, bf16[64,4096]{1,0:T(8,128)(2,1)}, u32[]{:S(2)}, u32[]{:S(2)}) collective-permute-start(bf16[64,4096]{1,0:T(8,128)(2,1)S(1)} %collective-permute-done.2.refs_6_.refs_7_), channel_id=1, source_target_pairs={{0,6},{2,0},{4,2},{6,4},{1,7},{3,1},{5,3},{7,5},{8,14},{10,8},{12,... | collective-permute-start | bytes 1572872 | tf_op jit(solution)/shard_map/ppermute | solution.py:267
  40.2 20.6 %all-to-all-start.1 = ((bf16[8,128,128]{2,1,0:T(8,128)(2,1)}), bf16[8,128,128]{2,1,0:T(8,128)(2,1)S(1)}, u32[]{:S(2)}, u32[]{:S(2)}) async-start(bf16[8,128,128]{2,1,0:T(8,128)(2,1)} %broadcast_in_dim.85), calls=%async_computation.1 | async-start | bytes 524288 | tf_op jit(solution)/shard_map/all_to_all | solution.py:38
  48.2 13.7 %copy-start.1 = (bf16[64,4096]{1,0:T(8,128)(2,1)}, bf16[64,4096]{1,0:T(8,128)(2,1)S(1)}, u32[]{:S(2)}) copy-start(bf16[64,4096]{1,0:T(8,128)(2,1)S(1)} %collective-permute-done.3.refs_2_.refs_3_) | copy-start | bytes 1572868
  48.3 13.6 %copy-start.3 = (bf16[64,4096]{1,0:T(8,128)(2,1)}, bf16[64,4096]{1,0:T(8,128)(2,1)S(1)}, u32[]{:S(2)}) copy-start(bf16[64,4096]{1,0:T(8,128)(2,1)S(1)} %collective-permute-done.4.refs_5_.refs_6_) | copy-start | bytes 1572868
  61.9 14.2 %all-to-all-start.2 = ((bf16[4,1024,128]{2,1,0:T(8,128)(2,1)}), bf16[4,1024,128]{2,1,0:T(8,128)(2,1)S(1)}, u32[]{:S(2)}, u32[]{:S(2)}) async-start(bf16[4,1024,128]{2,1,0:T(8,128)(2,1)} %broadcast_in_dim.86), calls=%async_computation.2 | async-start | bytes 2097152 | tf_op jit(solution)/shard_map/all_to_all | solution.py:38
  76.1 18.7 %collective-permute-start.7 = (bf16[32,128,128]{2,1,0:T(8,128)(2,1)S(1)}, bf16[32,128,128]{2,1,0:T(8,128)(2,1)S(1)}, u32[]{:S(2)}, u32[]{:S(2)}) collective-permute-start(bf16[32,128,128]{2,1,0:T(8,128)(2,1)S(1)} %bitcast.49), channel_id=1, source_target_pairs={{0,1},{1,0},{2,3},{3,2},{4,5},{5,4},{6,7},{7,6},{8,9},{9,8},{10,11... | collective-permute-start | bytes 3145736 | tf_op jit(solution)/shard_map/ppermute | solution.py:280
  80.5 24.4 %collective-permute-start.8 = (bf16[128,1024]{1,0:T(8,128)(2,1)}, bf16[128,1024]{1,0:T(8,128)(2,1)}, u32[]{:S(2)}, u32[]{:S(2)}) collective-permute-start(bf16[128,1024]{1,0:T(8,128)(2,1)} %get-tuple-element.44), channel_id=1, source_target_pairs={{0,128},{128,256},{256,384},{384,0},{1,129},{129,257},{257,385},{3... | collective-permute-start | bytes 786440 | tf_op jit(solution)/shard_map/ppermute | solution.py:279
  83.0 21.9 %collective-permute-start.9 = (bf16[128,1024]{1,0:T(8,128)(2,1)}, bf16[128,1024]{1,0:T(8,128)(2,1)}, u32[]{:S(2)}, u32[]{:S(2)}) collective-permute-start(bf16[128,1024]{1,0:T(8,128)(2,1)} %get-tuple-element.45), channel_id=1, source_target_pairs={{0,256},{128,384},{256,0},{384,128},{1,257},{129,385},{257,1},{385... | collective-permute-start | bytes 786440 | tf_op jit(solution)/shard_map/ppermute | solution.py:279
  85.7 19.3 %collective-permute-start.10 = (bf16[128,1024]{1,0:T(8,128)(2,1)}, bf16[128,1024]{1,0:T(8,128)(2,1)}, u32[]{:S(2)}, u32[]{:S(2)}) collective-permute-start(bf16[128,1024]{1,0:T(8,128)(2,1)} %get-tuple-element.46), channel_id=1, source_target_pairs={{0,384},{128,0},{256,128},{384,256},{1,385},{129,1},{257,129},{385... | collective-permute-start | bytes 786440 | tf_op jit(solution)/shard_map/ppermute | solution.py:279
  90.1 1.0 copy-start.2
  91.2 1.0 copy-start.4
  94.7 19.3 %copy-start.6 = (s32[1,4096]{1,0:T(1,128)S(1)}, s32[1,4096]{1,0:T(1,128)}, u32[]{:S(2)}) copy-start(s32[1,4096]{1,0:T(1,128)} %param.8) | copy-start | bytes 49156
  98.2 12.5 %all-to-all-start.3 = ((bf16[4,2,128,128]{3,2,1,0:T(8,128)(2,1)}), bf16[4,2,128,128]{3,2,1,0:T(8,128)(2,1)}, u32[]{:S(2)}, u32[]{:S(2)}) async-start(bf16[4,2,128,128]{3,2,1,0:T(8,128)(2,1)} %shard_map.56), calls=%async_computation.3 | async-start | bytes 524288 | tf_op jit(solution)/shard_map/all_to_all | solution.py:38
  110.6 11.6 %all-to-all-start.4 = ((bf16[4,2,128,128]{3,2,1,0:T(8,128)(2,1)}), bf16[4,2,128,128]{3,2,1,0:T(8,128)(2,1)S(1)}, u32[]{:S(2)}, u32[]{:S(2)}) async-start(bf16[4,2,128,128]{3,2,1,0:T(8,128)(2,1)} %all-to-all-done.3), calls=%async_computation.4 | async-start | bytes 524288 | tf_op jit(solution)/shard_map/all_to_all | solution.py:38
  122.2 8.4 %collective-permute-start.11 = (bf16[4,2,128,128]{3,2,1,0:T(8,128)(2,1)S(1)}, bf16[4,2,128,128]{3,2,1,0:T(8,128)(2,1)S(1)}, u32[]{:S(2)}, u32[]{:S(2)}) collective-permute-start(bf16[4,2,128,128]{3,2,1,0:T(8,128)(2,1)S(1)} %all-to-all-done.4.refs_0_), channel_id=1, source_target_pairs={{0,16},{16,32},{32,48},{48,64},{64,80},{80,96},{96,112},{112,0},{1... | collective-permute-start | bytes 786440 | tf_op jit(solution)/shard_map/ppermute | solution.py:309
  124.8 8.5 %collective-permute-start.14 = (bf16[4,2,128,128]{3,2,1,0:T(8,128)(2,1)S(1)}, bf16[4,2,128,128]{3,2,1,0:T(8,128)(2,1)S(1)}, u32[]{:S(2)}, u32[]{:S(2)}) collective-permute-start(bf16[4,2,128,128]{3,2,1,0:T(8,128)(2,1)S(1)} %all-to-all-done.4.refs_0_), channel_id=1, source_target_pairs={{0,112},{16,0},{32,16},{48,32},{64,48},{80,64},{96,80},{112,96},{1... | collective-permute-start | bytes 786440 | tf_op jit(solution)/shard_map/ppermute | solution.py:311
  130.6 8.3 %collective-permute-start.12 = (bf16[4,2,128,128]{3,2,1,0:T(8,128)(2,1)S(1)}, bf16[4,2,128,128]{3,2,1,0:T(8,128)(2,1)S(1)}, u32[]{:S(2)}, u32[]{:S(2)}) collective-permute-start(bf16[4,2,128,128]{3,2,1,0:T(8,128)(2,1)S(1)} %collective-permute-done.11.refs_1_), channel_id=1, source_target_pairs={{0,16},{16,32},{32,48},{48,64},{64,80},{80,96},{96,112},{112,0},{1... | collective-permute-start | bytes 786440 | tf_op jit(solution)/shard_map/ppermute | solution.py:309
  133.4 9.3 %collective-permute-start.15 = (bf16[4,2,128,128]{3,2,1,0:T(8,128)(2,1)S(1)}, bf16[4,2,128,128]{3,2,1,0:T(8,128)(2,1)S(1)}, u32[]{:S(2)}, u32[]{:S(2)}) collective-permute-start(bf16[4,2,128,128]{3,2,1,0:T(8,128)(2,1)S(1)} %collective-permute-done.14.refs_3_), channel_id=1, source_target_pairs={{0,112},{16,0},{32,16},{48,32},{64,48},{80,64},{96,80},{112,96},{1... | collective-permute-start | bytes 786440 | tf_op jit(solution)/shard_map/ppermute | solution.py:311
  138.9 14.4 %collective-permute-start.13 = (bf16[4,2,128,128]{3,2,1,0:T(8,128)(2,1)S(1)}, bf16[4,2,128,128]{3,2,1,0:T(8,128)(2,1)S(1)}, u32[]{:S(2)}, u32[]{:S(2)}) collective-permute-start(bf16[4,2,128,128]{3,2,1,0:T(8,128)(2,1)S(1)} %collective-permute-done.12.refs_2_), channel_id=1, source_target_pairs={{0,16},{16,32},{32,48},{48,64},{64,80},{80,96},{96,112},{112,0},{1... | collective-permute-start | bytes 786440 | tf_op jit(solution)/shard_map/ppermute | solution.py:309
  142.6 10.8 %collective-permute-start.16 = (bf16[4,2,128,128]{3,2,1,0:T(8,128)(2,1)S(1)}, bf16[4,2,128,128]{3,2,1,0:T(8,128)(2,1)S(1)}, u32[]{:S(2)}, u32[]{:S(2)}) collective-permute-start(bf16[4,2,128,128]{3,2,1,0:T(8,128)(2,1)S(1)} %collective-permute-done.15.refs_4_), channel_id=1, source_target_pairs={{0,112},{16,0},{32,16},{48,32},{64,48},{80,64},{96,80},{112,96},{1... | collective-permute-start | bytes 786440 | tf_op jit(solution)/shard_map/ppermute | solution.py:311
  153.4 8.3 %collective-permute-start.17 = (bf16[4,2,128,128]{3,2,1,0:T(8,128)(2,1)S(1)}, bf16[4,2,128,128]{3,2,1,0:T(8,128)(2,1)S(1)}, u32[]{:S(2)}, u32[]{:S(2)}) collective-permute-start(bf16[4,2,128,128]{3,2,1,0:T(8,128)(2,1)S(1)} %collective-permute-done.13.refs_0_), channel_id=1, source_target_pairs={{0,16},{16,32},{32,48},{48,64},{64,80},{80,96},{96,112},{112,0},{1... | collective-permute-start | bytes 786440 | tf_op jit(solution)/shard_map/ppermute | solution.py:309

commit v4 on v2

--- a/solution.py
+++ b/solution.py
@@ -73,32 +73,32 @@
     )
 
 
-def turn_kernel(where_ref, *refs):
-    parts, (cos_ref, sin_ref, out_ref) = refs[:4], refs[4:]
+def turn_kernel(q_ref, cos_ref, sin_ref, out_ref):
     half = HEAD_DIM // 2
-    for d in range(4):
-        z = (where_ref[0] - d) & 3
+
+    @pl.loop(0, 4)
+    def _(z):
         cosine, sine = cos_ref[z], sin_ref[z]
         for h in range(GROUP):
             cols = slice(h * HEAD_DIM, (h + 1) * HEAD_DIM)
-            t = parts[d][:, cols].astype(jnp.float32).T
+            t = q_ref[z, :, cols].astype(jnp.float32).T
             a, b = t[:half], t[half:]
             out_ref[z, :half, cols] = (a * cosine - b * sine).astype(jnp.bfloat16)
             out_ref[z, half:, cols] = (b * cosine + a * sine).astype(jnp.bfloat16)
 
 
-def turn_queries(where, parts, cosine, sine):
+def turn_queries(q, cosine, sine):
     return call(
         turn_kernel,
         jax.ShapeDtypeStruct((4, HEAD_DIM, GROUP * BLOCK), jnp.bfloat16),
-        [SMEM] + [VMEM] * 6,
+        [VMEM] * 3,
         (4 * 2**20, 2 * 2**20),
-    )(where, *parts, cosine, sine)
+    )(q, cosine, sine)
 
 
 def multiply(hidden_refs, weight_ref, out_ref):
-    for row, hidden_ref in enumerate(hidden_refs):
-        at = (0, 128, 256, 320, 384)[row]
+    at = 0
+    for hidden_ref in hidden_refs:
         total = None
         for block in range(0, 32, 2):
             z1, z0, y1 = block // 16, block // 8 % 2, block // 2 % 4
@@ -111,6 +111,7 @@
             )
             total = term if total is None else total + term
         out_ref[at : at + hidden_ref.shape[0]] = total
+        at += hidden_ref.shape[0]
 
 
 def project_first_kernel(*refs):
@@ -253,30 +254,22 @@
     piece = pick(got[:, :BLOCK], origin % 8)
     rows_along = pick(got.reshape(4, 2, 160, 128)[:, :, BLOCK:], c, 1)
     piece = jnp.where(zh == origin // 8, piece, lax.ppermute(piece, "zh", ring(2, 1)))
-    part = spread(piece, ("z1", "y1"), 8).reshape(8 * BLOCK, 128)
-    mine = spread(part, ("z0", "y0"), 4).reshape(32, BLOCK, 128)
-    other = lax.ppermute(mine, "c", ring(2, 1))
 
     own = hidden[0]
     left = lax.ppermute(own, "x", ring(4, 1))
     right = lax.ppermute(own, "x", ring(4, -1))
-    far0 = lax.ppermute(left[:64], "x", ring(4, 1))
-    far1 = lax.ppermute(right[64:], "x", ring(4, -1))
-    rows = [own, left, far0, far1, right]
-
-    after_part = lax.optimization_barrier((queries[0], part))[0].reshape(BLOCK, 4, -1)
-    q_parts = []
-    for d in range(4):
-        chunk = pick(after_part, (z + d) % 4, 1)
-        q_parts.append(lax.ppermute(chunk, Z, ring(4, d)) if d else chunk)
+    part = spread(piece, ("z1", "y1"), 8).reshape(8 * BLOCK, 128)
+    part, left, right = lax.optimization_barrier((part, left, right))
+    mine = spread(part, ("z0", "y0"), 4).reshape(32, BLOCK, 128)
+    other = lax.ppermute(mine, "c", ring(2, 1))
+    far_low = lax.ppermute(left[:64], "x", ring(4, 1))
+    far_high = lax.ppermute(right[64:], "x", ring(4, -1))
+    rows = [own, left, far_low, far_high, right]
 
     blocks = segment_row.reshape(4, 8, BLOCK)
     start = starts_of(segment_row, pick(blocks, y, 1))
     token = (jnp.arange(4)[:, None] * 8 + y) * BLOCK + jnp.arange(BLOCK)[None]
     q_angles = jnp.swapaxes(angles_of(token - start), 1, 2)
-    q_turned = turn_queries(
-        z[None].astype(jnp.int32), q_parts, jnp.cos(q_angles), jnp.sin(q_angles)
-    )
 
     rows_along = rows_along.astype(jnp.int32)
     along = pick(rows_along, z * 8 + y, 1)
@@ -289,15 +282,22 @@
     )
     own_kv = exchange(exchange(both, "x"), Z)
 
+    split = queries[0].reshape(BLOCK, 4, GROUP * HEAD_DIM).transpose(1, 0, 2)
+    own_kv, split = lax.optimization_barrier((own_kv, split))
+    q_turned = turn_queries(exchange(split, Z), jnp.cos(q_angles), jnp.sin(q_angles))
+
+    where = jnp.concatenate([y[None], start[:, 0]]).astype(jnp.int32)
+    start = start[:, None, :]
     kv = {0: own_kv}
     for step in range(1, 5):
+        if step == 4:
+            state = attend(((0,), (1, 2), (-1, -2)), where, q_turned, start, kv)
+            kv[3], kv[-3], *state = lax.optimization_barrier((kv[3], kv[-3], *state))
         kv[step] = lax.ppermute(kv[step - 1], Y, ring(8, 1))
         if step < 4:
             kv[-step] = lax.ppermute(kv[1 - step], Y, ring(8, -1))
-    where = jnp.concatenate([y[None], start[:, 0]]).astype(jnp.int32)
-    start = start[:, None, :]
-    state = attend(((0,), (1, 2), (-1, -2)), where, q_turned, start, kv)
-    mixed = attend(((-3,), (3, 4)), where, q_turned, start, kv, state, closing=True)
+    state = attend(((3,), (-3,)), where, q_turned, start, kv, state)
+    mixed = attend(((4,),), where, q_turned, start, kv, state, closing=True)
     back = exchange(mixed, Z)
     return back.transpose(1, 0, 2).reshape(1, BLOCK, HEADS * HEAD_DIM)
 

time: 203 us -> 194 us (0.956); the launches traced: 202 us -> 190 us
  starting transfers between devices: 75.3 us -> 66.1 us
  waiting for transfers between devices: 42 us -> 36 us
  blocking collectives: 46.9 us -> 52.3 us
    ppermute x1, waiting for transfers between devices: 11.8 us -> 0.01 us  [on_device(): left = lax.ppermute(own, 'x', ring(4, 1))]
    ppermute x5 -> x2, starting transfers between devices: 18.6 us -> 7.05 us  [the longest x1 4.59 us: on_device(): far_high = lax.ppermute(right[64:], 'x', ring(4, -1))]
    all_to_all x3, blocking collectives: 46.9 us -> 52.3 us  [exchange(): return lax.all_to_all(value, axes, split_axis=0, concat_axis=0, tiled=True)]
    ppermute x5 -> x2, waiting for transfers between devices: 6.23 us -> 10.8 us  [the longest x1 9.22 us: on_device(): far_low = lax.ppermute(left[:64], 'x', ring(4, 1))]
    all_to_all x3 -> x4, waiting for transfers between devices: 12.7 us -> 15.5 us  [exchange(): return lax.all_to_all(value, axes, split_axis=0, concat_axis=0, tiled=True)]
    ppermute x4, starting transfers between devices: 14.3 us -> 16.7 us  [on_device(): kv[step] = lax.ppermute(kv[step - 1], Y, ring(8, 1))]
    ppermute x3, waiting for transfers between devices: 6.27 us -> 4.11 us  [on_device(): kv[-step] = lax.ppermute(kv[1 - step], Y, ring(8, -1))]
    dynamic_slice x1 -> x0, local copies, waits for them, and re-layouts: 2.16 us -> none  [pick(): return lax.dynamic_index_in_dim(value, index, axis, keepdims=False)]
  transfers between devices with their start and end apart: 19 -> 17, of which waited for: 12 -> 9; matrix products, arithmetic and copies ran while one was open for 5% -> 5% of each run, Pallas kernels for 6% -> 7%
where the time goes in v4:
time: 194 us; the launch traced here: 190 us
  starting transfers between devices  66.1 us (34%)
  blocking collectives  52.3 us (27%)
  waiting for transfers between devices  36 us (19%)
  Pallas kernels  17.8 us (9%)
  local copies, waits for them, and re-layouts  9.17 us (5%)
  other arithmetic  7.98 us (4%)
    all_to_all x3, blocking collectives, exchange(): return lax.all_to_all(value, axes, split_axis=0, concat_axis=0, tiled=True)  52.3 us
    ppermute x4, starting transfers between devices, on_device(): kv[step] = lax.ppermute(kv[step - 1], Y, ring(8, 1))  16.7 us
    all_to_all x4, starting transfers between devices, exchange(): return lax.all_to_all(value, axes, split_axis=0, concat_axis=0, tiled=True)  16.2 us
    all_to_all x4, waiting for transfers between devices, exchange(): return lax.all_to_all(value, axes, split_axis=0, concat_axis=0, tiled=True)  15.5 us
    pallas_call x3, Pallas kernels, attend(): call(functools.partial(attend_kernel, tiles, state is None, closing), out...  12.7 us
    ppermute x1, starting transfers between devices, on_device(): lax.ppermute(piece, 'zh', ring(2, 1))  10.9 us
    ppermute x1, waiting for transfers between devices, on_device(): far_low = lax.ppermute(left[:64], 'x', ring(4, 1))  9.22 us
    ppermute x3, starting transfers between devices, on_device(): kv[-step] = lax.ppermute(kv[1 - step], Y, ring(8, -1))  6.37 us
  transfers between devices with their start and end apart: 17, of which 9 were waited for; matrix products, arithmetic and copies ran while one was open for 5% of the time, Pallas kernels for 7%

profile of v4, /device:TPU:56, one launch (start us, length us, event | category | flops | bytes accessed | tf_op | source)
XLA Modules:
  0.0 190.4 jit_solution(211908146659697192)
XLA Ops:
  0.0 0.9 convert_reduce_fusion.5
  1.0 1.1 copy.48
  2.3 0.9 copy.50
  3.2 4.3 %all-to-all-start = ((bf16[8,160,128]{2,1,0:T(8,128)(2,1)}), bf16[8,160,128]{2,1,0:T(8,128)(2,1)S(1)}, u32[]{:S(2)}, u32[]{:S(2)}) async-start(bf16[8,160,128]{2,1,0:T(8,128)(2,1)} %bitcast.9), calls=%async_computation | async-start | bytes 655360 | tf_op jit(solution)/shard_map/all_to_all | solution.py:38
  7.5 3.9 %collective-permute-start.1 = (bf16[128,4096]{1,0:T(8,128)(2,1)S(1)}, bf16[128,4096]{1,0:T(8,128)(2,1)S(1)}, u32[]{:S(2)}, u32[]{:S(2)}) collective-permute-start(bf16[128,4096]{1,0:T(8,128)(2,1)S(1)} %bitcast.36), channel_id=1, source_target_pairs={{0,2},{2,4},{4,6},{6,0},{1,3},{3,5},{5,7},{7,1},{8,10},{10,12},{12... | collective-permute-start | bytes 3145736 | tf_op jit(solution)/shard_map/ppermute | solution.py:259
  11.4 3.1 %collective-permute-start.2 = (bf16[128,4096]{1,0:T(8,128)(2,1)S(1)}, bf16[128,4096]{1,0:T(8,128)(2,1)S(1)}, u32[]{:S(2)}, u32[]{:S(2)}) collective-permute-start(bf16[128,4096]{1,0:T(8,128)(2,1)S(1)} %bitcast.37), channel_id=1, source_target_pairs={{0,6},{2,0},{4,2},{6,4},{1,7},{3,1},{5,3},{7,5},{8,14},{10,8},{12,... | collective-permute-start | bytes 3145736 | tf_op jit(solution)/shard_map/ppermute | solution.py:260
  15.3 1.0 all-to-all-done
  16.3 0.7 copy-done.1
  16.9 10.9 %collective-permute-start = (bf16[128,128]{1,0:T(8,128)(2,1)S(1)}, bf16[128,128]{1,0:T(8,128)(2,1)S(1)}, u32[]{:S(2)}, u32[]{:S(2)}) collective-permute-start(bf16[128,128]{1,0:T(8,128)(2,1)S(1)} %dynamic-slice_bitcast_fusion), channel_id=1, source_target_pairs={{0,8},{8,0},{1,9},{9,1},{2,10},{10,2},{3,11},{11,3},{4,12},{12,4},... | collective-permute-start | bytes 98312 | tf_op jit(solution)/shard_map/ppermute | solution.py:256
  27.9 1.9 collective-permute-done
  29.8 0.8 broadcast_select_fusion
  30.6 17.2 %all_to_all.35 = bf16[8,128,128]{2,1,0:T(8,128)(2,1)S(1)} all-to-all(bf16[8,128,128]{2,1,0:T(8,128)(2,1)S(1)} %broadcast_in_dim.81), channel_id=1, replica_groups=mesh['z1'=2,'z0'=2,'y1'=4,'y0'=2,'zh'=2,'x'=4,'c'=2] {'z1','y1'}, dimensions={0} | all-to-all | bytes 524288 | tf_op jit(solution)/shard_map/all_to_all | solution.py:38
  47.7 1.1 broadcast_in_dim.82
  48.8 5.0 %all-to-all-start.2 = ((bf16[4,1024,128]{2,1,0:T(8,128)(2,1)}), bf16[4,1024,128]{2,1,0:T(8,128)(2,1)}, u32[]{:S(2)}, u32[]{:S(2)}) async-start(bf16[4,1024,128]{2,1,0:T(8,128)(2,1)} %broadcast_in_dim.82), calls=%async_computation.2 | async-start | bytes 2097152 | tf_op jit(solution)/shard_map/all_to_all | solution.py:38
  53.8 10.8 %all-to-all-done.2 = bf16[4,1024,128]{2,1,0:T(8,128)(2,1)} async-done(((bf16[4,1024,128]{2,1,0:T(8,128)(2,1)}), bf16[4,1024,128]{2,1,0:T(8,128)(2,1)}, u32[]{:S(2)}, u32[]{:S(2)}) %all-to-all-start.2) | async-done | bytes 1048608 | tf_op jit(solution)/shard_map/all_to_all | solution.py:38
  64.6 1.9 %collective-permute-start.5 = (bf16[32,128,128]{2,1,0:T(8,128)(2,1)}, bf16[32,128,128]{2,1,0:T(8,128)(2,1)S(1)}, u32[]{:S(2)}, u32[]{:S(2)}) collective-permute-start(bf16[32,128,128]{2,1,0:T(8,128)(2,1)} %bitcast.12.refs_5_), channel_id=1, source_target_pairs={{0,1},{1,0},{2,3},{3,2},{4,5},{5,4},{6,7},{7,6},{8,9},{9,8},{10,11... | collective-permute-start | bytes 3145736 | tf_op jit(solution)/shard_map/ppermute | solution.py:264
  67.1 2.5 %collective-permute-start.3 = (bf16[64,4096]{1,0:T(8,128)(2,1)S(1)}, bf16[64,4096]{1,0:T(8,128)(2,1)S(1)}, u32[]{:S(2)}, u32[]{:S(2)}) collective-permute-start(bf16[64,4096]{1,0:T(8,128)(2,1)S(1)} %slice.17), channel_id=1, source_target_pairs={{0,2},{2,4},{4,6},{6,0},{1,3},{3,5},{5,7},{7,1},{8,10},{10,12},{12... | collective-permute-start | bytes 1572872 | tf_op jit(solution)/shard_map/ppermute | solution.py:265
  69.6 4.6 %collective-permute-start.4 = (bf16[64,4096]{1,0:T(8,128)(2,1)S(1)}, bf16[64,4096]{1,0:T(8,128)(2,1)S(1)}, u32[]{:S(2)}, u32[]{:S(2)}) collective-permute-start(bf16[64,4096]{1,0:T(8,128)(2,1)S(1)} %slice.18), channel_id=1, source_target_pairs={{0,6},{2,0},{4,2},{6,4},{1,7},{3,1},{5,3},{7,5},{8,14},{10,8},{12,... | collective-permute-start | bytes 1572872 | tf_op jit(solution)/shard_map/ppermute | solution.py:266
  74.3 1.0 multiply_sine_fusion
  75.3 9.2 %collective-permute-done.3.refs_2_.refs_3_ = bf16[64,4096]{1,0:T(8,128)(2,1)S(1)} collective-permute-done((bf16[64,4096]{1,0:T(8,128)(2,1)S(1)}, bf16[64,4096]{1,0:T(8,128)(2,1)S(1)}, u32[]{:S(2)}, u32[]{:S(2)}) %collective-permute-start.3) | collective-permute-done | bytes 524320 | tf_op jit(solution)/shard_map/ppermute | solution.py:265
  84.5 1.6 collective-permute-done.4.refs_3_.refs_4_
  86.1 2.5 %shard_map.55.refs_7_ = f32[512,128]{1,0:T(8,128)S(1)} custom-call(bf16[128,4096]{1,0:T(8,128)(2,1)S(1)} %bitcast.38, bf16[128,4096]{1,0:T(8,128)(2,1)S(1)} %collective-permute-done.1.refs_1_.refs_2_, bf16[64,4096]{1,0:T(8,128)(2,1)S(1)} %collective-permute-done.3.refs_2_.refs_3_, bf16[64,4096]{1,0:T(8,128)(2,1)S(1)} %collective-permute-done.4.refs_3_.refs_4_, ...), custom_call_target="tpu_custom_call" | custom-call | flops 536870912 | bytes 5242880 | tf_op jit(solution)/shard_map/pallas_call | solution.py:122
  88.6 2.0 %shard_map.56 = bf16[4,2,128,128]{3,2,1,0:T(8,128)(2,1)S(1)} custom-call(s32[2]{0:T(128)S(1)} %pad_add_fusion.1.refs_0_, bf16[128,4096]{1,0:T(8,128)(2,1)S(1)} %bitcast.39, bf16[128,4096]{1,0:T(8,128)(2,1)S(1)} %collective-permute-done.1.refs_1_.refs_2_, bf16[64,4096]{1,0:T(8,128)(2,1)S(1)} %collective-permute-done.3.refs_2_.refs_3_, ...), custom_call_target="tpu_custom_call" | custom-call | flops 536870912 | bytes 5242880 | tf_op jit(solution)/shard_map/pallas_call | solution.py:148
  90.6 11.2 %all_to_all.36 = bf16[4,2,128,128]{3,2,1,0:T(8,128)(2,1)} all-to-all(bf16[4,2,128,128]{3,2,1,0:T(8,128)(2,1)S(1)} %shard_map.56), channel_id=1, replica_groups=mesh['z1'=2,'z0'=2,'y1'=4,'y0'=2,'zh'=2,'x'=4,'c'=2] {'x'}, dimensions={0} | all-to-all | bytes 524288 | tf_op jit(solution)/shard_map/all_to_all | solution.py:38
  101.8 3.4 %all-to-all-start.4 = ((bf16[4,2,128,128]{3,2,1,0:T(8,128)(2,1)}), bf16[4,2,128,128]{3,2,1,0:T(8,128)(2,1)S(1)}, u32[]{:S(2)}, u32[]{:S(2)}) async-start(bf16[4,2,128,128]{3,2,1,0:T(8,128)(2,1)} %all_to_all.36), calls=%async_computation.4 | async-start | bytes 524288 | tf_op jit(solution)/shard_map/all_to_all | solution.py:38
  105.2 1.6 copy.51
  106.8 1.3 copy.52
  108.2 3.8 %all-to-all-done.4.refs_0_ = bf16[4,2,128,128]{3,2,1,0:T(8,128)(2,1)S(1)} async-done(((bf16[4,2,128,128]{3,2,1,0:T(8,128)(2,1)}), bf16[4,2,128,128]{3,2,1,0:T(8,128)(2,1)S(1)}, u32[]{:S(2)}, u32[]{:S(2)}) %all-to-all-start.4) | async-done | bytes 262176 | tf_op jit(solution)/shard_map/all_to_all | solution.py:38
  112.0 3.5 %all-to-all-start.5 = ((bf16[4,128,1024]{2,1,0:T(8,128)(2,1)}), bf16[4,128,1024]{2,1,0:T(8,128)(2,1)S(1)}, u32[]{:S(2)}, u32[]{:S(2)}) async-start(bf16[4,128,1024]{2,1,0:T(8,128)(2,1)} %bitcast.15), calls=%async_computation.5 | async-start | bytes 2097152 | tf_op jit(solution)/shard_map/all_to_all | solution.py:38
  115.5 0.8 fusion.2
  116.3 3.1 %compare_select_fusion.4.start_ref = s32[4,1,128]{2,1,0:T(1,128)S(1)} fusion(s32[4,8,128]{2,1,0:T(8,128)S(1)} %bitcast.48, s32[]{:T(128)S(6)} %select_n.126, s32[]{:T(128)} %get-tuple-element.45, s32[]{:T(128)} %get-tuple-element.44, s32[]{:T(128)} %get-tuple-element.46, s32[]{:T(128)} %get-tuple-element.43, s32[]{:T(128)} %get-tuple-element.42), kind=kLoop, calls=%fused_computation.33 | loop fusion | flops 5120 | bytes 4120 | tf_op jit(solution)/shard_map/jit(_where)/select_n | solution.py:55
  119.5 2.6 %collective-permute-start.9 = (bf16[4,2,128,128]{3,2,1,0:T(8,128)(2,1)S(1)}, bf16[4,2,128,128]{3,2,1,0:T(8,128)(2,1)S(1)}, u32[]{:S(2)}, u32[]{:S(2)}) collective-permute-start(bf16[4,2,128,128]{3,2,1,0:T(8,128)(2,1)S(1)} %all-to-all-done.4.refs_0_), channel_id=1, source_target_pairs={{0,112},{16,0},{32,16},{48,32},{64,48},{80,64},{96,80},{112,96},{1... | collective-permute-start | bytes 786440 | tf_op jit(solution)/shard_map/ppermute | solution.py:298
  122.1 4.5 %collective-permute-start.6 = (bf16[4,2,128,128]{3,2,1,0:T(8,128)(2,1)S(1)}, bf16[4,2,128,128]{3,2,1,0:T(8,128)(2,1)S(1)}, u32[]{:S(2)}, u32[]{:S(2)}) collective-permute-start(bf16[4,2,128,128]{3,2,1,0:T(8,128)(2,1)S(1)} %all-to-all-done.4.refs_0_), channel_id=1, source_target_pairs={{0,16},{16,32},{32,48},{48,64},{64,80},{80,96},{96,112},{112,0},{1... | collective-permute-start | bytes 786440 | tf_op jit(solution)/shard_map/ppermute | solution.py:296
  126.7 2.3 %collective-permute-done.9.refs_3_ = bf16[4,2,128,128]{3,2,1,0:T(8,128)(2,1)S(1)} collective-permute-done((bf16[4,2,128,128]{3,2,1,0:T(8,128)(2,1)S(1)}, bf16[4,2,128,128]{3,2,1,0:T(8,128)(2,1)S(1)}, u32[]{:S(2)}, u32[]{:S(2)}) %collective-permute-start.9) | collective-permute-done | bytes 262176 | tf_op jit(solution)/shard_map/ppermute | solution.py:298
  129.0 1.9 %collective-permute-start.10 = (bf16[4,2,128,128]{3,2,1,0:T(8,128)(2,1)S(1)}, bf16[4,2,128,128]{3,2,1,0:T(8,128)(2,1)S(1)}, u32[]{:S(2)}, u32[]{:S(2)}) collective-permute-start(bf16[4,2,128,128]{3,2,1,0:T(8,128)(2,1)S(1)} %collective-permute-done.9.refs_3_), channel_id=1, source_target_pairs={{0,112},{16,0},{32,16},{48,32},{64,48},{80,64},{96,80},{112,96},{1... | collective-permute-start | bytes 786440 | tf_op jit(solution)/shard_map/ppermute | solution.py:298
  130.9 5.1 %collective-permute-start.7 = (bf16[4,2,128,128]{3,2,1,0:T(8,128)(2,1)S(1)}, bf16[4,2,128,128]{3,2,1,0:T(8,128)(2,1)S(1)}, u32[]{:S(2)}, u32[]{:S(2)}) collective-permute-start(bf16[4,2,128,128]{3,2,1,0:T(8,128)(2,1)S(1)} %collective-permute-done.6.refs_1_), channel_id=1, source_target_pairs={{0,16},{16,32},{32,48},{48,64},{64,80},{80,96},{96,112},{112,0},{1... | collective-permute-start | bytes 786440 | tf_op jit(solution)/shard_map/ppermute | solution.py:296
  136.7 1.8 collective-permute-done.10.refs_4_
  138.5 1.9 %collective-permute-start.11 = (bf16[4,2,128,128]{3,2,1,0:T(8,128)(2,1)S(1)}, bf16[4,2,128,128]{3,2,1,0:T(8,128)(2,1)S(1)}, u32[]{:S(2)}, u32[]{:S(2)}) collective-permute-start(bf16[4,2,128,128]{3,2,1,0:T(8,128)(2,1)S(1)} %collective-permute-done.10.refs_4_), channel_id=1, source_target_pairs={{0,112},{16,0},{32,16},{48,32},{64,48},{80,64},{96,80},{112,96},{1... | collective-permute-start | bytes 786440 | tf_op jit(solution)/shard_map/ppermute | solution.py:298
  140.4 5.1 %collective-permute-start.8 = (bf16[4,2,128,128]{3,2,1,0:T(8,128)(2,1)S(1)}, bf16[4,2,128,128]{3,2,1,0:T(8,128)(2,1)S(1)}, u32[]{:S(2)}, u32[]{:S(2)}) collective-permute-start(bf16[4,2,128,128]{3,2,1,0:T(8,128)(2,1)S(1)} %collective-permute-done.7.refs_2_), channel_id=1, source_target_pairs={{0,16},{16,32},{32,48},{48,64},{64,80},{80,96},{96,112},{112,0},{1... | collective-permute-start | bytes 786440 | tf_op jit(solution)/shard_map/ppermute | solution.py:296
  145.5 0.7 shard_map.57.q_ref
  146.2 7.8 %shard_map.58 = (f32[4,128,1024]{2,1,0:T(8,128)S(1)}, f32[4,1,1024]{2,1,0:T(1,128)S(1)}, f32[4,1,1024]{2,1,0:T(1,128)S(1)}) custom-call(s32[5]{0:T(128)S(1)} %pad_add_fusion.where_ref, bf16[4,128,1024]{2,1,0:T(8,128)(2,1)S(1)} %shard_map.57.q_ref, s32[4,1,128]{2,1,0:T(1,128)S(1)} %compare_select_fusion.4.start_ref, ...), custom_call_target="tpu_custom_call" | custom-call | flops 5368709120 | bytes 4194304 | tf_op jit(solution)/shard_map/pallas_call | solution.py:235
  154.0 1.9 %collective-permute-start.12 = (bf16[4,2,128,128]{3,2,1,0:T(8,128)(2,1)S(1)}, bf16[4,2,128,128]{3,2,1,0:T(8,128)(2,1)S(1)}, u32[]{:S(2)}, u32[]{:S(2)}) collective-permute-start(bf16[4,2,128,128]{3,2,1,0:T(8,128)(2,1)S(1)} %collective-permute-done.8.refs_0_), channel_id=1, source_target_pairs={{0,16},{16,32},{32,48},{48,64},{64,80},{80,96},{96,112},{112,0},{1... | collective-permute-start | bytes 786440 | tf_op jit(solution)/shard_map/ppermute | solution.py:296
  155.9 2.7 %shard_map.59 = (f32[4,128,1024]{2,1,0:T(8,128)S(1)}, f32[4,1,1024]{2,1,0:T(1,128)S(1)}, f32[4,1,1024]{2,1,0:T(1,128)S(1)}) custom-call(s32[5]{0:T(128)S(1)} %pad_add_fusion.where_ref, bf16[4,128,1024]{2,1,0:T(8,128)(2,1)S(1)} %shard_map.57.q_ref, s32[4,1,128]{2,1,0:T(1,128)S(1)} %compare_select_fusion.4.start_ref, ...), custom_call_target="tpu_custom_call" | custom-call | flops 2147483648 | bytes 4194304 | tf_op jit(solution)/shard_map/pallas_call | solution.py:235
  158.6 3.6 %collective-permute-done.12.refs_0_ = bf16[4,2,128,128]{3,2,1,0:T(8,128)(2,1)S(1)} collective-permute-done((bf16[4,2,128,128]{3,2,1,0:T(8,128)(2,1)S(1)}, bf16[4,2,128,128]{3,2,1,0:T(8,128)(2,1)S(1)}, u32[]{:S(2)}, u32[]{:S(2)}) %collective-permute-start.12) | collective-permute-done | bytes 262176 | tf_op jit(solution)/shard_map/ppermute | solution.py:296
  162.3 2.3 %shard_map.60 = bf16[4,128,1024]{2,1,0:T(8,128)(2,1)S(1)} custom-call(s32[5]{0:T(128)S(1)} %pad_add_fusion.where_ref, bf16[4,128,1024]{2,1,0:T(8,128)(2,1)S(1)} %shard_map.57.q_ref, s32[4,1,128]{2,1,0:T(1,128)S(1)} %compare_select_fusion.4.start_ref, bf16[4,2,128,128]{3,2,1,0:T(8,128)(2,1)S(1)} %collective-permute-done.12.refs_0_, ...), custom_call_target="tpu_custom_call" | custom-call | flops 1073741824 | bytes 4194304 | tf_op jit(solution)/shard_map/pallas_call | solution.py:235
  164.5 23.9 %all_to_all.37 = bf16[4,128,1024]{2,1,0:T(8,128)(2,1)S(1)} all-to-all(bf16[4,128,1024]{2,1,0:T(8,128)(2,1)S(1)} %shard_map.60), channel_id=1, replica_groups=mesh['z1'=2,'z0'=2,'y1'=4,'y0'=2,'zh'=2,'x'=4,'c'=2] {'z1','z0'}, dimensions={0} | all-to-all | bytes 2097152 | tf_op jit(solution)/shard_map/all_to_all | solution.py:38
  188.5 0.7 copy.53
  189.1 1.3 copy.54
  (34 shorter events, 1.9 us)
Async XLA Ops:
  0.0 7.5 %copy-start = (bf16[1,128,4096]{2,1,0:T(8,128)(2,1)S(1)}, bf16[1,128,4096]{2,1,0:T(8,128)(2,1)}, u32[]{:S(2)}) copy-start(bf16[1,128,4096]{2,1,0:T(8,128)(2,1)} %param.5) | copy-start | bytes 3145732
  3.2 13.0 %all-to-all-start = ((bf16[8,160,128]{2,1,0:T(8,128)(2,1)}), bf16[8,160,128]{2,1,0:T(8,128)(2,1)S(1)}, u32[]{:S(2)}, u32[]{:S(2)}) async-start(bf16[8,160,128]{2,1,0:T(8,128)(2,1)} %bitcast.9), calls=%async_computation | async-start | bytes 655360 | tf_op jit(solution)/shard_map/all_to_all | solution.py:38
  7.5 40.2 %collective-permute-start.1 = (bf16[128,4096]{1,0:T(8,128)(2,1)S(1)}, bf16[128,4096]{1,0:T(8,128)(2,1)S(1)}, u32[]{:S(2)}, u32[]{:S(2)}) collective-permute-start(bf16[128,4096]{1,0:T(8,128)(2,1)S(1)} %bitcast.36), channel_id=1, source_target_pairs={{0,2},{2,4},{4,6},{6,0},{1,3},{3,5},{5,7},{7,1},{8,10},{10,12},{12... | collective-permute-start | bytes 3145736 | tf_op jit(solution)/shard_map/ppermute | solution.py:259
  11.4 36.3 %collective-permute-start.2 = (bf16[128,4096]{1,0:T(8,128)(2,1)S(1)}, bf16[128,4096]{1,0:T(8,128)(2,1)S(1)}, u32[]{:S(2)}, u32[]{:S(2)}) collective-permute-start(bf16[128,4096]{1,0:T(8,128)(2,1)S(1)} %bitcast.37), channel_id=1, source_target_pairs={{0,6},{2,0},{4,2},{6,4},{1,7},{3,1},{5,3},{7,5},{8,14},{10,8},{12,... | collective-permute-start | bytes 3145736 | tf_op jit(solution)/shard_map/ppermute | solution.py:260
  16.2 0.7 copy-start.1
  16.9 12.8 %collective-permute-start = (bf16[128,128]{1,0:T(8,128)(2,1)S(1)}, bf16[128,128]{1,0:T(8,128)(2,1)S(1)}, u32[]{:S(2)}, u32[]{:S(2)}) collective-permute-start(bf16[128,128]{1,0:T(8,128)(2,1)S(1)} %dynamic-slice_bitcast_fusion), channel_id=1, source_target_pairs={{0,8},{8,0},{1,9},{9,1},{2,10},{10,2},{3,11},{11,3},{4,12},{12,4},... | collective-permute-start | bytes 98312 | tf_op jit(solution)/shard_map/ppermute | solution.py:256
  48.8 15.7 %all-to-all-start.2 = ((bf16[4,1024,128]{2,1,0:T(8,128)(2,1)}), bf16[4,1024,128]{2,1,0:T(8,128)(2,1)}, u32[]{:S(2)}, u32[]{:S(2)}) async-start(bf16[4,1024,128]{2,1,0:T(8,128)(2,1)} %broadcast_in_dim.82), calls=%async_computation.2 | async-start | bytes 2097152 | tf_op jit(solution)/shard_map/all_to_all | solution.py:38
  64.6 24.1 %collective-permute-start.5 = (bf16[32,128,128]{2,1,0:T(8,128)(2,1)}, bf16[32,128,128]{2,1,0:T(8,128)(2,1)S(1)}, u32[]{:S(2)}, u32[]{:S(2)}) collective-permute-start(bf16[32,128,128]{2,1,0:T(8,128)(2,1)} %bitcast.12.refs_5_), channel_id=1, source_target_pairs={{0,1},{1,0},{2,3},{3,2},{4,5},{5,4},{6,7},{7,6},{8,9},{9,8},{10,11... | collective-permute-start | bytes 3145736 | tf_op jit(solution)/shard_map/ppermute | solution.py:264
  67.1 17.4 %collective-permute-start.3 = (bf16[64,4096]{1,0:T(8,128)(2,1)S(1)}, bf16[64,4096]{1,0:T(8,128)(2,1)S(1)}, u32[]{:S(2)}, u32[]{:S(2)}) collective-permute-start(bf16[64,4096]{1,0:T(8,128)(2,1)S(1)} %slice.17), channel_id=1, source_target_pairs={{0,2},{2,4},{4,6},{6,0},{1,3},{3,5},{5,7},{7,1},{8,10},{10,12},{12... | collective-permute-start | bytes 1572872 | tf_op jit(solution)/shard_map/ppermute | solution.py:265
  69.6 16.5 %collective-permute-start.4 = (bf16[64,4096]{1,0:T(8,128)(2,1)S(1)}, bf16[64,4096]{1,0:T(8,128)(2,1)S(1)}, u32[]{:S(2)}, u32[]{:S(2)}) collective-permute-start(bf16[64,4096]{1,0:T(8,128)(2,1)S(1)} %slice.18), channel_id=1, source_target_pairs={{0,6},{2,0},{4,2},{6,4},{1,7},{3,1},{5,3},{7,5},{8,14},{10,8},{12,... | collective-permute-start | bytes 1572872 | tf_op jit(solution)/shard_map/ppermute | solution.py:266
  101.8 10.2 %all-to-all-start.4 = ((bf16[4,2,128,128]{3,2,1,0:T(8,128)(2,1)}), bf16[4,2,128,128]{3,2,1,0:T(8,128)(2,1)S(1)}, u32[]{:S(2)}, u32[]{:S(2)}) async-start(bf16[4,2,128,128]{3,2,1,0:T(8,128)(2,1)} %all_to_all.36), calls=%async_computation.4 | async-start | bytes 524288 | tf_op jit(solution)/shard_map/all_to_all | solution.py:38
  106.8 8.7 %copy-start.2 = (s32[1,4096]{1,0:T(1,128)S(1)}, s32[1,4096]{1,0:T(1,128)}, u32[]{:S(2)}) copy-start(s32[1,4096]{1,0:T(1,128)} %param.8) | copy-start | bytes 49156
  112.0 33.6 %all-to-all-start.5 = ((bf16[4,128,1024]{2,1,0:T(8,128)(2,1)}), bf16[4,128,1024]{2,1,0:T(8,128)(2,1)S(1)}, u32[]{:S(2)}, u32[]{:S(2)}) async-start(bf16[4,128,1024]{2,1,0:T(8,128)(2,1)} %bitcast.15), calls=%async_computation.5 | async-start | bytes 2097152 | tf_op jit(solution)/shard_map/all_to_all | solution.py:38
  119.5 9.5 %collective-permute-start.9 = (bf16[4,2,128,128]{3,2,1,0:T(8,128)(2,1)S(1)}, bf16[4,2,128,128]{3,2,1,0:T(8,128)(2,1)S(1)}, u32[]{:S(2)}, u32[]{:S(2)}) collective-permute-start(bf16[4,2,128,128]{3,2,1,0:T(8,128)(2,1)S(1)} %all-to-all-done.4.refs_0_), channel_id=1, source_target_pairs={{0,112},{16,0},{32,16},{48,32},{64,48},{80,64},{96,80},{112,96},{1... | collective-permute-start | bytes 786440 | tf_op jit(solution)/shard_map/ppermute | solution.py:298
  122.1 8.8 %collective-permute-start.6 = (bf16[4,2,128,128]{3,2,1,0:T(8,128)(2,1)S(1)}, bf16[4,2,128,128]{3,2,1,0:T(8,128)(2,1)S(1)}, u32[]{:S(2)}, u32[]{:S(2)}) collective-permute-start(bf16[4,2,128,128]{3,2,1,0:T(8,128)(2,1)S(1)} %all-to-all-done.4.refs_0_), channel_id=1, source_target_pairs={{0,16},{16,32},{32,48},{48,64},{64,80},{80,96},{96,112},{112,0},{1... | collective-permute-start | bytes 786440 | tf_op jit(solution)/shard_map/ppermute | solution.py:296
  129.0 9.5 %collective-permute-start.10 = (bf16[4,2,128,128]{3,2,1,0:T(8,128)(2,1)S(1)}, bf16[4,2,128,128]{3,2,1,0:T(8,128)(2,1)S(1)}, u32[]{:S(2)}, u32[]{:S(2)}) collective-permute-start(bf16[4,2,128,128]{3,2,1,0:T(8,128)(2,1)S(1)} %collective-permute-done.9.refs_3_), channel_id=1, source_target_pairs={{0,112},{16,0},{32,16},{48,32},{64,48},{80,64},{96,80},{112,96},{1... | collective-permute-start | bytes 786440 | tf_op jit(solution)/shard_map/ppermute | solution.py:298
  130.9 9.5 %collective-permute-start.7 = (bf16[4,2,128,128]{3,2,1,0:T(8,128)(2,1)S(1)}, bf16[4,2,128,128]{3,2,1,0:T(8,128)(2,1)S(1)}, u32[]{:S(2)}, u32[]{:S(2)}) collective-permute-start(bf16[4,2,128,128]{3,2,1,0:T(8,128)(2,1)S(1)} %collective-permute-done.6.refs_1_), channel_id=1, source_target_pairs={{0,16},{16,32},{32,48},{48,64},{64,80},{80,96},{96,112},{112,0},{1... | collective-permute-start | bytes 786440 | tf_op jit(solution)/shard_map/ppermute | solution.py:296
  138.5 15.5 %collective-permute-start.11 = (bf16[4,2,128,128]{3,2,1,0:T(8,128)(2,1)S(1)}, bf16[4,2,128,128]{3,2,1,0:T(8,128)(2,1)S(1)}, u32[]{:S(2)}, u32[]{:S(2)}) collective-permute-start(bf16[4,2,128,128]{3,2,1,0:T(8,128)(2,1)S(1)} %collective-permute-done.10.refs_4_), channel_id=1, source_target_pairs={{0,112},{16,0},{32,16},{48,32},{64,48},{80,64},{96,80},{112,96},{1... | collective-permute-start | bytes 786440 | tf_op jit(solution)/shard_map/ppermute | solution.py:298
  140.4 13.6 %collective-permute-start.8 = (bf16[4,2,128,128]{3,2,1,0:T(8,128)(2,1)S(1)}, bf16[4,2,128,128]{3,2,1,0:T(8,128)(2,1)S(1)}, u32[]{:S(2)}, u32[]{:S(2)}) collective-permute-start(bf16[4,2,128,128]{3,2,1,0:T(8,128)(2,1)S(1)} %collective-permute-done.7.refs_2_), channel_id=1, source_target_pairs={{0,16},{16,32},{32,48},{48,64},{64,80},{80,96},{96,112},{112,0},{1... | collective-permute-start | bytes 786440 | tf_op jit(solution)/shard_map/ppermute | solution.py:296
  154.0 8.3 %collective-permute-start.12 = (bf16[4,2,128,128]{3,2,1,0:T(8,128)(2,1)S(1)}, bf16[4,2,128,128]{3,2,1,0:T(8,128)(2,1)S(1)}, u32[]{:S(2)}, u32[]{:S(2)}) collective-permute-start(bf16[4,2,128,128]{3,2,1,0:T(8,128)(2,1)S(1)} %collective-permute-done.8.refs_0_), channel_id=1, source_target_pairs={{0,16},{16,32},{32,48},{48,64},{64,80},{80,96},{96,112},{112,0},{1... | collective-permute-start | bytes 786440 | tf_op jit(solution)/shard_map/ppermute | solution.py:296

commit v5 on v4

--- a/solution.py
+++ b/solution.py
@@ -17,6 +17,7 @@
 BLOCK = 128
 LOW = -1e30
 DOCS = 6
+FAR_LOW, FAR_HIGH = 4, -4
 
 AXES = ("z1", "z0", "y1", "y0", "zh", "x", "c")
 SIZES = (2, 2, 4, 2, 2, 4, 2)
@@ -189,10 +190,17 @@
                     for place in places
                 ]
 
-                @pl.when(functools.reduce(jnp.logical_or, needed))
-                def _():
-                    key = jnp.concatenate([kv[shift][zz, 0] for shift in tile], axis=0)
-                    val = jnp.concatenate([kv[shift][zz, 1] for shift in tile], axis=1)
+                if tile == (FAR_LOW,):
+                    needed.append(zz < 2)
+                if tile == (FAR_HIGH,):
+                    needed.append(zz >= 2)
+                halved = tile in ((FAR_LOW,), (FAR_HIGH,))
+                row = zz & 1 if halved else zz
+
+                @pl.when(functools.reduce(jnp.logical_and if halved else jnp.logical_or, needed))
+                def _(row=row, tile=tile, places=places):
+                    key = jnp.concatenate([kv[shift][row, 0] for shift in tile], axis=0)
+                    val = jnp.concatenate([kv[shift][row, 1] for shift in tile], axis=1)
                     allowed = []
                     for place in places:
                         at = place * BLOCK + lax.broadcasted_iota(jnp.int32, (BLOCK, BLOCK), 0)
@@ -261,30 +269,35 @@
     part = spread(piece, ("z1", "y1"), 8).reshape(8 * BLOCK, 128)
     part, left, right = lax.optimization_barrier((part, left, right))
     mine = spread(part, ("z0", "y0"), 4).reshape(32, BLOCK, 128)
-    other = lax.ppermute(mine, "c", ring(2, 1))
     far_low = lax.ppermute(left[:64], "x", ring(4, 1))
     far_high = lax.ppermute(right[64:], "x", ring(4, -1))
-    rows = [own, left, far_low, far_high, right]
 
     blocks = segment_row.reshape(4, 8, BLOCK)
     start = starts_of(segment_row, pick(blocks, y, 1))
     token = (jnp.arange(4)[:, None] * 8 + y) * BLOCK + jnp.arange(BLOCK)[None]
     q_angles = jnp.swapaxes(angles_of(token - start), 1, 2)
+    q_turns = (jnp.cos(q_angles), jnp.sin(q_angles))
+    split = queries[0].reshape(BLOCK, 4, GROUP * HEAD_DIM).transpose(1, 0, 2)
 
     rows_along = rows_along.astype(jnp.int32)
     along = pick(rows_along, z * 8 + y, 1)
     start_along = jax.vmap(starts_of)(rows_along, along)
     k_angles = angles_of((z * 8 + y) * BLOCK + jnp.arange(BLOCK)[None] - start_along)
-
+    k_turns = (jnp.cos(k_angles), jnp.sin(k_angles))
+
+    mine, far_low, far_high, start, q_turns, split, k_turns = lax.optimization_barrier(
+        (mine, far_low, far_high, start, q_turns, split, k_turns)
+    )
+    other = lax.ppermute(mine, "c", ring(2, 1))
+    rows = [own, left, far_low, far_high, right]
     first = project_first(rows, mine)
     both = project_second(
-        jnp.stack([x, c]).astype(jnp.int32), rows, other, first, jnp.cos(k_angles), jnp.sin(k_angles)
+        jnp.stack([x, c]).astype(jnp.int32), rows, other, first, *k_turns
     )
     own_kv = exchange(exchange(both, "x"), Z)
 
-    split = queries[0].reshape(BLOCK, 4, GROUP * HEAD_DIM).transpose(1, 0, 2)
     own_kv, split = lax.optimization_barrier((own_kv, split))
-    q_turned = turn_queries(exchange(split, Z), jnp.cos(q_angles), jnp.sin(q_angles))
+    q_turned = turn_queries(exchange(split, Z), *q_turns)
 
     where = jnp.concatenate([y[None], start[:, 0]]).astype(jnp.int32)
     start = start[:, None, :]
@@ -293,11 +306,13 @@
         if step == 4:
             state = attend(((0,), (1, 2), (-1, -2)), where, q_turned, start, kv)
             kv[3], kv[-3], *state = lax.optimization_barrier((kv[3], kv[-3], *state))
-        kv[step] = lax.ppermute(kv[step - 1], Y, ring(8, 1))
-        if step < 4:
+            kv[FAR_LOW] = lax.ppermute(kv[3][:2], Y, ring(8, 1))
+            kv[FAR_HIGH] = lax.ppermute(kv[-3][2:], Y, ring(8, -1))
+        else:
+            kv[step] = lax.ppermute(kv[step - 1], Y, ring(8, 1))
             kv[-step] = lax.ppermute(kv[1 - step], Y, ring(8, -1))
     state = attend(((3,), (-3,)), where, q_turned, start, kv, state)
-    mixed = attend(((4,),), where, q_turned, start, kv, state, closing=True)
+    mixed = attend(((FAR_LOW,), (FAR_HIGH,)), where, q_turned, start, kv, state, closing=True)
     back = exchange(mixed, Z)
     return back.transpose(1, 0, 2).reshape(1, BLOCK, HEADS * HEAD_DIM)
 

time: 194 us -> 195 us (level)
  waiting for transfers between devices: 36 us -> 18.8 us
  starting transfers between devices: 66.1 us -> 74.9 us
  local copies, waits for them, and re-layouts: 9.17 us -> 17 us
  Pallas kernels: 17.8 us -> 21.4 us
  blocking collectives: 52.3 us -> 48.7 us
    all_to_all x4, waiting for transfers between devices: 15.5 us -> 4.99 us  [exchange(): return lax.all_to_all(value, axes, split_axis=0, concat_axis=0, tiled=True)]
    ppermute x0 -> x2, starting transfers between devices: none -> 6.41 us  [the longest x1 4.3 us: on_device(): kv[FAR_LOW] = lax.ppermute(kv[3][:2], Y, ring(8, 1))]
    all_to_all x4, starting transfers between devices: 16.2 us -> 21.9 us  [exchange(): return lax.all_to_all(value, axes, split_axis=0, concat_axis=0, tiled=True)]
    unnamed x8 -> x22, local copies, waits for them, and re-layouts: 3.45 us -> 7.8 us
    ppermute x1, waiting for transfers between devices: 9.22 us -> 4.87 us  [on_device(): far_low = lax.ppermute(left[:64], 'x', ring(4, 1))]
    ppermute x3, waiting for transfers between devices: 4.11 us -> 0.03 us  [on_device(): kv[-step] = lax.ppermute(kv[1 - step], Y, ring(8, -1))]
    all_to_all x3, blocking collectives: 52.3 us -> 48.7 us  [exchange(): return lax.all_to_all(value, axes, split_axis=0, concat_axis=0, tiled=True)]
    ppermute x4 -> x3, starting transfers between devices: 16.7 us -> 13.3 us  [on_device(): kv[step] = lax.ppermute(kv[step - 1], Y, ring(8, 1))]
  transfers between devices with their start and end apart: 17 -> 18, of which waited for: 9 -> 9; matrix products, arithmetic and copies ran while one was open for 5% -> 8% of each run, Pallas kernels for 7% -> 8%
where the time goes in v5:
time: 195 us; the launch traced here: 191 us
  starting transfers between devices  74.9 us (38%)
  blocking collectives  48.7 us (25%)
  Pallas kernels  21.4 us (11%)
  waiting for transfers between devices  18.8 us (10%)
  local copies, waits for them, and re-layouts  17 us (9%)
  other arithmetic  9.42 us (5%)
    all_to_all x3, blocking collectives, exchange(): return lax.all_to_all(value, axes, split_axis=0, concat_axis=0, tiled=True)  48.7 us
    all_to_all x4, starting transfers between devices, exchange(): return lax.all_to_all(value, axes, split_axis=0, concat_axis=0, tiled=True)  21.9 us
    pallas_call x3, Pallas kernels, attend(): call(functools.partial(attend_kernel, tiles, state is None, closing), out...  15.6 us
    ppermute x3, starting transfers between devices, on_device(): kv[step] = lax.ppermute(kv[step - 1], Y, ring(8, 1))  13.3 us
    ppermute x1, starting transfers between devices, on_device(): lax.ppermute(piece, 'zh', ring(2, 1))  10.9 us
    unnamed x22, local copies, waits for them, and re-layouts  7.8 us
    ppermute x3, starting transfers between devices, on_device(): kv[-step] = lax.ppermute(kv[1 - step], Y, ring(8, -1))  6.41 us
    all_to_all x4, waiting for transfers between devices, exchange(): return lax.all_to_all(value, axes, split_axis=0, concat_axis=0, tiled=True)  4.99 us
  transfers between devices with their start and end apart: 18, of which 9 were waited for; matrix products, arithmetic and copies ran while one was open for 8% of the time, Pallas kernels for 8%

profile of v5, /device:TPU:56, one launch (start us, length us, event | category | flops | bytes accessed | tf_op | source)
XLA Modules:
  0.0 191.4 jit_solution(7090221979812032714)
XLA Ops:
  0.0 0.9 convert_reduce_fusion.5
  1.0 1.1 copy.53
  2.3 0.9 copy.55
  3.2 4.3 %all-to-all-start = ((bf16[8,160,128]{2,1,0:T(8,128)(2,1)}), bf16[8,160,128]{2,1,0:T(8,128)(2,1)S(1)}, u32[]{:S(2)}, u32[]{:S(2)}) async-start(bf16[8,160,128]{2,1,0:T(8,128)(2,1)} %bitcast.4), calls=%async_computation | async-start | bytes 655360 | tf_op jit(solution)/shard_map/all_to_all | solution.py:39
  7.5 3.9 %collective-permute-start.1 = (bf16[128,4096]{1,0:T(8,128)(2,1)S(1)}, bf16[128,4096]{1,0:T(8,128)(2,1)S(1)}, u32[]{:S(2)}, u32[]{:S(2)}) collective-permute-start(bf16[128,4096]{1,0:T(8,128)(2,1)S(1)} %bitcast.40), channel_id=1, source_target_pairs={{0,2},{2,4},{4,6},{6,0},{1,3},{3,5},{5,7},{7,1},{8,10},{10,12},{12... | collective-permute-start | bytes 3145736 | tf_op jit(solution)/shard_map/ppermute | solution.py:267
  11.4 3.1 %collective-permute-start.2 = (bf16[128,4096]{1,0:T(8,128)(2,1)S(1)}, bf16[128,4096]{1,0:T(8,128)(2,1)S(1)}, u32[]{:S(2)}, u32[]{:S(2)}) collective-permute-start(bf16[128,4096]{1,0:T(8,128)(2,1)S(1)} %bitcast.41), channel_id=1, source_target_pairs={{0,6},{2,0},{4,2},{6,4},{1,7},{3,1},{5,3},{7,5},{8,14},{10,8},{12,... | collective-permute-start | bytes 3145736 | tf_op jit(solution)/shard_map/ppermute | solution.py:268
  15.3 1.0 all-to-all-done
  17.0 10.9 %collective-permute-start = (bf16[128,128]{1,0:T(8,128)(2,1)S(1)}, bf16[128,128]{1,0:T(8,128)(2,1)S(1)}, u32[]{:S(2)}, u32[]{:S(2)}) collective-permute-start(bf16[128,128]{1,0:T(8,128)(2,1)S(1)} %dynamic-slice_bitcast_fusion), channel_id=1, source_target_pairs={{0,8},{8,0},{1,9},{9,1},{2,10},{10,2},{3,11},{11,3},{4,12},{12,4},... | collective-permute-start | bytes 98312 | tf_op jit(solution)/shard_map/ppermute | solution.py:264
  27.9 1.9 collective-permute-done
  31.3 9.1 %all-to-all-start.1 = ((bf16[8,128,128]{2,1,0:T(8,128)(2,1)}), bf16[8,128,128]{2,1,0:T(8,128)(2,1)}, u32[]{:S(2)}, u32[]{:S(2)}) async-start(bf16[8,128,128]{2,1,0:T(8,128)(2,1)} %broadcast_in_dim.73), calls=%async_computation.1 | async-start | bytes 524288 | tf_op jit(solution)/shard_map/all_to_all | solution.py:39
  40.4 2.3 %copy.57 = bf16[1,128,4096]{1,2,0:T(8,128)(2,1)} copy(bf16[1,128,4096]{2,1,0:T(8,128)(2,1)} %param.6) | data formatting | bytes 2097152 | tf_op args[1]
  42.7 2.3 %copy.58 = bf16[128,4,1024]{2,0,1:T(8,128)(2,1)} copy(bf16[128,4,1024]{0,2,1:T(8,128)(2,1)} %bitcast.50) | data formatting | bytes 2097152 | tf_op jit(solution)/shard_map/reshape;squeeze | solution.py:280
  45.0 3.8 %all-to-all-done.1 = bf16[8,128,128]{2,1,0:T(8,128)(2,1)} async-done(((bf16[8,128,128]{2,1,0:T(8,128)(2,1)}), bf16[8,128,128]{2,1,0:T(8,128)(2,1)}, u32[]{:S(2)}, u32[]{:S(2)}) %all-to-all-start.1) | async-done | bytes 262176 | tf_op jit(solution)/shard_map/all_to_all | solution.py:39
  48.8 2.1 %broadcast_in_dim.74 = bf16[4,1024,128]{2,1,0:T(8,128)(2,1)} broadcast(bf16[1024,128]{1,0:T(8,128)(2,1)} %bitcast.6), dimensions={1,2} | broadcast | bytes 1310720 | tf_op jit(solution)/shard_map/broadcast_in_dim | solution.py:43
  50.9 5.0 %all-to-all-start.2 = ((bf16[4,1024,128]{2,1,0:T(8,128)(2,1)}), bf16[4,1024,128]{2,1,0:T(8,128)(2,1)}, u32[]{:S(2)}, u32[]{:S(2)}) async-start(bf16[4,1024,128]{2,1,0:T(8,128)(2,1)} %broadcast_in_dim.74), calls=%async_computation.2 | async-start | bytes 2097152 | tf_op jit(solution)/shard_map/all_to_all | solution.py:39
  56.6 3.3 %subtract_convert_fusion.1 = (f32[4,128]{1,0:T(4,128)S(1)}, s32[4,128]{1,0:T(4,128)S(1)}) fusion(s32[4]{0:T(128)S(1)} %add_multiply_fusion, s32[]{:T(128)} %get-tuple-element.63, s32[4,1,128]{2,0,1:T(4,128)S(1)} %bitcast.55, s32[]{:T(128)} %get-tuple-element.64, s32[]{:T(128)} %get-tuple-element.60, s32[]{:T(128)} %get-tuple-element.61, s32[]{:T(128)} %get-tuple-element.62), kind=kLoop, calls=%fused_computation.32 | loop fusion | flops 6656 | bytes 6180 | tf_op jit(solution)/shard_map/convert_element_type | solution.py:49
  59.9 1.2 multiply_sine_fusion.1
  61.1 0.8 slice.29
  62.5 2.2 %collective-permute-start.3 = (bf16[64,4096]{1,0:T(8,128)(2,1)S(1)}, bf16[64,4096]{1,0:T(8,128)(2,1)S(1)}, u32[]{:S(2)}, u32[]{:S(2)}) collective-permute-start(bf16[64,4096]{1,0:T(8,128)(2,1)S(1)} %slice.22), channel_id=1, source_target_pairs={{0,2},{2,4},{4,6},{6,0},{1,3},{3,5},{5,7},{7,1},{8,10},{10,12},{12... | collective-permute-start | bytes 1572872 | tf_op jit(solution)/shard_map/ppermute | solution.py:272
  64.7 4.9 %collective-permute-start.4 = (bf16[64,4096]{1,0:T(8,128)(2,1)S(1)}, bf16[64,4096]{1,0:T(8,128)(2,1)S(1)}, u32[]{:S(2)}, u32[]{:S(2)}) collective-permute-start(bf16[64,4096]{1,0:T(8,128)(2,1)S(1)} %slice.23), channel_id=1, source_target_pairs={{0,6},{2,0},{4,2},{6,4},{1,7},{3,1},{5,3},{7,5},{8,14},{10,8},{12,... | collective-permute-start | bytes 1572872 | tf_op jit(solution)/shard_map/ppermute | solution.py:273
  69.7 1.7 multiply_sine_fusion
  71.4 4.9 %collective-permute-done.3.refs_2_.refs_3_ = bf16[64,4096]{1,0:T(8,128)(2,1)S(1)} collective-permute-done((bf16[64,4096]{1,0:T(8,128)(2,1)S(1)}, bf16[64,4096]{1,0:T(8,128)(2,1)S(1)}, u32[]{:S(2)}, u32[]{:S(2)}) %collective-permute-start.3) | collective-permute-done | bytes 524320 | tf_op jit(solution)/shard_map/ppermute | solution.py:272
  77.1 0.8 collective-permute-done.4.refs_3_.refs_4_
  77.9 0.8 copy-done.3
  78.7 1.9 collective-permute-start.5
  80.7 1.0 copy-done.2
  81.7 1.0 copy-done.4
  82.8 2.5 %shard_map.55.refs_7_ = f32[512,128]{1,0:T(8,128)S(1)} custom-call(bf16[128,4096]{1,0:T(8,128)(2,1)S(1)} %bitcast.42, bf16[128,4096]{1,0:T(8,128)(2,1)S(1)} %collective-permute-done.1.refs_1_.refs_2_, bf16[64,4096]{1,0:T(8,128)(2,1)S(1)} %copy-done.2, bf16[64,4096]{1,0:T(8,128)(2,1)S(1)} %copy-done.4, ...), custom_call_target="tpu_custom_call" | custom-call | flops 536870912 | bytes 5242880 | tf_op jit(solution)/shard_map/pallas_call | solution.py:123
  85.3 2.6 %shard_map.56 = bf16[4,2,128,128]{3,2,1,0:T(8,128)(2,1)S(1)} custom-call(s32[2]{0:T(128)S(1)} %pad_add_fusion.1.refs_0_, bf16[128,4096]{1,0:T(8,128)(2,1)S(1)} %bitcast.43, bf16[128,4096]{1,0:T(8,128)(2,1)S(1)} %collective-permute-done.1.refs_1_.refs_2_, bf16[64,4096]{1,0:T(8,128)(2,1)S(1)} %copy-done.2, bf16[64,4096]{1,0:T(8,128)(2,1)S(1)} %copy-done.4, ...), custom_call_target="tpu_custom_call" | custom-call | flops 536870912 | bytes 5242880 | tf_op jit(solution)/shard_map/pallas_call | solution.py:149
  87.9 11.8 %all_to_all.35 = bf16[4,2,128,128]{3,2,1,0:T(8,128)(2,1)S(1)} all-to-all(bf16[4,2,128,128]{3,2,1,0:T(8,128)(2,1)S(1)} %shard_map.56), channel_id=1, replica_groups=mesh['z1'=2,'z0'=2,'y1'=4,'y0'=2,'zh'=2,'x'=4,'c'=2] {'x'}, dimensions={0} | all-to-all | bytes 524288 | tf_op jit(solution)/shard_map/all_to_all | solution.py:39
  99.8 11.7 %all_to_all.36.refs_0_ = bf16[4,2,128,128]{3,2,1,0:T(8,128)(2,1)S(1)} all-to-all(bf16[4,2,128,128]{3,2,1,0:T(8,128)(2,1)S(1)} %all_to_all.35), channel_id=1, replica_groups=mesh['z1'=2,'z0'=2,'y1'=4,'y0'=2,'zh'=2,'x'=4,'c'=2] {'z1','z0'}, dimensions={0} | all-to-all | bytes 524288 | tf_op jit(solution)/shard_map/all_to_all | solution.py:39
  111.4 3.5 %all-to-all-start.5 = ((bf16[4,128,1024]{2,1,0:T(8,128)(2,1)}), bf16[4,128,1024]{2,1,0:T(8,128)(2,1)S(1)}, u32[]{:S(2)}, u32[]{:S(2)}) async-start(bf16[4,128,1024]{2,1,0:T(8,128)(2,1)} %bitcast.47), calls=%async_computation.5 | async-start | bytes 2097152 | tf_op jit(solution)/shard_map/all_to_all | solution.py:39
  115.0 3.3 %collective-permute-start.6 = (bf16[4,2,128,128]{3,2,1,0:T(8,128)(2,1)S(1)}, bf16[4,2,128,128]{3,2,1,0:T(8,128)(2,1)S(1)}, u32[]{:S(2)}, u32[]{:S(2)}) collective-permute-start(bf16[4,2,128,128]{3,2,1,0:T(8,128)(2,1)S(1)} %all_to_all.36.refs_0_), channel_id=1, source_target_pairs={{0,16},{16,32},{32,48},{48,64},{64,80},{80,96},{96,112},{112,0},{1... | collective-permute-start | bytes 786440 | tf_op jit(solution)/shard_map/ppermute | solution.py:312
  118.2 2.6 %collective-permute-start.9 = (bf16[4,2,128,128]{3,2,1,0:T(8,128)(2,1)S(1)}, bf16[4,2,128,128]{3,2,1,0:T(8,128)(2,1)S(1)}, u32[]{:S(2)}, u32[]{:S(2)}) collective-permute-start(bf16[4,2,128,128]{3,2,1,0:T(8,128)(2,1)S(1)} %all_to_all.36.refs_0_), channel_id=1, source_target_pairs={{0,112},{16,0},{32,16},{48,32},{64,48},{80,64},{96,80},{112,96},{1... | collective-permute-start | bytes 786440 | tf_op jit(solution)/shard_map/ppermute | solution.py:313
  120.8 2.5 %collective-permute-done.6.refs_1_ = bf16[4,2,128,128]{3,2,1,0:T(8,128)(2,1)S(1)} collective-permute-done((bf16[4,2,128,128]{3,2,1,0:T(8,128)(2,1)S(1)}, bf16[4,2,128,128]{3,2,1,0:T(8,128)(2,1)S(1)}, u32[]{:S(2)}, u32[]{:S(2)}) %collective-permute-start.6) | collective-permute-done | bytes 262176 | tf_op jit(solution)/shard_map/ppermute | solution.py:312
  123.4 4.5 %collective-permute-start.7 = (bf16[4,2,128,128]{3,2,1,0:T(8,128)(2,1)S(1)}, bf16[4,2,128,128]{3,2,1,0:T(8,128)(2,1)S(1)}, u32[]{:S(2)}, u32[]{:S(2)}) collective-permute-start(bf16[4,2,128,128]{3,2,1,0:T(8,128)(2,1)S(1)} %collective-permute-done.6.refs_1_), channel_id=1, source_target_pairs={{0,16},{16,32},{32,48},{48,64},{64,80},{80,96},{96,112},{112,0},{1... | collective-permute-start | bytes 786440 | tf_op jit(solution)/shard_map/ppermute | solution.py:312
  127.8 1.9 %collective-permute-start.10 = (bf16[4,2,128,128]{3,2,1,0:T(8,128)(2,1)S(1)}, bf16[4,2,128,128]{3,2,1,0:T(8,128)(2,1)S(1)}, u32[]{:S(2)}, u32[]{:S(2)}) collective-permute-start(bf16[4,2,128,128]{3,2,1,0:T(8,128)(2,1)S(1)} %collective-permute-done.9.refs_3_), channel_id=1, source_target_pairs={{0,112},{16,0},{32,16},{48,32},{64,48},{80,64},{96,80},{112,96},{1... | collective-permute-start | bytes 786440 | tf_op jit(solution)/shard_map/ppermute | solution.py:313
  130.0 1.7 collective-permute-done.7.refs_2_
  131.7 5.6 %collective-permute-start.8 = (bf16[4,2,128,128]{3,2,1,0:T(8,128)(2,1)S(1)}, bf16[4,2,128,128]{3,2,1,0:T(8,128)(2,1)S(1)}, u32[]{:S(2)}, u32[]{:S(2)}) collective-permute-start(bf16[4,2,128,128]{3,2,1,0:T(8,128)(2,1)S(1)} %collective-permute-done.7.refs_2_), channel_id=1, source_target_pairs={{0,16},{16,32},{32,48},{48,64},{64,80},{80,96},{96,112},{112,0},{1... | collective-permute-start | bytes 786440 | tf_op jit(solution)/shard_map/ppermute | solution.py:312
  137.3 1.9 collective-permute-start.11
  140.1 8.4 %shard_map.58 = (f32[4,128,1024]{2,1,0:T(8,128)S(1)}, f32[4,1,1024]{2,1,0:T(1,128)S(1)}, f32[4,1,1024]{2,1,0:T(1,128)S(1)}) custom-call(s32[5]{0:T(128)S(1)} %pad_add_fusion.where_ref, bf16[4,128,1024]{2,1,0:T(8,128)(2,1)S(1)} %shard_map.57.q_ref, s32[4,1,128]{2,1,0:T(1,128)S(1)} %bitcast.44, bf16[4,2,128,128]{3,2,1,0:T(8,128)(2,1)S(1)} %all_to_all.36.refs_0_, ...), custom_call_target="tpu_custom_call" | custom-call | flops 5368709120 | bytes 4194304 | tf_op jit(solution)/shard_map/pallas_call | solution.py:243
  148.5 4.3 %collective-permute-start.12 = (bf16[2,2,128,128]{3,2,1,0:T(8,128)(2,1)S(1)}, bf16[2,2,128,128]{3,2,1,0:T(8,128)(2,1)S(1)}, u32[]{:S(2)}, u32[]{:S(2)}) collective-permute-start(bf16[2,2,128,128]{3,2,1,0:T(8,128)(2,1)S(1)} %slice.26), channel_id=1, source_target_pairs={{0,16},{16,32},{32,48},{48,64},{64,80},{80,96},{96,112},{112,0},{1... | collective-permute-start | bytes 393224 | tf_op jit(solution)/shard_map/ppermute | solution.py:309
  152.9 2.1 %collective-permute-start.13 = (bf16[2,2,128,128]{3,2,1,0:T(8,128)(2,1)S(1)}, bf16[2,2,128,128]{3,2,1,0:T(8,128)(2,1)S(1)}, u32[]{:S(2)}, u32[]{:S(2)}) collective-permute-start(bf16[2,2,128,128]{3,2,1,0:T(8,128)(2,1)S(1)} %slice.27), channel_id=1, source_target_pairs={{0,112},{16,0},{32,16},{48,32},{64,48},{80,64},{96,80},{112,96},{1... | collective-permute-start | bytes 393224 | tf_op jit(solution)/shard_map/ppermute | solution.py:310
  155.0 4.0 %shard_map.59 = (f32[4,128,1024]{2,1,0:T(8,128)S(1)}, f32[4,1,1024]{2,1,0:T(1,128)S(1)}, f32[4,1,1024]{2,1,0:T(1,128)S(1)}) custom-call(s32[5]{0:T(128)S(1)} %pad_add_fusion.where_ref, bf16[4,128,1024]{2,1,0:T(8,128)(2,1)S(1)} %shard_map.57.q_ref, s32[4,1,128]{2,1,0:T(1,128)S(1)} %bitcast.45, bf16[4,2,128,128]{3,2,1,0:T(8,128)(2,1)S(1)} %collective-permute-done.8.refs_0_, ...), custom_call_target="tpu_custom_call" | custom-call | flops 2147483648 | bytes 4194304 | tf_op jit(solution)/shard_map/pallas_call | solution.py:243
  159.0 1.9 %collective-permute-done.13.refs_1_ = bf16[2,2,128,128]{3,2,1,0:T(8,128)(2,1)S(1)} collective-permute-done((bf16[2,2,128,128]{3,2,1,0:T(8,128)(2,1)S(1)}, bf16[2,2,128,128]{3,2,1,0:T(8,128)(2,1)S(1)}, u32[]{:S(2)}, u32[]{:S(2)}) %collective-permute-start.13) | collective-permute-done | bytes 131104 | tf_op jit(solution)/shard_map/ppermute | solution.py:310
  160.9 3.3 %shard_map.60 = bf16[4,128,1024]{2,1,0:T(8,128)(2,1)S(1)} custom-call(s32[5]{0:T(128)S(1)} %pad_add_fusion.where_ref, bf16[4,128,1024]{2,1,0:T(8,128)(2,1)S(1)} %shard_map.57.q_ref, s32[4,1,128]{2,1,0:T(1,128)S(1)} %bitcast.46, bf16[2,2,128,128]{3,2,1,0:T(8,128)(2,1)S(1)} %collective-permute-done.12.refs_0_, ...), custom_call_target="tpu_custom_call" | custom-call | flops 2147483648 | bytes 4194304 | tf_op jit(solution)/shard_map/pallas_call | solution.py:243
  164.2 25.2 %all_to_all.37 = bf16[4,128,1024]{2,1,0:T(8,128)(2,1)S(1)} all-to-all(bf16[4,128,1024]{2,1,0:T(8,128)(2,1)S(1)} %shard_map.60), channel_id=1, replica_groups=mesh['z1'=2,'z0'=2,'y1'=4,'y0'=2,'zh'=2,'x'=4,'c'=2] {'z1','z0'}, dimensions={0} | all-to-all | bytes 2097152 | tf_op jit(solution)/shard_map/all_to_all | solution.py:39
  190.1 1.3 copy.60
  (52 shorter events, 6.6 us)
Async XLA Ops:
  0.0 7.5 %copy-start = (bf16[1,128,4096]{2,1,0:T(8,128)(2,1)S(1)}, bf16[1,128,4096]{2,1,0:T(8,128)(2,1)}, u32[]{:S(2)}) copy-start(bf16[1,128,4096]{2,1,0:T(8,128)(2,1)} %param.5) | copy-start | bytes 3145732
  3.2 13.0 %all-to-all-start = ((bf16[8,160,128]{2,1,0:T(8,128)(2,1)}), bf16[8,160,128]{2,1,0:T(8,128)(2,1)S(1)}, u32[]{:S(2)}, u32[]{:S(2)}) async-start(bf16[8,160,128]{2,1,0:T(8,128)(2,1)} %bitcast.4), calls=%async_computation | async-start | bytes 655360 | tf_op jit(solution)/shard_map/all_to_all | solution.py:39
  7.5 41.3 %collective-permute-start.1 = (bf16[128,4096]{1,0:T(8,128)(2,1)S(1)}, bf16[128,4096]{1,0:T(8,128)(2,1)S(1)}, u32[]{:S(2)}, u32[]{:S(2)}) collective-permute-start(bf16[128,4096]{1,0:T(8,128)(2,1)S(1)} %bitcast.40), channel_id=1, source_target_pairs={{0,2},{2,4},{4,6},{6,0},{1,3},{3,5},{5,7},{7,1},{8,10},{10,12},{12... | collective-permute-start | bytes 3145736 | tf_op jit(solution)/shard_map/ppermute | solution.py:267
  11.4 37.4 %collective-permute-start.2 = (bf16[128,4096]{1,0:T(8,128)(2,1)S(1)}, bf16[128,4096]{1,0:T(8,128)(2,1)S(1)}, u32[]{:S(2)}, u32[]{:S(2)}) collective-permute-start(bf16[128,4096]{1,0:T(8,128)(2,1)S(1)} %bitcast.41), channel_id=1, source_target_pairs={{0,6},{2,0},{4,2},{6,4},{1,7},{3,1},{5,3},{7,5},{8,14},{10,8},{12,... | collective-permute-start | bytes 3145736 | tf_op jit(solution)/shard_map/ppermute | solution.py:268
  16.2 43.7 %copy-start.7 = (bf16[8,160,128]{2,1,0:T(8,128)(2,1)}, bf16[8,160,128]{2,1,0:T(8,128)(2,1)S(1)}, u32[]{:S(2)}) copy-start(bf16[8,160,128]{2,1,0:T(8,128)(2,1)S(1)} %all-to-all-done) | copy-start | bytes 983044
  16.2 0.8 copy-start.8
  17.0 12.8 %collective-permute-start = (bf16[128,128]{1,0:T(8,128)(2,1)S(1)}, bf16[128,128]{1,0:T(8,128)(2,1)S(1)}, u32[]{:S(2)}, u32[]{:S(2)}) collective-permute-start(bf16[128,128]{1,0:T(8,128)(2,1)S(1)} %dynamic-slice_bitcast_fusion), channel_id=1, source_target_pairs={{0,8},{8,0},{1,9},{9,1},{2,10},{10,2},{3,11},{11,3},{4,12},{12,4},... | collective-permute-start | bytes 98312 | tf_op jit(solution)/shard_map/ppermute | solution.py:264
  31.3 17.5 %all-to-all-start.1 = ((bf16[8,128,128]{2,1,0:T(8,128)(2,1)}), bf16[8,128,128]{2,1,0:T(8,128)(2,1)}, u32[]{:S(2)}, u32[]{:S(2)}) async-start(bf16[8,128,128]{2,1,0:T(8,128)(2,1)} %broadcast_in_dim.73), calls=%async_computation.1 | async-start | bytes 524288 | tf_op jit(solution)/shard_map/all_to_all | solution.py:39
  45.0 10.9 %copy-start.9 = (s32[1,4096]{1,0:T(1,128)S(1)}, s32[1,4096]{1,0:T(1,128)}, u32[]{:S(2)}) copy-start(s32[1,4096]{1,0:T(1,128)} %param.8) | copy-start | bytes 49156
  50.9 27.8 %all-to-all-start.2 = ((bf16[4,1024,128]{2,1,0:T(8,128)(2,1)}), bf16[4,1024,128]{2,1,0:T(8,128)(2,1)}, u32[]{:S(2)}, u32[]{:S(2)}) async-start(bf16[4,1024,128]{2,1,0:T(8,128)(2,1)} %broadcast_in_dim.74), calls=%async_computation.2 | async-start | bytes 2097152 | tf_op jit(solution)/shard_map/all_to_all | solution.py:39
  62.5 13.8 %collective-permute-start.3 = (bf16[64,4096]{1,0:T(8,128)(2,1)S(1)}, bf16[64,4096]{1,0:T(8,128)(2,1)S(1)}, u32[]{:S(2)}, u32[]{:S(2)}) collective-permute-start(bf16[64,4096]{1,0:T(8,128)(2,1)S(1)} %slice.22), channel_id=1, source_target_pairs={{0,2},{2,4},{4,6},{6,0},{1,3},{3,5},{5,7},{7,1},{8,10},{10,12},{12... | collective-permute-start | bytes 1572872 | tf_op jit(solution)/shard_map/ppermute | solution.py:272
  64.7 13.2 %collective-permute-start.4 = (bf16[64,4096]{1,0:T(8,128)(2,1)S(1)}, bf16[64,4096]{1,0:T(8,128)(2,1)S(1)}, u32[]{:S(2)}, u32[]{:S(2)}) collective-permute-start(bf16[64,4096]{1,0:T(8,128)(2,1)S(1)} %slice.23), channel_id=1, source_target_pairs={{0,6},{2,0},{4,2},{6,4},{1,7},{3,1},{5,3},{7,5},{8,14},{10,8},{12,... | collective-permute-start | bytes 1572872 | tf_op jit(solution)/shard_map/ppermute | solution.py:273
  76.3 0.8 copy-start.1
  77.9 0.8 copy-start.3
  78.7 6.6 %collective-permute-start.5 = (bf16[32,128,128]{2,1,0:T(8,128)(2,1)}, bf16[32,128,128]{2,1,0:T(8,128)(2,1)}, u32[]{:S(2)}, u32[]{:S(2)}) collective-permute-start(bf16[32,128,128]{2,1,0:T(8,128)(2,1)} %bitcast.8.refs_5_), channel_id=1, source_target_pairs={{0,1},{1,0},{2,3},{3,2},{4,5},{5,4},{6,7},{7,6},{8,9},{9,8},{10,11... | collective-permute-start | bytes 3145736 | tf_op jit(solution)/shard_map/ppermute | solution.py:291
  80.7 1.0 copy-start.2
  81.7 1.0 copy-start.4
  82.8 2.5 %copy-start.5 = (f32[4,128,64]{2,1,0:T(8,128)S(1)}, f32[4,128,64]{2,1,0:T(8,128)}, u32[]{:S(2)}) copy-start(f32[4,128,64]{2,1,0:T(8,128)} %get-tuple-element.37.refs_8_) | copy-start | bytes 393220
  87.9 51.5 %copy-start.6 = (f32[4,64,128]{2,1,0:T(8,128)S(1)}, f32[4,64,128]{2,1,0:T(8,128)}, u32[]{:S(2)}) copy-start(f32[4,64,128]{2,1,0:T(8,128)} %get-tuple-element.41.cos_ref) | copy-start | bytes 393220
  111.4 28.0 %all-to-all-start.5 = ((bf16[4,128,1024]{2,1,0:T(8,128)(2,1)}), bf16[4,128,1024]{2,1,0:T(8,128)(2,1)S(1)}, u32[]{:S(2)}, u32[]{:S(2)}) async-start(bf16[4,128,1024]{2,1,0:T(8,128)(2,1)} %bitcast.47), calls=%async_computation.5 | async-start | bytes 2097152 | tf_op jit(solution)/shard_map/all_to_all | solution.py:39
  115.0 8.4 %collective-permute-start.6 = (bf16[4,2,128,128]{3,2,1,0:T(8,128)(2,1)S(1)}, bf16[4,2,128,128]{3,2,1,0:T(8,128)(2,1)S(1)}, u32[]{:S(2)}, u32[]{:S(2)}) collective-permute-start(bf16[4,2,128,128]{3,2,1,0:T(8,128)(2,1)S(1)} %all_to_all.36.refs_0_), channel_id=1, source_target_pairs={{0,16},{16,32},{32,48},{48,64},{64,80},{80,96},{96,112},{112,0},{1... | collective-permute-start | bytes 786440 | tf_op jit(solution)/shard_map/ppermute | solution.py:312
  118.2 9.6 %collective-permute-start.9 = (bf16[4,2,128,128]{3,2,1,0:T(8,128)(2,1)S(1)}, bf16[4,2,128,128]{3,2,1,0:T(8,128)(2,1)S(1)}, u32[]{:S(2)}, u32[]{:S(2)}) collective-permute-start(bf16[4,2,128,128]{3,2,1,0:T(8,128)(2,1)S(1)} %all_to_all.36.refs_0_), channel_id=1, source_target_pairs={{0,112},{16,0},{32,16},{48,32},{64,48},{80,64},{96,80},{112,96},{1... | collective-permute-start | bytes 786440 | tf_op jit(solution)/shard_map/ppermute | solution.py:313
  123.4 8.3 %collective-permute-start.7 = (bf16[4,2,128,128]{3,2,1,0:T(8,128)(2,1)S(1)}, bf16[4,2,128,128]{3,2,1,0:T(8,128)(2,1)S(1)}, u32[]{:S(2)}, u32[]{:S(2)}) collective-permute-start(bf16[4,2,128,128]{3,2,1,0:T(8,128)(2,1)S(1)} %collective-permute-done.6.refs_1_), channel_id=1, source_target_pairs={{0,16},{16,32},{32,48},{48,64},{64,80},{80,96},{96,112},{112,0},{1... | collective-permute-start | bytes 786440 | tf_op jit(solution)/shard_map/ppermute | solution.py:312
  127.8 9.5 %collective-permute-start.10 = (bf16[4,2,128,128]{3,2,1,0:T(8,128)(2,1)S(1)}, bf16[4,2,128,128]{3,2,1,0:T(8,128)(2,1)S(1)}, u32[]{:S(2)}, u32[]{:S(2)}) collective-permute-start(bf16[4,2,128,128]{3,2,1,0:T(8,128)(2,1)S(1)} %collective-permute-done.9.refs_3_), channel_id=1, source_target_pairs={{0,112},{16,0},{32,16},{48,32},{64,48},{80,64},{96,80},{112,96},{1... | collective-permute-start | bytes 786440 | tf_op jit(solution)/shard_map/ppermute | solution.py:313
  131.7 16.8 %collective-permute-start.8 = (bf16[4,2,128,128]{3,2,1,0:T(8,128)(2,1)S(1)}, bf16[4,2,128,128]{3,2,1,0:T(8,128)(2,1)S(1)}, u32[]{:S(2)}, u32[]{:S(2)}) collective-permute-start(bf16[4,2,128,128]{3,2,1,0:T(8,128)(2,1)S(1)} %collective-permute-done.7.refs_2_), channel_id=1, source_target_pairs={{0,16},{16,32},{32,48},{48,64},{64,80},{80,96},{96,112},{112,0},{1... | collective-permute-start | bytes 786440 | tf_op jit(solution)/shard_map/ppermute | solution.py:312
  137.3 11.2 %collective-permute-start.11 = (bf16[4,2,128,128]{3,2,1,0:T(8,128)(2,1)S(1)}, bf16[4,2,128,128]{3,2,1,0:T(8,128)(2,1)S(1)}, u32[]{:S(2)}, u32[]{:S(2)}) collective-permute-start(bf16[4,2,128,128]{3,2,1,0:T(8,128)(2,1)S(1)} %collective-permute-done.10.refs_4_), channel_id=1, source_target_pairs={{0,112},{16,0},{32,16},{48,32},{64,48},{80,64},{96,80},{112,96},{1... | collective-permute-start | bytes 786440 | tf_op jit(solution)/shard_map/ppermute | solution.py:313
  148.5 10.5 %collective-permute-start.12 = (bf16[2,2,128,128]{3,2,1,0:T(8,128)(2,1)S(1)}, bf16[2,2,128,128]{3,2,1,0:T(8,128)(2,1)S(1)}, u32[]{:S(2)}, u32[]{:S(2)}) collective-permute-start(bf16[2,2,128,128]{3,2,1,0:T(8,128)(2,1)S(1)} %slice.26), channel_id=1, source_target_pairs={{0,16},{16,32},{32,48},{48,64},{64,80},{80,96},{96,112},{112,0},{1... | collective-permute-start | bytes 393224 | tf_op jit(solution)/shard_map/ppermute | solution.py:309
  152.9 8.1 %collective-permute-start.13 = (bf16[2,2,128,128]{3,2,1,0:T(8,128)(2,1)S(1)}, bf16[2,2,128,128]{3,2,1,0:T(8,128)(2,1)S(1)}, u32[]{:S(2)}, u32[]{:S(2)}) collective-permute-start(bf16[2,2,128,128]{3,2,1,0:T(8,128)(2,1)S(1)} %slice.27), channel_id=1, source_target_pairs={{0,112},{16,0},{32,16},{48,32},{64,48},{80,64},{96,80},{112,96},{1... | collective-permute-start | bytes 393224 | tf_op jit(solution)/shard_map/ppermute | solution.py:310

commit v6 on v5

--- a/solution.py
+++ b/solution.py
@@ -263,15 +263,6 @@
     rows_along = pick(got.reshape(4, 2, 160, 128)[:, :, BLOCK:], c, 1)
     piece = jnp.where(zh == origin // 8, piece, lax.ppermute(piece, "zh", ring(2, 1)))
 
-    own = hidden[0]
-    left = lax.ppermute(own, "x", ring(4, 1))
-    right = lax.ppermute(own, "x", ring(4, -1))
-    part = spread(piece, ("z1", "y1"), 8).reshape(8 * BLOCK, 128)
-    part, left, right = lax.optimization_barrier((part, left, right))
-    mine = spread(part, ("z0", "y0"), 4).reshape(32, BLOCK, 128)
-    far_low = lax.ppermute(left[:64], "x", ring(4, 1))
-    far_high = lax.ppermute(right[64:], "x", ring(4, -1))
-
     blocks = segment_row.reshape(4, 8, BLOCK)
     start = starts_of(segment_row, pick(blocks, y, 1))
     token = (jnp.arange(4)[:, None] * 8 + y) * BLOCK + jnp.arange(BLOCK)[None]
@@ -285,9 +276,18 @@
     k_angles = angles_of((z * 8 + y) * BLOCK + jnp.arange(BLOCK)[None] - start_along)
     k_turns = (jnp.cos(k_angles), jnp.sin(k_angles))
 
-    mine, far_low, far_high, start, q_turns, split, k_turns = lax.optimization_barrier(
-        (mine, far_low, far_high, start, q_turns, split, k_turns)
-    )
+    own = hidden[0]
+    left = lax.ppermute(own, "x", ring(4, 1))
+    right = lax.ppermute(own, "x", ring(4, -1))
+    part = spread(piece, ("z1", "y1"), 8).reshape(8 * BLOCK, 128)
+    tokens = (left[:8, :128], right[:8, :128])
+    part, tokens, start, q_turns, split, k_turns = lax.optimization_barrier(
+        (part, tokens, start, q_turns, split, k_turns)
+    )
+    mine = spread(part, ("z0", "y0"), 4).reshape(32, BLOCK, 128)
+    far_low = lax.ppermute(left[:64], "x", ring(4, 1))
+    far_high = lax.ppermute(right[64:], "x", ring(4, -1))
+    mine, tokens = lax.optimization_barrier((mine, (far_low[:8, :128], far_high[:8, :128])))
     other = lax.ppermute(mine, "c", ring(2, 1))
     rows = [own, left, far_low, far_high, right]
     first = project_first(rows, mine)

time: 195 us -> 210 us (1.077)
  the two profiles are of different devices: /device:TPU:56 before, /device:TPU:24 now
where the time goes in v6:
time: 210 us; the launch traced here: 209 us
  starting transfers between devices  74.4 us (35%)
  waiting for transfers between devices  50.2 us (24%)
  blocking collectives  42.7 us (20%)
  Pallas kernels  21.8 us (10%)
  local copies, waits for them, and re-layouts  9.91 us (5%)
  other arithmetic  8.63 us (4%)
    all_to_all x3, blocking collectives, exchange(): return lax.all_to_all(value, axes, split_axis=0, concat_axis=0, tiled=True)  42.7 us
    all_to_all x4, starting transfers between devices, exchange(): return lax.all_to_all(value, axes, split_axis=0, concat_axis=0, tiled=True)  23.3 us
    all_to_all x4, waiting for transfers between devices, exchange(): return lax.all_to_all(value, axes, split_axis=0, concat_axis=0, tiled=True)  15.4 us
    pallas_call x3, Pallas kernels, attend(): call(functools.partial(attend_kernel, tiles, state is None, closing), out...  15.3 us
    ppermute x1, waiting for transfers between devices, on_device(): left = lax.ppermute(own, 'x', ring(4, 1))  12.4 us
    ppermute x3, starting transfers between devices, on_device(): kv[-step] = lax.ppermute(kv[1 - step], Y, ring(8, -1))  11.2 us
    ppermute x1, starting transfers between devices, on_device(): lax.ppermute(piece, 'zh', ring(2, 1))  10.9 us
    ppermute x3, waiting for transfers between devices, on_device(): kv[step] = lax.ppermute(kv[step - 1], Y, ring(8, 1))  9.38 us
  transfers between devices with their start and end apart: 18, of which 10 were waited for; matrix products, arithmetic and copies ran while one was open for 5% of the time, Pallas kernels for 8%

profile of v6, /device:TPU:24, one launch (start us, length us, event | category | flops | bytes accessed | tf_op | source)
XLA Modules:
  0.0 208.7 jit_solution(15294962394710632828)
XLA Ops:
  0.0 0.9 convert_reduce_fusion.5
  1.0 1.1 copy.53
  2.3 0.9 copy.55
  3.2 4.3 %all-to-all-start = ((bf16[8,160,128]{2,1,0:T(8,128)(2,1)}), bf16[8,160,128]{2,1,0:T(8,128)(2,1)S(1)}, u32[]{:S(2)}, u32[]{:S(2)}) async-start(bf16[8,160,128]{2,1,0:T(8,128)(2,1)} %bitcast.4), calls=%async_computation | async-start | bytes 655360 | tf_op jit(solution)/shard_map/all_to_all | solution.py:39
  7.5 0.8 fusion.2
  8.3 3.2 %subtract_convert_fusion.1 = (f32[4,128]{1,0:T(4,128)S(1)}, s32[4,128]{1,0:T(4,128)S(1)}) fusion(s32[4]{0:T(128)S(1)} %add_multiply_fusion, s32[]{:T(128)} %get-tuple-element.53, s32[4,1,128]{2,0,1:T(4,128)S(1)} %bitcast.56, s32[]{:T(128)} %get-tuple-element.54, s32[]{:T(128)} %get-tuple-element.50, s32[]{:T(128)} %get-tuple-element.51, s32[]{:T(128)} %get-tuple-element.52), kind=kLoop, calls=%fused_computation.32 | loop fusion | flops 6656 | bytes 6180 | tf_op jit(solution)/shard_map/convert_element_type | solution.py:49
  12.9 1.3 copy.58
  14.2 1.2 multiply_sine_fusion.1
  15.8 10.9 %collective-permute-start = (bf16[128,128]{1,0:T(8,128)(2,1)S(1)}, bf16[128,128]{1,0:T(8,128)(2,1)S(1)}, u32[]{:S(2)}, u32[]{:S(2)}) collective-permute-start(bf16[128,128]{1,0:T(8,128)(2,1)S(1)} %dynamic-slice_bitcast_fusion), channel_id=1, source_target_pairs={{0,8},{8,0},{1,9},{9,1},{2,10},{10,2},{3,11},{11,3},{4,12},{12,4},... | collective-permute-start | bytes 98312 | tf_op jit(solution)/shard_map/ppermute | solution.py:264
  27.2 1.3 collective-permute-done
  28.6 0.7 broadcast_in_dim.73
  29.3 8.9 %all-to-all-start.1 = ((bf16[8,128,128]{2,1,0:T(8,128)(2,1)}), bf16[8,128,128]{2,1,0:T(8,128)(2,1)S(1)}, u32[]{:S(2)}, u32[]{:S(2)}) async-start(bf16[8,128,128]{2,1,0:T(8,128)(2,1)} %broadcast_in_dim.73), calls=%async_computation.1 | async-start | bytes 524288 | tf_op jit(solution)/shard_map/all_to_all | solution.py:39
  38.3 1.7 multiply_sine_fusion
  40.0 8.7 %all-to-all-done.1 = bf16[8,128,128]{2,1,0:T(8,128)(2,1)S(1)} async-done(((bf16[8,128,128]{2,1,0:T(8,128)(2,1)}), bf16[8,128,128]{2,1,0:T(8,128)(2,1)S(1)}, u32[]{:S(2)}, u32[]{:S(2)}) %all-to-all-start.1) | async-done | bytes 262176 | tf_op jit(solution)/shard_map/all_to_all | solution.py:39
  48.7 1.2 broadcast_in_dim.86
  49.9 6.6 %all-to-all-start.2 = ((bf16[4,1024,128]{2,1,0:T(8,128)(2,1)}), bf16[4,1024,128]{2,1,0:T(8,128)(2,1)}, u32[]{:S(2)}, u32[]{:S(2)}) async-start(bf16[4,1024,128]{2,1,0:T(8,128)(2,1)} %broadcast_in_dim.86), calls=%async_computation.2 | async-start | bytes 2097152 | tf_op jit(solution)/shard_map/all_to_all | solution.py:39
  56.5 3.4 %collective-permute-start.1 = (bf16[128,4096]{1,0:T(8,128)(2,1)S(1)}, bf16[128,4096]{1,0:T(8,128)(2,1)S(1)}, u32[]{:S(2)}, u32[]{:S(2)}) collective-permute-start(bf16[128,4096]{1,0:T(8,128)(2,1)S(1)} %bitcast.40), channel_id=1, source_target_pairs={{0,2},{2,4},{4,6},{6,0},{1,3},{3,5},{5,7},{7,1},{8,10},{10,12},{12... | collective-permute-start | bytes 3145736 | tf_op jit(solution)/shard_map/ppermute | solution.py:280
  59.9 3.6 %collective-permute-start.3 = (bf16[128,4096]{1,0:T(8,128)(2,1)S(1)}, bf16[128,4096]{1,0:T(8,128)(2,1)S(1)}, u32[]{:S(2)}, u32[]{:S(2)}) collective-permute-start(bf16[128,4096]{1,0:T(8,128)(2,1)S(1)} %bitcast.41), channel_id=1, source_target_pairs={{0,6},{2,0},{4,2},{6,4},{1,7},{3,1},{5,3},{7,5},{8,14},{10,8},{12,... | collective-permute-start | bytes 3145736 | tf_op jit(solution)/shard_map/ppermute | solution.py:281
  63.5 6.3 %all-to-all-done.2 = bf16[4,1024,128]{2,1,0:T(8,128)(2,1)} async-done(((bf16[4,1024,128]{2,1,0:T(8,128)(2,1)}), bf16[4,1024,128]{2,1,0:T(8,128)(2,1)}, u32[]{:S(2)}, u32[]{:S(2)}) %all-to-all-start.2) | async-done | bytes 1048608 | tf_op jit(solution)/shard_map/all_to_all | solution.py:39
  69.8 1.9 collective-permute-start.5
  71.7 12.4 %collective-permute-done.1.refs_1_.refs_2_ = bf16[128,4096]{1,0:T(8,128)(2,1)S(1)} collective-permute-done((bf16[128,4096]{1,0:T(8,128)(2,1)S(1)}, bf16[128,4096]{1,0:T(8,128)(2,1)S(1)}, u32[]{:S(2)}, u32[]{:S(2)}) %collective-permute-start.1) | collective-permute-done | bytes 1048608 | tf_op jit(solution)/shard_map/ppermute | solution.py:280
  84.1 0.8 slice.34
  84.9 2.3 %collective-permute-start.2 = (bf16[64,4096]{1,0:T(8,128)(2,1)}, bf16[64,4096]{1,0:T(8,128)(2,1)}, u32[]{:S(2)}, u32[]{:S(2)}) collective-permute-start(bf16[64,4096]{1,0:T(8,128)(2,1)} %slice.34), channel_id=1, source_target_pairs={{0,2},{2,4},{4,6},{6,0},{1,3},{3,5},{5,7},{7,1},{8,10},{10,12},{12... | collective-permute-start | bytes 1572872 | tf_op jit(solution)/shard_map/ppermute | solution.py:288
  87.3 0.8 slice.35
  88.1 4.7 %collective-permute-start.4 = (bf16[64,4096]{1,0:T(8,128)(2,1)}, bf16[64,4096]{1,0:T(8,128)(2,1)}, u32[]{:S(2)}, u32[]{:S(2)}) collective-permute-start(bf16[64,4096]{1,0:T(8,128)(2,1)} %slice.35), channel_id=1, source_target_pairs={{0,6},{2,0},{4,2},{6,4},{1,7},{3,1},{5,3},{7,5},{8,14},{10,8},{12,... | collective-permute-start | bytes 1572872 | tf_op jit(solution)/shard_map/ppermute | solution.py:289
  92.9 7.8 %collective-permute-done.2.refs_2_.refs_3_ = bf16[64,4096]{1,0:T(8,128)(2,1)} collective-permute-done((bf16[64,4096]{1,0:T(8,128)(2,1)}, bf16[64,4096]{1,0:T(8,128)(2,1)}, u32[]{:S(2)}, u32[]{:S(2)}) %collective-permute-start.2) | collective-permute-done | bytes 524320 | tf_op jit(solution)/shard_map/ppermute | solution.py:288
  100.7 2.0 collective-permute-done.4.refs_3_.refs_4_
  102.8 2.8 %shard_map.55.refs_7_ = f32[512,128]{1,0:T(8,128)S(1)} custom-call(bf16[128,4096]{1,0:T(8,128)(2,1)S(1)} %bitcast.42, bf16[128,4096]{1,0:T(8,128)(2,1)S(1)} %collective-permute-done.1.refs_1_.refs_2_, bf16[64,4096]{1,0:T(8,128)(2,1)} %collective-permute-done.2.refs_2_.refs_3_, bf16[64,4096]{1,0:T(8,128)(2,1)} %collective-permute-done.4.refs_3_.refs_4_, ...), custom_call_target="tpu_custom_call" | custom-call | flops 536870912 | bytes 5242880 | tf_op jit(solution)/shard_map/pallas_call | solution.py:123
  105.6 3.0 %shard_map.56 = bf16[4,2,128,128]{3,2,1,0:T(8,128)(2,1)S(1)} custom-call(s32[2]{0:T(128)S(1)} %pad_add_fusion.1.refs_0_, bf16[128,4096]{1,0:T(8,128)(2,1)S(1)} %bitcast.43, bf16[128,4096]{1,0:T(8,128)(2,1)S(1)} %collective-permute-done.1.refs_1_.refs_2_, bf16[64,4096]{1,0:T(8,128)(2,1)} %collective-permute-done.2.refs_2_.refs_3_, ...), custom_call_target="tpu_custom_call" | custom-call | flops 536870912 | bytes 5242880 | tf_op jit(solution)/shard_map/pallas_call | solution.py:149
  108.6 11.6 %all_to_all.35 = bf16[4,2,128,128]{3,2,1,0:T(8,128)(2,1)S(1)} all-to-all(bf16[4,2,128,128]{3,2,1,0:T(8,128)(2,1)S(1)} %shard_map.56), channel_id=1, replica_groups=mesh['z1'=2,'z0'=2,'y1'=4,'y0'=2,'zh'=2,'x'=4,'c'=2] {'x'}, dimensions={0} | all-to-all | bytes 524288 | tf_op jit(solution)/shard_map/all_to_all | solution.py:39
  120.2 9.7 %all_to_all.36.refs_0_ = bf16[4,2,128,128]{3,2,1,0:T(8,128)(2,1)S(1)} all-to-all(bf16[4,2,128,128]{3,2,1,0:T(8,128)(2,1)S(1)} %all_to_all.35), channel_id=1, replica_groups=mesh['z1'=2,'z0'=2,'y1'=4,'y0'=2,'zh'=2,'x'=4,'c'=2] {'z1','z0'}, dimensions={0} | all-to-all | bytes 524288 | tf_op jit(solution)/shard_map/all_to_all | solution.py:39
  129.9 3.5 %all-to-all-start.5 = ((bf16[4,128,1024]{2,1,0:T(8,128)(2,1)}), bf16[4,128,1024]{2,1,0:T(8,128)(2,1)S(1)}, u32[]{:S(2)}, u32[]{:S(2)}) async-start(bf16[4,128,1024]{2,1,0:T(8,128)(2,1)} %bitcast.47), calls=%async_computation.5 | async-start | bytes 2097152 | tf_op jit(solution)/shard_map/all_to_all | solution.py:39
  133.4 1.9 collective-permute-start.6
  135.3 3.9 %collective-permute-start.9 = (bf16[4,2,128,128]{3,2,1,0:T(8,128)(2,1)S(1)}, bf16[4,2,128,128]{3,2,1,0:T(8,128)(2,1)S(1)}, u32[]{:S(2)}, u32[]{:S(2)}) collective-permute-start(bf16[4,2,128,128]{3,2,1,0:T(8,128)(2,1)S(1)} %all_to_all.36.refs_0_), channel_id=1, source_target_pairs={{0,112},{16,0},{32,16},{48,32},{64,48},{80,64},{96,80},{112,96},{1... | collective-permute-start | bytes 786440 | tf_op jit(solution)/shard_map/ppermute | solution.py:313
  139.2 4.5 %collective-permute-done.6.refs_1_ = bf16[4,2,128,128]{3,2,1,0:T(8,128)(2,1)S(1)} collective-permute-done((bf16[4,2,128,128]{3,2,1,0:T(8,128)(2,1)S(1)}, bf16[4,2,128,128]{3,2,1,0:T(8,128)(2,1)S(1)}, u32[]{:S(2)}, u32[]{:S(2)}) %collective-permute-start.6) | collective-permute-done | bytes 262176 | tf_op jit(solution)/shard_map/ppermute | solution.py:312
  143.7 1.9 collective-permute-start.7
  145.7 3.9 %collective-permute-start.10 = (bf16[4,2,128,128]{3,2,1,0:T(8,128)(2,1)S(1)}, bf16[4,2,128,128]{3,2,1,0:T(8,128)(2,1)S(1)}, u32[]{:S(2)}, u32[]{:S(2)}) collective-permute-start(bf16[4,2,128,128]{3,2,1,0:T(8,128)(2,1)S(1)} %collective-permute-done.9.refs_3_), channel_id=1, source_target_pairs={{0,112},{16,0},{32,16},{48,32},{64,48},{80,64},{96,80},{112,96},{1... | collective-permute-start | bytes 786440 | tf_op jit(solution)/shard_map/ppermute | solution.py:313
  149.8 4.9 %collective-permute-done.7.refs_2_ = bf16[4,2,128,128]{3,2,1,0:T(8,128)(2,1)S(1)} collective-permute-done((bf16[4,2,128,128]{3,2,1,0:T(8,128)(2,1)S(1)}, bf16[4,2,128,128]{3,2,1,0:T(8,128)(2,1)S(1)}, u32[]{:S(2)}, u32[]{:S(2)}) %collective-permute-start.7) | collective-permute-done | bytes 262176 | tf_op jit(solution)/shard_map/ppermute | solution.py:312
  154.7 2.5 %collective-permute-start.8 = (bf16[4,2,128,128]{3,2,1,0:T(8,128)(2,1)S(1)}, bf16[4,2,128,128]{3,2,1,0:T(8,128)(2,1)S(1)}, u32[]{:S(2)}, u32[]{:S(2)}) collective-permute-start(bf16[4,2,128,128]{3,2,1,0:T(8,128)(2,1)S(1)} %collective-permute-done.7.refs_2_), channel_id=1, source_target_pairs={{0,16},{16,32},{32,48},{48,64},{64,80},{80,96},{96,112},{112,0},{1... | collective-permute-start | bytes 786440 | tf_op jit(solution)/shard_map/ppermute | solution.py:312
  157.2 3.3 %collective-permute-start.11 = (bf16[4,2,128,128]{3,2,1,0:T(8,128)(2,1)S(1)}, bf16[4,2,128,128]{3,2,1,0:T(8,128)(2,1)S(1)}, u32[]{:S(2)}, u32[]{:S(2)}) collective-permute-start(bf16[4,2,128,128]{3,2,1,0:T(8,128)(2,1)S(1)} %collective-permute-done.10.refs_4_), channel_id=1, source_target_pairs={{0,112},{16,0},{32,16},{48,32},{64,48},{80,64},{96,80},{112,96},{1... | collective-permute-start | bytes 786440 | tf_op jit(solution)/shard_map/ppermute | solution.py:313
  161.2 8.5 %shard_map.58 = (f32[4,128,1024]{2,1,0:T(8,128)S(1)}, f32[4,1,1024]{2,1,0:T(1,128)S(1)}, f32[4,1,1024]{2,1,0:T(1,128)S(1)}) custom-call(s32[5]{0:T(128)S(1)} %pad_add_fusion.where_ref, bf16[4,128,1024]{2,1,0:T(8,128)(2,1)S(1)} %shard_map.57.q_ref, s32[4,1,128]{2,1,0:T(1,128)S(1)} %bitcast.44, bf16[4,2,128,128]{3,2,1,0:T(8,128)(2,1)S(1)} %all_to_all.36.refs_0_, ...), custom_call_target="tpu_custom_call" | custom-call | flops 5368709120 | bytes 4194304 | tf_op jit(solution)/shard_map/pallas_call | solution.py:243
  169.7 4.6 %collective-permute-start.12 = (bf16[2,2,128,128]{3,2,1,0:T(8,128)(2,1)S(1)}, bf16[2,2,128,128]{3,2,1,0:T(8,128)(2,1)S(1)}, u32[]{:S(2)}, u32[]{:S(2)}) collective-permute-start(bf16[2,2,128,128]{3,2,1,0:T(8,128)(2,1)S(1)} %slice.30), channel_id=1, source_target_pairs={{0,16},{16,32},{32,48},{48,64},{64,80},{80,96},{96,112},{112,0},{1... | collective-permute-start | bytes 393224 | tf_op jit(solution)/shard_map/ppermute | solution.py:309
  174.4 2.1 %collective-permute-start.13 = (bf16[2,2,128,128]{3,2,1,0:T(8,128)(2,1)S(1)}, bf16[2,2,128,128]{3,2,1,0:T(8,128)(2,1)S(1)}, u32[]{:S(2)}, u32[]{:S(2)}) collective-permute-start(bf16[2,2,128,128]{3,2,1,0:T(8,128)(2,1)S(1)} %slice.31), channel_id=1, source_target_pairs={{0,112},{16,0},{32,16},{48,32},{64,48},{80,64},{96,80},{112,96},{1... | collective-permute-start | bytes 393224 | tf_op jit(solution)/shard_map/ppermute | solution.py:310
  176.5 4.0 %shard_map.59 = (f32[4,128,1024]{2,1,0:T(8,128)S(1)}, f32[4,1,1024]{2,1,0:T(1,128)S(1)}, f32[4,1,1024]{2,1,0:T(1,128)S(1)}) custom-call(s32[5]{0:T(128)S(1)} %pad_add_fusion.where_ref, bf16[4,128,1024]{2,1,0:T(8,128)(2,1)S(1)} %shard_map.57.q_ref, s32[4,1,128]{2,1,0:T(1,128)S(1)} %bitcast.45, bf16[4,2,128,128]{3,2,1,0:T(8,128)(2,1)S(1)} %collective-permute-done.8.refs_0_, ...), custom_call_target="tpu_custom_call" | custom-call | flops 2147483648 | bytes 4194304 | tf_op jit(solution)/shard_map/pallas_call | solution.py:243
  180.5 1.9 collective-permute-done.13.refs_1_
  182.5 2.8 %shard_map.60 = bf16[4,128,1024]{2,1,0:T(8,128)(2,1)S(1)} custom-call(s32[5]{0:T(128)S(1)} %pad_add_fusion.where_ref, bf16[4,128,1024]{2,1,0:T(8,128)(2,1)S(1)} %shard_map.57.q_ref, s32[4,1,128]{2,1,0:T(1,128)S(1)} %bitcast.46, bf16[2,2,128,128]{3,2,1,0:T(8,128)(2,1)S(1)} %collective-permute-done.12.refs_0_, ...), custom_call_target="tpu_custom_call" | custom-call | flops 2147483648 | bytes 4194304 | tf_op jit(solution)/shard_map/pallas_call | solution.py:243
  185.3 21.4 %all_to_all.37 = bf16[4,128,1024]{2,1,0:T(8,128)(2,1)S(1)} all-to-all(bf16[4,128,1024]{2,1,0:T(8,128)(2,1)S(1)} %shard_map.60), channel_id=1, replica_groups=mesh['z1'=2,'z0'=2,'y1'=4,'y0'=2,'zh'=2,'x'=4,'c'=2] {'z1','z0'}, dimensions={0} | all-to-all | bytes 2097152 | tf_op jit(solution)/shard_map/all_to_all | solution.py:39
  207.4 1.3 copy.60
  (42 shorter events, 3.6 us)
Async XLA Ops:
  0.0 7.5 %copy-start.4 = (s32[1,4096]{1,0:T(1,128)S(1)}, s32[1,4096]{1,0:T(1,128)}, u32[]{:S(2)}) copy-start(s32[1,4096]{1,0:T(1,128)} %param.8) | copy-start | bytes 49156
  0.0 12.2 %copy-start.3 = (bf16[1,128,4096]{2,1,0:T(8,128)(2,1)S(1)}, bf16[1,128,4096]{2,1,0:T(8,128)(2,1)}, u32[]{:S(2)}) copy-start(bf16[1,128,4096]{2,1,0:T(8,128)(2,1)} %param.6) | copy-start | bytes 3145732
  3.2 12.5 %all-to-all-start = ((bf16[8,160,128]{2,1,0:T(8,128)(2,1)}), bf16[8,160,128]{2,1,0:T(8,128)(2,1)S(1)}, u32[]{:S(2)}, u32[]{:S(2)}) async-start(bf16[8,160,128]{2,1,0:T(8,128)(2,1)} %bitcast.4), calls=%async_computation | async-start | bytes 655360 | tf_op jit(solution)/shard_map/all_to_all | solution.py:39
  15.8 12.8 %collective-permute-start = (bf16[128,128]{1,0:T(8,128)(2,1)S(1)}, bf16[128,128]{1,0:T(8,128)(2,1)S(1)}, u32[]{:S(2)}, u32[]{:S(2)}) collective-permute-start(bf16[128,128]{1,0:T(8,128)(2,1)S(1)} %dynamic-slice_bitcast_fusion), channel_id=1, source_target_pairs={{0,8},{8,0},{1,9},{9,1},{2,10},{10,2},{3,11},{11,3},{4,12},{12,4},... | collective-permute-start | bytes 98312 | tf_op jit(solution)/shard_map/ppermute | solution.py:264
  29.3 19.4 %all-to-all-start.1 = ((bf16[8,128,128]{2,1,0:T(8,128)(2,1)}), bf16[8,128,128]{2,1,0:T(8,128)(2,1)S(1)}, u32[]{:S(2)}, u32[]{:S(2)}) async-start(bf16[8,128,128]{2,1,0:T(8,128)(2,1)} %broadcast_in_dim.73), calls=%async_computation.1 | async-start | bytes 524288 | tf_op jit(solution)/shard_map/all_to_all | solution.py:39
  38.2 18.3 %copy-start = (bf16[1,128,4096]{2,1,0:T(8,128)(2,1)S(1)}, bf16[1,128,4096]{2,1,0:T(8,128)(2,1)}, u32[]{:S(2)}) copy-start(bf16[1,128,4096]{2,1,0:T(8,128)(2,1)} %param.5) | copy-start | bytes 3145732
  49.9 19.9 %all-to-all-start.2 = ((bf16[4,1024,128]{2,1,0:T(8,128)(2,1)}), bf16[4,1024,128]{2,1,0:T(8,128)(2,1)}, u32[]{:S(2)}, u32[]{:S(2)}) async-start(bf16[4,1024,128]{2,1,0:T(8,128)(2,1)} %broadcast_in_dim.86), calls=%async_computation.2 | async-start | bytes 2097152 | tf_op jit(solution)/shard_map/all_to_all | solution.py:39
  56.5 27.6 %collective-permute-start.1 = (bf16[128,4096]{1,0:T(8,128)(2,1)S(1)}, bf16[128,4096]{1,0:T(8,128)(2,1)S(1)}, u32[]{:S(2)}, u32[]{:S(2)}) collective-permute-start(bf16[128,4096]{1,0:T(8,128)(2,1)S(1)} %bitcast.40), channel_id=1, source_target_pairs={{0,2},{2,4},{4,6},{6,0},{1,3},{3,5},{5,7},{7,1},{8,10},{10,12},{12... | collective-permute-start | bytes 3145736 | tf_op jit(solution)/shard_map/ppermute | solution.py:280
  59.9 27.4 %collective-permute-start.3 = (bf16[128,4096]{1,0:T(8,128)(2,1)S(1)}, bf16[128,4096]{1,0:T(8,128)(2,1)S(1)}, u32[]{:S(2)}, u32[]{:S(2)}) collective-permute-start(bf16[128,4096]{1,0:T(8,128)(2,1)S(1)} %bitcast.41), channel_id=1, source_target_pairs={{0,6},{2,0},{4,2},{6,4},{1,7},{3,1},{5,3},{7,5},{8,14},{10,8},{12,... | collective-permute-start | bytes 3145736 | tf_op jit(solution)/shard_map/ppermute | solution.py:281
  69.8 35.8 %collective-permute-start.5 = (bf16[32,128,128]{2,1,0:T(8,128)(2,1)}, bf16[32,128,128]{2,1,0:T(8,128)(2,1)}, u32[]{:S(2)}, u32[]{:S(2)}) collective-permute-start(bf16[32,128,128]{2,1,0:T(8,128)(2,1)} %bitcast.15.refs_5_), channel_id=1, source_target_pairs={{0,1},{1,0},{2,3},{3,2},{4,5},{5,4},{6,7},{7,6},{8,9},{9,8},{10,11... | collective-permute-start | bytes 3145736 | tf_op jit(solution)/shard_map/ppermute | solution.py:291
  84.9 15.8 %collective-permute-start.2 = (bf16[64,4096]{1,0:T(8,128)(2,1)}, bf16[64,4096]{1,0:T(8,128)(2,1)}, u32[]{:S(2)}, u32[]{:S(2)}) collective-permute-start(bf16[64,4096]{1,0:T(8,128)(2,1)} %slice.34), channel_id=1, source_target_pairs={{0,2},{2,4},{4,6},{6,0},{1,3},{3,5},{5,7},{7,1},{8,10},{10,12},{12... | collective-permute-start | bytes 1572872 | tf_op jit(solution)/shard_map/ppermute | solution.py:288
  88.1 14.6 %collective-permute-start.4 = (bf16[64,4096]{1,0:T(8,128)(2,1)}, bf16[64,4096]{1,0:T(8,128)(2,1)}, u32[]{:S(2)}, u32[]{:S(2)}) collective-permute-start(bf16[64,4096]{1,0:T(8,128)(2,1)} %slice.35), channel_id=1, source_target_pairs={{0,6},{2,0},{4,2},{6,4},{1,7},{3,1},{5,3},{7,5},{8,14},{10,8},{12,... | collective-permute-start | bytes 1572872 | tf_op jit(solution)/shard_map/ppermute | solution.py:289
  92.9 12.7 %copy-start.1 = (f32[4,128,64]{2,1,0:T(8,128)S(1)}, f32[4,128,64]{2,1,0:T(8,128)}, u32[]{:S(2)}) copy-start(f32[4,128,64]{2,1,0:T(8,128)} %get-tuple-element.27.refs_8_) | copy-start | bytes 393220
  108.6 51.9 %copy-start.2 = (f32[4,64,128]{2,1,0:T(8,128)S(1)}, f32[4,64,128]{2,1,0:T(8,128)}, u32[]{:S(2)}) copy-start(f32[4,64,128]{2,1,0:T(8,128)} %get-tuple-element.31.cos_ref) | copy-start | bytes 393220
  129.9 30.7 %all-to-all-start.5 = ((bf16[4,128,1024]{2,1,0:T(8,128)(2,1)}), bf16[4,128,1024]{2,1,0:T(8,128)(2,1)S(1)}, u32[]{:S(2)}, u32[]{:S(2)}) async-start(bf16[4,128,1024]{2,1,0:T(8,128)(2,1)} %bitcast.47), calls=%async_computation.5 | async-start | bytes 2097152 | tf_op jit(solution)/shard_map/all_to_all | solution.py:39
  133.4 10.4 %collective-permute-start.6 = (bf16[4,2,128,128]{3,2,1,0:T(8,128)(2,1)S(1)}, bf16[4,2,128,128]{3,2,1,0:T(8,128)(2,1)S(1)}, u32[]{:S(2)}, u32[]{:S(2)}) collective-permute-start(bf16[4,2,128,128]{3,2,1,0:T(8,128)(2,1)S(1)} %all_to_all.36.refs_0_), channel_id=1, source_target_pairs={{0,16},{16,32},{32,48},{48,64},{64,80},{80,96},{96,112},{112,0},{1... | collective-permute-start | bytes 786440 | tf_op jit(solution)/shard_map/ppermute | solution.py:312
  135.3 10.3 %collective-permute-start.9 = (bf16[4,2,128,128]{3,2,1,0:T(8,128)(2,1)S(1)}, bf16[4,2,128,128]{3,2,1,0:T(8,128)(2,1)S(1)}, u32[]{:S(2)}, u32[]{:S(2)}) collective-permute-start(bf16[4,2,128,128]{3,2,1,0:T(8,128)(2,1)S(1)} %all_to_all.36.refs_0_), channel_id=1, source_target_pairs={{0,112},{16,0},{32,16},{48,32},{64,48},{80,64},{96,80},{112,96},{1... | collective-permute-start | bytes 786440 | tf_op jit(solution)/shard_map/ppermute | solution.py:313
  143.7 10.9 %collective-permute-start.7 = (bf16[4,2,128,128]{3,2,1,0:T(8,128)(2,1)S(1)}, bf16[4,2,128,128]{3,2,1,0:T(8,128)(2,1)S(1)}, u32[]{:S(2)}, u32[]{:S(2)}) collective-permute-start(bf16[4,2,128,128]{3,2,1,0:T(8,128)(2,1)S(1)} %collective-permute-done.6.refs_1_), channel_id=1, source_target_pairs={{0,16},{16,32},{32,48},{48,64},{64,80},{80,96},{96,112},{112,0},{1... | collective-permute-start | bytes 786440 | tf_op jit(solution)/shard_map/ppermute | solution.py:312
  145.7 11.5 %collective-permute-start.10 = (bf16[4,2,128,128]{3,2,1,0:T(8,128)(2,1)S(1)}, bf16[4,2,128,128]{3,2,1,0:T(8,128)(2,1)S(1)}, u32[]{:S(2)}, u32[]{:S(2)}) collective-permute-start(bf16[4,2,128,128]{3,2,1,0:T(8,128)(2,1)S(1)} %collective-permute-done.9.refs_3_), channel_id=1, source_target_pairs={{0,112},{16,0},{32,16},{48,32},{64,48},{80,64},{96,80},{112,96},{1... | collective-permute-start | bytes 786440 | tf_op jit(solution)/shard_map/ppermute | solution.py:313
  154.7 15.0 %collective-permute-start.8 = (bf16[4,2,128,128]{3,2,1,0:T(8,128)(2,1)S(1)}, bf16[4,2,128,128]{3,2,1,0:T(8,128)(2,1)S(1)}, u32[]{:S(2)}, u32[]{:S(2)}) collective-permute-start(bf16[4,2,128,128]{3,2,1,0:T(8,128)(2,1)S(1)} %collective-permute-done.7.refs_2_), channel_id=1, source_target_pairs={{0,16},{16,32},{32,48},{48,64},{64,80},{80,96},{96,112},{112,0},{1... | collective-permute-start | bytes 786440 | tf_op jit(solution)/shard_map/ppermute | solution.py:312
  157.2 12.5 %collective-permute-start.11 = (bf16[4,2,128,128]{3,2,1,0:T(8,128)(2,1)S(1)}, bf16[4,2,128,128]{3,2,1,0:T(8,128)(2,1)S(1)}, u32[]{:S(2)}, u32[]{:S(2)}) collective-permute-start(bf16[4,2,128,128]{3,2,1,0:T(8,128)(2,1)S(1)} %collective-permute-done.10.refs_4_), channel_id=1, source_target_pairs={{0,112},{16,0},{32,16},{48,32},{64,48},{80,64},{96,80},{112,96},{1... | collective-permute-start | bytes 786440 | tf_op jit(solution)/shard_map/ppermute | solution.py:313
  169.7 10.8 %collective-permute-start.12 = (bf16[2,2,128,128]{3,2,1,0:T(8,128)(2,1)S(1)}, bf16[2,2,128,128]{3,2,1,0:T(8,128)(2,1)S(1)}, u32[]{:S(2)}, u32[]{:S(2)}) collective-permute-start(bf16[2,2,128,128]{3,2,1,0:T(8,128)(2,1)S(1)} %slice.30), channel_id=1, source_target_pairs={{0,16},{16,32},{32,48},{48,64},{64,80},{80,96},{96,112},{112,0},{1... | collective-permute-start | bytes 393224 | tf_op jit(solution)/shard_map/ppermute | solution.py:309
  174.4 8.1 %collective-permute-start.13 = (bf16[2,2,128,128]{3,2,1,0:T(8,128)(2,1)S(1)}, bf16[2,2,128,128]{3,2,1,0:T(8,128)(2,1)S(1)}, u32[]{:S(2)}, u32[]{:S(2)}) collective-permute-start(bf16[2,2,128,128]{3,2,1,0:T(8,128)(2,1)S(1)} %slice.31), channel_id=1, source_target_pairs={{0,112},{16,0},{32,16},{48,32},{64,48},{80,64},{96,80},{112,96},{1... | collective-permute-start | bytes 393224 | tf_op jit(solution)/shard_map/ppermute | solution.py:310

commit v7 on v6

--- a/solution.py
+++ b/solution.py
@@ -116,16 +116,16 @@
 
 
 def project_first_kernel(*refs):
-    multiply(refs[:5], refs[5], refs[6])
-
-
-def project_first(hidden, weight):
+    multiply(refs[:5], refs[5], refs[8])
+
+
+def project_first(hidden, weight, arrived):
     return call(
         project_first_kernel,
         jax.ShapeDtypeStruct((4 * BLOCK, HEAD_DIM), jnp.float32),
-        [VMEM] * 6,
+        [VMEM] * 8,
         (2**29, 5 * 2**20),
-    )(*hidden, weight)
+    )(*hidden, weight, *arrived)
 
 
 def project_second_kernel(*refs):
@@ -280,17 +280,16 @@
     left = lax.ppermute(own, "x", ring(4, 1))
     right = lax.ppermute(own, "x", ring(4, -1))
     part = spread(piece, ("z1", "y1"), 8).reshape(8 * BLOCK, 128)
-    tokens = (left[:8, :128], right[:8, :128])
-    part, tokens, start, q_turns, split, k_turns = lax.optimization_barrier(
-        (part, tokens, start, q_turns, split, k_turns)
+    part, left, right, start, q_turns, split, k_turns = lax.optimization_barrier(
+        (part, left, right, start, q_turns, split, k_turns)
     )
     mine = spread(part, ("z0", "y0"), 4).reshape(32, BLOCK, 128)
     far_low = lax.ppermute(left[:64], "x", ring(4, 1))
     far_high = lax.ppermute(right[64:], "x", ring(4, -1))
-    mine, tokens = lax.optimization_barrier((mine, (far_low[:8, :128], far_high[:8, :128])))
+    mine, *arrived = lax.optimization_barrier((mine, far_low[:8, :128], far_high[:8, :128]))
     other = lax.ppermute(mine, "c", ring(2, 1))
     rows = [own, left, far_low, far_high, right]
-    first = project_first(rows, mine)
+    first = project_first(rows, mine, arrived)
     both = project_second(
         jnp.stack([x, c]).astype(jnp.int32), rows, other, first, *k_turns
     )

time: 210 us -> 209 us (level)
  the two profiles are of different devices: /device:TPU:24 before, /device:TPU:1 now
where the time goes in v7:
time: 209 us; the launch traced here: 208 us
  starting transfers between devices  88.1 us (42%)
  blocking collectives  47 us (22%)
  waiting for transfers between devices  26.6 us (13%)
  Pallas kernels  21.9 us (10%)
  local copies, waits for them, and re-layouts  14.7 us (7%)
  other arithmetic  8.6 us (4%)
    all_to_all x3, blocking collectives, exchange(): return lax.all_to_all(value, axes, split_axis=0, concat_axis=0, tiled=True)  47 us
    all_to_all x4, starting transfers between devices, exchange(): return lax.all_to_all(value, axes, split_axis=0, concat_axis=0, tiled=True)  29.2 us
    pallas_call x3, Pallas kernels, attend(): call(functools.partial(attend_kernel, tiles, state is None, closing), out...  16.1 us
    all_to_all x4, waiting for transfers between devices, exchange(): return lax.all_to_all(value, axes, split_axis=0, concat_axis=0, tiled=True)  13.4 us
    ppermute x3, starting transfers between devices, on_device(): kv[-step] = lax.ppermute(kv[1 - step], Y, ring(8, -1))  12.5 us
    ppermute x1, starting transfers between devices, on_device(): lax.ppermute(piece, 'zh', ring(2, 1))  10.6 us
    ppermute x3, starting transfers between devices, on_device(): kv[step] = lax.ppermute(kv[step - 1], Y, ring(8, 1))  6.91 us
    ppermute x1, starting transfers between devices, on_device(): other = lax.ppermute(mine, 'c', ring(2, 1))  6.61 us
  transfers between devices with their start and end apart: 18, of which 8 were waited for; matrix products, arithmetic and copies ran while one was open for 8% of the time, Pallas kernels for 8%

profile of v7, /device:TPU:1, one launch (start us, length us, event | category | flops | bytes accessed | tf_op | source)
XLA Modules:
  0.0 207.9 jit_solution(8016165958307205947)
XLA Ops:
  0.0 4.1 %collective-permute-start.1 = (bf16[128,4096]{1,0:T(8,128)(2,1)}, bf16[128,4096]{1,0:T(8,128)(2,1)S(1)}, u32[]{:S(2)}, u32[]{:S(2)}) collective-permute-start(bf16[128,4096]{1,0:T(8,128)(2,1)} %bitcast.40), channel_id=1, source_target_pairs={{0,2},{2,4},{4,6},{6,0},{1,3},{3,5},{5,7},{7,1},{8,10},{10,12},{12... | collective-permute-start | bytes 3145736 | tf_op jit(solution)/shard_map/ppermute | solution.py:280
  4.1 3.2 %collective-permute-start.2 = (bf16[128,4096]{1,0:T(8,128)(2,1)}, bf16[128,4096]{1,0:T(8,128)(2,1)S(1)}, u32[]{:S(2)}, u32[]{:S(2)}) collective-permute-start(bf16[128,4096]{1,0:T(8,128)(2,1)} %bitcast.41), channel_id=1, source_target_pairs={{0,6},{2,0},{4,2},{6,4},{1,7},{3,1},{5,3},{7,5},{8,14},{10,8},{12,... | collective-permute-start | bytes 3145736 | tf_op jit(solution)/shard_map/ppermute | solution.py:281
  8.2 1.1 copy.53
  9.5 0.9 copy.55
  10.4 10.7 %all-to-all-start = ((bf16[8,160,128]{2,1,0:T(8,128)(2,1)}), bf16[8,160,128]{2,1,0:T(8,128)(2,1)}, u32[]{:S(2)}, u32[]{:S(2)}) async-start(bf16[8,160,128]{2,1,0:T(8,128)(2,1)} %bitcast.4), calls=%async_computation | async-start | bytes 655360 | tf_op jit(solution)/shard_map/all_to_all | solution.py:39
  21.1 0.8 fusion.2
  22.0 3.2 %subtract_convert_fusion.1 = (f32[4,128]{1,0:T(4,128)S(1)}, s32[4,128]{1,0:T(4,128)S(1)}) fusion(s32[4]{0:T(128)S(1)} %add_multiply_fusion, s32[]{:T(128)} %get-tuple-element.63, s32[4,1,128]{2,0,1:T(4,128)S(1)} %bitcast.55, s32[]{:T(128)} %get-tuple-element.64, s32[]{:T(128)} %get-tuple-element.60, s32[]{:T(128)} %get-tuple-element.61, s32[]{:T(128)} %get-tuple-element.62), kind=kLoop, calls=%fused_computation.32 | loop fusion | flops 6656 | bytes 6180 | tf_op jit(solution)/shard_map/convert_element_type | solution.py:49
  25.2 1.2 multiply_sine_fusion.1
  27.1 1.6 copy.57
  28.7 1.3 copy.58
  30.0 3.6 %all-to-all-done = bf16[8,160,128]{2,1,0:T(8,128)(2,1)} async-done(((bf16[8,160,128]{2,1,0:T(8,128)(2,1)}), bf16[8,160,128]{2,1,0:T(8,128)(2,1)}, u32[]{:S(2)}, u32[]{:S(2)}) %all-to-all-start) | async-done | bytes 327712 | tf_op jit(solution)/shard_map/all_to_all | solution.py:39
  33.7 1.0 slice.36
  34.7 10.6 %collective-permute-start = (bf16[128,128]{1,0:T(8,128)(2,1)S(1)}, bf16[128,128]{1,0:T(8,128)(2,1)S(1)}, u32[]{:S(2)}, u32[]{:S(2)}) collective-permute-start(bf16[128,128]{1,0:T(8,128)(2,1)S(1)} %dynamic-slice_bitcast_fusion), channel_id=1, source_target_pairs={{0,8},{8,0},{1,9},{9,1},{2,10},{10,2},{3,11},{11,3},{4,12},{12,4},... | collective-permute-start | bytes 98312 | tf_op jit(solution)/shard_map/ppermute | solution.py:264
  45.3 0.9 slice.37
  47.4 9.0 %all-to-all-start.1 = ((bf16[8,128,128]{2,1,0:T(8,128)(2,1)}), bf16[8,128,128]{2,1,0:T(8,128)(2,1)S(1)}, u32[]{:S(2)}, u32[]{:S(2)}) async-start(bf16[8,128,128]{2,1,0:T(8,128)(2,1)} %broadcast_in_dim.73), calls=%async_computation.1 | async-start | bytes 524288 | tf_op jit(solution)/shard_map/all_to_all | solution.py:39
  56.5 1.7 multiply_sine_fusion
  58.2 8.0 %all-to-all-done.1 = bf16[8,128,128]{2,1,0:T(8,128)(2,1)S(1)} async-done(((bf16[8,128,128]{2,1,0:T(8,128)(2,1)}), bf16[8,128,128]{2,1,0:T(8,128)(2,1)S(1)}, u32[]{:S(2)}, u32[]{:S(2)}) %all-to-all-start.1) | async-done | bytes 262176 | tf_op jit(solution)/shard_map/all_to_all | solution.py:39
  66.3 1.2 broadcast_in_dim.86
  67.4 4.4 %all-to-all-start.2 = ((bf16[4,1024,128]{2,1,0:T(8,128)(2,1)}), bf16[4,1024,128]{2,1,0:T(8,128)(2,1)}, u32[]{:S(2)}, u32[]{:S(2)}) async-start(bf16[4,1024,128]{2,1,0:T(8,128)(2,1)} %broadcast_in_dim.86), calls=%async_computation.2 | async-start | bytes 2097152 | tf_op jit(solution)/shard_map/all_to_all | solution.py:39
  71.8 4.2 %collective-permute-start.3 = (bf16[64,4096]{1,0:T(8,128)(2,1)S(1)}, bf16[64,4096]{1,0:T(8,128)(2,1)S(1)}, u32[]{:S(2)}, u32[]{:S(2)}) collective-permute-start(bf16[64,4096]{1,0:T(8,128)(2,1)S(1)} %slice.30), channel_id=1, source_target_pairs={{0,2},{2,4},{4,6},{6,0},{1,3},{3,5},{5,7},{7,1},{8,10},{10,12},{12... | collective-permute-start | bytes 1572872 | tf_op jit(solution)/shard_map/ppermute | solution.py:287
  76.1 2.3 %collective-permute-start.4 = (bf16[64,4096]{1,0:T(8,128)(2,1)S(1)}, bf16[64,4096]{1,0:T(8,128)(2,1)S(1)}, u32[]{:S(2)}, u32[]{:S(2)}) collective-permute-start(bf16[64,4096]{1,0:T(8,128)(2,1)S(1)} %slice.31), channel_id=1, source_target_pairs={{0,6},{2,0},{4,2},{6,4},{1,7},{3,1},{5,3},{7,5},{8,14},{10,8},{12,... | collective-permute-start | bytes 1572872 | tf_op jit(solution)/shard_map/ppermute | solution.py:288
  78.4 6.5 %collective-permute-done.3.refs_2_.refs_3_ = bf16[64,4096]{1,0:T(8,128)(2,1)S(1)} collective-permute-done((bf16[64,4096]{1,0:T(8,128)(2,1)S(1)}, bf16[64,4096]{1,0:T(8,128)(2,1)S(1)}, u32[]{:S(2)}, u32[]{:S(2)}) %collective-permute-start.3) | collective-permute-done | bytes 524320 | tf_op jit(solution)/shard_map/ppermute | solution.py:287
  85.7 1.9 collective-permute-done.4.refs_3_.refs_4_
  88.4 6.6 %collective-permute-start.5 = (bf16[32,128,128]{2,1,0:T(8,128)(2,1)}, bf16[32,128,128]{2,1,0:T(8,128)(2,1)}, u32[]{:S(2)}, u32[]{:S(2)}) collective-permute-start(bf16[32,128,128]{2,1,0:T(8,128)(2,1)} %bitcast.15.refs_5_), channel_id=1, source_target_pairs={{0,1},{1,0},{2,3},{3,2},{4,5},{5,4},{6,7},{7,6},{8,9},{9,8},{10,11... | collective-permute-start | bytes 3145736 | tf_op jit(solution)/shard_map/ppermute | solution.py:290
  95.1 1.0 copy-done.2
  96.2 1.0 copy-done.4
  97.2 2.5 %shard_map.55.refs_7_ = f32[512,128]{1,0:T(8,128)S(1)} custom-call(bf16[128,4096]{1,0:T(8,128)(2,1)S(1)} %bitcast.42, bf16[128,4096]{1,0:T(8,128)(2,1)S(1)} %collective-permute-done.1.refs_1_.refs_2_, bf16[64,4096]{1,0:T(8,128)(2,1)S(1)} %copy-done.2, bf16[64,4096]{1,0:T(8,128)(2,1)S(1)} %copy-done.4, ...), custom_call_target="tpu_custom_call" | custom-call | flops 536870912 | bytes 5242880 | tf_op jit(solution)/shard_map/pallas_call | solution.py:123
  99.7 2.6 %shard_map.56 = bf16[4,2,128,128]{3,2,1,0:T(8,128)(2,1)S(1)} custom-call(s32[2]{0:T(128)S(1)} %pad_add_fusion.1.refs_0_, bf16[128,4096]{1,0:T(8,128)(2,1)S(1)} %bitcast.43, bf16[128,4096]{1,0:T(8,128)(2,1)S(1)} %collective-permute-done.1.refs_1_.refs_2_, bf16[64,4096]{1,0:T(8,128)(2,1)S(1)} %copy-done.2, bf16[64,4096]{1,0:T(8,128)(2,1)S(1)} %copy-done.4, ...), custom_call_target="tpu_custom_call" | custom-call | flops 536870912 | bytes 5242880 | tf_op jit(solution)/shard_map/pallas_call | solution.py:149
  102.4 9.3 %all_to_all.35 = bf16[4,2,128,128]{3,2,1,0:T(8,128)(2,1)S(1)} all-to-all(bf16[4,2,128,128]{3,2,1,0:T(8,128)(2,1)S(1)} %shard_map.56), channel_id=1, replica_groups=mesh['z1'=2,'z0'=2,'y1'=4,'y0'=2,'zh'=2,'x'=4,'c'=2] {'x'}, dimensions={0} | all-to-all | bytes 524288 | tf_op jit(solution)/shard_map/all_to_all | solution.py:39
  111.7 8.9 %all_to_all.36.refs_0_ = bf16[4,2,128,128]{3,2,1,0:T(8,128)(2,1)S(1)} all-to-all(bf16[4,2,128,128]{3,2,1,0:T(8,128)(2,1)S(1)} %all_to_all.35), channel_id=1, replica_groups=mesh['z1'=2,'z0'=2,'y1'=4,'y0'=2,'zh'=2,'x'=4,'c'=2] {'z1','z0'}, dimensions={0} | all-to-all | bytes 524288 | tf_op jit(solution)/shard_map/all_to_all | solution.py:39
  120.6 5.1 %all-to-all-start.5 = ((bf16[4,128,1024]{2,1,0:T(8,128)(2,1)}), bf16[4,128,1024]{2,1,0:T(8,128)(2,1)S(1)}, u32[]{:S(2)}, u32[]{:S(2)}) async-start(bf16[4,128,1024]{2,1,0:T(8,128)(2,1)} %bitcast.47), calls=%async_computation.5 | async-start | bytes 2097152 | tf_op jit(solution)/shard_map/all_to_all | solution.py:39
  125.7 3.1 %collective-permute-start.6 = (bf16[4,2,128,128]{3,2,1,0:T(8,128)(2,1)S(1)}, bf16[4,2,128,128]{3,2,1,0:T(8,128)(2,1)S(1)}, u32[]{:S(2)}, u32[]{:S(2)}) collective-permute-start(bf16[4,2,128,128]{3,2,1,0:T(8,128)(2,1)S(1)} %all_to_all.36.refs_0_), channel_id=1, source_target_pairs={{0,16},{16,32},{32,48},{48,64},{64,80},{80,96},{96,112},{112,0},{1... | collective-permute-start | bytes 786440 | tf_op jit(solution)/shard_map/ppermute | solution.py:311
  128.8 3.4 %collective-permute-start.9 = (bf16[4,2,128,128]{3,2,1,0:T(8,128)(2,1)S(1)}, bf16[4,2,128,128]{3,2,1,0:T(8,128)(2,1)S(1)}, u32[]{:S(2)}, u32[]{:S(2)}) collective-permute-start(bf16[4,2,128,128]{3,2,1,0:T(8,128)(2,1)S(1)} %all_to_all.36.refs_0_), channel_id=1, source_target_pairs={{0,112},{16,0},{32,16},{48,32},{64,48},{80,64},{96,80},{112,96},{1... | collective-permute-start | bytes 786440 | tf_op jit(solution)/shard_map/ppermute | solution.py:312
  132.2 2.2 %collective-permute-done.6.refs_1_ = bf16[4,2,128,128]{3,2,1,0:T(8,128)(2,1)S(1)} collective-permute-done((bf16[4,2,128,128]{3,2,1,0:T(8,128)(2,1)S(1)}, bf16[4,2,128,128]{3,2,1,0:T(8,128)(2,1)S(1)}, u32[]{:S(2)}, u32[]{:S(2)}) %collective-permute-start.6) | collective-permute-done | bytes 262176 | tf_op jit(solution)/shard_map/ppermute | solution.py:311
  134.4 1.9 collective-permute-start.7
  136.3 4.6 %collective-permute-start.10 = (bf16[4,2,128,128]{3,2,1,0:T(8,128)(2,1)S(1)}, bf16[4,2,128,128]{3,2,1,0:T(8,128)(2,1)S(1)}, u32[]{:S(2)}, u32[]{:S(2)}) collective-permute-start(bf16[4,2,128,128]{3,2,1,0:T(8,128)(2,1)S(1)} %collective-permute-done.9.refs_3_), channel_id=1, source_target_pairs={{0,112},{16,0},{32,16},{48,32},{64,48},{80,64},{96,80},{112,96},{1... | collective-permute-start | bytes 786440 | tf_op jit(solution)/shard_map/ppermute | solution.py:312
  141.1 1.6 collective-permute-done.7.refs_2_
  142.7 1.9 collective-permute-start.8
  144.6 4.6 %collective-permute-start.11 = (bf16[4,2,128,128]{3,2,1,0:T(8,128)(2,1)S(1)}, bf16[4,2,128,128]{3,2,1,0:T(8,128)(2,1)S(1)}, u32[]{:S(2)}, u32[]{:S(2)}) collective-permute-start(bf16[4,2,128,128]{3,2,1,0:T(8,128)(2,1)S(1)} %collective-permute-done.10.refs_4_), channel_id=1, source_target_pairs={{0,112},{16,0},{32,16},{48,32},{64,48},{80,64},{96,80},{112,96},{1... | collective-permute-start | bytes 786440 | tf_op jit(solution)/shard_map/ppermute | solution.py:312
  149.2 1.7 all-to-all-done.5.q_ref
  151.6 8.4 %shard_map.58 = (f32[4,128,1024]{2,1,0:T(8,128)S(1)}, f32[4,1,1024]{2,1,0:T(1,128)S(1)}, f32[4,1,1024]{2,1,0:T(1,128)S(1)}) custom-call(s32[5]{0:T(128)S(1)} %pad_add_fusion.where_ref, bf16[4,128,1024]{2,1,0:T(8,128)(2,1)S(1)} %shard_map.57.q_ref, s32[4,1,128]{2,1,0:T(1,128)S(1)} %bitcast.44, bf16[4,2,128,128]{3,2,1,0:T(8,128)(2,1)S(1)} %all_to_all.36.refs_0_, ...), custom_call_target="tpu_custom_call" | custom-call | flops 5368709120 | bytes 4194304 | tf_op jit(solution)/shard_map/pallas_call | solution.py:243
  160.0 6.5 %collective-permute-start.12 = (bf16[2,2,128,128]{3,2,1,0:T(8,128)(2,1)S(1)}, bf16[2,2,128,128]{3,2,1,0:T(8,128)(2,1)S(1)}, u32[]{:S(2)}, u32[]{:S(2)}) collective-permute-start(bf16[2,2,128,128]{3,2,1,0:T(8,128)(2,1)S(1)} %slice.34), channel_id=1, source_target_pairs={{0,16},{16,32},{32,48},{48,64},{64,80},{80,96},{96,112},{112,0},{1... | collective-permute-start | bytes 393224 | tf_op jit(solution)/shard_map/ppermute | solution.py:308
  166.6 1.9 collective-permute-start.13
  168.5 4.4 %shard_map.59 = (f32[4,128,1024]{2,1,0:T(8,128)S(1)}, f32[4,1,1024]{2,1,0:T(1,128)S(1)}, f32[4,1,1024]{2,1,0:T(1,128)S(1)}) custom-call(s32[5]{0:T(128)S(1)} %pad_add_fusion.where_ref, bf16[4,128,1024]{2,1,0:T(8,128)(2,1)S(1)} %shard_map.57.q_ref, s32[4,1,128]{2,1,0:T(1,128)S(1)} %bitcast.45, bf16[4,2,128,128]{3,2,1,0:T(8,128)(2,1)S(1)} %collective-permute-done.8.refs_0_, ...), custom_call_target="tpu_custom_call" | custom-call | flops 2147483648 | bytes 4194304 | tf_op jit(solution)/shard_map/pallas_call | solution.py:243
  172.9 1.0 collective-permute-done.13.refs_1_
  173.9 3.3 %shard_map.60 = bf16[4,128,1024]{2,1,0:T(8,128)(2,1)S(1)} custom-call(s32[5]{0:T(128)S(1)} %pad_add_fusion.where_ref, bf16[4,128,1024]{2,1,0:T(8,128)(2,1)S(1)} %shard_map.57.q_ref, s32[4,1,128]{2,1,0:T(1,128)S(1)} %bitcast.46, bf16[2,2,128,128]{3,2,1,0:T(8,128)(2,1)S(1)} %collective-permute-done.12.refs_0_, ...), custom_call_target="tpu_custom_call" | custom-call | flops 2147483648 | bytes 4194304 | tf_op jit(solution)/shard_map/pallas_call | solution.py:243
  177.2 28.8 %all_to_all.37 = bf16[4,128,1024]{2,1,0:T(8,128)(2,1)S(1)} all-to-all(bf16[4,128,1024]{2,1,0:T(8,128)(2,1)S(1)} %shard_map.60), channel_id=1, replica_groups=mesh['z1'=2,'z0'=2,'y1'=4,'y0'=2,'zh'=2,'x'=4,'c'=2] {'z1','z0'}, dimensions={0} | all-to-all | bytes 2097152 | tf_op jit(solution)/shard_map/all_to_all | solution.py:39
  206.6 1.3 copy.60
  (50 shorter events, 5.7 us)
Async XLA Ops:
  0.0 21.1 %copy-start.7 = (s32[1,4096]{1,0:T(1,128)S(1)}, s32[1,4096]{1,0:T(1,128)}, u32[]{:S(2)}) copy-start(s32[1,4096]{1,0:T(1,128)} %param.8) | copy-start | bytes 49156
  0.0 66.2 %collective-permute-start.1 = (bf16[128,4096]{1,0:T(8,128)(2,1)}, bf16[128,4096]{1,0:T(8,128)(2,1)S(1)}, u32[]{:S(2)}, u32[]{:S(2)}) collective-permute-start(bf16[128,4096]{1,0:T(8,128)(2,1)} %bitcast.40), channel_id=1, source_target_pairs={{0,2},{2,4},{4,6},{6,0},{1,3},{3,5},{5,7},{7,1},{8,10},{10,12},{12... | collective-permute-start | bytes 3145736 | tf_op jit(solution)/shard_map/ppermute | solution.py:280
  4.1 62.2 %collective-permute-start.2 = (bf16[128,4096]{1,0:T(8,128)(2,1)}, bf16[128,4096]{1,0:T(8,128)(2,1)S(1)}, u32[]{:S(2)}, u32[]{:S(2)}) collective-permute-start(bf16[128,4096]{1,0:T(8,128)(2,1)} %bitcast.41), channel_id=1, source_target_pairs={{0,6},{2,0},{4,2},{6,4},{1,7},{3,1},{5,3},{7,5},{8,14},{10,8},{12,... | collective-permute-start | bytes 3145736 | tf_op jit(solution)/shard_map/ppermute | solution.py:281
  10.4 23.3 %all-to-all-start = ((bf16[8,160,128]{2,1,0:T(8,128)(2,1)}), bf16[8,160,128]{2,1,0:T(8,128)(2,1)}, u32[]{:S(2)}, u32[]{:S(2)}) async-start(bf16[8,160,128]{2,1,0:T(8,128)(2,1)} %bitcast.4), calls=%async_computation | async-start | bytes 655360 | tf_op jit(solution)/shard_map/all_to_all | solution.py:39
  34.7 12.0 %collective-permute-start = (bf16[128,128]{1,0:T(8,128)(2,1)S(1)}, bf16[128,128]{1,0:T(8,128)(2,1)S(1)}, u32[]{:S(2)}, u32[]{:S(2)}) collective-permute-start(bf16[128,128]{1,0:T(8,128)(2,1)S(1)} %dynamic-slice_bitcast_fusion), channel_id=1, source_target_pairs={{0,8},{8,0},{1,9},{9,1},{2,10},{10,2},{3,11},{11,3},{4,12},{12,4},... | collective-permute-start | bytes 98312 | tf_op jit(solution)/shard_map/ppermute | solution.py:264
  47.4 18.8 %all-to-all-start.1 = ((bf16[8,128,128]{2,1,0:T(8,128)(2,1)}), bf16[8,128,128]{2,1,0:T(8,128)(2,1)S(1)}, u32[]{:S(2)}, u32[]{:S(2)}) async-start(bf16[8,128,128]{2,1,0:T(8,128)(2,1)} %broadcast_in_dim.73), calls=%async_computation.1 | async-start | bytes 524288 | tf_op jit(solution)/shard_map/all_to_all | solution.py:39
  67.4 27.7 %copy-start = (bf16[1,128,4096]{2,1,0:T(8,128)(2,1)S(1)}, bf16[1,128,4096]{2,1,0:T(8,128)(2,1)}, u32[]{:S(2)}) copy-start(bf16[1,128,4096]{2,1,0:T(8,128)(2,1)} %param.5) | copy-start | bytes 3145732
  67.4 21.0 %all-to-all-start.2 = ((bf16[4,1024,128]{2,1,0:T(8,128)(2,1)}), bf16[4,1024,128]{2,1,0:T(8,128)(2,1)}, u32[]{:S(2)}, u32[]{:S(2)}) async-start(bf16[4,1024,128]{2,1,0:T(8,128)(2,1)} %broadcast_in_dim.86), calls=%async_computation.2 | async-start | bytes 2097152 | tf_op jit(solution)/shard_map/all_to_all | solution.py:39
  71.8 13.1 %collective-permute-start.3 = (bf16[64,4096]{1,0:T(8,128)(2,1)S(1)}, bf16[64,4096]{1,0:T(8,128)(2,1)S(1)}, u32[]{:S(2)}, u32[]{:S(2)}) collective-permute-start(bf16[64,4096]{1,0:T(8,128)(2,1)S(1)} %slice.30), channel_id=1, source_target_pairs={{0,2},{2,4},{4,6},{6,0},{1,3},{3,5},{5,7},{7,1},{8,10},{10,12},{12... | collective-permute-start | bytes 1572872 | tf_op jit(solution)/shard_map/ppermute | solution.py:287
  76.1 11.5 %collective-permute-start.4 = (bf16[64,4096]{1,0:T(8,128)(2,1)S(1)}, bf16[64,4096]{1,0:T(8,128)(2,1)S(1)}, u32[]{:S(2)}, u32[]{:S(2)}) collective-permute-start(bf16[64,4096]{1,0:T(8,128)(2,1)S(1)} %slice.31), channel_id=1, source_target_pairs={{0,6},{2,0},{4,2},{6,4},{1,7},{3,1},{5,3},{7,5},{8,14},{10,8},{12,... | collective-permute-start | bytes 1572872 | tf_op jit(solution)/shard_map/ppermute | solution.py:288
  84.9 0.8 copy-start.1
  87.6 0.8 copy-start.3
  88.4 11.3 %collective-permute-start.5 = (bf16[32,128,128]{2,1,0:T(8,128)(2,1)}, bf16[32,128,128]{2,1,0:T(8,128)(2,1)}, u32[]{:S(2)}, u32[]{:S(2)}) collective-permute-start(bf16[32,128,128]{2,1,0:T(8,128)(2,1)} %bitcast.15.refs_5_), channel_id=1, source_target_pairs={{0,1},{1,0},{2,3},{3,2},{4,5},{5,4},{6,7},{7,6},{8,9},{9,8},{10,11... | collective-permute-start | bytes 3145736 | tf_op jit(solution)/shard_map/ppermute | solution.py:290
  95.1 1.0 copy-start.2
  96.2 1.0 copy-start.4
  97.2 2.5 %copy-start.5 = (f32[4,128,64]{2,1,0:T(8,128)S(1)}, f32[4,128,64]{2,1,0:T(8,128)}, u32[]{:S(2)}) copy-start(f32[4,128,64]{2,1,0:T(8,128)} %get-tuple-element.37.refs_8_) | copy-start | bytes 393220
  102.4 48.5 %copy-start.6 = (f32[4,64,128]{2,1,0:T(8,128)S(1)}, f32[4,64,128]{2,1,0:T(8,128)}, u32[]{:S(2)}) copy-start(f32[4,64,128]{2,1,0:T(8,128)} %get-tuple-element.41.cos_ref) | copy-start | bytes 393220
  120.6 30.3 %all-to-all-start.5 = ((bf16[4,128,1024]{2,1,0:T(8,128)(2,1)}), bf16[4,128,1024]{2,1,0:T(8,128)(2,1)S(1)}, u32[]{:S(2)}, u32[]{:S(2)}) async-start(bf16[4,128,1024]{2,1,0:T(8,128)(2,1)} %bitcast.47), calls=%async_computation.5 | async-start | bytes 2097152 | tf_op jit(solution)/shard_map/all_to_all | solution.py:39
  125.7 8.7 %collective-permute-start.6 = (bf16[4,2,128,128]{3,2,1,0:T(8,128)(2,1)S(1)}, bf16[4,2,128,128]{3,2,1,0:T(8,128)(2,1)S(1)}, u32[]{:S(2)}, u32[]{:S(2)}) collective-permute-start(bf16[4,2,128,128]{3,2,1,0:T(8,128)(2,1)S(1)} %all_to_all.36.refs_0_), channel_id=1, source_target_pairs={{0,16},{16,32},{32,48},{48,64},{64,80},{80,96},{96,112},{112,0},{1... | collective-permute-start | bytes 786440 | tf_op jit(solution)/shard_map/ppermute | solution.py:311
  128.8 7.5 %collective-permute-start.9 = (bf16[4,2,128,128]{3,2,1,0:T(8,128)(2,1)S(1)}, bf16[4,2,128,128]{3,2,1,0:T(8,128)(2,1)S(1)}, u32[]{:S(2)}, u32[]{:S(2)}) collective-permute-start(bf16[4,2,128,128]{3,2,1,0:T(8,128)(2,1)S(1)} %all_to_all.36.refs_0_), channel_id=1, source_target_pairs={{0,112},{16,0},{32,16},{48,32},{64,48},{80,64},{96,80},{112,96},{1... | collective-permute-start | bytes 786440 | tf_op jit(solution)/shard_map/ppermute | solution.py:312
  134.4 8.3 %collective-permute-start.7 = (bf16[4,2,128,128]{3,2,1,0:T(8,128)(2,1)S(1)}, bf16[4,2,128,128]{3,2,1,0:T(8,128)(2,1)S(1)}, u32[]{:S(2)}, u32[]{:S(2)}) collective-permute-start(bf16[4,2,128,128]{3,2,1,0:T(8,128)(2,1)S(1)} %collective-permute-done.6.refs_1_), channel_id=1, source_target_pairs={{0,16},{16,32},{32,48},{48,64},{64,80},{80,96},{96,112},{112,0},{1... | collective-permute-start | bytes 786440 | tf_op jit(solution)/shard_map/ppermute | solution.py:311
  136.3 8.3 %collective-permute-start.10 = (bf16[4,2,128,128]{3,2,1,0:T(8,128)(2,1)S(1)}, bf16[4,2,128,128]{3,2,1,0:T(8,128)(2,1)S(1)}, u32[]{:S(2)}, u32[]{:S(2)}) collective-permute-start(bf16[4,2,128,128]{3,2,1,0:T(8,128)(2,1)S(1)} %collective-permute-done.9.refs_3_), channel_id=1, source_target_pairs={{0,112},{16,0},{32,16},{48,32},{64,48},{80,64},{96,80},{112,96},{1... | collective-permute-start | bytes 786440 | tf_op jit(solution)/shard_map/ppermute | solution.py:312
  142.7 17.3 %collective-permute-start.8 = (bf16[4,2,128,128]{3,2,1,0:T(8,128)(2,1)S(1)}, bf16[4,2,128,128]{3,2,1,0:T(8,128)(2,1)S(1)}, u32[]{:S(2)}, u32[]{:S(2)}) collective-permute-start(bf16[4,2,128,128]{3,2,1,0:T(8,128)(2,1)S(1)} %collective-permute-done.7.refs_2_), channel_id=1, source_target_pairs={{0,16},{16,32},{32,48},{48,64},{64,80},{80,96},{96,112},{112,0},{1... | collective-permute-start | bytes 786440 | tf_op jit(solution)/shard_map/ppermute | solution.py:311
  144.6 15.4 %collective-permute-start.11 = (bf16[4,2,128,128]{3,2,1,0:T(8,128)(2,1)S(1)}, bf16[4,2,128,128]{3,2,1,0:T(8,128)(2,1)S(1)}, u32[]{:S(2)}, u32[]{:S(2)}) collective-permute-start(bf16[4,2,128,128]{3,2,1,0:T(8,128)(2,1)S(1)} %collective-permute-done.10.refs_4_), channel_id=1, source_target_pairs={{0,112},{16,0},{32,16},{48,32},{64,48},{80,64},{96,80},{112,96},{1... | collective-permute-start | bytes 786440 | tf_op jit(solution)/shard_map/ppermute | solution.py:312
  160.0 12.9 %collective-permute-start.12 = (bf16[2,2,128,128]{3,2,1,0:T(8,128)(2,1)S(1)}, bf16[2,2,128,128]{3,2,1,0:T(8,128)(2,1)S(1)}, u32[]{:S(2)}, u32[]{:S(2)}) collective-permute-start(bf16[2,2,128,128]{3,2,1,0:T(8,128)(2,1)S(1)} %slice.34), channel_id=1, source_target_pairs={{0,16},{16,32},{32,48},{48,64},{64,80},{80,96},{96,112},{112,0},{1... | collective-permute-start | bytes 393224 | tf_op jit(solution)/shard_map/ppermute | solution.py:308
  166.6 7.4 %collective-permute-start.13 = (bf16[2,2,128,128]{3,2,1,0:T(8,128)(2,1)S(1)}, bf16[2,2,128,128]{3,2,1,0:T(8,128)(2,1)S(1)}, u32[]{:S(2)}, u32[]{:S(2)}) collective-permute-start(bf16[2,2,128,128]{3,2,1,0:T(8,128)(2,1)S(1)} %slice.35), channel_id=1, source_target_pairs={{0,112},{16,0},{32,16},{48,32},{64,48},{80,64},{96,80},{112,96},{1... | collective-permute-start | bytes 393224 | tf_op jit(solution)/shard_map/ppermute | solution.py:309

commit v8 on v7

--- a/solution.py
+++ b/solution.py
@@ -259,6 +259,7 @@
     row = segment_row.astype(jnp.bfloat16).reshape(1, 1, 32, 128)
     pieces = jnp.concatenate([pieces, jnp.broadcast_to(row, (4, 2, 32, 128))], axis=2)
     got = exchange(pieces.reshape(8, 160, 128), ("x", "c"))
+    got, sent = lax.optimization_barrier((got, hidden[0]))
     piece = pick(got[:, :BLOCK], origin % 8)
     rows_along = pick(got.reshape(4, 2, 160, 128)[:, :, BLOCK:], c, 1)
     piece = jnp.where(zh == origin // 8, piece, lax.ppermute(piece, "zh", ring(2, 1)))
@@ -277,8 +278,8 @@
     k_turns = (jnp.cos(k_angles), jnp.sin(k_angles))
 
     own = hidden[0]
-    left = lax.ppermute(own, "x", ring(4, 1))
-    right = lax.ppermute(own, "x", ring(4, -1))
+    left = lax.ppermute(sent, "x", ring(4, 1))
+    right = lax.ppermute(sent, "x", ring(4, -1))
     part = spread(piece, ("z1", "y1"), 8).reshape(8 * BLOCK, 128)
     part, left, right, start, q_turns, split, k_turns = lax.optimization_barrier(
         (part, left, right, start, q_turns, split, k_turns)

time: 209 us -> 201 us (0.962)
  the two profiles are of different devices: /device:TPU:1 before, /device:TPU:54 now
where the time goes in v8:
time: 201 us; the launch traced here: 199 us
  starting transfers between devices  70.8 us (35%)
  blocking collectives  51.8 us (26%)
  waiting for transfers between devices  25.7 us (13%)
  Pallas kernels  23.5 us (12%)
  local copies, waits for them, and re-layouts  17.9 us (9%)
  other arithmetic  8.56 us (4%)
    all_to_all x3, blocking collectives, exchange(): return lax.all_to_all(value, axes, split_axis=0, concat_axis=0, tiled=True)  51.8 us
    all_to_all x4, starting transfers between devices, exchange(): return lax.all_to_all(value, axes, split_axis=0, concat_axis=0, tiled=True)  21.6 us
    pallas_call x3, Pallas kernels, attend(): call(functools.partial(attend_kernel, tiles, state is None, closing), out...  17.5 us
    ppermute x1, starting transfers between devices, on_device(): lax.ppermute(piece, 'zh', ring(2, 1))  10.9 us
    ppermute x3, starting transfers between devices, on_device(): kv[step] = lax.ppermute(kv[step - 1], Y, ring(8, 1))  10.5 us
    all_to_all x4, waiting for transfers between devices, exchange(): return lax.all_to_all(value, axes, split_axis=0, concat_axis=0, tiled=True)  8.66 us
    unnamed x20, local copies, waits for them, and re-layouts  7.78 us
    ppermute x3, starting transfers between devices, on_device(): kv[-step] = lax.ppermute(kv[1 - step], Y, ring(8, -1))  6.86 us
  transfers between devices with their start and end apart: 18, of which 10 were waited for; matrix products, arithmetic and copies ran while one was open for 7% of the time, Pallas kernels for 9%

profile of v8, /device:TPU:54, one launch (start us, length us, event | category | flops | bytes accessed | tf_op | source)
XLA Modules:
  0.0 199.3 jit_solution(9024307529803796544)
XLA Ops:
  0.0 0.9 convert_reduce_fusion.5
  1.0 1.1 copy.53
  2.3 0.9 copy.55
  3.2 4.8 %all-to-all-start = ((bf16[8,160,128]{2,1,0:T(8,128)(2,1)}), bf16[8,160,128]{2,1,0:T(8,128)(2,1)S(1)}, u32[]{:S(2)}, u32[]{:S(2)}) async-start(bf16[8,160,128]{2,1,0:T(8,128)(2,1)} %bitcast.4), calls=%async_computation | async-start | bytes 655360 | tf_op jit(solution)/shard_map/all_to_all | solution.py:39
  8.0 0.8 fusion.2
  8.8 3.1 %subtract_convert_fusion.1 = (f32[4,128]{1,0:T(4,128)S(1)}, s32[4,128]{1,0:T(4,128)S(1)}) fusion(s32[4]{0:T(128)S(1)} %add_multiply_fusion, s32[]{:T(128)} %get-tuple-element.67, s32[4,1,128]{2,0,1:T(4,128)S(1)} %bitcast.55, s32[]{:T(128)} %get-tuple-element.68, s32[]{:T(128)} %get-tuple-element.64, s32[]{:T(128)} %get-tuple-element.65, s32[]{:T(128)} %get-tuple-element.66), kind=kLoop, calls=%fused_computation.32 | loop fusion | flops 6656 | bytes 6180 | tf_op jit(solution)/shard_map/convert_element_type | solution.py:49
  11.9 1.2 multiply_sine_fusion.1
  13.1 1.1 all-to-all-done
  14.9 4.0 %collective-permute-start.1 = (bf16[128,4096]{1,0:T(8,128)(2,1)S(1)}, bf16[128,4096]{1,0:T(8,128)(2,1)S(1)}, u32[]{:S(2)}, u32[]{:S(2)}) collective-permute-start(bf16[128,4096]{1,0:T(8,128)(2,1)S(1)} %bitcast.40), channel_id=1, source_target_pairs={{0,2},{2,4},{4,6},{6,0},{1,3},{3,5},{5,7},{7,1},{8,10},{10,12},{12... | collective-permute-start | bytes 3145736 | tf_op jit(solution)/shard_map/ppermute | solution.py:281
  18.9 1.9 collective-permute-start.2
  21.5 2.3 %copy.57 = bf16[1,128,4096]{1,2,0:T(8,128)(2,1)} copy(bf16[1,128,4096]{2,1,0:T(8,128)(2,1)} %param.6) | data formatting | bytes 2097152 | tf_op args[1]
  23.8 2.3 %copy.58 = bf16[128,4,1024]{2,0,1:T(8,128)(2,1)} copy(bf16[128,4,1024]{0,2,1:T(8,128)(2,1)} %bitcast.50) | data formatting | bytes 2097152 | tf_op jit(solution)/shard_map/reshape;squeeze | solution.py:272
  26.0 1.0 slice.27
  27.0 10.9 %collective-permute-start = (bf16[128,128]{1,0:T(8,128)(2,1)S(1)}, bf16[128,128]{1,0:T(8,128)(2,1)S(1)}, u32[]{:S(2)}, u32[]{:S(2)}) collective-permute-start(bf16[128,128]{1,0:T(8,128)(2,1)S(1)} %dynamic-slice_bitcast_fusion), channel_id=1, source_target_pairs={{0,8},{8,0},{1,9},{9,1},{2,10},{10,2},{3,11},{11,3},{4,12},{12,4},... | collective-permute-start | bytes 98312 | tf_op jit(solution)/shard_map/ppermute | solution.py:265
  37.9 0.9 slice.36
  40.6 9.1 %all-to-all-start.1 = ((bf16[8,128,128]{2,1,0:T(8,128)(2,1)}), bf16[8,128,128]{2,1,0:T(8,128)(2,1)}, u32[]{:S(2)}, u32[]{:S(2)}) async-start(bf16[8,128,128]{2,1,0:T(8,128)(2,1)} %broadcast_in_dim.73), calls=%async_computation.1 | async-start | bytes 524288 | tf_op jit(solution)/shard_map/all_to_all | solution.py:39
  49.8 1.7 multiply_sine_fusion
  51.5 6.0 %all-to-all-done.1 = bf16[8,128,128]{2,1,0:T(8,128)(2,1)} async-done(((bf16[8,128,128]{2,1,0:T(8,128)(2,1)}), bf16[8,128,128]{2,1,0:T(8,128)(2,1)}, u32[]{:S(2)}, u32[]{:S(2)}) %all-to-all-start.1) | async-done | bytes 262176 | tf_op jit(solution)/shard_map/all_to_all | solution.py:39
  57.5 2.1 %broadcast_in_dim.86 = bf16[4,1024,128]{2,1,0:T(8,128)(2,1)} broadcast(bf16[1024,128]{1,0:T(8,128)(2,1)} %bitcast.7), dimensions={1,2} | broadcast | bytes 1310720 | tf_op jit(solution)/shard_map/broadcast_in_dim | solution.py:43
  59.5 4.2 %all-to-all-start.2 = ((bf16[4,1024,128]{2,1,0:T(8,128)(2,1)}), bf16[4,1024,128]{2,1,0:T(8,128)(2,1)}, u32[]{:S(2)}, u32[]{:S(2)}) async-start(bf16[4,1024,128]{2,1,0:T(8,128)(2,1)} %broadcast_in_dim.86), calls=%async_computation.2 | async-start | bytes 2097152 | tf_op jit(solution)/shard_map/all_to_all | solution.py:39
  63.8 5.1 %collective-permute-start.3 = (bf16[64,4096]{1,0:T(8,128)(2,1)S(1)}, bf16[64,4096]{1,0:T(8,128)(2,1)S(1)}, u32[]{:S(2)}, u32[]{:S(2)}) collective-permute-start(bf16[64,4096]{1,0:T(8,128)(2,1)S(1)} %slice.30), channel_id=1, source_target_pairs={{0,2},{2,4},{4,6},{6,0},{1,3},{3,5},{5,7},{7,1},{8,10},{10,12},{12... | collective-permute-start | bytes 1572872 | tf_op jit(solution)/shard_map/ppermute | solution.py:288
  69.0 1.9 collective-permute-start.4
  70.9 6.3 %collective-permute-done.3.refs_2_.refs_3_ = bf16[64,4096]{1,0:T(8,128)(2,1)S(1)} collective-permute-done((bf16[64,4096]{1,0:T(8,128)(2,1)S(1)}, bf16[64,4096]{1,0:T(8,128)(2,1)S(1)}, u32[]{:S(2)}, u32[]{:S(2)}) %collective-permute-start.3) | collective-permute-done | bytes 524320 | tf_op jit(solution)/shard_map/ppermute | solution.py:288
  78.0 4.6 %collective-permute-done.4.refs_3_.refs_4_ = bf16[64,4096]{1,0:T(8,128)(2,1)S(1)} collective-permute-done((bf16[64,4096]{1,0:T(8,128)(2,1)S(1)}, bf16[64,4096]{1,0:T(8,128)(2,1)S(1)}, u32[]{:S(2)}, u32[]{:S(2)}) %collective-permute-start.4) | collective-permute-done | bytes 524320 | tf_op jit(solution)/shard_map/ppermute | solution.py:289
  83.4 1.9 collective-permute-start.5
  85.4 1.0 copy-done.2
  86.5 1.0 copy-done.4
  87.5 2.6 %shard_map.55.refs_7_ = f32[512,128]{1,0:T(8,128)S(1)} custom-call(bf16[128,4096]{1,0:T(8,128)(2,1)S(1)} %bitcast.42, bf16[128,4096]{1,0:T(8,128)(2,1)S(1)} %collective-permute-done.1.refs_1_.refs_2_, bf16[64,4096]{1,0:T(8,128)(2,1)S(1)} %copy-done.2, bf16[64,4096]{1,0:T(8,128)(2,1)S(1)} %copy-done.4, ...), custom_call_target="tpu_custom_call" | custom-call | flops 536870912 | bytes 5242880 | tf_op jit(solution)/shard_map/pallas_call | solution.py:123
  90.1 2.7 %shard_map.56 = bf16[4,2,128,128]{3,2,1,0:T(8,128)(2,1)S(1)} custom-call(s32[2]{0:T(128)S(1)} %pad_add_fusion.1.refs_0_, bf16[128,4096]{1,0:T(8,128)(2,1)S(1)} %bitcast.43, bf16[128,4096]{1,0:T(8,128)(2,1)S(1)} %collective-permute-done.1.refs_1_.refs_2_, bf16[64,4096]{1,0:T(8,128)(2,1)S(1)} %copy-done.2, bf16[64,4096]{1,0:T(8,128)(2,1)S(1)} %copy-done.4, ...), custom_call_target="tpu_custom_call" | custom-call | flops 536870912 | bytes 5242880 | tf_op jit(solution)/shard_map/pallas_call | solution.py:149
  92.8 9.7 %all_to_all.35 = bf16[4,2,128,128]{3,2,1,0:T(8,128)(2,1)S(1)} all-to-all(bf16[4,2,128,128]{3,2,1,0:T(8,128)(2,1)S(1)} %shard_map.56), channel_id=1, replica_groups=mesh['z1'=2,'z0'=2,'y1'=4,'y0'=2,'zh'=2,'x'=4,'c'=2] {'x'}, dimensions={0} | all-to-all | bytes 524288 | tf_op jit(solution)/shard_map/all_to_all | solution.py:39
  102.5 11.5 %all_to_all.36.refs_0_ = bf16[4,2,128,128]{3,2,1,0:T(8,128)(2,1)S(1)} all-to-all(bf16[4,2,128,128]{3,2,1,0:T(8,128)(2,1)S(1)} %all_to_all.35), channel_id=1, replica_groups=mesh['z1'=2,'z0'=2,'y1'=4,'y0'=2,'zh'=2,'x'=4,'c'=2] {'z1','z0'}, dimensions={0} | all-to-all | bytes 524288 | tf_op jit(solution)/shard_map/all_to_all | solution.py:39
  114.0 3.5 %all-to-all-start.5 = ((bf16[4,128,1024]{2,1,0:T(8,128)(2,1)}), bf16[4,128,1024]{2,1,0:T(8,128)(2,1)S(1)}, u32[]{:S(2)}, u32[]{:S(2)}) async-start(bf16[4,128,1024]{2,1,0:T(8,128)(2,1)} %bitcast.47), calls=%async_computation.5 | async-start | bytes 2097152 | tf_op jit(solution)/shard_map/all_to_all | solution.py:39
  117.5 3.4 %collective-permute-start.6 = (bf16[4,2,128,128]{3,2,1,0:T(8,128)(2,1)S(1)}, bf16[4,2,128,128]{3,2,1,0:T(8,128)(2,1)S(1)}, u32[]{:S(2)}, u32[]{:S(2)}) collective-permute-start(bf16[4,2,128,128]{3,2,1,0:T(8,128)(2,1)S(1)} %all_to_all.36.refs_0_), channel_id=1, source_target_pairs={{0,16},{16,32},{32,48},{48,64},{64,80},{80,96},{96,112},{112,0},{1... | collective-permute-start | bytes 786440 | tf_op jit(solution)/shard_map/ppermute | solution.py:312
  120.9 2.5 %collective-permute-start.9 = (bf16[4,2,128,128]{3,2,1,0:T(8,128)(2,1)S(1)}, bf16[4,2,128,128]{3,2,1,0:T(8,128)(2,1)S(1)}, u32[]{:S(2)}, u32[]{:S(2)}) collective-permute-start(bf16[4,2,128,128]{3,2,1,0:T(8,128)(2,1)S(1)} %all_to_all.36.refs_0_), channel_id=1, source_target_pairs={{0,112},{16,0},{32,16},{48,32},{64,48},{80,64},{96,80},{112,96},{1... | collective-permute-start | bytes 786440 | tf_op jit(solution)/shard_map/ppermute | solution.py:313
  123.4 2.5 %collective-permute-done.6.refs_1_ = bf16[4,2,128,128]{3,2,1,0:T(8,128)(2,1)S(1)} collective-permute-done((bf16[4,2,128,128]{3,2,1,0:T(8,128)(2,1)S(1)}, bf16[4,2,128,128]{3,2,1,0:T(8,128)(2,1)S(1)}, u32[]{:S(2)}, u32[]{:S(2)}) %collective-permute-start.6) | collective-permute-done | bytes 262176 | tf_op jit(solution)/shard_map/ppermute | solution.py:312
  125.9 3.4 %collective-permute-start.7 = (bf16[4,2,128,128]{3,2,1,0:T(8,128)(2,1)S(1)}, bf16[4,2,128,128]{3,2,1,0:T(8,128)(2,1)S(1)}, u32[]{:S(2)}, u32[]{:S(2)}) collective-permute-start(bf16[4,2,128,128]{3,2,1,0:T(8,128)(2,1)S(1)} %collective-permute-done.6.refs_1_), channel_id=1, source_target_pairs={{0,16},{16,32},{32,48},{48,64},{64,80},{80,96},{96,112},{112,0},{1... | collective-permute-start | bytes 786440 | tf_op jit(solution)/shard_map/ppermute | solution.py:312
  129.3 2.5 %collective-permute-start.10 = (bf16[4,2,128,128]{3,2,1,0:T(8,128)(2,1)S(1)}, bf16[4,2,128,128]{3,2,1,0:T(8,128)(2,1)S(1)}, u32[]{:S(2)}, u32[]{:S(2)}) collective-permute-start(bf16[4,2,128,128]{3,2,1,0:T(8,128)(2,1)S(1)} %collective-permute-done.9.refs_3_), channel_id=1, source_target_pairs={{0,112},{16,0},{32,16},{48,32},{64,48},{80,64},{96,80},{112,96},{1... | collective-permute-start | bytes 786440 | tf_op jit(solution)/shard_map/ppermute | solution.py:313
  132.0 2.2 %collective-permute-done.7.refs_2_ = bf16[4,2,128,128]{3,2,1,0:T(8,128)(2,1)S(1)} collective-permute-done((bf16[4,2,128,128]{3,2,1,0:T(8,128)(2,1)S(1)}, bf16[4,2,128,128]{3,2,1,0:T(8,128)(2,1)S(1)}, u32[]{:S(2)}, u32[]{:S(2)}) %collective-permute-start.7) | collective-permute-done | bytes 262176 | tf_op jit(solution)/shard_map/ppermute | solution.py:312
  134.2 3.8 %collective-permute-start.8 = (bf16[4,2,128,128]{3,2,1,0:T(8,128)(2,1)S(1)}, bf16[4,2,128,128]{3,2,1,0:T(8,128)(2,1)S(1)}, u32[]{:S(2)}, u32[]{:S(2)}) collective-permute-start(bf16[4,2,128,128]{3,2,1,0:T(8,128)(2,1)S(1)} %collective-permute-done.7.refs_2_), channel_id=1, source_target_pairs={{0,16},{16,32},{32,48},{48,64},{64,80},{80,96},{96,112},{112,0},{1... | collective-permute-start | bytes 786440 | tf_op jit(solution)/shard_map/ppermute | solution.py:312
  138.5 1.9 collective-permute-start.11
  140.4 1.6 all-to-all-done.5.q_ref
  142.7 9.8 %shard_map.58 = (f32[4,128,1024]{2,1,0:T(8,128)S(1)}, f32[4,1,1024]{2,1,0:T(1,128)S(1)}, f32[4,1,1024]{2,1,0:T(1,128)S(1)}) custom-call(s32[5]{0:T(128)S(1)} %pad_add_fusion.where_ref, bf16[4,128,1024]{2,1,0:T(8,128)(2,1)S(1)} %shard_map.57.q_ref, s32[4,1,128]{2,1,0:T(1,128)S(1)} %bitcast.44, bf16[4,2,128,128]{3,2,1,0:T(8,128)(2,1)S(1)} %all_to_all.36.refs_0_, ...), custom_call_target="tpu_custom_call" | custom-call | flops 5368709120 | bytes 4194304 | tf_op jit(solution)/shard_map/pallas_call | solution.py:243
  152.5 3.3 %collective-permute-start.12 = (bf16[2,2,128,128]{3,2,1,0:T(8,128)(2,1)S(1)}, bf16[2,2,128,128]{3,2,1,0:T(8,128)(2,1)S(1)}, u32[]{:S(2)}, u32[]{:S(2)}) collective-permute-start(bf16[2,2,128,128]{3,2,1,0:T(8,128)(2,1)S(1)} %slice.34), channel_id=1, source_target_pairs={{0,16},{16,32},{32,48},{48,64},{64,80},{80,96},{96,112},{112,0},{1... | collective-permute-start | bytes 393224 | tf_op jit(solution)/shard_map/ppermute | solution.py:309
  155.8 2.7 %collective-permute-start.13 = (bf16[2,2,128,128]{3,2,1,0:T(8,128)(2,1)S(1)}, bf16[2,2,128,128]{3,2,1,0:T(8,128)(2,1)S(1)}, u32[]{:S(2)}, u32[]{:S(2)}) collective-permute-start(bf16[2,2,128,128]{3,2,1,0:T(8,128)(2,1)S(1)} %slice.35), channel_id=1, source_target_pairs={{0,112},{16,0},{32,16},{48,32},{64,48},{80,64},{96,80},{112,96},{1... | collective-permute-start | bytes 393224 | tf_op jit(solution)/shard_map/ppermute | solution.py:310
  158.6 4.5 %shard_map.59 = (f32[4,128,1024]{2,1,0:T(8,128)S(1)}, f32[4,1,1024]{2,1,0:T(1,128)S(1)}, f32[4,1,1024]{2,1,0:T(1,128)S(1)}) custom-call(s32[5]{0:T(128)S(1)} %pad_add_fusion.where_ref, bf16[4,128,1024]{2,1,0:T(8,128)(2,1)S(1)} %shard_map.57.q_ref, s32[4,1,128]{2,1,0:T(1,128)S(1)} %bitcast.45, bf16[4,2,128,128]{3,2,1,0:T(8,128)(2,1)S(1)} %collective-permute-done.8.refs_0_, ...), custom_call_target="tpu_custom_call" | custom-call | flops 2147483648 | bytes 4194304 | tf_op jit(solution)/shard_map/pallas_call | solution.py:243
  163.4 3.3 %shard_map.60 = bf16[4,128,1024]{2,1,0:T(8,128)(2,1)S(1)} custom-call(s32[5]{0:T(128)S(1)} %pad_add_fusion.where_ref, bf16[4,128,1024]{2,1,0:T(8,128)(2,1)S(1)} %shard_map.57.q_ref, s32[4,1,128]{2,1,0:T(1,128)S(1)} %bitcast.46, bf16[2,2,128,128]{3,2,1,0:T(8,128)(2,1)S(1)} %collective-permute-done.12.refs_0_, ...), custom_call_target="tpu_custom_call" | custom-call | flops 2147483648 | bytes 4194304 | tf_op jit(solution)/shard_map/pallas_call | solution.py:243
  166.7 30.7 %all_to_all.37 = bf16[4,128,1024]{2,1,0:T(8,128)(2,1)S(1)} all-to-all(bf16[4,128,1024]{2,1,0:T(8,128)(2,1)S(1)} %shard_map.60), channel_id=1, replica_groups=mesh['z1'=2,'z0'=2,'y1'=4,'y0'=2,'zh'=2,'x'=4,'c'=2] {'z1','z0'}, dimensions={0} | all-to-all | bytes 2097152 | tf_op jit(solution)/shard_map/all_to_all | solution.py:39
  198.0 1.3 copy.60
  (52 shorter events, 7.1 us)
Async XLA Ops:
  0.0 8.0 %copy-start.8 = (s32[1,4096]{1,0:T(1,128)S(1)}, s32[1,4096]{1,0:T(1,128)}, u32[]{:S(2)}) copy-start(s32[1,4096]{1,0:T(1,128)} %param.8) | copy-start | bytes 49156
  0.0 14.9 %copy-start = (bf16[1,128,4096]{2,1,0:T(8,128)(2,1)S(1)}, bf16[1,128,4096]{2,1,0:T(8,128)(2,1)}, u32[]{:S(2)}) copy-start(bf16[1,128,4096]{2,1,0:T(8,128)(2,1)} %param.5) | copy-start | bytes 3145732
  3.2 11.0 %all-to-all-start = ((bf16[8,160,128]{2,1,0:T(8,128)(2,1)}), bf16[8,160,128]{2,1,0:T(8,128)(2,1)S(1)}, u32[]{:S(2)}, u32[]{:S(2)}) async-start(bf16[8,160,128]{2,1,0:T(8,128)(2,1)} %bitcast.4), calls=%async_computation | async-start | bytes 655360 | tf_op jit(solution)/shard_map/all_to_all | solution.py:39
  14.2 0.7 copy-start.7
  14.9 42.6 %collective-permute-start.1 = (bf16[128,4096]{1,0:T(8,128)(2,1)S(1)}, bf16[128,4096]{1,0:T(8,128)(2,1)S(1)}, u32[]{:S(2)}, u32[]{:S(2)}) collective-permute-start(bf16[128,4096]{1,0:T(8,128)(2,1)S(1)} %bitcast.40), channel_id=1, source_target_pairs={{0,2},{2,4},{4,6},{6,0},{1,3},{3,5},{5,7},{7,1},{8,10},{10,12},{12... | collective-permute-start | bytes 3145736 | tf_op jit(solution)/shard_map/ppermute | solution.py:281
  18.9 38.6 %collective-permute-start.2 = (bf16[128,4096]{1,0:T(8,128)(2,1)S(1)}, bf16[128,4096]{1,0:T(8,128)(2,1)S(1)}, u32[]{:S(2)}, u32[]{:S(2)}) collective-permute-start(bf16[128,4096]{1,0:T(8,128)(2,1)S(1)} %bitcast.41), channel_id=1, source_target_pairs={{0,6},{2,0},{4,2},{6,4},{1,7},{3,1},{5,3},{7,5},{8,14},{10,8},{12,... | collective-permute-start | bytes 3145736 | tf_op jit(solution)/shard_map/ppermute | solution.py:282
  27.0 12.8 %collective-permute-start = (bf16[128,128]{1,0:T(8,128)(2,1)S(1)}, bf16[128,128]{1,0:T(8,128)(2,1)S(1)}, u32[]{:S(2)}, u32[]{:S(2)}) collective-permute-start(bf16[128,128]{1,0:T(8,128)(2,1)S(1)} %dynamic-slice_bitcast_fusion), channel_id=1, source_target_pairs={{0,8},{8,0},{1,9},{9,1},{2,10},{10,2},{3,11},{11,3},{4,12},{12,4},... | collective-permute-start | bytes 98312 | tf_op jit(solution)/shard_map/ppermute | solution.py:265
  40.6 16.9 %all-to-all-start.1 = ((bf16[8,128,128]{2,1,0:T(8,128)(2,1)}), bf16[8,128,128]{2,1,0:T(8,128)(2,1)}, u32[]{:S(2)}, u32[]{:S(2)}) async-start(bf16[8,128,128]{2,1,0:T(8,128)(2,1)} %broadcast_in_dim.73), calls=%async_computation.1 | async-start | bytes 524288 | tf_op jit(solution)/shard_map/all_to_all | solution.py:39
  59.5 23.9 %all-to-all-start.2 = ((bf16[4,1024,128]{2,1,0:T(8,128)(2,1)}), bf16[4,1024,128]{2,1,0:T(8,128)(2,1)}, u32[]{:S(2)}, u32[]{:S(2)}) async-start(bf16[4,1024,128]{2,1,0:T(8,128)(2,1)} %broadcast_in_dim.86), calls=%async_computation.2 | async-start | bytes 2097152 | tf_op jit(solution)/shard_map/all_to_all | solution.py:39
  63.8 13.4 %collective-permute-start.3 = (bf16[64,4096]{1,0:T(8,128)(2,1)S(1)}, bf16[64,4096]{1,0:T(8,128)(2,1)S(1)}, u32[]{:S(2)}, u32[]{:S(2)}) collective-permute-start(bf16[64,4096]{1,0:T(8,128)(2,1)S(1)} %slice.30), channel_id=1, source_target_pairs={{0,2},{2,4},{4,6},{6,0},{1,3},{3,5},{5,7},{7,1},{8,10},{10,12},{12... | collective-permute-start | bytes 1572872 | tf_op jit(solution)/shard_map/ppermute | solution.py:288
  69.0 13.6 %collective-permute-start.4 = (bf16[64,4096]{1,0:T(8,128)(2,1)S(1)}, bf16[64,4096]{1,0:T(8,128)(2,1)S(1)}, u32[]{:S(2)}, u32[]{:S(2)}) collective-permute-start(bf16[64,4096]{1,0:T(8,128)(2,1)S(1)} %slice.31), channel_id=1, source_target_pairs={{0,6},{2,0},{4,2},{6,4},{1,7},{3,1},{5,3},{7,5},{8,14},{10,8},{12,... | collective-permute-start | bytes 1572872 | tf_op jit(solution)/shard_map/ppermute | solution.py:289
  77.3 0.8 copy-start.1
  82.6 0.8 copy-start.3
  83.4 6.7 %collective-permute-start.5 = (bf16[32,128,128]{2,1,0:T(8,128)(2,1)}, bf16[32,128,128]{2,1,0:T(8,128)(2,1)}, u32[]{:S(2)}, u32[]{:S(2)}) collective-permute-start(bf16[32,128,128]{2,1,0:T(8,128)(2,1)} %bitcast.15.refs_5_), channel_id=1, source_target_pairs={{0,1},{1,0},{2,3},{3,2},{4,5},{5,4},{6,7},{7,6},{8,9},{9,8},{10,11... | collective-permute-start | bytes 3145736 | tf_op jit(solution)/shard_map/ppermute | solution.py:291
  85.4 1.0 copy-start.2
  86.5 1.0 copy-start.4
  87.5 2.6 %copy-start.5 = (f32[4,128,64]{2,1,0:T(8,128)S(1)}, f32[4,128,64]{2,1,0:T(8,128)}, u32[]{:S(2)}) copy-start(f32[4,128,64]{2,1,0:T(8,128)} %get-tuple-element.41.refs_8_) | copy-start | bytes 393220
  92.8 49.2 %copy-start.6 = (f32[4,64,128]{2,1,0:T(8,128)S(1)}, f32[4,64,128]{2,1,0:T(8,128)}, u32[]{:S(2)}) copy-start(f32[4,64,128]{2,1,0:T(8,128)} %get-tuple-element.45.cos_ref) | copy-start | bytes 393220
  114.0 28.0 %all-to-all-start.5 = ((bf16[4,128,1024]{2,1,0:T(8,128)(2,1)}), bf16[4,128,1024]{2,1,0:T(8,128)(2,1)S(1)}, u32[]{:S(2)}, u32[]{:S(2)}) async-start(bf16[4,128,1024]{2,1,0:T(8,128)(2,1)} %bitcast.47), calls=%async_computation.5 | async-start | bytes 2097152 | tf_op jit(solution)/shard_map/all_to_all | solution.py:39
  117.5 8.4 %collective-permute-start.6 = (bf16[4,2,128,128]{3,2,1,0:T(8,128)(2,1)S(1)}, bf16[4,2,128,128]{3,2,1,0:T(8,128)(2,1)S(1)}, u32[]{:S(2)}, u32[]{:S(2)}) collective-permute-start(bf16[4,2,128,128]{3,2,1,0:T(8,128)(2,1)S(1)} %all_to_all.36.refs_0_), channel_id=1, source_target_pairs={{0,16},{16,32},{32,48},{48,64},{64,80},{80,96},{96,112},{112,0},{1... | collective-permute-start | bytes 786440 | tf_op jit(solution)/shard_map/ppermute | solution.py:312
  120.9 8.4 %collective-permute-start.9 = (bf16[4,2,128,128]{3,2,1,0:T(8,128)(2,1)S(1)}, bf16[4,2,128,128]{3,2,1,0:T(8,128)(2,1)S(1)}, u32[]{:S(2)}, u32[]{:S(2)}) collective-permute-start(bf16[4,2,128,128]{3,2,1,0:T(8,128)(2,1)S(1)} %all_to_all.36.refs_0_), channel_id=1, source_target_pairs={{0,112},{16,0},{32,16},{48,32},{64,48},{80,64},{96,80},{112,96},{1... | collective-permute-start | bytes 786440 | tf_op jit(solution)/shard_map/ppermute | solution.py:313
  125.9 8.3 %collective-permute-start.7 = (bf16[4,2,128,128]{3,2,1,0:T(8,128)(2,1)S(1)}, bf16[4,2,128,128]{3,2,1,0:T(8,128)(2,1)S(1)}, u32[]{:S(2)}, u32[]{:S(2)}) collective-permute-start(bf16[4,2,128,128]{3,2,1,0:T(8,128)(2,1)S(1)} %collective-permute-done.6.refs_1_), channel_id=1, source_target_pairs={{0,16},{16,32},{32,48},{48,64},{64,80},{80,96},{96,112},{112,0},{1... | collective-permute-start | bytes 786440 | tf_op jit(solution)/shard_map/ppermute | solution.py:312
  129.3 9.1 %collective-permute-start.10 = (bf16[4,2,128,128]{3,2,1,0:T(8,128)(2,1)S(1)}, bf16[4,2,128,128]{3,2,1,0:T(8,128)(2,1)S(1)}, u32[]{:S(2)}, u32[]{:S(2)}) collective-permute-start(bf16[4,2,128,128]{3,2,1,0:T(8,128)(2,1)S(1)} %collective-permute-done.9.refs_3_), channel_id=1, source_target_pairs={{0,112},{16,0},{32,16},{48,32},{64,48},{80,64},{96,80},{112,96},{1... | collective-permute-start | bytes 786440 | tf_op jit(solution)/shard_map/ppermute | solution.py:313
  134.2 18.3 %collective-permute-start.8 = (bf16[4,2,128,128]{3,2,1,0:T(8,128)(2,1)S(1)}, bf16[4,2,128,128]{3,2,1,0:T(8,128)(2,1)S(1)}, u32[]{:S(2)}, u32[]{:S(2)}) collective-permute-start(bf16[4,2,128,128]{3,2,1,0:T(8,128)(2,1)S(1)} %collective-permute-done.7.refs_2_), channel_id=1, source_target_pairs={{0,16},{16,32},{32,48},{48,64},{64,80},{80,96},{96,112},{112,0},{1... | collective-permute-start | bytes 786440 | tf_op jit(solution)/shard_map/ppermute | solution.py:312
  138.5 14.0 %collective-permute-start.11 = (bf16[4,2,128,128]{3,2,1,0:T(8,128)(2,1)S(1)}, bf16[4,2,128,128]{3,2,1,0:T(8,128)(2,1)S(1)}, u32[]{:S(2)}, u32[]{:S(2)}) collective-permute-start(bf16[4,2,128,128]{3,2,1,0:T(8,128)(2,1)S(1)} %collective-permute-done.10.refs_4_), channel_id=1, source_target_pairs={{0,112},{16,0},{32,16},{48,32},{64,48},{80,64},{96,80},{112,96},{1... | collective-permute-start | bytes 786440 | tf_op jit(solution)/shard_map/ppermute | solution.py:313
  152.5 10.5 %collective-permute-start.12 = (bf16[2,2,128,128]{3,2,1,0:T(8,128)(2,1)S(1)}, bf16[2,2,128,128]{3,2,1,0:T(8,128)(2,1)S(1)}, u32[]{:S(2)}, u32[]{:S(2)}) collective-permute-start(bf16[2,2,128,128]{3,2,1,0:T(8,128)(2,1)S(1)} %slice.34), channel_id=1, source_target_pairs={{0,16},{16,32},{32,48},{48,64},{64,80},{80,96},{96,112},{112,0},{1... | collective-permute-start | bytes 393224 | tf_op jit(solution)/shard_map/ppermute | solution.py:309
  155.8 7.6 %collective-permute-start.13 = (bf16[2,2,128,128]{3,2,1,0:T(8,128)(2,1)S(1)}, bf16[2,2,128,128]{3,2,1,0:T(8,128)(2,1)S(1)}, u32[]{:S(2)}, u32[]{:S(2)}) collective-permute-start(bf16[2,2,128,128]{3,2,1,0:T(8,128)(2,1)S(1)} %slice.35), channel_id=1, source_target_pairs={{0,112},{16,0},{32,16},{48,32},{64,48},{80,64},{96,80},{112,96},{1... | collective-permute-start | bytes 393224 | tf_op jit(solution)/shard_map/ppermute | solution.py:310

commit v9 on v5

--- a/solution.py
+++ b/solution.py
@@ -49,12 +49,11 @@
     return positions.astype(jnp.float32)[..., None] * freqs
 
 
-def starts_of(segment_row, segments):
-    first = jnp.zeros(segments.shape, jnp.int32)
-    for doc in range(1, DOCS):
-        begin = jnp.sum((segment_row < doc).astype(jnp.int32))
-        first = jnp.where(segments >= doc, begin, first)
-    return first
+def starts_of(segment_rows, segments):
+    docs = jnp.arange(1, DOCS, dtype=jnp.int32)
+    begins = jnp.sum((segment_rows[..., None, :] < docs[:, None]).astype(jnp.int32), axis=-1)
+    passed = segments[..., None, :] >= docs[:, None]
+    return jnp.max(jnp.where(passed, begins[..., None], 0), axis=-2)
 
 
 VMEM = pl.BlockSpec(memory_space=pltpu.VMEM)
@@ -273,7 +272,7 @@
     far_high = lax.ppermute(right[64:], "x", ring(4, -1))
 
     blocks = segment_row.reshape(4, 8, BLOCK)
-    start = starts_of(segment_row, pick(blocks, y, 1))
+    start = starts_of(segment_row, pick(blocks, y, 1).reshape(-1)).reshape(4, BLOCK)
     token = (jnp.arange(4)[:, None] * 8 + y) * BLOCK + jnp.arange(BLOCK)[None]
     q_angles = jnp.swapaxes(angles_of(token - start), 1, 2)
     q_turns = (jnp.cos(q_angles), jnp.sin(q_angles))
@@ -281,7 +280,7 @@
 
     rows_along = rows_along.astype(jnp.int32)
     along = pick(rows_along, z * 8 + y, 1)
-    start_along = jax.vmap(starts_of)(rows_along, along)
+    start_along = starts_of(rows_along.reshape(4, -1), along)
     k_angles = angles_of((z * 8 + y) * BLOCK + jnp.arange(BLOCK)[None] - start_along)
     k_turns = (jnp.cos(k_angles), jnp.sin(k_angles))
 

time: 195 us -> 191 us (0.979)
  Pallas kernels: 21.4 us -> 17.1 us
  other arithmetic: 9.42 us -> 5.61 us
  blocking collectives: 48.7 us -> 51.1 us
    pallas_call x3, Pallas kernels: 15.6 us -> 11.3 us  [attend(): call(functools.partial(attend_kernel, tiles, state is None, closing), out...]
    convert_element_type x2, other arithmetic: 3.34 us -> 0.08 us  [angles_of(): return positions.astype(jnp.float32)[..., None] * freqs]
    all_to_all x3, blocking collectives: 48.7 us -> 51.1 us  [exchange(): return lax.all_to_all(value, axes, split_axis=0, concat_axis=0, tiled=True)]
    unnamed x22 -> x23, local copies, waits for them, and re-layouts: 7.8 us -> 7.86 us
  transfers between devices with their start and end apart: 18 -> 18, of which waited for: 9 -> 9; matrix products, arithmetic and copies ran while one was open for 8% -> 6% of each run, Pallas kernels for 8% -> 7%
where the time goes in v9:
time: 191 us; the launch traced here: 187 us
  starting transfers between devices  76.4 us (40%)
  blocking collectives  51.1 us (27%)
  waiting for transfers between devices  18.8 us (10%)
  local copies, waits for them, and re-layouts  17.1 us (9%)
  Pallas kernels  17.1 us (9%)
  other arithmetic  5.61 us (3%)
    all_to_all x3, blocking collectives, exchange(): return lax.all_to_all(value, axes, split_axis=0, concat_axis=0, tiled=True)  51.1 us
    all_to_all x4, starting transfers between devices, exchange(): return lax.all_to_all(value, axes, split_axis=0, concat_axis=0, tiled=True)  21.9 us
    ppermute x3, starting transfers between devices, on_device(): kv[step] = lax.ppermute(kv[step - 1], Y, ring(8, 1))  13.3 us
    pallas_call x3, Pallas kernels, attend(): call(functools.partial(attend_kernel, tiles, state is None, closing), out...  11.3 us
    ppermute x1, starting transfers between devices, on_device(): lax.ppermute(piece, 'zh', ring(2, 1))  10.9 us
    unnamed x23, local copies, waits for them, and re-layouts  7.86 us
    ppermute x3, starting transfers between devices, on_device(): kv[-step] = lax.ppermute(kv[1 - step], Y, ring(8, -1))  6.4 us
    ppermute x1, starting transfers between devices, on_device(): far_high = lax.ppermute(right[64:], 'x', ring(4, -1))  4.89 us
  transfers between devices with their start and end apart: 18, of which 9 were waited for; matrix products, arithmetic and copies ran while one was open for 6% of the time, Pallas kernels for 7%

profile of v9, /device:TPU:56, one launch (start us, length us, event | category | flops | bytes accessed | tf_op | source)
XLA Modules:
  0.0 187.1 jit_solution(15342060070803195820)
XLA Ops:
  0.0 0.9 convert_reduce_fusion.2
  1.0 1.1 copy.17
  2.3 0.9 copy.19
  3.2 4.3 %all-to-all-start = ((bf16[8,160,128]{2,1,0:T(8,128)(2,1)}), bf16[8,160,128]{2,1,0:T(8,128)(2,1)S(1)}, u32[]{:S(2)}, u32[]{:S(2)}) async-start(bf16[8,160,128]{2,1,0:T(8,128)(2,1)} %bitcast.4), calls=%async_computation | async-start | bytes 655360 | tf_op jit(solution)/shard_map/all_to_all | solution.py:39
  7.5 3.9 %collective-permute-start.1 = (bf16[128,4096]{1,0:T(8,128)(2,1)S(1)}, bf16[128,4096]{1,0:T(8,128)(2,1)S(1)}, u32[]{:S(2)}, u32[]{:S(2)}) collective-permute-start(bf16[128,4096]{1,0:T(8,128)(2,1)S(1)} %bitcast.37), channel_id=1, source_target_pairs={{0,2},{2,4},{4,6},{6,0},{1,3},{3,5},{5,7},{7,1},{8,10},{10,12},{12... | collective-permute-start | bytes 3145736 | tf_op jit(solution)/shard_map/ppermute | solution.py:266
  11.4 3.1 %collective-permute-start.2 = (bf16[128,4096]{1,0:T(8,128)(2,1)S(1)}, bf16[128,4096]{1,0:T(8,128)(2,1)S(1)}, u32[]{:S(2)}, u32[]{:S(2)}) collective-permute-start(bf16[128,4096]{1,0:T(8,128)(2,1)S(1)} %bitcast.38), channel_id=1, source_target_pairs={{0,6},{2,0},{4,2},{6,4},{1,7},{3,1},{5,3},{7,5},{8,14},{10,8},{12,... | collective-permute-start | bytes 3145736 | tf_op jit(solution)/shard_map/ppermute | solution.py:267
  15.3 1.0 all-to-all-done
  17.0 10.9 %collective-permute-start = (bf16[128,128]{1,0:T(8,128)(2,1)S(1)}, bf16[128,128]{1,0:T(8,128)(2,1)S(1)}, u32[]{:S(2)}, u32[]{:S(2)}) collective-permute-start(bf16[128,128]{1,0:T(8,128)(2,1)S(1)} %dynamic-slice_bitcast_fusion), channel_id=1, source_target_pairs={{0,8},{8,0},{1,9},{9,1},{2,10},{10,2},{3,11},{11,3},{4,12},{12,4},... | collective-permute-start | bytes 98312 | tf_op jit(solution)/shard_map/ppermute | solution.py:263
  27.9 1.9 %collective-permute-done = bf16[128,128]{1,0:T(8,128)(2,1)S(1)} collective-permute-done((bf16[128,128]{1,0:T(8,128)(2,1)S(1)}, bf16[128,128]{1,0:T(8,128)(2,1)S(1)}, u32[]{:S(2)}, u32[]{:S(2)}) %collective-permute-start) | collective-permute-done | bytes 32800 | tf_op jit(solution)/shard_map/ppermute | solution.py:263
  31.3 9.1 %all-to-all-start.1 = ((bf16[8,128,128]{2,1,0:T(8,128)(2,1)}), bf16[8,128,128]{2,1,0:T(8,128)(2,1)}, u32[]{:S(2)}, u32[]{:S(2)}) async-start(bf16[8,128,128]{2,1,0:T(8,128)(2,1)} %broadcast_in_dim.36), calls=%async_computation.1 | async-start | bytes 524288 | tf_op jit(solution)/shard_map/all_to_all | solution.py:39
  40.4 2.3 %copy.20 = bf16[1,128,4096]{1,2,0:T(8,128)(2,1)} copy(bf16[1,128,4096]{2,1,0:T(8,128)(2,1)} %param.6) | data formatting | bytes 2097152 | tf_op args[1]
  42.7 2.3 %copy.21 = bf16[128,4,1024]{2,0,1:T(8,128)(2,1)} copy(bf16[128,4,1024]{0,2,1:T(8,128)(2,1)} %bitcast.48) | data formatting | bytes 2097152 | tf_op jit(solution)/shard_map/reshape;squeeze | solution.py:279
  45.2 3.5 %all-to-all-done.1 = bf16[8,128,128]{2,1,0:T(8,128)(2,1)} async-done(((bf16[8,128,128]{2,1,0:T(8,128)(2,1)}), bf16[8,128,128]{2,1,0:T(8,128)(2,1)}, u32[]{:S(2)}, u32[]{:S(2)}) %all-to-all-start.1) | async-done | bytes 262176 | tf_op jit(solution)/shard_map/all_to_all | solution.py:39
  48.8 2.1 %broadcast_in_dim.37 = bf16[4,1024,128]{2,1,0:T(8,128)(2,1)} broadcast(bf16[1024,128]{1,0:T(8,128)(2,1)} %bitcast.6), dimensions={1,2} | broadcast | bytes 1310720 | tf_op jit(solution)/shard_map/broadcast_in_dim | solution.py:43
  50.8 5.0 %all-to-all-start.2 = ((bf16[4,1024,128]{2,1,0:T(8,128)(2,1)}), bf16[4,1024,128]{2,1,0:T(8,128)(2,1)}, u32[]{:S(2)}, u32[]{:S(2)}) async-start(bf16[4,1024,128]{2,1,0:T(8,128)(2,1)} %broadcast_in_dim.37), calls=%async_computation.2 | async-start | bytes 2097152 | tf_op jit(solution)/shard_map/all_to_all | solution.py:39
  56.0 1.2 multiply_sine_fusion.1
  57.2 0.8 slice.29
  58.4 2.2 %collective-permute-start.3 = (bf16[64,4096]{1,0:T(8,128)(2,1)S(1)}, bf16[64,4096]{1,0:T(8,128)(2,1)S(1)}, u32[]{:S(2)}, u32[]{:S(2)}) collective-permute-start(bf16[64,4096]{1,0:T(8,128)(2,1)S(1)} %slice.22), channel_id=1, source_target_pairs={{0,2},{2,4},{4,6},{6,0},{1,3},{3,5},{5,7},{7,1},{8,10},{10,12},{12... | collective-permute-start | bytes 1572872 | tf_op jit(solution)/shard_map/ppermute | solution.py:271
  60.7 4.9 %collective-permute-start.4 = (bf16[64,4096]{1,0:T(8,128)(2,1)S(1)}, bf16[64,4096]{1,0:T(8,128)(2,1)S(1)}, u32[]{:S(2)}, u32[]{:S(2)}) collective-permute-start(bf16[64,4096]{1,0:T(8,128)(2,1)S(1)} %slice.23), channel_id=1, source_target_pairs={{0,6},{2,0},{4,2},{6,4},{1,7},{3,1},{5,3},{7,5},{8,14},{10,8},{12,... | collective-permute-start | bytes 1572872 | tf_op jit(solution)/shard_map/ppermute | solution.py:272
  65.7 1.8 multiply_sine_fusion
  67.4 4.9 %collective-permute-done.3.refs_2_.refs_3_ = bf16[64,4096]{1,0:T(8,128)(2,1)S(1)} collective-permute-done((bf16[64,4096]{1,0:T(8,128)(2,1)S(1)}, bf16[64,4096]{1,0:T(8,128)(2,1)S(1)}, u32[]{:S(2)}, u32[]{:S(2)}) %collective-permute-start.3) | collective-permute-done | bytes 524320 | tf_op jit(solution)/shard_map/ppermute | solution.py:271
  72.3 0.8 copy-done.1
  73.1 0.8 collective-permute-done.4.refs_3_.refs_4_
  73.9 0.8 copy-done.3
  74.7 1.9 %collective-permute-start.5 = (bf16[32,128,128]{2,1,0:T(8,128)(2,1)}, bf16[32,128,128]{2,1,0:T(8,128)(2,1)}, u32[]{:S(2)}, u32[]{:S(2)}) collective-permute-start(bf16[32,128,128]{2,1,0:T(8,128)(2,1)} %bitcast.8.refs_5_), channel_id=1, source_target_pairs={{0,1},{1,0},{2,3},{3,2},{4,5},{5,4},{6,7},{7,6},{8,9},{9,8},{10,11... | collective-permute-start | bytes 3145736 | tf_op jit(solution)/shard_map/ppermute | solution.py:290
  76.7 1.0 copy-done.2
  77.7 1.0 copy-done.4
  78.7 2.5 %shard_map.55.refs_7_ = f32[512,128]{1,0:T(8,128)S(1)} custom-call(bf16[128,4096]{1,0:T(8,128)(2,1)S(1)} %bitcast.39, bf16[128,4096]{1,0:T(8,128)(2,1)S(1)} %collective-permute-done.1.refs_1_.refs_2_, bf16[64,4096]{1,0:T(8,128)(2,1)S(1)} %copy-done.2, bf16[64,4096]{1,0:T(8,128)(2,1)S(1)} %copy-done.4, ...), custom_call_target="tpu_custom_call" | custom-call | flops 536870912 | bytes 5242880 | tf_op jit(solution)/shard_map/pallas_call | solution.py:122
  81.3 2.6 %shard_map.56 = bf16[4,2,128,128]{3,2,1,0:T(8,128)(2,1)S(1)} custom-call(s32[2]{0:T(128)S(1)} %pad_add_fusion.1.refs_0_, bf16[128,4096]{1,0:T(8,128)(2,1)S(1)} %bitcast.40, bf16[128,4096]{1,0:T(8,128)(2,1)S(1)} %collective-permute-done.1.refs_1_.refs_2_, bf16[64,4096]{1,0:T(8,128)(2,1)S(1)} %copy-done.2, bf16[64,4096]{1,0:T(8,128)(2,1)S(1)} %copy-done.4, ...), custom_call_target="tpu_custom_call" | custom-call | flops 536870912 | bytes 5242880 | tf_op jit(solution)/shard_map/pallas_call | solution.py:148
  83.9 11.9 %all_to_all.35 = bf16[4,2,128,128]{3,2,1,0:T(8,128)(2,1)S(1)} all-to-all(bf16[4,2,128,128]{3,2,1,0:T(8,128)(2,1)S(1)} %shard_map.56), channel_id=1, replica_groups=mesh['z1'=2,'z0'=2,'y1'=4,'y0'=2,'zh'=2,'x'=4,'c'=2] {'x'}, dimensions={0} | all-to-all | bytes 524288 | tf_op jit(solution)/shard_map/all_to_all | solution.py:39
  95.8 11.6 %all_to_all.36.refs_0_ = bf16[4,2,128,128]{3,2,1,0:T(8,128)(2,1)S(1)} all-to-all(bf16[4,2,128,128]{3,2,1,0:T(8,128)(2,1)S(1)} %all_to_all.35), channel_id=1, replica_groups=mesh['z1'=2,'z0'=2,'y1'=4,'y0'=2,'zh'=2,'x'=4,'c'=2] {'z1','z0'}, dimensions={0} | all-to-all | bytes 524288 | tf_op jit(solution)/shard_map/all_to_all | solution.py:39
  107.4 3.5 %all-to-all-start.5 = ((bf16[4,128,1024]{2,1,0:T(8,128)(2,1)}), bf16[4,128,1024]{2,1,0:T(8,128)(2,1)S(1)}, u32[]{:S(2)}, u32[]{:S(2)}) async-start(bf16[4,128,1024]{2,1,0:T(8,128)(2,1)} %bitcast.45), calls=%async_computation.5 | async-start | bytes 2097152 | tf_op jit(solution)/shard_map/all_to_all | solution.py:39
  110.9 3.3 %collective-permute-start.6 = (bf16[4,2,128,128]{3,2,1,0:T(8,128)(2,1)S(1)}, bf16[4,2,128,128]{3,2,1,0:T(8,128)(2,1)S(1)}, u32[]{:S(2)}, u32[]{:S(2)}) collective-permute-start(bf16[4,2,128,128]{3,2,1,0:T(8,128)(2,1)S(1)} %all_to_all.36.refs_0_), channel_id=1, source_target_pairs={{0,16},{16,32},{32,48},{48,64},{64,80},{80,96},{96,112},{112,0},{1... | collective-permute-start | bytes 786440 | tf_op jit(solution)/shard_map/ppermute | solution.py:311
  114.2 2.6 %collective-permute-start.9 = (bf16[4,2,128,128]{3,2,1,0:T(8,128)(2,1)S(1)}, bf16[4,2,128,128]{3,2,1,0:T(8,128)(2,1)S(1)}, u32[]{:S(2)}, u32[]{:S(2)}) collective-permute-start(bf16[4,2,128,128]{3,2,1,0:T(8,128)(2,1)S(1)} %all_to_all.36.refs_0_), channel_id=1, source_target_pairs={{0,112},{16,0},{32,16},{48,32},{64,48},{80,64},{96,80},{112,96},{1... | collective-permute-start | bytes 786440 | tf_op jit(solution)/shard_map/ppermute | solution.py:312
  116.8 2.5 %collective-permute-done.6.refs_1_ = bf16[4,2,128,128]{3,2,1,0:T(8,128)(2,1)S(1)} collective-permute-done((bf16[4,2,128,128]{3,2,1,0:T(8,128)(2,1)S(1)}, bf16[4,2,128,128]{3,2,1,0:T(8,128)(2,1)S(1)}, u32[]{:S(2)}, u32[]{:S(2)}) %collective-permute-start.6) | collective-permute-done | bytes 262176 | tf_op jit(solution)/shard_map/ppermute | solution.py:311
  119.3 4.5 %collective-permute-start.7 = (bf16[4,2,128,128]{3,2,1,0:T(8,128)(2,1)S(1)}, bf16[4,2,128,128]{3,2,1,0:T(8,128)(2,1)S(1)}, u32[]{:S(2)}, u32[]{:S(2)}) collective-permute-start(bf16[4,2,128,128]{3,2,1,0:T(8,128)(2,1)S(1)} %collective-permute-done.6.refs_1_), channel_id=1, source_target_pairs={{0,16},{16,32},{32,48},{48,64},{64,80},{80,96},{96,112},{112,0},{1... | collective-permute-start | bytes 786440 | tf_op jit(solution)/shard_map/ppermute | solution.py:311
  123.8 1.9 %collective-permute-start.10 = (bf16[4,2,128,128]{3,2,1,0:T(8,128)(2,1)S(1)}, bf16[4,2,128,128]{3,2,1,0:T(8,128)(2,1)S(1)}, u32[]{:S(2)}, u32[]{:S(2)}) collective-permute-start(bf16[4,2,128,128]{3,2,1,0:T(8,128)(2,1)S(1)} %collective-permute-done.9.refs_3_), channel_id=1, source_target_pairs={{0,112},{16,0},{32,16},{48,32},{64,48},{80,64},{96,80},{112,96},{1... | collective-permute-start | bytes 786440 | tf_op jit(solution)/shard_map/ppermute | solution.py:312
  126.0 1.7 collective-permute-done.7.refs_2_
  127.7 5.6 %collective-permute-start.8 = (bf16[4,2,128,128]{3,2,1,0:T(8,128)(2,1)S(1)}, bf16[4,2,128,128]{3,2,1,0:T(8,128)(2,1)S(1)}, u32[]{:S(2)}, u32[]{:S(2)}) collective-permute-start(bf16[4,2,128,128]{3,2,1,0:T(8,128)(2,1)S(1)} %collective-permute-done.7.refs_2_), channel_id=1, source_target_pairs={{0,16},{16,32},{32,48},{48,64},{64,80},{80,96},{96,112},{112,0},{1... | collective-permute-start | bytes 786440 | tf_op jit(solution)/shard_map/ppermute | solution.py:311
  133.3 1.9 %collective-permute-start.11 = (bf16[4,2,128,128]{3,2,1,0:T(8,128)(2,1)S(1)}, bf16[4,2,128,128]{3,2,1,0:T(8,128)(2,1)S(1)}, u32[]{:S(2)}, u32[]{:S(2)}) collective-permute-start(bf16[4,2,128,128]{3,2,1,0:T(8,128)(2,1)S(1)} %collective-permute-done.10.refs_4_), channel_id=1, source_target_pairs={{0,112},{16,0},{32,16},{48,32},{64,48},{80,64},{96,80},{112,96},{1... | collective-permute-start | bytes 786440 | tf_op jit(solution)/shard_map/ppermute | solution.py:312
  136.1 7.1 %shard_map.58 = (f32[4,128,1024]{2,1,0:T(8,128)S(1)}, f32[4,1,1024]{2,1,0:T(1,128)S(1)}, f32[4,1,1024]{2,1,0:T(1,128)S(1)}) custom-call(s32[5]{0:T(128)S(1)} %pad_add_fusion.where_ref, bf16[4,128,1024]{2,1,0:T(8,128)(2,1)S(1)} %shard_map.57.q_ref, s32[4,1,128]{2,1,0:T(1,128)S(1)} %bitcast.42, bf16[4,2,128,128]{3,2,1,0:T(8,128)(2,1)S(1)} %all_to_all.36.refs_0_, ...), custom_call_target="tpu_custom_call" | custom-call | flops 5368709120 | bytes 4194304 | tf_op jit(solution)/shard_map/pallas_call | solution.py:242
  143.2 4.3 %collective-permute-start.12 = (bf16[2,2,128,128]{3,2,1,0:T(8,128)(2,1)S(1)}, bf16[2,2,128,128]{3,2,1,0:T(8,128)(2,1)S(1)}, u32[]{:S(2)}, u32[]{:S(2)}) collective-permute-start(bf16[2,2,128,128]{3,2,1,0:T(8,128)(2,1)S(1)} %slice.26), channel_id=1, source_target_pairs={{0,16},{16,32},{32,48},{48,64},{64,80},{80,96},{96,112},{112,0},{1... | collective-permute-start | bytes 393224 | tf_op jit(solution)/shard_map/ppermute | solution.py:308
  147.6 3.5 %collective-permute-start.13 = (bf16[2,2,128,128]{3,2,1,0:T(8,128)(2,1)S(1)}, bf16[2,2,128,128]{3,2,1,0:T(8,128)(2,1)S(1)}, u32[]{:S(2)}, u32[]{:S(2)}) collective-permute-start(bf16[2,2,128,128]{3,2,1,0:T(8,128)(2,1)S(1)} %slice.27), channel_id=1, source_target_pairs={{0,112},{16,0},{32,16},{48,32},{64,48},{80,64},{96,80},{112,96},{1... | collective-permute-start | bytes 393224 | tf_op jit(solution)/shard_map/ppermute | solution.py:309
  151.1 2.2 %shard_map.59 = (f32[4,128,1024]{2,1,0:T(8,128)S(1)}, f32[4,1,1024]{2,1,0:T(1,128)S(1)}, f32[4,1,1024]{2,1,0:T(1,128)S(1)}) custom-call(s32[5]{0:T(128)S(1)} %pad_add_fusion.where_ref, bf16[4,128,1024]{2,1,0:T(8,128)(2,1)S(1)} %shard_map.57.q_ref, s32[4,1,128]{2,1,0:T(1,128)S(1)} %bitcast.43, bf16[4,2,128,128]{3,2,1,0:T(8,128)(2,1)S(1)} %collective-permute-done.8.refs_0_, ...), custom_call_target="tpu_custom_call" | custom-call | flops 2147483648 | bytes 4194304 | tf_op jit(solution)/shard_map/pallas_call | solution.py:242
  153.4 2.3 %collective-permute-done.13.refs_1_ = bf16[2,2,128,128]{3,2,1,0:T(8,128)(2,1)S(1)} collective-permute-done((bf16[2,2,128,128]{3,2,1,0:T(8,128)(2,1)S(1)}, bf16[2,2,128,128]{3,2,1,0:T(8,128)(2,1)S(1)}, u32[]{:S(2)}, u32[]{:S(2)}) %collective-permute-start.13) | collective-permute-done | bytes 131104 | tf_op jit(solution)/shard_map/ppermute | solution.py:309
  155.6 1.9 %shard_map.60 = bf16[4,128,1024]{2,1,0:T(8,128)(2,1)S(1)} custom-call(s32[5]{0:T(128)S(1)} %pad_add_fusion.where_ref, bf16[4,128,1024]{2,1,0:T(8,128)(2,1)S(1)} %shard_map.57.q_ref, s32[4,1,128]{2,1,0:T(1,128)S(1)} %bitcast.44, bf16[2,2,128,128]{3,2,1,0:T(8,128)(2,1)S(1)} %collective-permute-done.12.refs_0_, ...), custom_call_target="tpu_custom_call" | custom-call | flops 2147483648 | bytes 4194304 | tf_op jit(solution)/shard_map/pallas_call | solution.py:242
  157.6 27.6 %all_to_all.37 = bf16[4,128,1024]{2,1,0:T(8,128)(2,1)S(1)} all-to-all(bf16[4,128,1024]{2,1,0:T(8,128)(2,1)S(1)} %shard_map.60), channel_id=1, replica_groups=mesh['z1'=2,'z0'=2,'y1'=4,'y0'=2,'zh'=2,'x'=4,'c'=2] {'z1','z0'}, dimensions={0} | all-to-all | bytes 2097152 | tf_op jit(solution)/shard_map/all_to_all | solution.py:39
  185.8 1.3 copy.23
  (56 shorter events, 5.3 us)
Async XLA Ops:
  0.0 7.5 %copy-start = (bf16[1,128,4096]{2,1,0:T(8,128)(2,1)S(1)}, bf16[1,128,4096]{2,1,0:T(8,128)(2,1)}, u32[]{:S(2)}) copy-start(bf16[1,128,4096]{2,1,0:T(8,128)(2,1)} %param.5) | copy-start | bytes 3145732
  3.2 13.0 %all-to-all-start = ((bf16[8,160,128]{2,1,0:T(8,128)(2,1)}), bf16[8,160,128]{2,1,0:T(8,128)(2,1)S(1)}, u32[]{:S(2)}, u32[]{:S(2)}) async-start(bf16[8,160,128]{2,1,0:T(8,128)(2,1)} %bitcast.4), calls=%async_computation | async-start | bytes 655360 | tf_op jit(solution)/shard_map/all_to_all | solution.py:39
  7.5 41.3 %collective-permute-start.1 = (bf16[128,4096]{1,0:T(8,128)(2,1)S(1)}, bf16[128,4096]{1,0:T(8,128)(2,1)S(1)}, u32[]{:S(2)}, u32[]{:S(2)}) collective-permute-start(bf16[128,4096]{1,0:T(8,128)(2,1)S(1)} %bitcast.37), channel_id=1, source_target_pairs={{0,2},{2,4},{4,6},{6,0},{1,3},{3,5},{5,7},{7,1},{8,10},{10,12},{12... | collective-permute-start | bytes 3145736 | tf_op jit(solution)/shard_map/ppermute | solution.py:266
  11.4 37.4 %collective-permute-start.2 = (bf16[128,4096]{1,0:T(8,128)(2,1)S(1)}, bf16[128,4096]{1,0:T(8,128)(2,1)S(1)}, u32[]{:S(2)}, u32[]{:S(2)}) collective-permute-start(bf16[128,4096]{1,0:T(8,128)(2,1)S(1)} %bitcast.38), channel_id=1, source_target_pairs={{0,6},{2,0},{4,2},{6,4},{1,7},{3,1},{5,3},{7,5},{8,14},{10,8},{12,... | collective-permute-start | bytes 3145736 | tf_op jit(solution)/shard_map/ppermute | solution.py:267
  16.2 39.7 %copy-start.7 = (bf16[8,160,128]{2,1,0:T(8,128)(2,1)}, bf16[8,160,128]{2,1,0:T(8,128)(2,1)S(1)}, u32[]{:S(2)}) copy-start(bf16[8,160,128]{2,1,0:T(8,128)(2,1)S(1)} %all-to-all-done) | copy-start | bytes 983044
  16.2 0.7 copy-start.8
  17.0 12.8 %collective-permute-start = (bf16[128,128]{1,0:T(8,128)(2,1)S(1)}, bf16[128,128]{1,0:T(8,128)(2,1)S(1)}, u32[]{:S(2)}, u32[]{:S(2)}) collective-permute-start(bf16[128,128]{1,0:T(8,128)(2,1)S(1)} %dynamic-slice_bitcast_fusion), channel_id=1, source_target_pairs={{0,8},{8,0},{1,9},{9,1},{2,10},{10,2},{3,11},{11,3},{4,12},{12,4},... | collective-permute-start | bytes 98312 | tf_op jit(solution)/shard_map/ppermute | solution.py:263
  31.3 17.5 %all-to-all-start.1 = ((bf16[8,128,128]{2,1,0:T(8,128)(2,1)}), bf16[8,128,128]{2,1,0:T(8,128)(2,1)}, u32[]{:S(2)}, u32[]{:S(2)}) async-start(bf16[8,128,128]{2,1,0:T(8,128)(2,1)} %broadcast_in_dim.36), calls=%async_computation.1 | async-start | bytes 524288 | tf_op jit(solution)/shard_map/all_to_all | solution.py:39
  40.4 4.6 %copy-start.9 = (s32[1,4096]{1,0:T(1,128)S(1)}, s32[1,4096]{1,0:T(1,128)}, u32[]{:S(2)}) copy-start(s32[1,4096]{1,0:T(1,128)} %param.8) | copy-start | bytes 49156
  50.8 23.8 %all-to-all-start.2 = ((bf16[4,1024,128]{2,1,0:T(8,128)(2,1)}), bf16[4,1024,128]{2,1,0:T(8,128)(2,1)}, u32[]{:S(2)}, u32[]{:S(2)}) async-start(bf16[4,1024,128]{2,1,0:T(8,128)(2,1)} %broadcast_in_dim.37), calls=%async_computation.2 | async-start | bytes 2097152 | tf_op jit(solution)/shard_map/all_to_all | solution.py:39
  58.4 13.8 %collective-permute-start.3 = (bf16[64,4096]{1,0:T(8,128)(2,1)S(1)}, bf16[64,4096]{1,0:T(8,128)(2,1)S(1)}, u32[]{:S(2)}, u32[]{:S(2)}) collective-permute-start(bf16[64,4096]{1,0:T(8,128)(2,1)S(1)} %slice.22), channel_id=1, source_target_pairs={{0,2},{2,4},{4,6},{6,0},{1,3},{3,5},{5,7},{7,1},{8,10},{10,12},{12... | collective-permute-start | bytes 1572872 | tf_op jit(solution)/shard_map/ppermute | solution.py:271
  60.7 13.2 %collective-permute-start.4 = (bf16[64,4096]{1,0:T(8,128)(2,1)S(1)}, bf16[64,4096]{1,0:T(8,128)(2,1)S(1)}, u32[]{:S(2)}, u32[]{:S(2)}) collective-permute-start(bf16[64,4096]{1,0:T(8,128)(2,1)S(1)} %slice.23), channel_id=1, source_target_pairs={{0,6},{2,0},{4,2},{6,4},{1,7},{3,1},{5,3},{7,5},{8,14},{10,8},{12,... | collective-permute-start | bytes 1572872 | tf_op jit(solution)/shard_map/ppermute | solution.py:272
  72.3 0.8 copy-start.1
  73.9 0.8 copy-start.3
  74.7 6.6 %collective-permute-start.5 = (bf16[32,128,128]{2,1,0:T(8,128)(2,1)}, bf16[32,128,128]{2,1,0:T(8,128)(2,1)}, u32[]{:S(2)}, u32[]{:S(2)}) collective-permute-start(bf16[32,128,128]{2,1,0:T(8,128)(2,1)} %bitcast.8.refs_5_), channel_id=1, source_target_pairs={{0,1},{1,0},{2,3},{3,2},{4,5},{5,4},{6,7},{7,6},{8,9},{9,8},{10,11... | collective-permute-start | bytes 3145736 | tf_op jit(solution)/shard_map/ppermute | solution.py:290
  76.7 1.0 copy-start.2
  77.7 1.0 copy-start.4
  78.7 2.5 %copy-start.5 = (f32[4,128,64]{2,1,0:T(8,128)S(1)}, f32[4,128,64]{2,1,0:T(8,128)}, u32[]{:S(2)}) copy-start(f32[4,128,64]{2,1,0:T(8,128)} %get-tuple-element.37.refs_8_) | copy-start | bytes 393220
  83.9 51.5 %copy-start.6 = (f32[4,64,128]{2,1,0:T(8,128)S(1)}, f32[4,64,128]{2,1,0:T(8,128)}, u32[]{:S(2)}) copy-start(f32[4,64,128]{2,1,0:T(8,128)} %get-tuple-element.41.cos_ref) | copy-start | bytes 393220
  107.4 28.0 %all-to-all-start.5 = ((bf16[4,128,1024]{2,1,0:T(8,128)(2,1)}), bf16[4,128,1024]{2,1,0:T(8,128)(2,1)S(1)}, u32[]{:S(2)}, u32[]{:S(2)}) async-start(bf16[4,128,1024]{2,1,0:T(8,128)(2,1)} %bitcast.45), calls=%async_computation.5 | async-start | bytes 2097152 | tf_op jit(solution)/shard_map/all_to_all | solution.py:39
  110.9 8.4 %collective-permute-start.6 = (bf16[4,2,128,128]{3,2,1,0:T(8,128)(2,1)S(1)}, bf16[4,2,128,128]{3,2,1,0:T(8,128)(2,1)S(1)}, u32[]{:S(2)}, u32[]{:S(2)}) collective-permute-start(bf16[4,2,128,128]{3,2,1,0:T(8,128)(2,1)S(1)} %all_to_all.36.refs_0_), channel_id=1, source_target_pairs={{0,16},{16,32},{32,48},{48,64},{64,80},{80,96},{96,112},{112,0},{1... | collective-permute-start | bytes 786440 | tf_op jit(solution)/shard_map/ppermute | solution.py:311
  114.2 9.6 %collective-permute-start.9 = (bf16[4,2,128,128]{3,2,1,0:T(8,128)(2,1)S(1)}, bf16[4,2,128,128]{3,2,1,0:T(8,128)(2,1)S(1)}, u32[]{:S(2)}, u32[]{:S(2)}) collective-permute-start(bf16[4,2,128,128]{3,2,1,0:T(8,128)(2,1)S(1)} %all_to_all.36.refs_0_), channel_id=1, source_target_pairs={{0,112},{16,0},{32,16},{48,32},{64,48},{80,64},{96,80},{112,96},{1... | collective-permute-start | bytes 786440 | tf_op jit(solution)/shard_map/ppermute | solution.py:312
  119.3 8.3 %collective-permute-start.7 = (bf16[4,2,128,128]{3,2,1,0:T(8,128)(2,1)S(1)}, bf16[4,2,128,128]{3,2,1,0:T(8,128)(2,1)S(1)}, u32[]{:S(2)}, u32[]{:S(2)}) collective-permute-start(bf16[4,2,128,128]{3,2,1,0:T(8,128)(2,1)S(1)} %collective-permute-done.6.refs_1_), channel_id=1, source_target_pairs={{0,16},{16,32},{32,48},{48,64},{64,80},{80,96},{96,112},{112,0},{1... | collective-permute-start | bytes 786440 | tf_op jit(solution)/shard_map/ppermute | solution.py:311
  123.8 9.5 %collective-permute-start.10 = (bf16[4,2,128,128]{3,2,1,0:T(8,128)(2,1)S(1)}, bf16[4,2,128,128]{3,2,1,0:T(8,128)(2,1)S(1)}, u32[]{:S(2)}, u32[]{:S(2)}) collective-permute-start(bf16[4,2,128,128]{3,2,1,0:T(8,128)(2,1)S(1)} %collective-permute-done.9.refs_3_), channel_id=1, source_target_pairs={{0,112},{16,0},{32,16},{48,32},{64,48},{80,64},{96,80},{112,96},{1... | collective-permute-start | bytes 786440 | tf_op jit(solution)/shard_map/ppermute | solution.py:312
  127.7 15.5 %collective-permute-start.8 = (bf16[4,2,128,128]{3,2,1,0:T(8,128)(2,1)S(1)}, bf16[4,2,128,128]{3,2,1,0:T(8,128)(2,1)S(1)}, u32[]{:S(2)}, u32[]{:S(2)}) collective-permute-start(bf16[4,2,128,128]{3,2,1,0:T(8,128)(2,1)S(1)} %collective-permute-done.7.refs_2_), channel_id=1, source_target_pairs={{0,16},{16,32},{32,48},{48,64},{64,80},{80,96},{96,112},{112,0},{1... | collective-permute-start | bytes 786440 | tf_op jit(solution)/shard_map/ppermute | solution.py:311
  133.3 9.9 %collective-permute-start.11 = (bf16[4,2,128,128]{3,2,1,0:T(8,128)(2,1)S(1)}, bf16[4,2,128,128]{3,2,1,0:T(8,128)(2,1)S(1)}, u32[]{:S(2)}, u32[]{:S(2)}) collective-permute-start(bf16[4,2,128,128]{3,2,1,0:T(8,128)(2,1)S(1)} %collective-permute-done.10.refs_4_), channel_id=1, source_target_pairs={{0,112},{16,0},{32,16},{48,32},{64,48},{80,64},{96,80},{112,96},{1... | collective-permute-start | bytes 786440 | tf_op jit(solution)/shard_map/ppermute | solution.py:312
  143.2 10.1 %collective-permute-start.12 = (bf16[2,2,128,128]{3,2,1,0:T(8,128)(2,1)S(1)}, bf16[2,2,128,128]{3,2,1,0:T(8,128)(2,1)S(1)}, u32[]{:S(2)}, u32[]{:S(2)}) collective-permute-start(bf16[2,2,128,128]{3,2,1,0:T(8,128)(2,1)S(1)} %slice.26), channel_id=1, source_target_pairs={{0,16},{16,32},{32,48},{48,64},{64,80},{80,96},{96,112},{112,0},{1... | collective-permute-start | bytes 393224 | tf_op jit(solution)/shard_map/ppermute | solution.py:308
  147.6 8.1 %collective-permute-start.13 = (bf16[2,2,128,128]{3,2,1,0:T(8,128)(2,1)S(1)}, bf16[2,2,128,128]{3,2,1,0:T(8,128)(2,1)S(1)}, u32[]{:S(2)}, u32[]{:S(2)}) collective-permute-start(bf16[2,2,128,128]{3,2,1,0:T(8,128)(2,1)S(1)} %slice.27), channel_id=1, source_target_pairs={{0,112},{16,0},{32,16},{48,32},{64,48},{80,64},{96,80},{112,96},{1... | collective-permute-start | bytes 393224 | tf_op jit(solution)/shard_map/ppermute | solution.py:309

commit v10 on v9

--- a/solution.py
+++ b/solution.py
@@ -301,16 +301,20 @@
     where = jnp.concatenate([y[None], start[:, 0]]).astype(jnp.int32)
     start = start[:, None, :]
     kv = {0: own_kv}
-    for step in range(1, 5):
-        if step == 4:
-            state = attend(((0,), (1, 2), (-1, -2)), where, q_turned, start, kv)
-            kv[3], kv[-3], *state = lax.optimization_barrier((kv[3], kv[-3], *state))
-            kv[FAR_LOW] = lax.ppermute(kv[3][:2], Y, ring(8, 1))
-            kv[FAR_HIGH] = lax.ppermute(kv[-3][2:], Y, ring(8, -1))
-        else:
-            kv[step] = lax.ppermute(kv[step - 1], Y, ring(8, 1))
-            kv[-step] = lax.ppermute(kv[1 - step], Y, ring(8, -1))
-    state = attend(((3,), (-3,)), where, q_turned, start, kv, state)
+    for step in (1, 2):
+        kv[step] = lax.ppermute(kv[step - 1], Y, ring(8, 1))
+        kv[-step] = lax.ppermute(kv[1 - step], Y, ring(8, -1))
+    kv[3] = lax.ppermute(kv[2], Y, ring(8, 1))
+    state = attend(((0,), (1, 2)), where, q_turned, start, kv)
+    kv[-2], *state = lax.optimization_barrier((kv[-2], *state))
+    kv[-3] = lax.ppermute(kv[-2], Y, ring(8, -1))
+    state = attend(((-1, -2),), where, q_turned, start, kv, state)
+    kv[3], *state = lax.optimization_barrier((kv[3], *state))
+    kv[FAR_LOW] = lax.ppermute(kv[3][:2], Y, ring(8, 1))
+    state = attend(((3,),), where, q_turned, start, kv, state)
+    kv[-3], *state = lax.optimization_barrier((kv[-3], *state))
+    kv[FAR_HIGH] = lax.ppermute(kv[-3][2:], Y, ring(8, -1))
+    state = attend(((-3,),), where, q_turned, start, kv, state)
     mixed = attend(((FAR_LOW,), (FAR_HIGH,)), where, q_turned, start, kv, state, closing=True)
     back = exchange(mixed, Z)
     return back.transpose(1, 0, 2).reshape(1, BLOCK, HEADS * HEAD_DIM)

time: 191 us -> 198 us (1.037)
  waiting for transfers between devices: 18.8 us -> 24.2 us
  Pallas kernels: 17.1 us -> 20.8 us
    ppermute x0 -> x2, starting transfers between devices: none -> 8.05 us  [the longest x1 5.59 us: on_device(): kv[3] = lax.ppermute(kv[2], Y, ring(8, 1))]
    ppermute x3 -> x2, starting transfers between devices: 13.3 us -> 7.75 us  [on_device(): kv[step] = lax.ppermute(kv[step - 1], Y, ring(8, 1))]
    pallas_call x3 -> x5, Pallas kernels: 11.3 us -> 15 us  [attend(): call(functools.partial(attend_kernel, tiles, state is None, closing), out...]
    ppermute x1, waiting for transfers between devices: 2.29 us -> 5.71 us  [on_device(): kv[FAR_HIGH] = lax.ppermute(kv[-3][2:], Y, ring(8, -1))]
    ppermute x3 -> x2, starting transfers between devices: 6.4 us -> 4.48 us  [on_device(): kv[-step] = lax.ppermute(kv[1 - step], Y, ring(8, -1))]
    ppermute x3 -> x2, waiting for transfers between devices: 4.28 us -> 4.29 us  [on_device(): kv[step] = lax.ppermute(kv[step - 1], Y, ring(8, 1))]
  transfers between devices with their start and end apart: 18 -> 18, of which waited for: 9 -> 9; matrix products, arithmetic and copies ran while one was open for 6% -> 6% of each run, Pallas kernels for 7% -> 8%
where the time goes in v10:
time: 198 us; the launch traced here: 196 us
  starting transfers between devices  75.6 us (38%)
  blocking collectives  51.7 us (26%)
  waiting for transfers between devices  24.2 us (12%)
  Pallas kernels  20.8 us (11%)
  local copies, waits for them, and re-layouts  17 us (9%)
  other arithmetic  5.62 us (3%)
    all_to_all x3, blocking collectives, exchange(): return lax.all_to_all(value, axes, split_axis=0, concat_axis=0, tiled=True)  51.7 us
    all_to_all x4, starting transfers between devices, exchange(): return lax.all_to_all(value, axes, split_axis=0, concat_axis=0, tiled=True)  21.9 us
    pallas_call x5, Pallas kernels, attend(): call(functools.partial(attend_kernel, tiles, state is None, closing), out...  15 us
    ppermute x1, starting transfers between devices, on_device(): lax.ppermute(piece, 'zh', ring(2, 1))  10.9 us
    unnamed x23, local copies, waits for them, and re-layouts  7.85 us
    ppermute x2, starting transfers between devices, on_device(): kv[step] = lax.ppermute(kv[step - 1], Y, ring(8, 1))  7.75 us
    all_to_all x4, waiting for transfers between devices, exchange(): return lax.all_to_all(value, axes, split_axis=0, concat_axis=0, tiled=True)  6.65 us
    ppermute x1, waiting for transfers between devices, on_device(): kv[FAR_HIGH] = lax.ppermute(kv[-3][2:], Y, ring(8, -1))  5.71 us
  transfers between devices with their start and end apart: 18, of which 9 were waited for; matrix products, arithmetic and copies ran while one was open for 6% of the time, Pallas kernels for 8%

profile of v10, /device:TPU:56, one launch (start us, length us, event | category | flops | bytes accessed | tf_op | source)
XLA Modules:
  0.0 196.1 jit_solution(3874256375928528104)
XLA Ops:
  0.0 0.9 convert_reduce_fusion.2
  1.0 1.1 copy.17
  2.3 0.9 copy.19
  3.2 4.3 %all-to-all-start = ((bf16[8,160,128]{2,1,0:T(8,128)(2,1)}), bf16[8,160,128]{2,1,0:T(8,128)(2,1)S(1)}, u32[]{:S(2)}, u32[]{:S(2)}) async-start(bf16[8,160,128]{2,1,0:T(8,128)(2,1)} %bitcast.4), calls=%async_computation | async-start | bytes 655360 | tf_op jit(solution)/shard_map/all_to_all | solution.py:39
  7.5 3.9 %collective-permute-start.1 = (bf16[128,4096]{1,0:T(8,128)(2,1)S(1)}, bf16[128,4096]{1,0:T(8,128)(2,1)S(1)}, u32[]{:S(2)}, u32[]{:S(2)}) collective-permute-start(bf16[128,4096]{1,0:T(8,128)(2,1)S(1)} %bitcast.37), channel_id=1, source_target_pairs={{0,2},{2,4},{4,6},{6,0},{1,3},{3,5},{5,7},{7,1},{8,10},{10,12},{12... | collective-permute-start | bytes 3145736 | tf_op jit(solution)/shard_map/ppermute | solution.py:266
  11.4 3.1 %collective-permute-start.2 = (bf16[128,4096]{1,0:T(8,128)(2,1)S(1)}, bf16[128,4096]{1,0:T(8,128)(2,1)S(1)}, u32[]{:S(2)}, u32[]{:S(2)}) collective-permute-start(bf16[128,4096]{1,0:T(8,128)(2,1)S(1)} %bitcast.38), channel_id=1, source_target_pairs={{0,6},{2,0},{4,2},{6,4},{1,7},{3,1},{5,3},{7,5},{8,14},{10,8},{12,... | collective-permute-start | bytes 3145736 | tf_op jit(solution)/shard_map/ppermute | solution.py:267
  15.3 1.0 all-to-all-done
  17.0 10.9 %collective-permute-start = (bf16[128,128]{1,0:T(8,128)(2,1)S(1)}, bf16[128,128]{1,0:T(8,128)(2,1)S(1)}, u32[]{:S(2)}, u32[]{:S(2)}) collective-permute-start(bf16[128,128]{1,0:T(8,128)(2,1)S(1)} %dynamic-slice_bitcast_fusion), channel_id=1, source_target_pairs={{0,8},{8,0},{1,9},{9,1},{2,10},{10,2},{3,11},{11,3},{4,12},{12,4},... | collective-permute-start | bytes 98312 | tf_op jit(solution)/shard_map/ppermute | solution.py:263
  27.9 1.9 collective-permute-done
  31.3 9.1 %all-to-all-start.1 = ((bf16[8,128,128]{2,1,0:T(8,128)(2,1)}), bf16[8,128,128]{2,1,0:T(8,128)(2,1)}, u32[]{:S(2)}, u32[]{:S(2)}) async-start(bf16[8,128,128]{2,1,0:T(8,128)(2,1)} %broadcast_in_dim.36), calls=%async_computation.1 | async-start | bytes 524288 | tf_op jit(solution)/shard_map/all_to_all | solution.py:39
  40.4 2.3 %copy.20 = bf16[1,128,4096]{1,2,0:T(8,128)(2,1)} copy(bf16[1,128,4096]{2,1,0:T(8,128)(2,1)} %param.6) | data formatting | bytes 2097152 | tf_op args[1]
  42.7 2.3 %copy.21 = bf16[128,4,1024]{2,0,1:T(8,128)(2,1)} copy(bf16[128,4,1024]{0,2,1:T(8,128)(2,1)} %bitcast.50) | data formatting | bytes 2097152 | tf_op jit(solution)/shard_map/reshape;squeeze | solution.py:279
  45.2 3.6 %all-to-all-done.1 = bf16[8,128,128]{2,1,0:T(8,128)(2,1)} async-done(((bf16[8,128,128]{2,1,0:T(8,128)(2,1)}), bf16[8,128,128]{2,1,0:T(8,128)(2,1)}, u32[]{:S(2)}, u32[]{:S(2)}) %all-to-all-start.1) | async-done | bytes 262176 | tf_op jit(solution)/shard_map/all_to_all | solution.py:39
  48.8 2.1 %broadcast_in_dim.37 = bf16[4,1024,128]{2,1,0:T(8,128)(2,1)} broadcast(bf16[1024,128]{1,0:T(8,128)(2,1)} %bitcast.6), dimensions={1,2} | broadcast | bytes 1310720 | tf_op jit(solution)/shard_map/broadcast_in_dim | solution.py:43
  50.8 5.0 %all-to-all-start.2 = ((bf16[4,1024,128]{2,1,0:T(8,128)(2,1)}), bf16[4,1024,128]{2,1,0:T(8,128)(2,1)}, u32[]{:S(2)}, u32[]{:S(2)}) async-start(bf16[4,1024,128]{2,1,0:T(8,128)(2,1)} %broadcast_in_dim.37), calls=%async_computation.2 | async-start | bytes 2097152 | tf_op jit(solution)/shard_map/all_to_all | solution.py:39
  56.0 1.2 multiply_sine_fusion.1
  57.2 0.8 slice.29
  58.4 2.2 %collective-permute-start.3 = (bf16[64,4096]{1,0:T(8,128)(2,1)S(1)}, bf16[64,4096]{1,0:T(8,128)(2,1)S(1)}, u32[]{:S(2)}, u32[]{:S(2)}) collective-permute-start(bf16[64,4096]{1,0:T(8,128)(2,1)S(1)} %slice.22), channel_id=1, source_target_pairs={{0,2},{2,4},{4,6},{6,0},{1,3},{3,5},{5,7},{7,1},{8,10},{10,12},{12... | collective-permute-start | bytes 1572872 | tf_op jit(solution)/shard_map/ppermute | solution.py:271
  60.6 4.9 %collective-permute-start.4 = (bf16[64,4096]{1,0:T(8,128)(2,1)S(1)}, bf16[64,4096]{1,0:T(8,128)(2,1)S(1)}, u32[]{:S(2)}, u32[]{:S(2)}) collective-permute-start(bf16[64,4096]{1,0:T(8,128)(2,1)S(1)} %slice.23), channel_id=1, source_target_pairs={{0,6},{2,0},{4,2},{6,4},{1,7},{3,1},{5,3},{7,5},{8,14},{10,8},{12,... | collective-permute-start | bytes 1572872 | tf_op jit(solution)/shard_map/ppermute | solution.py:272
  65.6 1.8 multiply_sine_fusion
  67.4 4.9 %collective-permute-done.3.refs_2_.refs_3_ = bf16[64,4096]{1,0:T(8,128)(2,1)S(1)} collective-permute-done((bf16[64,4096]{1,0:T(8,128)(2,1)S(1)}, bf16[64,4096]{1,0:T(8,128)(2,1)S(1)}, u32[]{:S(2)}, u32[]{:S(2)}) %collective-permute-start.3) | collective-permute-done | bytes 524320 | tf_op jit(solution)/shard_map/ppermute | solution.py:271
  74.6 1.9 collective-permute-start.5
  76.6 1.0 copy-done.2
  77.7 1.0 copy-done.4
  78.7 2.5 %shard_map.55.refs_7_ = f32[512,128]{1,0:T(8,128)S(1)} custom-call(bf16[128,4096]{1,0:T(8,128)(2,1)S(1)} %bitcast.39, bf16[128,4096]{1,0:T(8,128)(2,1)S(1)} %collective-permute-done.1.refs_1_.refs_2_, bf16[64,4096]{1,0:T(8,128)(2,1)S(1)} %copy-done.2, bf16[64,4096]{1,0:T(8,128)(2,1)S(1)} %copy-done.4, ...), custom_call_target="tpu_custom_call" | custom-call | flops 536870912 | bytes 5242880 | tf_op jit(solution)/shard_map/pallas_call | solution.py:122
  81.2 2.6 %shard_map.56 = bf16[4,2,128,128]{3,2,1,0:T(8,128)(2,1)S(1)} custom-call(s32[2]{0:T(128)S(1)} %pad_add_fusion.1.refs_0_, bf16[128,4096]{1,0:T(8,128)(2,1)S(1)} %bitcast.40, bf16[128,4096]{1,0:T(8,128)(2,1)S(1)} %collective-permute-done.1.refs_1_.refs_2_, bf16[64,4096]{1,0:T(8,128)(2,1)S(1)} %copy-done.2, bf16[64,4096]{1,0:T(8,128)(2,1)S(1)} %copy-done.4, ...), custom_call_target="tpu_custom_call" | custom-call | flops 536870912 | bytes 5242880 | tf_op jit(solution)/shard_map/pallas_call | solution.py:148
  83.9 11.9 %all_to_all.35 = bf16[4,2,128,128]{3,2,1,0:T(8,128)(2,1)S(1)} all-to-all(bf16[4,2,128,128]{3,2,1,0:T(8,128)(2,1)S(1)} %shard_map.56), channel_id=1, replica_groups=mesh['z1'=2,'z0'=2,'y1'=4,'y0'=2,'zh'=2,'x'=4,'c'=2] {'x'}, dimensions={0} | all-to-all | bytes 524288 | tf_op jit(solution)/shard_map/all_to_all | solution.py:39
  95.7 11.6 %all_to_all.36.refs_0_ = bf16[4,2,128,128]{3,2,1,0:T(8,128)(2,1)S(1)} all-to-all(bf16[4,2,128,128]{3,2,1,0:T(8,128)(2,1)S(1)} %all_to_all.35), channel_id=1, replica_groups=mesh['z1'=2,'z0'=2,'y1'=4,'y0'=2,'zh'=2,'x'=4,'c'=2] {'z1','z0'}, dimensions={0} | all-to-all | bytes 524288 | tf_op jit(solution)/shard_map/all_to_all | solution.py:39
  107.4 3.5 %all-to-all-start.5 = ((bf16[4,128,1024]{2,1,0:T(8,128)(2,1)}), bf16[4,128,1024]{2,1,0:T(8,128)(2,1)S(1)}, u32[]{:S(2)}, u32[]{:S(2)}) async-start(bf16[4,128,1024]{2,1,0:T(8,128)(2,1)} %bitcast.47), calls=%async_computation.5 | async-start | bytes 2097152 | tf_op jit(solution)/shard_map/all_to_all | solution.py:39
  110.9 3.3 %collective-permute-start.6 = (bf16[4,2,128,128]{3,2,1,0:T(8,128)(2,1)S(1)}, bf16[4,2,128,128]{3,2,1,0:T(8,128)(2,1)S(1)}, u32[]{:S(2)}, u32[]{:S(2)}) collective-permute-start(bf16[4,2,128,128]{3,2,1,0:T(8,128)(2,1)S(1)} %all_to_all.36.refs_0_), channel_id=1, source_target_pairs={{0,16},{16,32},{32,48},{48,64},{64,80},{80,96},{96,112},{112,0},{1... | collective-permute-start | bytes 786440 | tf_op jit(solution)/shard_map/ppermute | solution.py:305
  114.2 2.6 %collective-permute-start.9 = (bf16[4,2,128,128]{3,2,1,0:T(8,128)(2,1)S(1)}, bf16[4,2,128,128]{3,2,1,0:T(8,128)(2,1)S(1)}, u32[]{:S(2)}, u32[]{:S(2)}) collective-permute-start(bf16[4,2,128,128]{3,2,1,0:T(8,128)(2,1)S(1)} %all_to_all.36.refs_0_), channel_id=1, source_target_pairs={{0,112},{16,0},{32,16},{48,32},{64,48},{80,64},{96,80},{112,96},{1... | collective-permute-start | bytes 786440 | tf_op jit(solution)/shard_map/ppermute | solution.py:306
  116.8 2.5 %collective-permute-done.6.refs_1_ = bf16[4,2,128,128]{3,2,1,0:T(8,128)(2,1)S(1)} collective-permute-done((bf16[4,2,128,128]{3,2,1,0:T(8,128)(2,1)S(1)}, bf16[4,2,128,128]{3,2,1,0:T(8,128)(2,1)S(1)}, u32[]{:S(2)}, u32[]{:S(2)}) %collective-permute-start.6) | collective-permute-done | bytes 262176 | tf_op jit(solution)/shard_map/ppermute | solution.py:305
  119.3 4.5 %collective-permute-start.7 = (bf16[4,2,128,128]{3,2,1,0:T(8,128)(2,1)S(1)}, bf16[4,2,128,128]{3,2,1,0:T(8,128)(2,1)S(1)}, u32[]{:S(2)}, u32[]{:S(2)}) collective-permute-start(bf16[4,2,128,128]{3,2,1,0:T(8,128)(2,1)S(1)} %collective-permute-done.6.refs_1_), channel_id=1, source_target_pairs={{0,16},{16,32},{32,48},{48,64},{64,80},{80,96},{96,112},{112,0},{1... | collective-permute-start | bytes 786440 | tf_op jit(solution)/shard_map/ppermute | solution.py:305
  124.0 1.9 collective-permute-start.10
  125.9 1.8 collective-permute-done.7.refs_2_
  127.7 5.6 %collective-permute-start.8 = (bf16[4,2,128,128]{3,2,1,0:T(8,128)(2,1)S(1)}, bf16[4,2,128,128]{3,2,1,0:T(8,128)(2,1)S(1)}, u32[]{:S(2)}, u32[]{:S(2)}) collective-permute-start(bf16[4,2,128,128]{3,2,1,0:T(8,128)(2,1)S(1)} %collective-permute-done.7.refs_2_), channel_id=1, source_target_pairs={{0,16},{16,32},{32,48},{48,64},{64,80},{80,96},{96,112},{112,0},{1... | collective-permute-start | bytes 786440 | tf_op jit(solution)/shard_map/ppermute | solution.py:307
  133.3 2.1 %all-to-all-done.5.q_ref = bf16[4,128,1024]{2,1,0:T(8,128)(2,1)S(1)} async-done(((bf16[4,128,1024]{2,1,0:T(8,128)(2,1)}), bf16[4,128,1024]{2,1,0:T(8,128)(2,1)S(1)}, u32[]{:S(2)}, u32[]{:S(2)}) %all-to-all-start.5) | async-done | bytes 1048608 | tf_op jit(solution)/shard_map/all_to_all | solution.py:39
  136.1 6.3 %shard_map.58 = (f32[4,128,1024]{2,1,0:T(8,128)S(1)}, f32[4,1,1024]{2,1,0:T(1,128)S(1)}, f32[4,1,1024]{2,1,0:T(1,128)S(1)}) custom-call(s32[5]{0:T(128)S(1)} %pad_add_fusion.where_ref, bf16[4,128,1024]{2,1,0:T(8,128)(2,1)S(1)} %shard_map.57.q_ref, s32[4,1,128]{2,1,0:T(1,128)S(1)} %bitcast.42, bf16[4,2,128,128]{3,2,1,0:T(8,128)(2,1)S(1)} %all_to_all.36.refs_0_, ...), custom_call_target="tpu_custom_call" | custom-call | flops 3221225472 | bytes 4194304 | tf_op jit(solution)/shard_map/pallas_call | solution.py:242
  142.4 2.5 %collective-permute-start.12 = (bf16[4,2,128,128]{3,2,1,0:T(8,128)(2,1)S(1)}, bf16[4,2,128,128]{3,2,1,0:T(8,128)(2,1)S(1)}, u32[]{:S(2)}, u32[]{:S(2)}) collective-permute-start(bf16[4,2,128,128]{3,2,1,0:T(8,128)(2,1)S(1)} %collective-permute-done.10.refs_1_), channel_id=1, source_target_pairs={{0,112},{16,0},{32,16},{48,32},{64,48},{80,64},{96,80},{112,96},{1... | collective-permute-start | bytes 786440 | tf_op jit(solution)/shard_map/ppermute | solution.py:310
  144.9 1.5 shard_map.59
  146.4 4.6 %collective-permute-start.11 = (bf16[2,2,128,128]{3,2,1,0:T(8,128)(2,1)S(1)}, bf16[2,2,128,128]{3,2,1,0:T(8,128)(2,1)S(1)}, u32[]{:S(2)}, u32[]{:S(2)}) collective-permute-start(bf16[2,2,128,128]{3,2,1,0:T(8,128)(2,1)S(1)} %slice.26), channel_id=1, source_target_pairs={{0,16},{16,32},{32,48},{48,64},{64,80},{80,96},{96,112},{112,0},{1... | collective-permute-start | bytes 393224 | tf_op jit(solution)/shard_map/ppermute | solution.py:313
  151.0 2.6 %shard_map.60 = (f32[4,128,1024]{2,1,0:T(8,128)S(1)}, f32[4,1,1024]{2,1,0:T(1,128)S(1)}, f32[4,1,1024]{2,1,0:T(1,128)S(1)}) custom-call(s32[5]{0:T(128)S(1)} %pad_add_fusion.where_ref, bf16[4,128,1024]{2,1,0:T(8,128)(2,1)S(1)} %shard_map.57.q_ref, s32[4,1,128]{2,1,0:T(1,128)S(1)} %bitcast.44, bf16[4,2,128,128]{3,2,1,0:T(8,128)(2,1)S(1)} %collective-permute-done.8.refs_0_, ...), custom_call_target="tpu_custom_call" | custom-call | flops 1073741824 | bytes 4194304 | tf_op jit(solution)/shard_map/pallas_call | solution.py:242
  153.7 1.9 collective-permute-start.13
  155.6 1.3 shard_map.61
  156.9 5.7 %collective-permute-done.13.refs_1_ = bf16[2,2,128,128]{3,2,1,0:T(8,128)(2,1)S(1)} collective-permute-done((bf16[2,2,128,128]{3,2,1,0:T(8,128)(2,1)S(1)}, bf16[2,2,128,128]{3,2,1,0:T(8,128)(2,1)S(1)}, u32[]{:S(2)}, u32[]{:S(2)}) %collective-permute-start.13) | collective-permute-done | bytes 131104 | tf_op jit(solution)/shard_map/ppermute | solution.py:316
  162.6 3.3 %shard_map.62 = bf16[4,128,1024]{2,1,0:T(8,128)(2,1)S(1)} custom-call(s32[5]{0:T(128)S(1)} %pad_add_fusion.where_ref, bf16[4,128,1024]{2,1,0:T(8,128)(2,1)S(1)} %shard_map.57.q_ref, s32[4,1,128]{2,1,0:T(1,128)S(1)} %bitcast.46, bf16[2,2,128,128]{3,2,1,0:T(8,128)(2,1)S(1)} %collective-permute-done.11.refs_0_, ...), custom_call_target="tpu_custom_call" | custom-call | flops 2147483648 | bytes 4194304 | tf_op jit(solution)/shard_map/pallas_call | solution.py:242
  165.9 28.2 %all_to_all.37 = bf16[4,128,1024]{2,1,0:T(8,128)(2,1)S(1)} all-to-all(bf16[4,128,1024]{2,1,0:T(8,128)(2,1)S(1)} %shard_map.62), channel_id=1, replica_groups=mesh['z1'=2,'z0'=2,'y1'=4,'y0'=2,'zh'=2,'x'=4,'c'=2] {'z1','z0'}, dimensions={0} | all-to-all | bytes 2097152 | tf_op jit(solution)/shard_map/all_to_all | solution.py:39
  194.8 1.3 copy.23
  (58 shorter events, 7.5 us)
Async XLA Ops:
  0.0 7.5 %copy-start = (bf16[1,128,4096]{2,1,0:T(8,128)(2,1)S(1)}, bf16[1,128,4096]{2,1,0:T(8,128)(2,1)}, u32[]{:S(2)}) copy-start(bf16[1,128,4096]{2,1,0:T(8,128)(2,1)} %param.5) | copy-start | bytes 3145732
  3.2 13.0 %all-to-all-start = ((bf16[8,160,128]{2,1,0:T(8,128)(2,1)}), bf16[8,160,128]{2,1,0:T(8,128)(2,1)S(1)}, u32[]{:S(2)}, u32[]{:S(2)}) async-start(bf16[8,160,128]{2,1,0:T(8,128)(2,1)} %bitcast.4), calls=%async_computation | async-start | bytes 655360 | tf_op jit(solution)/shard_map/all_to_all | solution.py:39
  7.5 41.3 %collective-permute-start.1 = (bf16[128,4096]{1,0:T(8,128)(2,1)S(1)}, bf16[128,4096]{1,0:T(8,128)(2,1)S(1)}, u32[]{:S(2)}, u32[]{:S(2)}) collective-permute-start(bf16[128,4096]{1,0:T(8,128)(2,1)S(1)} %bitcast.37), channel_id=1, source_target_pairs={{0,2},{2,4},{4,6},{6,0},{1,3},{3,5},{5,7},{7,1},{8,10},{10,12},{12... | collective-permute-start | bytes 3145736 | tf_op jit(solution)/shard_map/ppermute | solution.py:266
  11.4 37.4 %collective-permute-start.2 = (bf16[128,4096]{1,0:T(8,128)(2,1)S(1)}, bf16[128,4096]{1,0:T(8,128)(2,1)S(1)}, u32[]{:S(2)}, u32[]{:S(2)}) collective-permute-start(bf16[128,4096]{1,0:T(8,128)(2,1)S(1)} %bitcast.38), channel_id=1, source_target_pairs={{0,6},{2,0},{4,2},{6,4},{1,7},{3,1},{5,3},{7,5},{8,14},{10,8},{12,... | collective-permute-start | bytes 3145736 | tf_op jit(solution)/shard_map/ppermute | solution.py:267
  16.2 39.7 %copy-start.7 = (bf16[8,160,128]{2,1,0:T(8,128)(2,1)}, bf16[8,160,128]{2,1,0:T(8,128)(2,1)S(1)}, u32[]{:S(2)}) copy-start(bf16[8,160,128]{2,1,0:T(8,128)(2,1)S(1)} %all-to-all-done) | copy-start | bytes 983044
  16.2 0.7 copy-start.8
  17.0 12.8 %collective-permute-start = (bf16[128,128]{1,0:T(8,128)(2,1)S(1)}, bf16[128,128]{1,0:T(8,128)(2,1)S(1)}, u32[]{:S(2)}, u32[]{:S(2)}) collective-permute-start(bf16[128,128]{1,0:T(8,128)(2,1)S(1)} %dynamic-slice_bitcast_fusion), channel_id=1, source_target_pairs={{0,8},{8,0},{1,9},{9,1},{2,10},{10,2},{3,11},{11,3},{4,12},{12,4},... | collective-permute-start | bytes 98312 | tf_op jit(solution)/shard_map/ppermute | solution.py:263
  31.3 17.5 %all-to-all-start.1 = ((bf16[8,128,128]{2,1,0:T(8,128)(2,1)}), bf16[8,128,128]{2,1,0:T(8,128)(2,1)}, u32[]{:S(2)}, u32[]{:S(2)}) async-start(bf16[8,128,128]{2,1,0:T(8,128)(2,1)} %broadcast_in_dim.36), calls=%async_computation.1 | async-start | bytes 524288 | tf_op jit(solution)/shard_map/all_to_all | solution.py:39
  40.4 4.6 %copy-start.9 = (s32[1,4096]{1,0:T(1,128)S(1)}, s32[1,4096]{1,0:T(1,128)}, u32[]{:S(2)}) copy-start(s32[1,4096]{1,0:T(1,128)} %param.8) | copy-start | bytes 49156
  50.8 23.8 %all-to-all-start.2 = ((bf16[4,1024,128]{2,1,0:T(8,128)(2,1)}), bf16[4,1024,128]{2,1,0:T(8,128)(2,1)}, u32[]{:S(2)}, u32[]{:S(2)}) async-start(bf16[4,1024,128]{2,1,0:T(8,128)(2,1)} %broadcast_in_dim.37), calls=%async_computation.2 | async-start | bytes 2097152 | tf_op jit(solution)/shard_map/all_to_all | solution.py:39
  58.4 13.8 %collective-permute-start.3 = (bf16[64,4096]{1,0:T(8,128)(2,1)S(1)}, bf16[64,4096]{1,0:T(8,128)(2,1)S(1)}, u32[]{:S(2)}, u32[]{:S(2)}) collective-permute-start(bf16[64,4096]{1,0:T(8,128)(2,1)S(1)} %slice.22), channel_id=1, source_target_pairs={{0,2},{2,4},{4,6},{6,0},{1,3},{3,5},{5,7},{7,1},{8,10},{10,12},{12... | collective-permute-start | bytes 1572872 | tf_op jit(solution)/shard_map/ppermute | solution.py:271
  60.6 13.2 %collective-permute-start.4 = (bf16[64,4096]{1,0:T(8,128)(2,1)S(1)}, bf16[64,4096]{1,0:T(8,128)(2,1)S(1)}, u32[]{:S(2)}, u32[]{:S(2)}) collective-permute-start(bf16[64,4096]{1,0:T(8,128)(2,1)S(1)} %slice.23), channel_id=1, source_target_pairs={{0,6},{2,0},{4,2},{6,4},{1,7},{3,1},{5,3},{7,5},{8,14},{10,8},{12,... | collective-permute-start | bytes 1572872 | tf_op jit(solution)/shard_map/ppermute | solution.py:272
  72.3 0.8 copy-start.1
  73.8 0.8 copy-start.3
  74.6 6.6 %collective-permute-start.5 = (bf16[32,128,128]{2,1,0:T(8,128)(2,1)}, bf16[32,128,128]{2,1,0:T(8,128)(2,1)}, u32[]{:S(2)}, u32[]{:S(2)}) collective-permute-start(bf16[32,128,128]{2,1,0:T(8,128)(2,1)} %bitcast.8.refs_5_), channel_id=1, source_target_pairs={{0,1},{1,0},{2,3},{3,2},{4,5},{5,4},{6,7},{7,6},{8,9},{9,8},{10,11... | collective-permute-start | bytes 3145736 | tf_op jit(solution)/shard_map/ppermute | solution.py:290
  76.6 1.0 copy-start.2
  77.7 1.0 copy-start.4
  78.7 2.5 %copy-start.5 = (f32[4,128,64]{2,1,0:T(8,128)S(1)}, f32[4,128,64]{2,1,0:T(8,128)}, u32[]{:S(2)}) copy-start(f32[4,128,64]{2,1,0:T(8,128)} %get-tuple-element.50.refs_8_) | copy-start | bytes 393220
  83.9 51.5 %copy-start.6 = (f32[4,64,128]{2,1,0:T(8,128)S(1)}, f32[4,64,128]{2,1,0:T(8,128)}, u32[]{:S(2)}) copy-start(f32[4,64,128]{2,1,0:T(8,128)} %get-tuple-element.54.cos_ref) | copy-start | bytes 393220
  107.4 28.0 %all-to-all-start.5 = ((bf16[4,128,1024]{2,1,0:T(8,128)(2,1)}), bf16[4,128,1024]{2,1,0:T(8,128)(2,1)S(1)}, u32[]{:S(2)}, u32[]{:S(2)}) async-start(bf16[4,128,1024]{2,1,0:T(8,128)(2,1)} %bitcast.47), calls=%async_computation.5 | async-start | bytes 2097152 | tf_op jit(solution)/shard_map/all_to_all | solution.py:39
  110.9 8.4 %collective-permute-start.6 = (bf16[4,2,128,128]{3,2,1,0:T(8,128)(2,1)S(1)}, bf16[4,2,128,128]{3,2,1,0:T(8,128)(2,1)S(1)}, u32[]{:S(2)}, u32[]{:S(2)}) collective-permute-start(bf16[4,2,128,128]{3,2,1,0:T(8,128)(2,1)S(1)} %all_to_all.36.refs_0_), channel_id=1, source_target_pairs={{0,16},{16,32},{32,48},{48,64},{64,80},{80,96},{96,112},{112,0},{1... | collective-permute-start | bytes 786440 | tf_op jit(solution)/shard_map/ppermute | solution.py:305
  114.2 9.8 %collective-permute-start.9 = (bf16[4,2,128,128]{3,2,1,0:T(8,128)(2,1)S(1)}, bf16[4,2,128,128]{3,2,1,0:T(8,128)(2,1)S(1)}, u32[]{:S(2)}, u32[]{:S(2)}) collective-permute-start(bf16[4,2,128,128]{3,2,1,0:T(8,128)(2,1)S(1)} %all_to_all.36.refs_0_), channel_id=1, source_target_pairs={{0,112},{16,0},{32,16},{48,32},{64,48},{80,64},{96,80},{112,96},{1... | collective-permute-start | bytes 786440 | tf_op jit(solution)/shard_map/ppermute | solution.py:306
  119.3 8.4 %collective-permute-start.7 = (bf16[4,2,128,128]{3,2,1,0:T(8,128)(2,1)S(1)}, bf16[4,2,128,128]{3,2,1,0:T(8,128)(2,1)S(1)}, u32[]{:S(2)}, u32[]{:S(2)}) collective-permute-start(bf16[4,2,128,128]{3,2,1,0:T(8,128)(2,1)S(1)} %collective-permute-done.6.refs_1_), channel_id=1, source_target_pairs={{0,16},{16,32},{32,48},{48,64},{64,80},{80,96},{96,112},{112,0},{1... | collective-permute-start | bytes 786440 | tf_op jit(solution)/shard_map/ppermute | solution.py:305
  124.0 18.4 %collective-permute-start.10 = (bf16[4,2,128,128]{3,2,1,0:T(8,128)(2,1)S(1)}, bf16[4,2,128,128]{3,2,1,0:T(8,128)(2,1)S(1)}, u32[]{:S(2)}, u32[]{:S(2)}) collective-permute-start(bf16[4,2,128,128]{3,2,1,0:T(8,128)(2,1)S(1)} %collective-permute-done.9.refs_0_), channel_id=1, source_target_pairs={{0,112},{16,0},{32,16},{48,32},{64,48},{80,64},{96,80},{112,96},{1... | collective-permute-start | bytes 786440 | tf_op jit(solution)/shard_map/ppermute | solution.py:306
  127.7 18.7 %collective-permute-start.8 = (bf16[4,2,128,128]{3,2,1,0:T(8,128)(2,1)S(1)}, bf16[4,2,128,128]{3,2,1,0:T(8,128)(2,1)S(1)}, u32[]{:S(2)}, u32[]{:S(2)}) collective-permute-start(bf16[4,2,128,128]{3,2,1,0:T(8,128)(2,1)S(1)} %collective-permute-done.7.refs_2_), channel_id=1, source_target_pairs={{0,16},{16,32},{32,48},{48,64},{64,80},{80,96},{96,112},{112,0},{1... | collective-permute-start | bytes 786440 | tf_op jit(solution)/shard_map/ppermute | solution.py:307
  142.4 11.2 %collective-permute-start.12 = (bf16[4,2,128,128]{3,2,1,0:T(8,128)(2,1)S(1)}, bf16[4,2,128,128]{3,2,1,0:T(8,128)(2,1)S(1)}, u32[]{:S(2)}, u32[]{:S(2)}) collective-permute-start(bf16[4,2,128,128]{3,2,1,0:T(8,128)(2,1)S(1)} %collective-permute-done.10.refs_1_), channel_id=1, source_target_pairs={{0,112},{16,0},{32,16},{48,32},{64,48},{80,64},{96,80},{112,96},{1... | collective-permute-start | bytes 786440 | tf_op jit(solution)/shard_map/ppermute | solution.py:310
  146.4 10.5 %collective-permute-start.11 = (bf16[2,2,128,128]{3,2,1,0:T(8,128)(2,1)S(1)}, bf16[2,2,128,128]{3,2,1,0:T(8,128)(2,1)S(1)}, u32[]{:S(2)}, u32[]{:S(2)}) collective-permute-start(bf16[2,2,128,128]{3,2,1,0:T(8,128)(2,1)S(1)} %slice.26), channel_id=1, source_target_pairs={{0,16},{16,32},{32,48},{48,64},{64,80},{80,96},{96,112},{112,0},{1... | collective-permute-start | bytes 393224 | tf_op jit(solution)/shard_map/ppermute | solution.py:313
  153.7 8.9 %collective-permute-start.13 = (bf16[2,2,128,128]{3,2,1,0:T(8,128)(2,1)S(1)}, bf16[2,2,128,128]{3,2,1,0:T(8,128)(2,1)S(1)}, u32[]{:S(2)}, u32[]{:S(2)}) collective-permute-start(bf16[2,2,128,128]{3,2,1,0:T(8,128)(2,1)S(1)} %slice.27), channel_id=1, source_target_pairs={{0,112},{16,0},{32,16},{48,32},{64,48},{80,64},{96,80},{112,96},{1... | collective-permute-start | bytes 393224 | tf_op jit(solution)/shard_map/ppermute | solution.py:316

commit v11 on v10

--- a/solution.py
+++ b/solution.py
@@ -17,7 +17,6 @@
 BLOCK = 128
 LOW = -1e30
 DOCS = 6
-FAR_LOW, FAR_HIGH = 4, -4
 
 AXES = ("z1", "z0", "y1", "y0", "zh", "x", "c")
 SIZES = (2, 2, 4, 2, 2, 4, 2)
@@ -189,17 +188,11 @@
                     for place in places
                 ]
 
-                if tile == (FAR_LOW,):
-                    needed.append(zz < 2)
-                if tile == (FAR_HIGH,):
-                    needed.append(zz >= 2)
-                halved = tile in ((FAR_LOW,), (FAR_HIGH,))
-                row = zz & 1 if halved else zz
-
-                @pl.when(functools.reduce(jnp.logical_and if halved else jnp.logical_or, needed))
-                def _(row=row, tile=tile, places=places):
-                    key = jnp.concatenate([kv[shift][row, 0] for shift in tile], axis=0)
-                    val = jnp.concatenate([kv[shift][row, 1] for shift in tile], axis=1)
+
+                @pl.when(functools.reduce(jnp.logical_or, needed))
+                def _(tile=tile, places=places):
+                    key = jnp.concatenate([kv[shift][zz, 0] for shift in tile], axis=0)
+                    val = jnp.concatenate([kv[shift][zz, 1] for shift in tile], axis=1)
                     allowed = []
                     for place in places:
                         at = place * BLOCK + lax.broadcasted_iota(jnp.int32, (BLOCK, BLOCK), 0)
@@ -301,21 +294,14 @@
     where = jnp.concatenate([y[None], start[:, 0]]).astype(jnp.int32)
     start = start[:, None, :]
     kv = {0: own_kv}
-    for step in (1, 2):
+    for step in (1, 2, 3):
         kv[step] = lax.ppermute(kv[step - 1], Y, ring(8, 1))
         kv[-step] = lax.ppermute(kv[1 - step], Y, ring(8, -1))
-    kv[3] = lax.ppermute(kv[2], Y, ring(8, 1))
     state = attend(((0,), (1, 2)), where, q_turned, start, kv)
-    kv[-2], *state = lax.optimization_barrier((kv[-2], *state))
-    kv[-3] = lax.ppermute(kv[-2], Y, ring(8, -1))
-    state = attend(((-1, -2),), where, q_turned, start, kv, state)
     kv[3], *state = lax.optimization_barrier((kv[3], *state))
-    kv[FAR_LOW] = lax.ppermute(kv[3][:2], Y, ring(8, 1))
-    state = attend(((3,),), where, q_turned, start, kv, state)
-    kv[-3], *state = lax.optimization_barrier((kv[-3], *state))
-    kv[FAR_HIGH] = lax.ppermute(kv[-3][2:], Y, ring(8, -1))
-    state = attend(((-3,),), where, q_turned, start, kv, state)
-    mixed = attend(((FAR_LOW,), (FAR_HIGH,)), where, q_turned, start, kv, state, closing=True)
+    kv[4] = lax.ppermute(kv[3], Y, ring(8, 1))
+    state = attend(((-1, -2), (3,), (-3,)), where, q_turned, start, kv, state)
+    mixed = attend(((4,),), where, q_turned, start, kv, state, closing=True)
     back = exchange(mixed, Z)
     return back.transpose(1, 0, 2).reshape(1, BLOCK, HEADS * HEAD_DIM)
 

time: 198 us -> 187 us (0.944)
  waiting for transfers between devices: 24.2 us -> 16.6 us
  starting transfers between devices: 75.6 us -> 72.8 us
    ppermute x4 -> x1, starting transfers between devices: 14.6 us -> 4.3 us  [on_device(): kv[4] = lax.ppermute(kv[3], Y, ring(8, 1))]
    ppermute x4 -> x1, waiting for transfers between devices: 5.72 us -> 0.04 us  [on_device(): kv[4] = lax.ppermute(kv[3], Y, ring(8, 1))]
    ppermute x2 -> x3, starting transfers between devices: 7.75 us -> 13.3 us  [on_device(): kv[step] = lax.ppermute(kv[step - 1], Y, ring(8, 1))]
    ppermute x2 -> x3, starting transfers between devices: 4.48 us -> 6.41 us  [on_device(): kv[-step] = lax.ppermute(kv[1 - step], Y, ring(8, -1))]
    pallas_call x5 -> x3, Pallas kernels: 15 us -> 14.3 us  [attend(): call(functools.partial(attend_kernel, tiles, state is None, closing), out...]
    ppermute x2 -> x3, waiting for transfers between devices: 4.29 us -> 4.28 us  [on_device(): kv[step] = lax.ppermute(kv[step - 1], Y, ring(8, 1))]
  transfers between devices with their start and end apart: 18 -> 17, of which waited for: 9 -> 8; matrix products, arithmetic and copies ran while one was open for 6% -> 6% of each run, Pallas kernels for 8% -> 8%
where the time goes in v11:
time: 187 us; the launch traced here: 184 us
  starting transfers between devices  72.8 us (39%)
  blocking collectives  51.1 us (27%)
  Pallas kernels  20.2 us (11%)
  local copies, waits for them, and re-layouts  17.1 us (9%)
  waiting for transfers between devices  16.6 us (9%)
  other arithmetic  5.63 us (3%)
    all_to_all x3, blocking collectives, exchange(): return lax.all_to_all(value, axes, split_axis=0, concat_axis=0, tiled=True)  51.1 us
    all_to_all x4, starting transfers between devices, exchange(): return lax.all_to_all(value, axes, split_axis=0, concat_axis=0, tiled=True)  21.9 us
    pallas_call x3, Pallas kernels, attend(): call(functools.partial(attend_kernel, tiles, state is None, closing), out...  14.3 us
    ppermute x3, starting transfers between devices, on_device(): kv[step] = lax.ppermute(kv[step - 1], Y, ring(8, 1))  13.3 us
    ppermute x1, starting transfers between devices, on_device(): lax.ppermute(piece, 'zh', ring(2, 1))  10.9 us
    unnamed x23, local copies, waits for them, and re-layouts  7.87 us
    ppermute x3, starting transfers between devices, on_device(): kv[-step] = lax.ppermute(kv[1 - step], Y, ring(8, -1))  6.41 us
    ppermute x1, starting transfers between devices, on_device(): far_high = lax.ppermute(right[64:], 'x', ring(4, -1))  4.89 us
  transfers between devices with their start and end apart: 17, of which 8 were waited for; matrix products, arithmetic and copies ran while one was open for 6% of the time, Pallas kernels for 8%

profile of v11, /device:TPU:56, one launch (start us, length us, event | category | flops | bytes accessed | tf_op | source)
XLA Modules:
  0.0 184.5 jit_solution(17044772175647882368)
XLA Ops:
  0.0 0.9 convert_reduce_fusion.2
  1.0 1.1 copy.17
  2.3 0.9 copy.19
  3.2 4.3 %all-to-all-start = ((bf16[8,160,128]{2,1,0:T(8,128)(2,1)}), bf16[8,160,128]{2,1,0:T(8,128)(2,1)S(1)}, u32[]{:S(2)}, u32[]{:S(2)}) async-start(bf16[8,160,128]{2,1,0:T(8,128)(2,1)} %bitcast.4), calls=%async_computation | async-start | bytes 655360 | tf_op jit(solution)/shard_map/all_to_all | solution.py:38
  7.5 3.9 %collective-permute-start.1 = (bf16[128,4096]{1,0:T(8,128)(2,1)S(1)}, bf16[128,4096]{1,0:T(8,128)(2,1)S(1)}, u32[]{:S(2)}, u32[]{:S(2)}) collective-permute-start(bf16[128,4096]{1,0:T(8,128)(2,1)S(1)} %bitcast.37), channel_id=1, source_target_pairs={{0,2},{2,4},{4,6},{6,0},{1,3},{3,5},{5,7},{7,1},{8,10},{10,12},{12... | collective-permute-start | bytes 3145736 | tf_op jit(solution)/shard_map/ppermute | solution.py:259
  11.4 3.1 %collective-permute-start.2 = (bf16[128,4096]{1,0:T(8,128)(2,1)S(1)}, bf16[128,4096]{1,0:T(8,128)(2,1)S(1)}, u32[]{:S(2)}, u32[]{:S(2)}) collective-permute-start(bf16[128,4096]{1,0:T(8,128)(2,1)S(1)} %bitcast.38), channel_id=1, source_target_pairs={{0,6},{2,0},{4,2},{6,4},{1,7},{3,1},{5,3},{7,5},{8,14},{10,8},{12,... | collective-permute-start | bytes 3145736 | tf_op jit(solution)/shard_map/ppermute | solution.py:260
  15.3 1.0 all-to-all-done
  17.0 10.9 %collective-permute-start = (bf16[128,128]{1,0:T(8,128)(2,1)S(1)}, bf16[128,128]{1,0:T(8,128)(2,1)S(1)}, u32[]{:S(2)}, u32[]{:S(2)}) collective-permute-start(bf16[128,128]{1,0:T(8,128)(2,1)S(1)} %dynamic-slice_bitcast_fusion), channel_id=1, source_target_pairs={{0,8},{8,0},{1,9},{9,1},{2,10},{10,2},{3,11},{11,3},{4,12},{12,4},... | collective-permute-start | bytes 98312 | tf_op jit(solution)/shard_map/ppermute | solution.py:256
  27.9 1.9 %collective-permute-done = bf16[128,128]{1,0:T(8,128)(2,1)S(1)} collective-permute-done((bf16[128,128]{1,0:T(8,128)(2,1)S(1)}, bf16[128,128]{1,0:T(8,128)(2,1)S(1)}, u32[]{:S(2)}, u32[]{:S(2)}) %collective-permute-start) | collective-permute-done | bytes 32800 | tf_op jit(solution)/shard_map/ppermute | solution.py:256
  29.8 0.8 broadcast_select_fusion
  30.6 0.7 broadcast_in_dim.36
  31.3 9.1 %all-to-all-start.1 = ((bf16[8,128,128]{2,1,0:T(8,128)(2,1)}), bf16[8,128,128]{2,1,0:T(8,128)(2,1)}, u32[]{:S(2)}, u32[]{:S(2)}) async-start(bf16[8,128,128]{2,1,0:T(8,128)(2,1)} %broadcast_in_dim.36), calls=%async_computation.1 | async-start | bytes 524288 | tf_op jit(solution)/shard_map/all_to_all | solution.py:38
  40.4 2.3 %copy.20 = bf16[1,128,4096]{1,2,0:T(8,128)(2,1)} copy(bf16[1,128,4096]{2,1,0:T(8,128)(2,1)} %param.6) | data formatting | bytes 2097152 | tf_op args[1]
  42.7 2.3 %copy.21 = bf16[128,4,1024]{2,0,1:T(8,128)(2,1)} copy(bf16[128,4,1024]{0,2,1:T(8,128)(2,1)} %bitcast.48) | data formatting | bytes 2097152 | tf_op jit(solution)/shard_map/reshape;squeeze | solution.py:272
  45.2 3.5 %all-to-all-done.1 = bf16[8,128,128]{2,1,0:T(8,128)(2,1)} async-done(((bf16[8,128,128]{2,1,0:T(8,128)(2,1)}), bf16[8,128,128]{2,1,0:T(8,128)(2,1)}, u32[]{:S(2)}, u32[]{:S(2)}) %all-to-all-start.1) | async-done | bytes 262176 | tf_op jit(solution)/shard_map/all_to_all | solution.py:38
  48.8 2.1 %broadcast_in_dim.37 = bf16[4,1024,128]{2,1,0:T(8,128)(2,1)} broadcast(bf16[1024,128]{1,0:T(8,128)(2,1)} %bitcast.6), dimensions={1,2} | broadcast | bytes 1310720 | tf_op jit(solution)/shard_map/broadcast_in_dim | solution.py:42
  50.8 5.0 %all-to-all-start.2 = ((bf16[4,1024,128]{2,1,0:T(8,128)(2,1)}), bf16[4,1024,128]{2,1,0:T(8,128)(2,1)}, u32[]{:S(2)}, u32[]{:S(2)}) async-start(bf16[4,1024,128]{2,1,0:T(8,128)(2,1)} %broadcast_in_dim.37), calls=%async_computation.2 | async-start | bytes 2097152 | tf_op jit(solution)/shard_map/all_to_all | solution.py:38
  56.0 1.2 multiply_sine_fusion.1
  57.2 0.8 slice.21
  58.4 2.2 %collective-permute-start.3 = (bf16[64,4096]{1,0:T(8,128)(2,1)S(1)}, bf16[64,4096]{1,0:T(8,128)(2,1)S(1)}, u32[]{:S(2)}, u32[]{:S(2)}) collective-permute-start(bf16[64,4096]{1,0:T(8,128)(2,1)S(1)} %slice.16), channel_id=1, source_target_pairs={{0,2},{2,4},{4,6},{6,0},{1,3},{3,5},{5,7},{7,1},{8,10},{10,12},{12... | collective-permute-start | bytes 1572872 | tf_op jit(solution)/shard_map/ppermute | solution.py:264
  60.6 4.9 %collective-permute-start.4 = (bf16[64,4096]{1,0:T(8,128)(2,1)S(1)}, bf16[64,4096]{1,0:T(8,128)(2,1)S(1)}, u32[]{:S(2)}, u32[]{:S(2)}) collective-permute-start(bf16[64,4096]{1,0:T(8,128)(2,1)S(1)} %slice.17), channel_id=1, source_target_pairs={{0,6},{2,0},{4,2},{6,4},{1,7},{3,1},{5,3},{7,5},{8,14},{10,8},{12,... | collective-permute-start | bytes 1572872 | tf_op jit(solution)/shard_map/ppermute | solution.py:265
  65.7 1.8 multiply_sine_fusion
  67.4 4.8 %collective-permute-done.3.refs_2_.refs_3_ = bf16[64,4096]{1,0:T(8,128)(2,1)S(1)} collective-permute-done((bf16[64,4096]{1,0:T(8,128)(2,1)S(1)}, bf16[64,4096]{1,0:T(8,128)(2,1)S(1)}, u32[]{:S(2)}, u32[]{:S(2)}) %collective-permute-start.3) | collective-permute-done | bytes 524320 | tf_op jit(solution)/shard_map/ppermute | solution.py:264
  72.3 0.8 copy-done.1
  73.1 0.8 collective-permute-done.4.refs_3_.refs_4_
  73.9 0.8 copy-done.3
  74.7 1.9 %collective-permute-start.5 = (bf16[32,128,128]{2,1,0:T(8,128)(2,1)}, bf16[32,128,128]{2,1,0:T(8,128)(2,1)}, u32[]{:S(2)}, u32[]{:S(2)}) collective-permute-start(bf16[32,128,128]{2,1,0:T(8,128)(2,1)} %bitcast.8.refs_5_), channel_id=1, source_target_pairs={{0,1},{1,0},{2,3},{3,2},{4,5},{5,4},{6,7},{7,6},{8,9},{9,8},{10,11... | collective-permute-start | bytes 3145736 | tf_op jit(solution)/shard_map/ppermute | solution.py:283
  76.7 1.0 copy-done.2
  77.7 1.0 copy-done.4
  78.7 2.5 %shard_map.55.refs_7_ = f32[512,128]{1,0:T(8,128)S(1)} custom-call(bf16[128,4096]{1,0:T(8,128)(2,1)S(1)} %bitcast.39, bf16[128,4096]{1,0:T(8,128)(2,1)S(1)} %collective-permute-done.1.refs_1_.refs_2_, bf16[64,4096]{1,0:T(8,128)(2,1)S(1)} %copy-done.2, bf16[64,4096]{1,0:T(8,128)(2,1)S(1)} %copy-done.4, ...), custom_call_target="tpu_custom_call" | custom-call | flops 536870912 | bytes 5242880 | tf_op jit(solution)/shard_map/pallas_call | solution.py:121
  81.3 2.7 %shard_map.56 = bf16[4,2,128,128]{3,2,1,0:T(8,128)(2,1)S(1)} custom-call(s32[2]{0:T(128)S(1)} %pad_add_fusion.1.refs_0_, bf16[128,4096]{1,0:T(8,128)(2,1)S(1)} %bitcast.40, bf16[128,4096]{1,0:T(8,128)(2,1)S(1)} %collective-permute-done.1.refs_1_.refs_2_, bf16[64,4096]{1,0:T(8,128)(2,1)S(1)} %copy-done.2, bf16[64,4096]{1,0:T(8,128)(2,1)S(1)} %copy-done.4, ...), custom_call_target="tpu_custom_call" | custom-call | flops 536870912 | bytes 5242880 | tf_op jit(solution)/shard_map/pallas_call | solution.py:147
  84.0 11.9 %all_to_all.35 = bf16[4,2,128,128]{3,2,1,0:T(8,128)(2,1)S(1)} all-to-all(bf16[4,2,128,128]{3,2,1,0:T(8,128)(2,1)S(1)} %shard_map.56), channel_id=1, replica_groups=mesh['z1'=2,'z0'=2,'y1'=4,'y0'=2,'zh'=2,'x'=4,'c'=2] {'x'}, dimensions={0} | all-to-all | bytes 524288 | tf_op jit(solution)/shard_map/all_to_all | solution.py:38
  95.8 11.7 %all_to_all.36.refs_0_ = bf16[4,2,128,128]{3,2,1,0:T(8,128)(2,1)S(1)} all-to-all(bf16[4,2,128,128]{3,2,1,0:T(8,128)(2,1)S(1)} %all_to_all.35), channel_id=1, replica_groups=mesh['z1'=2,'z0'=2,'y1'=4,'y0'=2,'zh'=2,'x'=4,'c'=2] {'z1','z0'}, dimensions={0} | all-to-all | bytes 524288 | tf_op jit(solution)/shard_map/all_to_all | solution.py:38
  107.5 3.5 %all-to-all-start.5 = ((bf16[4,128,1024]{2,1,0:T(8,128)(2,1)}), bf16[4,128,1024]{2,1,0:T(8,128)(2,1)S(1)}, u32[]{:S(2)}, u32[]{:S(2)}) async-start(bf16[4,128,1024]{2,1,0:T(8,128)(2,1)} %bitcast.45), calls=%async_computation.5 | async-start | bytes 2097152 | tf_op jit(solution)/shard_map/all_to_all | solution.py:38
  111.0 3.3 %collective-permute-start.6 = (bf16[4,2,128,128]{3,2,1,0:T(8,128)(2,1)S(1)}, bf16[4,2,128,128]{3,2,1,0:T(8,128)(2,1)S(1)}, u32[]{:S(2)}, u32[]{:S(2)}) collective-permute-start(bf16[4,2,128,128]{3,2,1,0:T(8,128)(2,1)S(1)} %all_to_all.36.refs_0_), channel_id=1, source_target_pairs={{0,16},{16,32},{32,48},{48,64},{64,80},{80,96},{96,112},{112,0},{1... | collective-permute-start | bytes 786440 | tf_op jit(solution)/shard_map/ppermute | solution.py:298
  114.3 2.6 %collective-permute-start.10 = (bf16[4,2,128,128]{3,2,1,0:T(8,128)(2,1)S(1)}, bf16[4,2,128,128]{3,2,1,0:T(8,128)(2,1)S(1)}, u32[]{:S(2)}, u32[]{:S(2)}) collective-permute-start(bf16[4,2,128,128]{3,2,1,0:T(8,128)(2,1)S(1)} %all_to_all.36.refs_0_), channel_id=1, source_target_pairs={{0,112},{16,0},{32,16},{48,32},{64,48},{80,64},{96,80},{112,96},{1... | collective-permute-start | bytes 786440 | tf_op jit(solution)/shard_map/ppermute | solution.py:299
  116.9 2.5 %collective-permute-done.6.refs_1_ = bf16[4,2,128,128]{3,2,1,0:T(8,128)(2,1)S(1)} collective-permute-done((bf16[4,2,128,128]{3,2,1,0:T(8,128)(2,1)S(1)}, bf16[4,2,128,128]{3,2,1,0:T(8,128)(2,1)S(1)}, u32[]{:S(2)}, u32[]{:S(2)}) %collective-permute-start.6) | collective-permute-done | bytes 262176 | tf_op jit(solution)/shard_map/ppermute | solution.py:298
  119.4 4.5 %collective-permute-start.7 = (bf16[4,2,128,128]{3,2,1,0:T(8,128)(2,1)S(1)}, bf16[4,2,128,128]{3,2,1,0:T(8,128)(2,1)S(1)}, u32[]{:S(2)}, u32[]{:S(2)}) collective-permute-start(bf16[4,2,128,128]{3,2,1,0:T(8,128)(2,1)S(1)} %collective-permute-done.6.refs_1_), channel_id=1, source_target_pairs={{0,16},{16,32},{32,48},{48,64},{64,80},{80,96},{96,112},{112,0},{1... | collective-permute-start | bytes 786440 | tf_op jit(solution)/shard_map/ppermute | solution.py:298
  123.9 1.9 %collective-permute-start.11 = (bf16[4,2,128,128]{3,2,1,0:T(8,128)(2,1)S(1)}, bf16[4,2,128,128]{3,2,1,0:T(8,128)(2,1)S(1)}, u32[]{:S(2)}, u32[]{:S(2)}) collective-permute-start(bf16[4,2,128,128]{3,2,1,0:T(8,128)(2,1)S(1)} %collective-permute-done.10.refs_0_), channel_id=1, source_target_pairs={{0,112},{16,0},{32,16},{48,32},{64,48},{80,64},{96,80},{112,96},{1... | collective-permute-start | bytes 786440 | tf_op jit(solution)/shard_map/ppermute | solution.py:299
  126.0 1.7 collective-permute-done.7.refs_2_
  127.8 5.6 %collective-permute-start.8 = (bf16[4,2,128,128]{3,2,1,0:T(8,128)(2,1)S(1)}, bf16[4,2,128,128]{3,2,1,0:T(8,128)(2,1)S(1)}, u32[]{:S(2)}, u32[]{:S(2)}) collective-permute-start(bf16[4,2,128,128]{3,2,1,0:T(8,128)(2,1)S(1)} %collective-permute-done.7.refs_2_), channel_id=1, source_target_pairs={{0,16},{16,32},{32,48},{48,64},{64,80},{80,96},{96,112},{112,0},{1... | collective-permute-start | bytes 786440 | tf_op jit(solution)/shard_map/ppermute | solution.py:298
  133.4 1.9 %collective-permute-start.12 = (bf16[4,2,128,128]{3,2,1,0:T(8,128)(2,1)S(1)}, bf16[4,2,128,128]{3,2,1,0:T(8,128)(2,1)S(1)}, u32[]{:S(2)}, u32[]{:S(2)}) collective-permute-start(bf16[4,2,128,128]{3,2,1,0:T(8,128)(2,1)S(1)} %collective-permute-done.11.refs_1_), channel_id=1, source_target_pairs={{0,112},{16,0},{32,16},{48,32},{64,48},{80,64},{96,80},{112,96},{1... | collective-permute-start | bytes 786440 | tf_op jit(solution)/shard_map/ppermute | solution.py:299
  136.2 6.4 %shard_map.58 = (f32[4,128,1024]{2,1,0:T(8,128)S(1)}, f32[4,1,1024]{2,1,0:T(1,128)S(1)}, f32[4,1,1024]{2,1,0:T(1,128)S(1)}) custom-call(s32[5]{0:T(128)S(1)} %pad_add_fusion.where_ref, bf16[4,128,1024]{2,1,0:T(8,128)(2,1)S(1)} %shard_map.57.q_ref, s32[4,1,128]{2,1,0:T(1,128)S(1)} %bitcast.42, bf16[4,2,128,128]{3,2,1,0:T(8,128)(2,1)S(1)} %all_to_all.36.refs_0_, ...), custom_call_target="tpu_custom_call" | custom-call | flops 3221225472 | bytes 4194304 | tf_op jit(solution)/shard_map/pallas_call | solution.py:235
  142.6 4.3 %collective-permute-start.9 = (bf16[4,2,128,128]{3,2,1,0:T(8,128)(2,1)S(1)}, bf16[4,2,128,128]{3,2,1,0:T(8,128)(2,1)S(1)}, u32[]{:S(2)}, u32[]{:S(2)}) collective-permute-start(bf16[4,2,128,128]{3,2,1,0:T(8,128)(2,1)S(1)} %collective-permute-done.8.refs_2_), channel_id=1, source_target_pairs={{0,16},{16,32},{32,48},{48,64},{64,80},{80,96},{96,112},{112,0},{1... | collective-permute-start | bytes 786440 | tf_op jit(solution)/shard_map/ppermute | solution.py:302
  146.9 4.8 %shard_map.59 = (f32[4,128,1024]{2,1,0:T(8,128)S(1)}, f32[4,1,1024]{2,1,0:T(1,128)S(1)}, f32[4,1,1024]{2,1,0:T(1,128)S(1)}) custom-call(s32[5]{0:T(128)S(1)} %pad_add_fusion.where_ref, bf16[4,128,1024]{2,1,0:T(8,128)(2,1)S(1)} %shard_map.57.q_ref, s32[4,1,128]{2,1,0:T(1,128)S(1)} %bitcast.43, bf16[4,2,128,128]{3,2,1,0:T(8,128)(2,1)S(1)} %collective-permute-done.10.refs_0_, ...), custom_call_target="tpu_custom_call" | custom-call | flops 4294967296 | bytes 4194304 | tf_op jit(solution)/shard_map/pallas_call | solution.py:235
  151.7 3.2 %shard_map.60 = bf16[4,128,1024]{2,1,0:T(8,128)(2,1)S(1)} custom-call(s32[5]{0:T(128)S(1)} %pad_add_fusion.where_ref, bf16[4,128,1024]{2,1,0:T(8,128)(2,1)S(1)} %shard_map.57.q_ref, s32[4,1,128]{2,1,0:T(1,128)S(1)} %bitcast.44, bf16[4,2,128,128]{3,2,1,0:T(8,128)(2,1)S(1)} %collective-permute-done.9.refs_0_, f32[4,128,1024]{2,1,0:T(8,128)S(1)} %get-tuple-element.50.refs_1_, ...), custom_call_target="tpu_custom_call" | custom-call | flops 1073741824 | bytes 4194304 | tf_op jit(solution)/shard_map/pallas_call | solution.py:235
  154.9 27.6 %all_to_all.37 = bf16[4,128,1024]{2,1,0:T(8,128)(2,1)S(1)} all-to-all(bf16[4,128,1024]{2,1,0:T(8,128)(2,1)S(1)} %shard_map.60), channel_id=1, replica_groups=mesh['z1'=2,'z0'=2,'y1'=4,'y0'=2,'zh'=2,'x'=4,'c'=2] {'z1','z0'}, dimensions={0} | all-to-all | bytes 2097152 | tf_op jit(solution)/shard_map/all_to_all | solution.py:38
  183.2 1.3 copy.23
  (52 shorter events, 3.8 us)
Async XLA Ops:
  0.0 7.5 %copy-start = (bf16[1,128,4096]{2,1,0:T(8,128)(2,1)S(1)}, bf16[1,128,4096]{2,1,0:T(8,128)(2,1)}, u32[]{:S(2)}) copy-start(bf16[1,128,4096]{2,1,0:T(8,128)(2,1)} %param.5) | copy-start | bytes 3145732
  3.2 13.0 %all-to-all-start = ((bf16[8,160,128]{2,1,0:T(8,128)(2,1)}), bf16[8,160,128]{2,1,0:T(8,128)(2,1)S(1)}, u32[]{:S(2)}, u32[]{:S(2)}) async-start(bf16[8,160,128]{2,1,0:T(8,128)(2,1)} %bitcast.4), calls=%async_computation | async-start | bytes 655360 | tf_op jit(solution)/shard_map/all_to_all | solution.py:38
  7.5 41.3 %collective-permute-start.1 = (bf16[128,4096]{1,0:T(8,128)(2,1)S(1)}, bf16[128,4096]{1,0:T(8,128)(2,1)S(1)}, u32[]{:S(2)}, u32[]{:S(2)}) collective-permute-start(bf16[128,4096]{1,0:T(8,128)(2,1)S(1)} %bitcast.37), channel_id=1, source_target_pairs={{0,2},{2,4},{4,6},{6,0},{1,3},{3,5},{5,7},{7,1},{8,10},{10,12},{12... | collective-permute-start | bytes 3145736 | tf_op jit(solution)/shard_map/ppermute | solution.py:259
  11.4 37.3 %collective-permute-start.2 = (bf16[128,4096]{1,0:T(8,128)(2,1)S(1)}, bf16[128,4096]{1,0:T(8,128)(2,1)S(1)}, u32[]{:S(2)}, u32[]{:S(2)}) collective-permute-start(bf16[128,4096]{1,0:T(8,128)(2,1)S(1)} %bitcast.38), channel_id=1, source_target_pairs={{0,6},{2,0},{4,2},{6,4},{1,7},{3,1},{5,3},{7,5},{8,14},{10,8},{12,... | collective-permute-start | bytes 3145736 | tf_op jit(solution)/shard_map/ppermute | solution.py:260
  16.2 28.7 %copy-start.7 = (bf16[8,160,128]{2,1,0:T(8,128)(2,1)}, bf16[8,160,128]{2,1,0:T(8,128)(2,1)S(1)}, u32[]{:S(2)}) copy-start(bf16[8,160,128]{2,1,0:T(8,128)(2,1)S(1)} %all-to-all-done) | copy-start | bytes 983044
  16.2 0.7 copy-start.8
  17.0 12.8 %collective-permute-start = (bf16[128,128]{1,0:T(8,128)(2,1)S(1)}, bf16[128,128]{1,0:T(8,128)(2,1)S(1)}, u32[]{:S(2)}, u32[]{:S(2)}) collective-permute-start(bf16[128,128]{1,0:T(8,128)(2,1)S(1)} %dynamic-slice_bitcast_fusion), channel_id=1, source_target_pairs={{0,8},{8,0},{1,9},{9,1},{2,10},{10,2},{3,11},{11,3},{4,12},{12,4},... | collective-permute-start | bytes 98312 | tf_op jit(solution)/shard_map/ppermute | solution.py:256
  31.3 17.5 %all-to-all-start.1 = ((bf16[8,128,128]{2,1,0:T(8,128)(2,1)}), bf16[8,128,128]{2,1,0:T(8,128)(2,1)}, u32[]{:S(2)}, u32[]{:S(2)}) async-start(bf16[8,128,128]{2,1,0:T(8,128)(2,1)} %broadcast_in_dim.36), calls=%async_computation.1 | async-start | bytes 524288 | tf_op jit(solution)/shard_map/all_to_all | solution.py:38
  40.4 4.6 %copy-start.9 = (s32[1,4096]{1,0:T(1,128)S(1)}, s32[1,4096]{1,0:T(1,128)}, u32[]{:S(2)}) copy-start(s32[1,4096]{1,0:T(1,128)} %param.8) | copy-start | bytes 49156
  50.8 23.8 %all-to-all-start.2 = ((bf16[4,1024,128]{2,1,0:T(8,128)(2,1)}), bf16[4,1024,128]{2,1,0:T(8,128)(2,1)}, u32[]{:S(2)}, u32[]{:S(2)}) async-start(bf16[4,1024,128]{2,1,0:T(8,128)(2,1)} %broadcast_in_dim.37), calls=%async_computation.2 | async-start | bytes 2097152 | tf_op jit(solution)/shard_map/all_to_all | solution.py:38
  58.4 13.8 %collective-permute-start.3 = (bf16[64,4096]{1,0:T(8,128)(2,1)S(1)}, bf16[64,4096]{1,0:T(8,128)(2,1)S(1)}, u32[]{:S(2)}, u32[]{:S(2)}) collective-permute-start(bf16[64,4096]{1,0:T(8,128)(2,1)S(1)} %slice.16), channel_id=1, source_target_pairs={{0,2},{2,4},{4,6},{6,0},{1,3},{3,5},{5,7},{7,1},{8,10},{10,12},{12... | collective-permute-start | bytes 1572872 | tf_op jit(solution)/shard_map/ppermute | solution.py:264
  60.6 13.2 %collective-permute-start.4 = (bf16[64,4096]{1,0:T(8,128)(2,1)S(1)}, bf16[64,4096]{1,0:T(8,128)(2,1)S(1)}, u32[]{:S(2)}, u32[]{:S(2)}) collective-permute-start(bf16[64,4096]{1,0:T(8,128)(2,1)S(1)} %slice.17), channel_id=1, source_target_pairs={{0,6},{2,0},{4,2},{6,4},{1,7},{3,1},{5,3},{7,5},{8,14},{10,8},{12,... | collective-permute-start | bytes 1572872 | tf_op jit(solution)/shard_map/ppermute | solution.py:265
  72.3 0.8 copy-start.1
  73.9 0.8 copy-start.3
  74.7 6.6 %collective-permute-start.5 = (bf16[32,128,128]{2,1,0:T(8,128)(2,1)}, bf16[32,128,128]{2,1,0:T(8,128)(2,1)}, u32[]{:S(2)}, u32[]{:S(2)}) collective-permute-start(bf16[32,128,128]{2,1,0:T(8,128)(2,1)} %bitcast.8.refs_5_), channel_id=1, source_target_pairs={{0,1},{1,0},{2,3},{3,2},{4,5},{5,4},{6,7},{7,6},{8,9},{9,8},{10,11... | collective-permute-start | bytes 3145736 | tf_op jit(solution)/shard_map/ppermute | solution.py:283
  76.7 1.0 copy-start.2
  77.7 1.0 copy-start.4
  78.7 2.6 %copy-start.5 = (f32[4,128,64]{2,1,0:T(8,128)S(1)}, f32[4,128,64]{2,1,0:T(8,128)}, u32[]{:S(2)}) copy-start(f32[4,128,64]{2,1,0:T(8,128)} %get-tuple-element.36.refs_8_) | copy-start | bytes 393220
  84.0 51.5 %copy-start.6 = (f32[4,64,128]{2,1,0:T(8,128)S(1)}, f32[4,64,128]{2,1,0:T(8,128)}, u32[]{:S(2)}) copy-start(f32[4,64,128]{2,1,0:T(8,128)} %get-tuple-element.40.cos_ref) | copy-start | bytes 393220
  107.5 28.0 %all-to-all-start.5 = ((bf16[4,128,1024]{2,1,0:T(8,128)(2,1)}), bf16[4,128,1024]{2,1,0:T(8,128)(2,1)S(1)}, u32[]{:S(2)}, u32[]{:S(2)}) async-start(bf16[4,128,1024]{2,1,0:T(8,128)(2,1)} %bitcast.45), calls=%async_computation.5 | async-start | bytes 2097152 | tf_op jit(solution)/shard_map/all_to_all | solution.py:38
  111.0 8.4 %collective-permute-start.6 = (bf16[4,2,128,128]{3,2,1,0:T(8,128)(2,1)S(1)}, bf16[4,2,128,128]{3,2,1,0:T(8,128)(2,1)S(1)}, u32[]{:S(2)}, u32[]{:S(2)}) collective-permute-start(bf16[4,2,128,128]{3,2,1,0:T(8,128)(2,1)S(1)} %all_to_all.36.refs_0_), channel_id=1, source_target_pairs={{0,16},{16,32},{32,48},{48,64},{64,80},{80,96},{96,112},{112,0},{1... | collective-permute-start | bytes 786440 | tf_op jit(solution)/shard_map/ppermute | solution.py:298
  114.3 9.6 %collective-permute-start.10 = (bf16[4,2,128,128]{3,2,1,0:T(8,128)(2,1)S(1)}, bf16[4,2,128,128]{3,2,1,0:T(8,128)(2,1)S(1)}, u32[]{:S(2)}, u32[]{:S(2)}) collective-permute-start(bf16[4,2,128,128]{3,2,1,0:T(8,128)(2,1)S(1)} %all_to_all.36.refs_0_), channel_id=1, source_target_pairs={{0,112},{16,0},{32,16},{48,32},{64,48},{80,64},{96,80},{112,96},{1... | collective-permute-start | bytes 786440 | tf_op jit(solution)/shard_map/ppermute | solution.py:299
  119.4 8.3 %collective-permute-start.7 = (bf16[4,2,128,128]{3,2,1,0:T(8,128)(2,1)S(1)}, bf16[4,2,128,128]{3,2,1,0:T(8,128)(2,1)S(1)}, u32[]{:S(2)}, u32[]{:S(2)}) collective-permute-start(bf16[4,2,128,128]{3,2,1,0:T(8,128)(2,1)S(1)} %collective-permute-done.6.refs_1_), channel_id=1, source_target_pairs={{0,16},{16,32},{32,48},{48,64},{64,80},{80,96},{96,112},{112,0},{1... | collective-permute-start | bytes 786440 | tf_op jit(solution)/shard_map/ppermute | solution.py:298
  123.9 9.5 %collective-permute-start.11 = (bf16[4,2,128,128]{3,2,1,0:T(8,128)(2,1)S(1)}, bf16[4,2,128,128]{3,2,1,0:T(8,128)(2,1)S(1)}, u32[]{:S(2)}, u32[]{:S(2)}) collective-permute-start(bf16[4,2,128,128]{3,2,1,0:T(8,128)(2,1)S(1)} %collective-permute-done.10.refs_0_), channel_id=1, source_target_pairs={{0,112},{16,0},{32,16},{48,32},{64,48},{80,64},{96,80},{112,96},{1... | collective-permute-start | bytes 786440 | tf_op jit(solution)/shard_map/ppermute | solution.py:299
  127.8 14.8 %collective-permute-start.8 = (bf16[4,2,128,128]{3,2,1,0:T(8,128)(2,1)S(1)}, bf16[4,2,128,128]{3,2,1,0:T(8,128)(2,1)S(1)}, u32[]{:S(2)}, u32[]{:S(2)}) collective-permute-start(bf16[4,2,128,128]{3,2,1,0:T(8,128)(2,1)S(1)} %collective-permute-done.7.refs_2_), channel_id=1, source_target_pairs={{0,16},{16,32},{32,48},{48,64},{64,80},{80,96},{96,112},{112,0},{1... | collective-permute-start | bytes 786440 | tf_op jit(solution)/shard_map/ppermute | solution.py:298
  133.4 13.5 %collective-permute-start.12 = (bf16[4,2,128,128]{3,2,1,0:T(8,128)(2,1)S(1)}, bf16[4,2,128,128]{3,2,1,0:T(8,128)(2,1)S(1)}, u32[]{:S(2)}, u32[]{:S(2)}) collective-permute-start(bf16[4,2,128,128]{3,2,1,0:T(8,128)(2,1)S(1)} %collective-permute-done.11.refs_1_), channel_id=1, source_target_pairs={{0,112},{16,0},{32,16},{48,32},{64,48},{80,64},{96,80},{112,96},{1... | collective-permute-start | bytes 786440 | tf_op jit(solution)/shard_map/ppermute | solution.py:299
  142.6 9.2 %collective-permute-start.9 = (bf16[4,2,128,128]{3,2,1,0:T(8,128)(2,1)S(1)}, bf16[4,2,128,128]{3,2,1,0:T(8,128)(2,1)S(1)}, u32[]{:S(2)}, u32[]{:S(2)}) collective-permute-start(bf16[4,2,128,128]{3,2,1,0:T(8,128)(2,1)S(1)} %collective-permute-done.8.refs_2_), channel_id=1, source_target_pairs={{0,16},{16,32},{32,48},{48,64},{64,80},{80,96},{96,112},{112,0},{1... | collective-permute-start | bytes 786440 | tf_op jit(solution)/shard_map/ppermute | solution.py:302

commit v12 on v11

--- a/solution.py
+++ b/solution.py
@@ -241,6 +241,31 @@
     )(where, q, start, *[kv[shift] for shift in shifts], *given)
 
 
+def lay_out_kernel(heads_ref, out_ref, done):
+    width = GROUP * HEAD_DIM
+    copies = [
+        pltpu.make_async_copy(
+            heads_ref.at[j], out_ref.at[:, pl.ds(j * width, width)], done.at[j]
+        )
+        for j in range(KV_HEADS)
+    ]
+    for copy in copies:
+        copy.start()
+    for copy in copies:
+        copy.wait()
+
+
+def lay_out(heads):
+    return pl.pallas_call(
+        lay_out_kernel,
+        out_shape=jax.ShapeDtypeStruct((BLOCK, HEADS * HEAD_DIM), jnp.bfloat16),
+        in_specs=[VMEM],
+        out_specs=pl.BlockSpec(memory_space=pl.ANY),
+        scratch_shapes=[pltpu.SemaphoreType.DMA((KV_HEADS,))],
+        compiler_params=pltpu.CompilerParams(vmem_limit_bytes=32 * 2**20),
+    )(heads)
+
+
 def on_device(hidden, queries, weight_copies, segment_ids, owner):
     y, z = lax.axis_index(Y), lax.axis_index(Z)
     x, c, zh = lax.axis_index("x"), lax.axis_index("c"), lax.axis_index("zh")
@@ -267,8 +292,6 @@
     blocks = segment_row.reshape(4, 8, BLOCK)
     start = starts_of(segment_row, pick(blocks, y, 1).reshape(-1)).reshape(4, BLOCK)
     token = (jnp.arange(4)[:, None] * 8 + y) * BLOCK + jnp.arange(BLOCK)[None]
-    q_angles = jnp.swapaxes(angles_of(token - start), 1, 2)
-    q_turns = (jnp.cos(q_angles), jnp.sin(q_angles))
     split = queries[0].reshape(BLOCK, 4, GROUP * HEAD_DIM).transpose(1, 0, 2)
 
     rows_along = rows_along.astype(jnp.int32)
@@ -277,9 +300,11 @@
     k_angles = angles_of((z * 8 + y) * BLOCK + jnp.arange(BLOCK)[None] - start_along)
     k_turns = (jnp.cos(k_angles), jnp.sin(k_angles))
 
-    mine, far_low, far_high, start, q_turns, split, k_turns = lax.optimization_barrier(
-        (mine, far_low, far_high, start, q_turns, split, k_turns)
-    )
+    mine, far_low, far_high, start, split, k_turns = lax.optimization_barrier(
+        (mine, far_low, far_high, start, split, k_turns)
+    )
+    q_angles = jnp.swapaxes(angles_of(token - start), 1, 2)
+    q_turns = (jnp.cos(q_angles), jnp.sin(q_angles))
     other = lax.ppermute(mine, "c", ring(2, 1))
     rows = [own, left, far_low, far_high, right]
     first = project_first(rows, mine)
@@ -303,7 +328,7 @@
     state = attend(((-1, -2), (3,), (-3,)), where, q_turned, start, kv, state)
     mixed = attend(((4,),), where, q_turned, start, kv, state, closing=True)
     back = exchange(mixed, Z)
-    return back.transpose(1, 0, 2).reshape(1, BLOCK, HEADS * HEAD_DIM)
+    return lay_out(back)[None]
 
 
 def solution(mesh):

time: 187 us -> 185 us (0.989)
  the two profiles are of different devices: /device:TPU:56 before, /device:TPU:8 now
where the time goes in v12:
time: 185 us; the launch traced here: 184 us
  starting transfers between devices  68 us (37%)
  blocking collectives  49.7 us (27%)
  Pallas kernels  23.5 us (13%)
  waiting for transfers between devices  22 us (12%)
  local copies, waits for them, and re-layouts  14.2 us (8%)
  other arithmetic  4.97 us (3%)
    all_to_all x3, blocking collectives, exchange(): return lax.all_to_all(value, axes, split_axis=0, concat_axis=0, tiled=True)  49.7 us
    all_to_all x4, starting transfers between devices, exchange(): return lax.all_to_all(value, axes, split_axis=0, concat_axis=0, tiled=True)  20.7 us
    pallas_call x3, Pallas kernels, attend(): call(functools.partial(attend_kernel, tiles, state is None, closing), out...  16.7 us
    ppermute x1, starting transfers between devices, on_device(): lax.ppermute(piece, 'zh', ring(2, 1))  10.9 us
    ppermute x3, starting transfers between devices, on_device(): kv[-step] = lax.ppermute(kv[1 - step], Y, ring(8, -1))  10.4 us
    all_to_all x4, waiting for transfers between devices, exchange(): return lax.all_to_all(value, axes, split_axis=0, concat_axis=0, tiled=True)  9.38 us
    ppermute x3, starting transfers between devices, on_device(): kv[step] = lax.ppermute(kv[step - 1], Y, ring(8, 1))  8.02 us
    unnamed x19, local copies, waits for them, and re-layouts  7.83 us
  transfers between devices with their start and end apart: 17, of which 9 were waited for; matrix products, arithmetic and copies ran while one was open for 5% of the time, Pallas kernels for 9%

profile of v12, /device:TPU:8, one launch (start us, length us, event | category | flops | bytes accessed | tf_op | source)
XLA Modules:
  0.0 183.5 jit_solution(4824518851345434252)
XLA Ops:
  0.0 0.9 convert_reduce_fusion.2
  1.0 1.1 copy.13
  2.3 0.9 copy.15
  3.2 4.3 %all-to-all-start = ((bf16[8,160,128]{2,1,0:T(8,128)(2,1)}), bf16[8,160,128]{2,1,0:T(8,128)(2,1)S(1)}, u32[]{:S(2)}, u32[]{:S(2)}) async-start(bf16[8,160,128]{2,1,0:T(8,128)(2,1)} %bitcast.4), calls=%async_computation | async-start | bytes 655360 | tf_op jit(solution)/shard_map/all_to_all | solution.py:38
  7.5 3.9 %collective-permute-start.1 = (bf16[128,4096]{1,0:T(8,128)(2,1)S(1)}, bf16[128,4096]{1,0:T(8,128)(2,1)S(1)}, u32[]{:S(2)}, u32[]{:S(2)}) collective-permute-start(bf16[128,4096]{1,0:T(8,128)(2,1)S(1)} %bitcast.35), channel_id=1, source_target_pairs={{0,2},{2,4},{4,6},{6,0},{1,3},{3,5},{5,7},{7,1},{8,10},{10,12},{12... | collective-permute-start | bytes 3145736 | tf_op jit(solution)/shard_map/ppermute | solution.py:284
  11.4 3.1 %collective-permute-start.2 = (bf16[128,4096]{1,0:T(8,128)(2,1)S(1)}, bf16[128,4096]{1,0:T(8,128)(2,1)S(1)}, u32[]{:S(2)}, u32[]{:S(2)}) collective-permute-start(bf16[128,4096]{1,0:T(8,128)(2,1)S(1)} %bitcast.36), channel_id=1, source_target_pairs={{0,6},{2,0},{4,2},{6,4},{1,7},{3,1},{5,3},{7,5},{8,14},{10,8},{12,... | collective-permute-start | bytes 3145736 | tf_op jit(solution)/shard_map/ppermute | solution.py:285
  15.3 1.0 all-to-all-done
  16.3 0.7 copy-done.6
  16.9 10.9 %collective-permute-start = (bf16[128,128]{1,0:T(8,128)(2,1)S(1)}, bf16[128,128]{1,0:T(8,128)(2,1)S(1)}, u32[]{:S(2)}, u32[]{:S(2)}) collective-permute-start(bf16[128,128]{1,0:T(8,128)(2,1)S(1)} %dynamic-slice_bitcast_fusion), channel_id=1, source_target_pairs={{0,8},{8,0},{1,9},{9,1},{2,10},{10,2},{3,11},{11,3},{4,12},{12,4},... | collective-permute-start | bytes 98312 | tf_op jit(solution)/shard_map/ppermute | solution.py:281
  27.9 1.9 %collective-permute-done = bf16[128,128]{1,0:T(8,128)(2,1)S(1)} collective-permute-done((bf16[128,128]{1,0:T(8,128)(2,1)S(1)}, bf16[128,128]{1,0:T(8,128)(2,1)S(1)}, u32[]{:S(2)}, u32[]{:S(2)}) %collective-permute-start) | collective-permute-done | bytes 32800 | tf_op jit(solution)/shard_map/ppermute | solution.py:281
  29.8 0.8 broadcast_select_fusion
  30.5 0.7 broadcast_in_dim.38
  31.3 8.3 %all-to-all-start.1 = ((bf16[8,128,128]{2,1,0:T(8,128)(2,1)}), bf16[8,128,128]{2,1,0:T(8,128)(2,1)}, u32[]{:S(2)}, u32[]{:S(2)}) async-start(bf16[8,128,128]{2,1,0:T(8,128)(2,1)} %broadcast_in_dim.38), calls=%async_computation.1 | async-start | bytes 524288 | tf_op jit(solution)/shard_map/all_to_all | solution.py:38
  39.6 2.3 %copy.16 = bf16[1,128,4096]{1,2,0:T(8,128)(2,1)} copy(bf16[1,128,4096]{2,1,0:T(8,128)(2,1)} %param.6) | data formatting | bytes 2097152 | tf_op args[1]
  41.9 2.3 %copy.17 = bf16[128,4,1024]{2,0,1:T(8,128)(2,1)} copy(bf16[128,4,1024]{0,2,1:T(8,128)(2,1)} %bitcast.45) | data formatting | bytes 2097152 | tf_op jit(solution)/shard_map/reshape;squeeze | solution.py:295
  44.1 7.4 %all-to-all-done.1 = bf16[8,128,128]{2,1,0:T(8,128)(2,1)} async-done(((bf16[8,128,128]{2,1,0:T(8,128)(2,1)}), bf16[8,128,128]{2,1,0:T(8,128)(2,1)}, u32[]{:S(2)}, u32[]{:S(2)}) %all-to-all-start.1) | async-done | bytes 262176 | tf_op jit(solution)/shard_map/all_to_all | solution.py:38
  51.6 2.1 %broadcast_in_dim.39 = bf16[4,1024,128]{2,1,0:T(8,128)(2,1)} broadcast(bf16[1024,128]{1,0:T(8,128)(2,1)} %bitcast.6), dimensions={1,2} | broadcast | bytes 1310720 | tf_op jit(solution)/shard_map/broadcast_in_dim | solution.py:42
  53.6 4.6 %all-to-all-start.2 = ((bf16[4,1024,128]{2,1,0:T(8,128)(2,1)}), bf16[4,1024,128]{2,1,0:T(8,128)(2,1)}, u32[]{:S(2)}, u32[]{:S(2)}) async-start(bf16[4,1024,128]{2,1,0:T(8,128)(2,1)} %broadcast_in_dim.39), calls=%async_computation.2 | async-start | bytes 2097152 | tf_op jit(solution)/shard_map/all_to_all | solution.py:38
  59.0 2.2 %collective-permute-start.3 = (bf16[64,4096]{1,0:T(8,128)(2,1)S(1)}, bf16[64,4096]{1,0:T(8,128)(2,1)S(1)}, u32[]{:S(2)}, u32[]{:S(2)}) collective-permute-start(bf16[64,4096]{1,0:T(8,128)(2,1)S(1)} %slice.16), channel_id=1, source_target_pairs={{0,2},{2,4},{4,6},{6,0},{1,3},{3,5},{5,7},{7,1},{8,10},{10,12},{12... | collective-permute-start | bytes 1572872 | tf_op jit(solution)/shard_map/ppermute | solution.py:289
  61.3 4.9 %collective-permute-start.4 = (bf16[64,4096]{1,0:T(8,128)(2,1)S(1)}, bf16[64,4096]{1,0:T(8,128)(2,1)S(1)}, u32[]{:S(2)}, u32[]{:S(2)}) collective-permute-start(bf16[64,4096]{1,0:T(8,128)(2,1)S(1)} %slice.17), channel_id=1, source_target_pairs={{0,6},{2,0},{4,2},{6,4},{1,7},{3,1},{5,3},{7,5},{8,14},{10,8},{12,... | collective-permute-start | bytes 1572872 | tf_op jit(solution)/shard_map/ppermute | solution.py:290
  66.3 1.8 multiply_sine_fusion
  68.0 4.2 %collective-permute-done.3.refs_2_.refs_3_ = bf16[64,4096]{1,0:T(8,128)(2,1)S(1)} collective-permute-done((bf16[64,4096]{1,0:T(8,128)(2,1)S(1)}, bf16[64,4096]{1,0:T(8,128)(2,1)S(1)}, u32[]{:S(2)}, u32[]{:S(2)}) %collective-permute-start.3) | collective-permute-done | bytes 524320 | tf_op jit(solution)/shard_map/ppermute | solution.py:289
  72.2 0.8 copy-done.1
  73.5 0.8 copy-done.3
  74.3 1.9 %collective-permute-start.5 = (bf16[32,128,128]{2,1,0:T(8,128)(2,1)}, bf16[32,128,128]{2,1,0:T(8,128)(2,1)}, u32[]{:S(2)}, u32[]{:S(2)}) collective-permute-start(bf16[32,128,128]{2,1,0:T(8,128)(2,1)} %bitcast.8.refs_5_), channel_id=1, source_target_pairs={{0,1},{1,0},{2,3},{3,2},{4,5},{5,4},{6,7},{7,6},{8,9},{9,8},{10,11... | collective-permute-start | bytes 3145736 | tf_op jit(solution)/shard_map/ppermute | solution.py:308
  76.3 1.0 copy-done.2
  77.3 1.0 copy-done.4
  78.3 2.5 %shard_map.55.refs_7_ = f32[512,128]{1,0:T(8,128)S(1)} custom-call(bf16[128,4096]{1,0:T(8,128)(2,1)S(1)} %bitcast.37, bf16[128,4096]{1,0:T(8,128)(2,1)S(1)} %collective-permute-done.1.refs_1_.refs_2_, bf16[64,4096]{1,0:T(8,128)(2,1)S(1)} %copy-done.2, bf16[64,4096]{1,0:T(8,128)(2,1)S(1)} %copy-done.4, ...), custom_call_target="tpu_custom_call" | custom-call | flops 536870912 | bytes 5242880 | tf_op jit(solution)/shard_map/pallas_call | solution.py:121
  80.9 2.6 %shard_map.56 = bf16[4,2,128,128]{3,2,1,0:T(8,128)(2,1)S(1)} custom-call(s32[2]{0:T(128)S(1)} %pad_add_fusion.1.refs_0_, bf16[128,4096]{1,0:T(8,128)(2,1)S(1)} %bitcast.38, bf16[128,4096]{1,0:T(8,128)(2,1)S(1)} %collective-permute-done.1.refs_1_.refs_2_, bf16[64,4096]{1,0:T(8,128)(2,1)S(1)} %copy-done.2, bf16[64,4096]{1,0:T(8,128)(2,1)S(1)} %copy-done.4, ...), custom_call_target="tpu_custom_call" | custom-call | flops 536870912 | bytes 5242880 | tf_op jit(solution)/shard_map/pallas_call | solution.py:147
  83.5 12.1 %all_to_all.35 = bf16[4,2,128,128]{3,2,1,0:T(8,128)(2,1)S(1)} all-to-all(bf16[4,2,128,128]{3,2,1,0:T(8,128)(2,1)S(1)} %shard_map.56), channel_id=1, replica_groups=mesh['z1'=2,'z0'=2,'y1'=4,'y0'=2,'zh'=2,'x'=4,'c'=2] {'x'}, dimensions={0} | all-to-all | bytes 524288 | tf_op jit(solution)/shard_map/all_to_all | solution.py:38
  95.6 11.3 %all_to_all.36.refs_0_ = bf16[4,2,128,128]{3,2,1,0:T(8,128)(2,1)S(1)} all-to-all(bf16[4,2,128,128]{3,2,1,0:T(8,128)(2,1)S(1)} %all_to_all.35), channel_id=1, replica_groups=mesh['z1'=2,'z0'=2,'y1'=4,'y0'=2,'zh'=2,'x'=4,'c'=2] {'z1','z0'}, dimensions={0} | all-to-all | bytes 524288 | tf_op jit(solution)/shard_map/all_to_all | solution.py:38
  106.9 3.5 %all-to-all-start.5 = ((bf16[4,128,1024]{2,1,0:T(8,128)(2,1)}), bf16[4,128,1024]{2,1,0:T(8,128)(2,1)S(1)}, u32[]{:S(2)}, u32[]{:S(2)}) async-start(bf16[4,128,1024]{2,1,0:T(8,128)(2,1)} %bitcast.44), calls=%async_computation.5 | async-start | bytes 2097152 | tf_op jit(solution)/shard_map/all_to_all | solution.py:38
  110.5 2.7 %collective-permute-start.6 = (bf16[4,2,128,128]{3,2,1,0:T(8,128)(2,1)S(1)}, bf16[4,2,128,128]{3,2,1,0:T(8,128)(2,1)S(1)}, u32[]{:S(2)}, u32[]{:S(2)}) collective-permute-start(bf16[4,2,128,128]{3,2,1,0:T(8,128)(2,1)S(1)} %all_to_all.36.refs_0_), channel_id=1, source_target_pairs={{0,16},{16,32},{32,48},{48,64},{64,80},{80,96},{96,112},{112,0},{1... | collective-permute-start | bytes 786440 | tf_op jit(solution)/shard_map/ppermute | solution.py:323
  113.1 3.2 %collective-permute-start.10 = (bf16[4,2,128,128]{3,2,1,0:T(8,128)(2,1)S(1)}, bf16[4,2,128,128]{3,2,1,0:T(8,128)(2,1)S(1)}, u32[]{:S(2)}, u32[]{:S(2)}) collective-permute-start(bf16[4,2,128,128]{3,2,1,0:T(8,128)(2,1)S(1)} %all_to_all.36.refs_0_), channel_id=1, source_target_pairs={{0,112},{16,0},{32,16},{48,32},{64,48},{80,64},{96,80},{112,96},{1... | collective-permute-start | bytes 786440 | tf_op jit(solution)/shard_map/ppermute | solution.py:324
  116.5 2.3 %collective-permute-done.6.refs_1_ = bf16[4,2,128,128]{3,2,1,0:T(8,128)(2,1)S(1)} collective-permute-done((bf16[4,2,128,128]{3,2,1,0:T(8,128)(2,1)S(1)}, bf16[4,2,128,128]{3,2,1,0:T(8,128)(2,1)S(1)}, u32[]{:S(2)}, u32[]{:S(2)}) %collective-permute-start.6) | collective-permute-done | bytes 262176 | tf_op jit(solution)/shard_map/ppermute | solution.py:323
  118.9 2.7 %collective-permute-start.7 = (bf16[4,2,128,128]{3,2,1,0:T(8,128)(2,1)S(1)}, bf16[4,2,128,128]{3,2,1,0:T(8,128)(2,1)S(1)}, u32[]{:S(2)}, u32[]{:S(2)}) collective-permute-start(bf16[4,2,128,128]{3,2,1,0:T(8,128)(2,1)S(1)} %collective-permute-done.6.refs_1_), channel_id=1, source_target_pairs={{0,16},{16,32},{32,48},{48,64},{64,80},{80,96},{96,112},{112,0},{1... | collective-permute-start | bytes 786440 | tf_op jit(solution)/shard_map/ppermute | solution.py:323
  121.5 3.2 %collective-permute-start.11 = (bf16[4,2,128,128]{3,2,1,0:T(8,128)(2,1)S(1)}, bf16[4,2,128,128]{3,2,1,0:T(8,128)(2,1)S(1)}, u32[]{:S(2)}, u32[]{:S(2)}) collective-permute-start(bf16[4,2,128,128]{3,2,1,0:T(8,128)(2,1)S(1)} %collective-permute-done.10.refs_0_), channel_id=1, source_target_pairs={{0,112},{16,0},{32,16},{48,32},{64,48},{80,64},{96,80},{112,96},{1... | collective-permute-start | bytes 786440 | tf_op jit(solution)/shard_map/ppermute | solution.py:324
  125.3 1.8 collective-permute-done.7.refs_2_
  127.1 2.7 %collective-permute-start.8 = (bf16[4,2,128,128]{3,2,1,0:T(8,128)(2,1)S(1)}, bf16[4,2,128,128]{3,2,1,0:T(8,128)(2,1)S(1)}, u32[]{:S(2)}, u32[]{:S(2)}) collective-permute-start(bf16[4,2,128,128]{3,2,1,0:T(8,128)(2,1)S(1)} %collective-permute-done.7.refs_2_), channel_id=1, source_target_pairs={{0,16},{16,32},{32,48},{48,64},{64,80},{80,96},{96,112},{112,0},{1... | collective-permute-start | bytes 786440 | tf_op jit(solution)/shard_map/ppermute | solution.py:323
  129.8 4.1 %collective-permute-start.12 = (bf16[4,2,128,128]{3,2,1,0:T(8,128)(2,1)S(1)}, bf16[4,2,128,128]{3,2,1,0:T(8,128)(2,1)S(1)}, u32[]{:S(2)}, u32[]{:S(2)}) collective-permute-start(bf16[4,2,128,128]{3,2,1,0:T(8,128)(2,1)S(1)} %collective-permute-done.11.refs_1_), channel_id=1, source_target_pairs={{0,112},{16,0},{32,16},{48,32},{64,48},{80,64},{96,80},{112,96},{1... | collective-permute-start | bytes 786440 | tf_op jit(solution)/shard_map/ppermute | solution.py:324
  133.9 1.0 all-to-all-done.5.q_ref
  135.6 8.3 %shard_map.58 = (f32[4,128,1024]{2,1,0:T(8,128)S(1)}, f32[4,1,1024]{2,1,0:T(1,128)S(1)}, f32[4,1,1024]{2,1,0:T(1,128)S(1)}) custom-call(s32[5]{0:T(128)S(1)} %pad_add_fusion.where_ref, bf16[4,128,1024]{2,1,0:T(8,128)(2,1)S(1)} %shard_map.57.q_ref, s32[4,1,128]{2,1,0:T(1,128)S(1)} %bitcast.41, bf16[4,2,128,128]{3,2,1,0:T(8,128)(2,1)S(1)} %all_to_all.36.refs_0_, ...), custom_call_target="tpu_custom_call" | custom-call | flops 3221225472 | bytes 4194304 | tf_op jit(solution)/shard_map/pallas_call | solution.py:235
  143.9 1.9 %collective-permute-start.9 = (bf16[4,2,128,128]{3,2,1,0:T(8,128)(2,1)S(1)}, bf16[4,2,128,128]{3,2,1,0:T(8,128)(2,1)S(1)}, u32[]{:S(2)}, u32[]{:S(2)}) collective-permute-start(bf16[4,2,128,128]{3,2,1,0:T(8,128)(2,1)S(1)} %collective-permute-done.8.refs_2_), channel_id=1, source_target_pairs={{0,16},{16,32},{32,48},{48,64},{64,80},{80,96},{96,112},{112,0},{1... | collective-permute-start | bytes 786440 | tf_op jit(solution)/shard_map/ppermute | solution.py:327
  145.9 5.2 %shard_map.59 = (f32[4,128,1024]{2,1,0:T(8,128)S(1)}, f32[4,1,1024]{2,1,0:T(1,128)S(1)}, f32[4,1,1024]{2,1,0:T(1,128)S(1)}) custom-call(s32[5]{0:T(128)S(1)} %pad_add_fusion.where_ref, bf16[4,128,1024]{2,1,0:T(8,128)(2,1)S(1)} %shard_map.57.q_ref, s32[4,1,128]{2,1,0:T(1,128)S(1)} %bitcast.42, bf16[4,2,128,128]{3,2,1,0:T(8,128)(2,1)S(1)} %collective-permute-done.10.refs_0_, ...), custom_call_target="tpu_custom_call" | custom-call | flops 4294967296 | bytes 4194304 | tf_op jit(solution)/shard_map/pallas_call | solution.py:235
  151.1 2.0 %collective-permute-done.9.refs_0_ = bf16[4,2,128,128]{3,2,1,0:T(8,128)(2,1)S(1)} collective-permute-done((bf16[4,2,128,128]{3,2,1,0:T(8,128)(2,1)S(1)}, bf16[4,2,128,128]{3,2,1,0:T(8,128)(2,1)S(1)}, u32[]{:S(2)}, u32[]{:S(2)}) %collective-permute-start.9) | collective-permute-done | bytes 262176 | tf_op jit(solution)/shard_map/ppermute | solution.py:327
  153.1 3.2 %shard_map.60 = bf16[4,128,1024]{2,1,0:T(8,128)(2,1)S(1)} custom-call(s32[5]{0:T(128)S(1)} %pad_add_fusion.where_ref, bf16[4,128,1024]{2,1,0:T(8,128)(2,1)S(1)} %shard_map.57.q_ref, s32[4,1,128]{2,1,0:T(1,128)S(1)} %bitcast.43, bf16[4,2,128,128]{3,2,1,0:T(8,128)(2,1)S(1)} %collective-permute-done.9.refs_0_, f32[4,128,1024]{2,1,0:T(8,128)S(1)} %get-tuple-element.46.refs_1_, ...), custom_call_target="tpu_custom_call" | custom-call | flops 1073741824 | bytes 4194304 | tf_op jit(solution)/shard_map/pallas_call | solution.py:235
  156.3 26.3 %all_to_all.37.heads_ref = bf16[4,128,1024]{2,1,0:T(8,128)(2,1)S(1)} all-to-all(bf16[4,128,1024]{2,1,0:T(8,128)(2,1)S(1)} %shard_map.60), channel_id=1, replica_groups=mesh['z1'=2,'z0'=2,'y1'=4,'y0'=2,'zh'=2,'x'=4,'c'=2] {'z1','z0'}, dimensions={0} | all-to-all | bytes 2097152 | tf_op jit(solution)/shard_map/all_to_all | solution.py:38
  182.5 1.0 shard_map.61
  (47 shorter events, 3.2 us)
Async XLA Ops:
  0.0 7.5 %copy-start = (bf16[1,128,4096]{2,1,0:T(8,128)(2,1)S(1)}, bf16[1,128,4096]{2,1,0:T(8,128)(2,1)}, u32[]{:S(2)}) copy-start(bf16[1,128,4096]{2,1,0:T(8,128)(2,1)} %param.5) | copy-start | bytes 3145732
  3.2 13.0 %all-to-all-start = ((bf16[8,160,128]{2,1,0:T(8,128)(2,1)}), bf16[8,160,128]{2,1,0:T(8,128)(2,1)S(1)}, u32[]{:S(2)}, u32[]{:S(2)}) async-start(bf16[8,160,128]{2,1,0:T(8,128)(2,1)} %bitcast.4), calls=%async_computation | async-start | bytes 655360 | tf_op jit(solution)/shard_map/all_to_all | solution.py:38
  7.5 44.1 %collective-permute-start.1 = (bf16[128,4096]{1,0:T(8,128)(2,1)S(1)}, bf16[128,4096]{1,0:T(8,128)(2,1)S(1)}, u32[]{:S(2)}, u32[]{:S(2)}) collective-permute-start(bf16[128,4096]{1,0:T(8,128)(2,1)S(1)} %bitcast.35), channel_id=1, source_target_pairs={{0,2},{2,4},{4,6},{6,0},{1,3},{3,5},{5,7},{7,1},{8,10},{10,12},{12... | collective-permute-start | bytes 3145736 | tf_op jit(solution)/shard_map/ppermute | solution.py:284
  11.4 40.1 %collective-permute-start.2 = (bf16[128,4096]{1,0:T(8,128)(2,1)S(1)}, bf16[128,4096]{1,0:T(8,128)(2,1)S(1)}, u32[]{:S(2)}, u32[]{:S(2)}) collective-permute-start(bf16[128,4096]{1,0:T(8,128)(2,1)S(1)} %bitcast.36), channel_id=1, source_target_pairs={{0,6},{2,0},{4,2},{6,4},{1,7},{3,1},{5,3},{7,5},{8,14},{10,8},{12,... | collective-permute-start | bytes 3145736 | tf_op jit(solution)/shard_map/ppermute | solution.py:285
  16.2 0.7 copy-start.6
  16.9 12.8 %collective-permute-start = (bf16[128,128]{1,0:T(8,128)(2,1)S(1)}, bf16[128,128]{1,0:T(8,128)(2,1)S(1)}, u32[]{:S(2)}, u32[]{:S(2)}) collective-permute-start(bf16[128,128]{1,0:T(8,128)(2,1)S(1)} %dynamic-slice_bitcast_fusion), channel_id=1, source_target_pairs={{0,8},{8,0},{1,9},{9,1},{2,10},{10,2},{3,11},{11,3},{4,12},{12,4},... | collective-permute-start | bytes 98312 | tf_op jit(solution)/shard_map/ppermute | solution.py:281
  31.3 20.3 %all-to-all-start.1 = ((bf16[8,128,128]{2,1,0:T(8,128)(2,1)}), bf16[8,128,128]{2,1,0:T(8,128)(2,1)}, u32[]{:S(2)}, u32[]{:S(2)}) async-start(bf16[8,128,128]{2,1,0:T(8,128)(2,1)} %broadcast_in_dim.38), calls=%async_computation.1 | async-start | bytes 524288 | tf_op jit(solution)/shard_map/all_to_all | solution.py:38
  44.1 14.1 %copy-start.7 = (s32[1,4096]{1,0:T(1,128)S(1)}, s32[1,4096]{1,0:T(1,128)}, u32[]{:S(2)}) copy-start(s32[1,4096]{1,0:T(1,128)} %param.8) | copy-start | bytes 49156
  53.6 20.6 %all-to-all-start.2 = ((bf16[4,1024,128]{2,1,0:T(8,128)(2,1)}), bf16[4,1024,128]{2,1,0:T(8,128)(2,1)}, u32[]{:S(2)}, u32[]{:S(2)}) async-start(bf16[4,1024,128]{2,1,0:T(8,128)(2,1)} %broadcast_in_dim.39), calls=%async_computation.2 | async-start | bytes 2097152 | tf_op jit(solution)/shard_map/all_to_all | solution.py:38
  59.0 13.2 %collective-permute-start.3 = (bf16[64,4096]{1,0:T(8,128)(2,1)S(1)}, bf16[64,4096]{1,0:T(8,128)(2,1)S(1)}, u32[]{:S(2)}, u32[]{:S(2)}) collective-permute-start(bf16[64,4096]{1,0:T(8,128)(2,1)S(1)} %slice.16), channel_id=1, source_target_pairs={{0,2},{2,4},{4,6},{6,0},{1,3},{3,5},{5,7},{7,1},{8,10},{10,12},{12... | collective-permute-start | bytes 1572872 | tf_op jit(solution)/shard_map/ppermute | solution.py:289
  61.3 12.2 %collective-permute-start.4 = (bf16[64,4096]{1,0:T(8,128)(2,1)S(1)}, bf16[64,4096]{1,0:T(8,128)(2,1)S(1)}, u32[]{:S(2)}, u32[]{:S(2)}) collective-permute-start(bf16[64,4096]{1,0:T(8,128)(2,1)S(1)} %slice.17), channel_id=1, source_target_pairs={{0,6},{2,0},{4,2},{6,4},{1,7},{3,1},{5,3},{7,5},{8,14},{10,8},{12,... | collective-permute-start | bytes 1572872 | tf_op jit(solution)/shard_map/ppermute | solution.py:290
  72.2 0.8 copy-start.1
  73.4 0.8 copy-start.3
  74.3 6.6 %collective-permute-start.5 = (bf16[32,128,128]{2,1,0:T(8,128)(2,1)}, bf16[32,128,128]{2,1,0:T(8,128)(2,1)}, u32[]{:S(2)}, u32[]{:S(2)}) collective-permute-start(bf16[32,128,128]{2,1,0:T(8,128)(2,1)} %bitcast.8.refs_5_), channel_id=1, source_target_pairs={{0,1},{1,0},{2,3},{3,2},{4,5},{5,4},{6,7},{7,6},{8,9},{9,8},{10,11... | collective-permute-start | bytes 3145736 | tf_op jit(solution)/shard_map/ppermute | solution.py:308
  76.3 1.0 copy-start.2
  77.3 1.0 copy-start.4
  78.3 2.5 %copy-start.5 = (f32[4,128,64]{2,1,0:T(8,128)S(1)}, f32[4,128,64]{2,1,0:T(8,128)}, u32[]{:S(2)}) copy-start(f32[4,128,64]{2,1,0:T(8,128)} %get-tuple-element.34.refs_8_) | copy-start | bytes 393220
  106.9 28.0 %all-to-all-start.5 = ((bf16[4,128,1024]{2,1,0:T(8,128)(2,1)}), bf16[4,128,1024]{2,1,0:T(8,128)(2,1)S(1)}, u32[]{:S(2)}, u32[]{:S(2)}) async-start(bf16[4,128,1024]{2,1,0:T(8,128)(2,1)} %bitcast.44), calls=%async_computation.5 | async-start | bytes 2097152 | tf_op jit(solution)/shard_map/all_to_all | solution.py:38
  110.5 8.4 %collective-permute-start.6 = (bf16[4,2,128,128]{3,2,1,0:T(8,128)(2,1)S(1)}, bf16[4,2,128,128]{3,2,1,0:T(8,128)(2,1)S(1)}, u32[]{:S(2)}, u32[]{:S(2)}) collective-permute-start(bf16[4,2,128,128]{3,2,1,0:T(8,128)(2,1)S(1)} %all_to_all.36.refs_0_), channel_id=1, source_target_pairs={{0,16},{16,32},{32,48},{48,64},{64,80},{80,96},{96,112},{112,0},{1... | collective-permute-start | bytes 786440 | tf_op jit(solution)/shard_map/ppermute | solution.py:323
  113.1 8.4 %collective-permute-start.10 = (bf16[4,2,128,128]{3,2,1,0:T(8,128)(2,1)S(1)}, bf16[4,2,128,128]{3,2,1,0:T(8,128)(2,1)S(1)}, u32[]{:S(2)}, u32[]{:S(2)}) collective-permute-start(bf16[4,2,128,128]{3,2,1,0:T(8,128)(2,1)S(1)} %all_to_all.36.refs_0_), channel_id=1, source_target_pairs={{0,112},{16,0},{32,16},{48,32},{64,48},{80,64},{96,80},{112,96},{1... | collective-permute-start | bytes 786440 | tf_op jit(solution)/shard_map/ppermute | solution.py:324
  118.9 8.3 %collective-permute-start.7 = (bf16[4,2,128,128]{3,2,1,0:T(8,128)(2,1)S(1)}, bf16[4,2,128,128]{3,2,1,0:T(8,128)(2,1)S(1)}, u32[]{:S(2)}, u32[]{:S(2)}) collective-permute-start(bf16[4,2,128,128]{3,2,1,0:T(8,128)(2,1)S(1)} %collective-permute-done.6.refs_1_), channel_id=1, source_target_pairs={{0,16},{16,32},{32,48},{48,64},{64,80},{80,96},{96,112},{112,0},{1... | collective-permute-start | bytes 786440 | tf_op jit(solution)/shard_map/ppermute | solution.py:323
  121.5 8.3 %collective-permute-start.11 = (bf16[4,2,128,128]{3,2,1,0:T(8,128)(2,1)S(1)}, bf16[4,2,128,128]{3,2,1,0:T(8,128)(2,1)S(1)}, u32[]{:S(2)}, u32[]{:S(2)}) collective-permute-start(bf16[4,2,128,128]{3,2,1,0:T(8,128)(2,1)S(1)} %collective-permute-done.10.refs_0_), channel_id=1, source_target_pairs={{0,112},{16,0},{32,16},{48,32},{64,48},{80,64},{96,80},{112,96},{1... | collective-permute-start | bytes 786440 | tf_op jit(solution)/shard_map/ppermute | solution.py:324
  127.1 16.8 %collective-permute-start.8 = (bf16[4,2,128,128]{3,2,1,0:T(8,128)(2,1)S(1)}, bf16[4,2,128,128]{3,2,1,0:T(8,128)(2,1)S(1)}, u32[]{:S(2)}, u32[]{:S(2)}) collective-permute-start(bf16[4,2,128,128]{3,2,1,0:T(8,128)(2,1)S(1)} %collective-permute-done.7.refs_2_), channel_id=1, source_target_pairs={{0,16},{16,32},{32,48},{48,64},{64,80},{80,96},{96,112},{112,0},{1... | collective-permute-start | bytes 786440 | tf_op jit(solution)/shard_map/ppermute | solution.py:323
  129.8 16.1 %collective-permute-start.12 = (bf16[4,2,128,128]{3,2,1,0:T(8,128)(2,1)S(1)}, bf16[4,2,128,128]{3,2,1,0:T(8,128)(2,1)S(1)}, u32[]{:S(2)}, u32[]{:S(2)}) collective-permute-start(bf16[4,2,128,128]{3,2,1,0:T(8,128)(2,1)S(1)} %collective-permute-done.11.refs_1_), channel_id=1, source_target_pairs={{0,112},{16,0},{32,16},{48,32},{64,48},{80,64},{96,80},{112,96},{1... | collective-permute-start | bytes 786440 | tf_op jit(solution)/shard_map/ppermute | solution.py:324
  143.9 9.2 %collective-permute-start.9 = (bf16[4,2,128,128]{3,2,1,0:T(8,128)(2,1)S(1)}, bf16[4,2,128,128]{3,2,1,0:T(8,128)(2,1)S(1)}, u32[]{:S(2)}, u32[]{:S(2)}) collective-permute-start(bf16[4,2,128,128]{3,2,1,0:T(8,128)(2,1)S(1)} %collective-permute-done.8.refs_2_), channel_id=1, source_target_pairs={{0,16},{16,32},{32,48},{48,64},{64,80},{80,96},{96,112},{112,0},{1... | collective-permute-start | bytes 786440 | tf_op jit(solution)/shard_map/ppermute | solution.py:327

commit v13 on v12

--- a/solution.py
+++ b/solution.py
@@ -241,6 +241,16 @@
     )(where, q, start, *[kv[shift] for shift in shifts], *given)
 
 
+def repeat_kernel(rows_ref, out_ref):
+    for j in range(4):
+        out_ref[j] = rows_ref[...]
+
+
+def repeat_rows(rows):
+    out = jax.ShapeDtypeStruct((4,) + rows.shape, rows.dtype)
+    return call(repeat_kernel, out, [VMEM], (0, 5 * 2**18))(rows)
+
+
 def lay_out_kernel(heads_ref, out_ref, done):
     width = GROUP * HEAD_DIM
     copies = [
@@ -285,7 +295,7 @@
     right = lax.ppermute(own, "x", ring(4, -1))
     part = spread(piece, ("z1", "y1"), 8).reshape(8 * BLOCK, 128)
     part, left, right = lax.optimization_barrier((part, left, right))
-    mine = spread(part, ("z0", "y0"), 4).reshape(32, BLOCK, 128)
+    mine = exchange(repeat_rows(part), ("z0", "y0")).reshape(32, BLOCK, 128)
     far_low = lax.ppermute(left[:64], "x", ring(4, 1))
     far_high = lax.ppermute(right[64:], "x", ring(4, -1))
 

time: 185 us -> 186 us (level)
  the two profiles are of different devices: /device:TPU:8 before, /device:TPU:56 now
where the time goes in v13:
time: 186 us; the launch traced here: 183 us
  starting transfers between devices  73.3 us (39%)
  blocking collectives  52.7 us (28%)
  Pallas kernels  20.7 us (11%)
  waiting for transfers between devices  17.3 us (9%)
  local copies, waits for them, and re-layouts  13.1 us (7%)
  other arithmetic  4.96 us (3%)
    all_to_all x3, blocking collectives, exchange(): return lax.all_to_all(value, axes, split_axis=0, concat_axis=0, tiled=True)  52.7 us
    all_to_all x4, starting transfers between devices, exchange(): return lax.all_to_all(value, axes, split_axis=0, concat_axis=0, tiled=True)  21.9 us
    ppermute x3, starting transfers between devices, on_device(): kv[step] = lax.ppermute(kv[step - 1], Y, ring(8, 1))  13.3 us
    pallas_call x3, Pallas kernels, attend(): call(functools.partial(attend_kernel, tiles, state is None, closing), out...  12.8 us
    ppermute x1, starting transfers between devices, on_device(): lax.ppermute(piece, 'zh', ring(2, 1))  10.9 us
    unnamed x21, local copies, waits for them, and re-layouts  7.86 us
    ppermute x3, starting transfers between devices, on_device(): kv[-step] = lax.ppermute(kv[1 - step], Y, ring(8, -1))  6.41 us
    ppermute x1, starting transfers between devices, on_device(): far_high = lax.ppermute(right[64:], 'x', ring(4, -1))  4.89 us
  transfers between devices with their start and end apart: 17, of which 9 were waited for; matrix products, arithmetic and copies ran while one was open for 6% of the time, Pallas kernels for 7%

profile of v13, /device:TPU:56, one launch (start us, length us, event | category | flops | bytes accessed | tf_op | source)
XLA Modules:
  0.0 183.1 jit_solution(10725405519678339467)
XLA Ops:
  0.0 0.9 convert_reduce_fusion.2
  1.0 1.1 copy.13
  2.3 0.9 copy.15
  3.2 4.3 %all-to-all-start = ((bf16[8,160,128]{2,1,0:T(8,128)(2,1)}), bf16[8,160,128]{2,1,0:T(8,128)(2,1)S(1)}, u32[]{:S(2)}, u32[]{:S(2)}) async-start(bf16[8,160,128]{2,1,0:T(8,128)(2,1)} %bitcast.4), calls=%async_computation | async-start | bytes 655360 | tf_op jit(solution)/shard_map/all_to_all | solution.py:38
  7.5 3.9 %collective-permute-start.1 = (bf16[128,4096]{1,0:T(8,128)(2,1)S(1)}, bf16[128,4096]{1,0:T(8,128)(2,1)S(1)}, u32[]{:S(2)}, u32[]{:S(2)}) collective-permute-start(bf16[128,4096]{1,0:T(8,128)(2,1)S(1)} %bitcast.35), channel_id=1, source_target_pairs={{0,2},{2,4},{4,6},{6,0},{1,3},{3,5},{5,7},{7,1},{8,10},{10,12},{12... | collective-permute-start | bytes 3145736 | tf_op jit(solution)/shard_map/ppermute | solution.py:294
  11.4 3.1 %collective-permute-start.2 = (bf16[128,4096]{1,0:T(8,128)(2,1)S(1)}, bf16[128,4096]{1,0:T(8,128)(2,1)S(1)}, u32[]{:S(2)}, u32[]{:S(2)}) collective-permute-start(bf16[128,4096]{1,0:T(8,128)(2,1)S(1)} %bitcast.36), channel_id=1, source_target_pairs={{0,6},{2,0},{4,2},{6,4},{1,7},{3,1},{5,3},{7,5},{8,14},{10,8},{12,... | collective-permute-start | bytes 3145736 | tf_op jit(solution)/shard_map/ppermute | solution.py:295
  15.3 1.0 all-to-all-done
  17.0 10.9 %collective-permute-start = (bf16[128,128]{1,0:T(8,128)(2,1)S(1)}, bf16[128,128]{1,0:T(8,128)(2,1)S(1)}, u32[]{:S(2)}, u32[]{:S(2)}) collective-permute-start(bf16[128,128]{1,0:T(8,128)(2,1)S(1)} %dynamic-slice_bitcast_fusion), channel_id=1, source_target_pairs={{0,8},{8,0},{1,9},{9,1},{2,10},{10,2},{3,11},{11,3},{4,12},{12,4},... | collective-permute-start | bytes 98312 | tf_op jit(solution)/shard_map/ppermute | solution.py:291
  27.9 1.9 %collective-permute-done = bf16[128,128]{1,0:T(8,128)(2,1)S(1)} collective-permute-done((bf16[128,128]{1,0:T(8,128)(2,1)S(1)}, bf16[128,128]{1,0:T(8,128)(2,1)S(1)}, u32[]{:S(2)}, u32[]{:S(2)}) %collective-permute-start) | collective-permute-done | bytes 32800 | tf_op jit(solution)/shard_map/ppermute | solution.py:291
  29.8 0.8 broadcast_select_fusion
  30.6 0.8 broadcast_in_dim.36
  31.3 9.1 %all-to-all-start.1 = ((bf16[8,128,128]{2,1,0:T(8,128)(2,1)}), bf16[8,128,128]{2,1,0:T(8,128)(2,1)S(1)}, u32[]{:S(2)}, u32[]{:S(2)}) async-start(bf16[8,128,128]{2,1,0:T(8,128)(2,1)} %broadcast_in_dim.36), calls=%async_computation.1 | async-start | bytes 524288 | tf_op jit(solution)/shard_map/all_to_all | solution.py:38
  40.4 2.3 %copy.16 = bf16[1,128,4096]{1,2,0:T(8,128)(2,1)} copy(bf16[1,128,4096]{2,1,0:T(8,128)(2,1)} %param.6) | data formatting | bytes 2097152 | tf_op args[1]
  42.7 2.3 %copy.17 = bf16[128,4,1024]{2,0,1:T(8,128)(2,1)} copy(bf16[128,4,1024]{0,2,1:T(8,128)(2,1)} %bitcast.46) | data formatting | bytes 2097152 | tf_op jit(solution)/shard_map/reshape;squeeze | solution.py:305
  45.0 3.7 %all-to-all-done.1 = bf16[8,128,128]{2,1,0:T(8,128)(2,1)S(1)} async-done(((bf16[8,128,128]{2,1,0:T(8,128)(2,1)}), bf16[8,128,128]{2,1,0:T(8,128)(2,1)S(1)}, u32[]{:S(2)}, u32[]{:S(2)}) %all-to-all-start.1) | async-done | bytes 262176 | tf_op jit(solution)/shard_map/all_to_all | solution.py:38
  48.7 1.1 shard_map.55
  49.8 5.0 %all-to-all-start.2 = ((bf16[4,1024,128]{2,1,0:T(8,128)(2,1)}), bf16[4,1024,128]{2,1,0:T(8,128)(2,1)}, u32[]{:S(2)}, u32[]{:S(2)}) async-start(bf16[4,1024,128]{2,1,0:T(8,128)(2,1)} %shard_map.55), calls=%async_computation.2 | async-start | bytes 2097152 | tf_op jit(solution)/shard_map/all_to_all | solution.py:38
  55.1 0.8 slice.21
  56.4 2.2 %collective-permute-start.3 = (bf16[64,4096]{1,0:T(8,128)(2,1)S(1)}, bf16[64,4096]{1,0:T(8,128)(2,1)S(1)}, u32[]{:S(2)}, u32[]{:S(2)}) collective-permute-start(bf16[64,4096]{1,0:T(8,128)(2,1)S(1)} %slice.16), channel_id=1, source_target_pairs={{0,2},{2,4},{4,6},{6,0},{1,3},{3,5},{5,7},{7,1},{8,10},{10,12},{12... | collective-permute-start | bytes 1572872 | tf_op jit(solution)/shard_map/ppermute | solution.py:299
  58.6 4.9 %collective-permute-start.4 = (bf16[64,4096]{1,0:T(8,128)(2,1)S(1)}, bf16[64,4096]{1,0:T(8,128)(2,1)S(1)}, u32[]{:S(2)}, u32[]{:S(2)}) collective-permute-start(bf16[64,4096]{1,0:T(8,128)(2,1)S(1)} %slice.17), channel_id=1, source_target_pairs={{0,6},{2,0},{4,2},{6,4},{1,7},{3,1},{5,3},{7,5},{8,14},{10,8},{12,... | collective-permute-start | bytes 1572872 | tf_op jit(solution)/shard_map/ppermute | solution.py:300
  63.6 1.8 multiply_sine_fusion
  65.4 4.9 %collective-permute-done.3.refs_2_.refs_3_ = bf16[64,4096]{1,0:T(8,128)(2,1)S(1)} collective-permute-done((bf16[64,4096]{1,0:T(8,128)(2,1)S(1)}, bf16[64,4096]{1,0:T(8,128)(2,1)S(1)}, u32[]{:S(2)}, u32[]{:S(2)}) %collective-permute-start.3) | collective-permute-done | bytes 524320 | tf_op jit(solution)/shard_map/ppermute | solution.py:299
  70.2 0.8 copy-done.1
  71.0 0.8 collective-permute-done.4.refs_3_.refs_4_
  71.8 0.8 copy-done.3
  72.6 1.9 %collective-permute-start.5 = (bf16[32,128,128]{2,1,0:T(8,128)(2,1)}, bf16[32,128,128]{2,1,0:T(8,128)(2,1)}, u32[]{:S(2)}, u32[]{:S(2)}) collective-permute-start(bf16[32,128,128]{2,1,0:T(8,128)(2,1)} %bitcast.8.refs_5_), channel_id=1, source_target_pairs={{0,1},{1,0},{2,3},{3,2},{4,5},{5,4},{6,7},{7,6},{8,9},{9,8},{10,11... | collective-permute-start | bytes 3145736 | tf_op jit(solution)/shard_map/ppermute | solution.py:318
  74.6 1.0 copy-done.2
  75.7 1.0 copy-done.4
  76.7 2.5 %shard_map.56.refs_7_ = f32[512,128]{1,0:T(8,128)S(1)} custom-call(bf16[128,4096]{1,0:T(8,128)(2,1)S(1)} %bitcast.37, bf16[128,4096]{1,0:T(8,128)(2,1)S(1)} %collective-permute-done.1.refs_1_.refs_2_, bf16[64,4096]{1,0:T(8,128)(2,1)S(1)} %copy-done.2, bf16[64,4096]{1,0:T(8,128)(2,1)S(1)} %copy-done.4, ...), custom_call_target="tpu_custom_call" | custom-call | flops 536870912 | bytes 5242880 | tf_op jit(solution)/shard_map/pallas_call | solution.py:121
  79.3 2.7 %shard_map.57 = bf16[4,2,128,128]{3,2,1,0:T(8,128)(2,1)S(1)} custom-call(s32[2]{0:T(128)S(1)} %pad_add_fusion.1.refs_0_, bf16[128,4096]{1,0:T(8,128)(2,1)S(1)} %bitcast.38, bf16[128,4096]{1,0:T(8,128)(2,1)S(1)} %collective-permute-done.1.refs_1_.refs_2_, bf16[64,4096]{1,0:T(8,128)(2,1)S(1)} %copy-done.2, bf16[64,4096]{1,0:T(8,128)(2,1)S(1)} %copy-done.4, ...), custom_call_target="tpu_custom_call" | custom-call | flops 536870912 | bytes 5242880 | tf_op jit(solution)/shard_map/pallas_call | solution.py:147
  82.0 11.7 %all_to_all.35 = bf16[4,2,128,128]{3,2,1,0:T(8,128)(2,1)S(1)} all-to-all(bf16[4,2,128,128]{3,2,1,0:T(8,128)(2,1)S(1)} %shard_map.57), channel_id=1, replica_groups=mesh['z1'=2,'z0'=2,'y1'=4,'y0'=2,'zh'=2,'x'=4,'c'=2] {'x'}, dimensions={0} | all-to-all | bytes 524288 | tf_op jit(solution)/shard_map/all_to_all | solution.py:38
  93.7 11.7 %all_to_all.36.refs_0_ = bf16[4,2,128,128]{3,2,1,0:T(8,128)(2,1)S(1)} all-to-all(bf16[4,2,128,128]{3,2,1,0:T(8,128)(2,1)S(1)} %all_to_all.35), channel_id=1, replica_groups=mesh['z1'=2,'z0'=2,'y1'=4,'y0'=2,'zh'=2,'x'=4,'c'=2] {'z1','z0'}, dimensions={0} | all-to-all | bytes 524288 | tf_op jit(solution)/shard_map/all_to_all | solution.py:38
  105.3 3.5 %all-to-all-start.5 = ((bf16[4,128,1024]{2,1,0:T(8,128)(2,1)}), bf16[4,128,1024]{2,1,0:T(8,128)(2,1)S(1)}, u32[]{:S(2)}, u32[]{:S(2)}) async-start(bf16[4,128,1024]{2,1,0:T(8,128)(2,1)} %bitcast.45), calls=%async_computation.5 | async-start | bytes 2097152 | tf_op jit(solution)/shard_map/all_to_all | solution.py:38
  108.9 3.3 %collective-permute-start.6 = (bf16[4,2,128,128]{3,2,1,0:T(8,128)(2,1)S(1)}, bf16[4,2,128,128]{3,2,1,0:T(8,128)(2,1)S(1)}, u32[]{:S(2)}, u32[]{:S(2)}) collective-permute-start(bf16[4,2,128,128]{3,2,1,0:T(8,128)(2,1)S(1)} %all_to_all.36.refs_0_), channel_id=1, source_target_pairs={{0,16},{16,32},{32,48},{48,64},{64,80},{80,96},{96,112},{112,0},{1... | collective-permute-start | bytes 786440 | tf_op jit(solution)/shard_map/ppermute | solution.py:333
  112.1 2.6 %collective-permute-start.10 = (bf16[4,2,128,128]{3,2,1,0:T(8,128)(2,1)S(1)}, bf16[4,2,128,128]{3,2,1,0:T(8,128)(2,1)S(1)}, u32[]{:S(2)}, u32[]{:S(2)}) collective-permute-start(bf16[4,2,128,128]{3,2,1,0:T(8,128)(2,1)S(1)} %all_to_all.36.refs_0_), channel_id=1, source_target_pairs={{0,112},{16,0},{32,16},{48,32},{64,48},{80,64},{96,80},{112,96},{1... | collective-permute-start | bytes 786440 | tf_op jit(solution)/shard_map/ppermute | solution.py:334
  114.9 2.3 %collective-permute-done.6.refs_1_ = bf16[4,2,128,128]{3,2,1,0:T(8,128)(2,1)S(1)} collective-permute-done((bf16[4,2,128,128]{3,2,1,0:T(8,128)(2,1)S(1)}, bf16[4,2,128,128]{3,2,1,0:T(8,128)(2,1)S(1)}, u32[]{:S(2)}, u32[]{:S(2)}) %collective-permute-start.6) | collective-permute-done | bytes 262176 | tf_op jit(solution)/shard_map/ppermute | solution.py:333
  117.3 4.5 %collective-permute-start.7 = (bf16[4,2,128,128]{3,2,1,0:T(8,128)(2,1)S(1)}, bf16[4,2,128,128]{3,2,1,0:T(8,128)(2,1)S(1)}, u32[]{:S(2)}, u32[]{:S(2)}) collective-permute-start(bf16[4,2,128,128]{3,2,1,0:T(8,128)(2,1)S(1)} %collective-permute-done.6.refs_1_), channel_id=1, source_target_pairs={{0,16},{16,32},{32,48},{48,64},{64,80},{80,96},{96,112},{112,0},{1... | collective-permute-start | bytes 786440 | tf_op jit(solution)/shard_map/ppermute | solution.py:333
  121.7 1.9 %collective-permute-start.11 = (bf16[4,2,128,128]{3,2,1,0:T(8,128)(2,1)S(1)}, bf16[4,2,128,128]{3,2,1,0:T(8,128)(2,1)S(1)}, u32[]{:S(2)}, u32[]{:S(2)}) collective-permute-start(bf16[4,2,128,128]{3,2,1,0:T(8,128)(2,1)S(1)} %collective-permute-done.10.refs_0_), channel_id=1, source_target_pairs={{0,112},{16,0},{32,16},{48,32},{64,48},{80,64},{96,80},{112,96},{1... | collective-permute-start | bytes 786440 | tf_op jit(solution)/shard_map/ppermute | solution.py:334
  124.3 1.3 collective-permute-done.7.refs_2_
  125.6 5.6 %collective-permute-start.8 = (bf16[4,2,128,128]{3,2,1,0:T(8,128)(2,1)S(1)}, bf16[4,2,128,128]{3,2,1,0:T(8,128)(2,1)S(1)}, u32[]{:S(2)}, u32[]{:S(2)}) collective-permute-start(bf16[4,2,128,128]{3,2,1,0:T(8,128)(2,1)S(1)} %collective-permute-done.7.refs_2_), channel_id=1, source_target_pairs={{0,16},{16,32},{32,48},{48,64},{64,80},{80,96},{96,112},{112,0},{1... | collective-permute-start | bytes 786440 | tf_op jit(solution)/shard_map/ppermute | solution.py:333
  131.2 1.9 %collective-permute-start.12 = (bf16[4,2,128,128]{3,2,1,0:T(8,128)(2,1)S(1)}, bf16[4,2,128,128]{3,2,1,0:T(8,128)(2,1)S(1)}, u32[]{:S(2)}, u32[]{:S(2)}) collective-permute-start(bf16[4,2,128,128]{3,2,1,0:T(8,128)(2,1)S(1)} %collective-permute-done.11.refs_1_), channel_id=1, source_target_pairs={{0,112},{16,0},{32,16},{48,32},{64,48},{80,64},{96,80},{112,96},{1... | collective-permute-start | bytes 786440 | tf_op jit(solution)/shard_map/ppermute | solution.py:334
  134.0 6.4 %shard_map.59 = (f32[4,128,1024]{2,1,0:T(8,128)S(1)}, f32[4,1,1024]{2,1,0:T(1,128)S(1)}, f32[4,1,1024]{2,1,0:T(1,128)S(1)}) custom-call(s32[5]{0:T(128)S(1)} %pad_add_fusion.where_ref, bf16[4,128,1024]{2,1,0:T(8,128)(2,1)S(1)} %shard_map.58.q_ref, s32[4,1,128]{2,1,0:T(1,128)S(1)} %bitcast.42, bf16[4,2,128,128]{3,2,1,0:T(8,128)(2,1)S(1)} %all_to_all.36.refs_0_, ...), custom_call_target="tpu_custom_call" | custom-call | flops 3221225472 | bytes 4194304 | tf_op jit(solution)/shard_map/pallas_call | solution.py:235
  140.4 4.7 %collective-permute-start.9 = (bf16[4,2,128,128]{3,2,1,0:T(8,128)(2,1)S(1)}, bf16[4,2,128,128]{3,2,1,0:T(8,128)(2,1)S(1)}, u32[]{:S(2)}, u32[]{:S(2)}) collective-permute-start(bf16[4,2,128,128]{3,2,1,0:T(8,128)(2,1)S(1)} %collective-permute-done.8.refs_2_), channel_id=1, source_target_pairs={{0,16},{16,32},{32,48},{48,64},{64,80},{80,96},{96,112},{112,0},{1... | collective-permute-start | bytes 786440 | tf_op jit(solution)/shard_map/ppermute | solution.py:337
  145.2 4.1 %shard_map.60 = (f32[4,128,1024]{2,1,0:T(8,128)S(1)}, f32[4,1,1024]{2,1,0:T(1,128)S(1)}, f32[4,1,1024]{2,1,0:T(1,128)S(1)}) custom-call(s32[5]{0:T(128)S(1)} %pad_add_fusion.where_ref, bf16[4,128,1024]{2,1,0:T(8,128)(2,1)S(1)} %shard_map.58.q_ref, s32[4,1,128]{2,1,0:T(1,128)S(1)} %bitcast.43, bf16[4,2,128,128]{3,2,1,0:T(8,128)(2,1)S(1)} %collective-permute-done.10.refs_0_, ...), custom_call_target="tpu_custom_call" | custom-call | flops 4294967296 | bytes 4194304 | tf_op jit(solution)/shard_map/pallas_call | solution.py:235
  149.3 1.2 collective-permute-done.9.refs_0_
  150.4 2.3 %shard_map.61 = bf16[4,128,1024]{2,1,0:T(8,128)(2,1)S(1)} custom-call(s32[5]{0:T(128)S(1)} %pad_add_fusion.where_ref, bf16[4,128,1024]{2,1,0:T(8,128)(2,1)S(1)} %shard_map.58.q_ref, s32[4,1,128]{2,1,0:T(1,128)S(1)} %bitcast.44, bf16[4,2,128,128]{3,2,1,0:T(8,128)(2,1)S(1)} %collective-permute-done.9.refs_0_, f32[4,128,1024]{2,1,0:T(8,128)S(1)} %get-tuple-element.46.refs_1_, ...), custom_call_target="tpu_custom_call" | custom-call | flops 1073741824 | bytes 4194304 | tf_op jit(solution)/shard_map/pallas_call | solution.py:235
  152.7 29.4 %all_to_all.37.heads_ref = bf16[4,128,1024]{2,1,0:T(8,128)(2,1)S(1)} all-to-all(bf16[4,128,1024]{2,1,0:T(8,128)(2,1)S(1)} %shard_map.61), channel_id=1, replica_groups=mesh['z1'=2,'z0'=2,'y1'=4,'y0'=2,'zh'=2,'x'=4,'c'=2] {'z1','z0'}, dimensions={0} | all-to-all | bytes 2097152 | tf_op jit(solution)/shard_map/all_to_all | solution.py:38
  182.1 1.0 shard_map.62
  (49 shorter events, 3.7 us)
Async XLA Ops:
  0.0 7.5 %copy-start = (bf16[1,128,4096]{2,1,0:T(8,128)(2,1)S(1)}, bf16[1,128,4096]{2,1,0:T(8,128)(2,1)}, u32[]{:S(2)}) copy-start(bf16[1,128,4096]{2,1,0:T(8,128)(2,1)} %param.5) | copy-start | bytes 3145732
  3.2 13.0 %all-to-all-start = ((bf16[8,160,128]{2,1,0:T(8,128)(2,1)}), bf16[8,160,128]{2,1,0:T(8,128)(2,1)S(1)}, u32[]{:S(2)}, u32[]{:S(2)}) async-start(bf16[8,160,128]{2,1,0:T(8,128)(2,1)} %bitcast.4), calls=%async_computation | async-start | bytes 655360 | tf_op jit(solution)/shard_map/all_to_all | solution.py:38
  7.5 41.2 %collective-permute-start.1 = (bf16[128,4096]{1,0:T(8,128)(2,1)S(1)}, bf16[128,4096]{1,0:T(8,128)(2,1)S(1)}, u32[]{:S(2)}, u32[]{:S(2)}) collective-permute-start(bf16[128,4096]{1,0:T(8,128)(2,1)S(1)} %bitcast.35), channel_id=1, source_target_pairs={{0,2},{2,4},{4,6},{6,0},{1,3},{3,5},{5,7},{7,1},{8,10},{10,12},{12... | collective-permute-start | bytes 3145736 | tf_op jit(solution)/shard_map/ppermute | solution.py:294
  11.4 37.3 %collective-permute-start.2 = (bf16[128,4096]{1,0:T(8,128)(2,1)S(1)}, bf16[128,4096]{1,0:T(8,128)(2,1)S(1)}, u32[]{:S(2)}, u32[]{:S(2)}) collective-permute-start(bf16[128,4096]{1,0:T(8,128)(2,1)S(1)} %bitcast.36), channel_id=1, source_target_pairs={{0,6},{2,0},{4,2},{6,4},{1,7},{3,1},{5,3},{7,5},{8,14},{10,8},{12,... | collective-permute-start | bytes 3145736 | tf_op jit(solution)/shard_map/ppermute | solution.py:295
  16.2 15.1 %copy-start.6 = (bf16[8,160,128]{2,1,0:T(8,128)(2,1)}, bf16[8,160,128]{2,1,0:T(8,128)(2,1)S(1)}, u32[]{:S(2)}) copy-start(bf16[8,160,128]{2,1,0:T(8,128)(2,1)S(1)} %all-to-all-done) | copy-start | bytes 983044
  16.2 0.7 copy-start.7
  17.0 12.8 %collective-permute-start = (bf16[128,128]{1,0:T(8,128)(2,1)S(1)}, bf16[128,128]{1,0:T(8,128)(2,1)S(1)}, u32[]{:S(2)}, u32[]{:S(2)}) collective-permute-start(bf16[128,128]{1,0:T(8,128)(2,1)S(1)} %dynamic-slice_bitcast_fusion), channel_id=1, source_target_pairs={{0,8},{8,0},{1,9},{9,1},{2,10},{10,2},{3,11},{11,3},{4,12},{12,4},... | collective-permute-start | bytes 98312 | tf_op jit(solution)/shard_map/ppermute | solution.py:291
  31.3 17.4 %all-to-all-start.1 = ((bf16[8,128,128]{2,1,0:T(8,128)(2,1)}), bf16[8,128,128]{2,1,0:T(8,128)(2,1)S(1)}, u32[]{:S(2)}, u32[]{:S(2)}) async-start(bf16[8,128,128]{2,1,0:T(8,128)(2,1)} %broadcast_in_dim.36), calls=%async_computation.1 | async-start | bytes 524288 | tf_op jit(solution)/shard_map/all_to_all | solution.py:38
  45.0 9.8 %copy-start.8 = (s32[1,4096]{1,0:T(1,128)S(1)}, s32[1,4096]{1,0:T(1,128)}, u32[]{:S(2)}) copy-start(s32[1,4096]{1,0:T(1,128)} %param.8) | copy-start | bytes 49156
  49.8 22.8 %all-to-all-start.2 = ((bf16[4,1024,128]{2,1,0:T(8,128)(2,1)}), bf16[4,1024,128]{2,1,0:T(8,128)(2,1)}, u32[]{:S(2)}, u32[]{:S(2)}) async-start(bf16[4,1024,128]{2,1,0:T(8,128)(2,1)} %shard_map.55), calls=%async_computation.2 | async-start | bytes 2097152 | tf_op jit(solution)/shard_map/all_to_all | solution.py:38
  56.4 13.8 %collective-permute-start.3 = (bf16[64,4096]{1,0:T(8,128)(2,1)S(1)}, bf16[64,4096]{1,0:T(8,128)(2,1)S(1)}, u32[]{:S(2)}, u32[]{:S(2)}) collective-permute-start(bf16[64,4096]{1,0:T(8,128)(2,1)S(1)} %slice.16), channel_id=1, source_target_pairs={{0,2},{2,4},{4,6},{6,0},{1,3},{3,5},{5,7},{7,1},{8,10},{10,12},{12... | collective-permute-start | bytes 1572872 | tf_op jit(solution)/shard_map/ppermute | solution.py:299
  58.6 13.2 %collective-permute-start.4 = (bf16[64,4096]{1,0:T(8,128)(2,1)S(1)}, bf16[64,4096]{1,0:T(8,128)(2,1)S(1)}, u32[]{:S(2)}, u32[]{:S(2)}) collective-permute-start(bf16[64,4096]{1,0:T(8,128)(2,1)S(1)} %slice.17), channel_id=1, source_target_pairs={{0,6},{2,0},{4,2},{6,4},{1,7},{3,1},{5,3},{7,5},{8,14},{10,8},{12,... | collective-permute-start | bytes 1572872 | tf_op jit(solution)/shard_map/ppermute | solution.py:300
  70.2 0.8 copy-start.1
  71.8 0.8 copy-start.3
  72.6 6.6 %collective-permute-start.5 = (bf16[32,128,128]{2,1,0:T(8,128)(2,1)}, bf16[32,128,128]{2,1,0:T(8,128)(2,1)}, u32[]{:S(2)}, u32[]{:S(2)}) collective-permute-start(bf16[32,128,128]{2,1,0:T(8,128)(2,1)} %bitcast.8.refs_5_), channel_id=1, source_target_pairs={{0,1},{1,0},{2,3},{3,2},{4,5},{5,4},{6,7},{7,6},{8,9},{9,8},{10,11... | collective-permute-start | bytes 3145736 | tf_op jit(solution)/shard_map/ppermute | solution.py:318
  74.6 1.0 copy-start.2
  75.7 1.0 copy-start.4
  76.7 2.6 %copy-start.5 = (f32[4,128,64]{2,1,0:T(8,128)S(1)}, f32[4,128,64]{2,1,0:T(8,128)}, u32[]{:S(2)}) copy-start(f32[4,128,64]{2,1,0:T(8,128)} %get-tuple-element.34.refs_8_) | copy-start | bytes 393220
  105.3 28.0 %all-to-all-start.5 = ((bf16[4,128,1024]{2,1,0:T(8,128)(2,1)}), bf16[4,128,1024]{2,1,0:T(8,128)(2,1)S(1)}, u32[]{:S(2)}, u32[]{:S(2)}) async-start(bf16[4,128,1024]{2,1,0:T(8,128)(2,1)} %bitcast.45), calls=%async_computation.5 | async-start | bytes 2097152 | tf_op jit(solution)/shard_map/all_to_all | solution.py:38
  108.9 8.4 %collective-permute-start.6 = (bf16[4,2,128,128]{3,2,1,0:T(8,128)(2,1)S(1)}, bf16[4,2,128,128]{3,2,1,0:T(8,128)(2,1)S(1)}, u32[]{:S(2)}, u32[]{:S(2)}) collective-permute-start(bf16[4,2,128,128]{3,2,1,0:T(8,128)(2,1)S(1)} %all_to_all.36.refs_0_), channel_id=1, source_target_pairs={{0,16},{16,32},{32,48},{48,64},{64,80},{80,96},{96,112},{112,0},{1... | collective-permute-start | bytes 786440 | tf_op jit(solution)/shard_map/ppermute | solution.py:333
  112.1 9.6 %collective-permute-start.10 = (bf16[4,2,128,128]{3,2,1,0:T(8,128)(2,1)S(1)}, bf16[4,2,128,128]{3,2,1,0:T(8,128)(2,1)S(1)}, u32[]{:S(2)}, u32[]{:S(2)}) collective-permute-start(bf16[4,2,128,128]{3,2,1,0:T(8,128)(2,1)S(1)} %all_to_all.36.refs_0_), channel_id=1, source_target_pairs={{0,112},{16,0},{32,16},{48,32},{64,48},{80,64},{96,80},{112,96},{1... | collective-permute-start | bytes 786440 | tf_op jit(solution)/shard_map/ppermute | solution.py:334
  117.3 8.3 %collective-permute-start.7 = (bf16[4,2,128,128]{3,2,1,0:T(8,128)(2,1)S(1)}, bf16[4,2,128,128]{3,2,1,0:T(8,128)(2,1)S(1)}, u32[]{:S(2)}, u32[]{:S(2)}) collective-permute-start(bf16[4,2,128,128]{3,2,1,0:T(8,128)(2,1)S(1)} %collective-permute-done.6.refs_1_), channel_id=1, source_target_pairs={{0,16},{16,32},{32,48},{48,64},{64,80},{80,96},{96,112},{112,0},{1... | collective-permute-start | bytes 786440 | tf_op jit(solution)/shard_map/ppermute | solution.py:333
  121.7 9.5 %collective-permute-start.11 = (bf16[4,2,128,128]{3,2,1,0:T(8,128)(2,1)S(1)}, bf16[4,2,128,128]{3,2,1,0:T(8,128)(2,1)S(1)}, u32[]{:S(2)}, u32[]{:S(2)}) collective-permute-start(bf16[4,2,128,128]{3,2,1,0:T(8,128)(2,1)S(1)} %collective-permute-done.10.refs_0_), channel_id=1, source_target_pairs={{0,112},{16,0},{32,16},{48,32},{64,48},{80,64},{96,80},{112,96},{1... | collective-permute-start | bytes 786440 | tf_op jit(solution)/shard_map/ppermute | solution.py:334
  125.6 14.8 %collective-permute-start.8 = (bf16[4,2,128,128]{3,2,1,0:T(8,128)(2,1)S(1)}, bf16[4,2,128,128]{3,2,1,0:T(8,128)(2,1)S(1)}, u32[]{:S(2)}, u32[]{:S(2)}) collective-permute-start(bf16[4,2,128,128]{3,2,1,0:T(8,128)(2,1)S(1)} %collective-permute-done.7.refs_2_), channel_id=1, source_target_pairs={{0,16},{16,32},{32,48},{48,64},{64,80},{80,96},{96,112},{112,0},{1... | collective-permute-start | bytes 786440 | tf_op jit(solution)/shard_map/ppermute | solution.py:333
  131.2 13.9 %collective-permute-start.12 = (bf16[4,2,128,128]{3,2,1,0:T(8,128)(2,1)S(1)}, bf16[4,2,128,128]{3,2,1,0:T(8,128)(2,1)S(1)}, u32[]{:S(2)}, u32[]{:S(2)}) collective-permute-start(bf16[4,2,128,128]{3,2,1,0:T(8,128)(2,1)S(1)} %collective-permute-done.11.refs_1_), channel_id=1, source_target_pairs={{0,112},{16,0},{32,16},{48,32},{64,48},{80,64},{96,80},{112,96},{1... | collective-permute-start | bytes 786440 | tf_op jit(solution)/shard_map/ppermute | solution.py:334
  140.4 10.0 %collective-permute-start.9 = (bf16[4,2,128,128]{3,2,1,0:T(8,128)(2,1)S(1)}, bf16[4,2,128,128]{3,2,1,0:T(8,128)(2,1)S(1)}, u32[]{:S(2)}, u32[]{:S(2)}) collective-permute-start(bf16[4,2,128,128]{3,2,1,0:T(8,128)(2,1)S(1)} %collective-permute-done.8.refs_2_), channel_id=1, source_target_pairs={{0,16},{16,32},{32,48},{48,64},{64,80},{80,96},{96,112},{112,0},{1... | collective-permute-start | bytes 786440 | tf_op jit(solution)/shard_map/ppermute | solution.py:337

commit v14 on v13

--- a/solution.py
+++ b/solution.py
@@ -67,7 +67,7 @@
         in_specs=specs,
         out_specs=jax.tree.map(lambda _: VMEM, out_shape),
         scratch_shapes=list(scratch),
-        compiler_params=pltpu.CompilerParams(vmem_limit_bytes=32 * 2**20),
+        compiler_params=pltpu.CompilerParams(vmem_limit_bytes=8 * 2**20),
         cost_estimate=pl.CostEstimate(flops=flops, bytes_accessed=moved, transcendentals=0),
     )
 
@@ -272,7 +272,7 @@
         in_specs=[VMEM],
         out_specs=pl.BlockSpec(memory_space=pl.ANY),
         scratch_shapes=[pltpu.SemaphoreType.DMA((KV_HEADS,))],
-        compiler_params=pltpu.CompilerParams(vmem_limit_bytes=32 * 2**20),
+        compiler_params=pltpu.CompilerParams(vmem_limit_bytes=8 * 2**20),
     )(heads)
 
 

time: 186 us -> 186 us (level)
  the two profiles are of different devices: /device:TPU:56 before, /device:TPU:2 now
where the time goes in v14:
time: 186 us; the launch traced here: 184 us
  starting transfers between devices  70.4 us (38%)
  blocking collectives  52.7 us (28%)
  waiting for transfers between devices  25 us (13%)
  Pallas kernels  16.7 us (9%)
  local copies, waits for them, and re-layouts  13.1 us (7%)
  other arithmetic  4.97 us (3%)
    all_to_all x3, blocking collectives, exchange(): return lax.all_to_all(value, axes, split_axis=0, concat_axis=0, tiled=True)  52.7 us
    all_to_all x4, starting transfers between devices, exchange(): return lax.all_to_all(value, axes, split_axis=0, concat_axis=0, tiled=True)  24.9 us
    ppermute x3, starting transfers between devices, on_device(): kv[-step] = lax.ppermute(kv[1 - step], Y, ring(8, -1))  13.7 us
    pallas_call x3, Pallas kernels, attend(): call(functools.partial(attend_kernel, tiles, state is None, closing), out...  8.85 us
    unnamed x21, local copies, waits for them, and re-layouts  7.86 us
    ppermute x3, starting transfers between devices, on_device(): kv[step] = lax.ppermute(kv[step - 1], Y, ring(8, 1))  7.44 us
    all_to_all x4, waiting for transfers between devices, exchange(): return lax.all_to_all(value, axes, split_axis=0, concat_axis=0, tiled=True)  6.78 us
    ppermute x1, starting transfers between devices, on_device(): lax.ppermute(piece, 'zh', ring(2, 1))  6.46 us
  transfers between devices with their start and end apart: 17, of which 8 were waited for; matrix products, arithmetic and copies ran while one was open for 6% of the time, Pallas kernels for 6%

profile of v14, /device:TPU:2, one launch (start us, length us, event | category | flops | bytes accessed | tf_op | source)
XLA Modules:
  0.0 183.9 jit_solution(13337632975748505989)
XLA Ops:
  0.0 0.9 convert_reduce_fusion.2
  1.0 1.1 copy.13
  2.3 0.9 copy.15
  3.2 9.2 %all-to-all-start = ((bf16[8,160,128]{2,1,0:T(8,128)(2,1)}), bf16[8,160,128]{2,1,0:T(8,128)(2,1)S(1)}, u32[]{:S(2)}, u32[]{:S(2)}) async-start(bf16[8,160,128]{2,1,0:T(8,128)(2,1)} %bitcast.4), calls=%async_computation | async-start | bytes 655360 | tf_op jit(solution)/shard_map/all_to_all | solution.py:38
  12.5 3.4 %collective-permute-start.1 = (bf16[128,4096]{1,0:T(8,128)(2,1)S(1)}, bf16[128,4096]{1,0:T(8,128)(2,1)S(1)}, u32[]{:S(2)}, u32[]{:S(2)}) collective-permute-start(bf16[128,4096]{1,0:T(8,128)(2,1)S(1)} %bitcast.35), channel_id=1, source_target_pairs={{0,2},{2,4},{4,6},{6,0},{1,3},{3,5},{5,7},{7,1},{8,10},{10,12},{12... | collective-permute-start | bytes 3145736 | tf_op jit(solution)/shard_map/ppermute | solution.py:294
  15.8 2.5 %collective-permute-start.2 = (bf16[128,4096]{1,0:T(8,128)(2,1)S(1)}, bf16[128,4096]{1,0:T(8,128)(2,1)S(1)}, u32[]{:S(2)}, u32[]{:S(2)}) collective-permute-start(bf16[128,4096]{1,0:T(8,128)(2,1)S(1)} %bitcast.36), channel_id=1, source_target_pairs={{0,6},{2,0},{4,2},{6,4},{1,7},{3,1},{5,3},{7,5},{8,14},{10,8},{12,... | collective-permute-start | bytes 3145736 | tf_op jit(solution)/shard_map/ppermute | solution.py:295
  19.3 0.7 copy-done.7
  20.0 6.5 %collective-permute-start = (bf16[128,128]{1,0:T(8,128)(2,1)S(1)}, bf16[128,128]{1,0:T(8,128)(2,1)S(1)}, u32[]{:S(2)}, u32[]{:S(2)}) collective-permute-start(bf16[128,128]{1,0:T(8,128)(2,1)S(1)} %dynamic-slice_bitcast_fusion), channel_id=1, source_target_pairs={{0,8},{8,0},{1,9},{9,1},{2,10},{10,2},{3,11},{11,3},{4,12},{12,4},... | collective-permute-start | bytes 98312 | tf_op jit(solution)/shard_map/ppermute | solution.py:291
  26.5 3.2 %collective-permute-done = bf16[128,128]{1,0:T(8,128)(2,1)S(1)} collective-permute-done((bf16[128,128]{1,0:T(8,128)(2,1)S(1)}, bf16[128,128]{1,0:T(8,128)(2,1)S(1)}, u32[]{:S(2)}, u32[]{:S(2)}) %collective-permute-start) | collective-permute-done | bytes 32800 | tf_op jit(solution)/shard_map/ppermute | solution.py:291
  29.7 0.8 broadcast_select_fusion
  30.5 0.8 broadcast_in_dim.36
  31.3 7.9 %all-to-all-start.1 = ((bf16[8,128,128]{2,1,0:T(8,128)(2,1)}), bf16[8,128,128]{2,1,0:T(8,128)(2,1)S(1)}, u32[]{:S(2)}, u32[]{:S(2)}) async-start(bf16[8,128,128]{2,1,0:T(8,128)(2,1)} %broadcast_in_dim.36), calls=%async_computation.1 | async-start | bytes 524288 | tf_op jit(solution)/shard_map/all_to_all | solution.py:38
  39.2 2.3 %copy.16 = bf16[1,128,4096]{1,2,0:T(8,128)(2,1)} copy(bf16[1,128,4096]{2,1,0:T(8,128)(2,1)} %param.6) | data formatting | bytes 2097152 | tf_op args[1]
  41.4 2.3 %copy.17 = bf16[128,4,1024]{2,0,1:T(8,128)(2,1)} copy(bf16[128,4,1024]{0,2,1:T(8,128)(2,1)} %bitcast.46) | data formatting | bytes 2097152 | tf_op jit(solution)/shard_map/reshape;squeeze | solution.py:305
  43.7 6.5 %all-to-all-done.1 = bf16[8,128,128]{2,1,0:T(8,128)(2,1)S(1)} async-done(((bf16[8,128,128]{2,1,0:T(8,128)(2,1)}), bf16[8,128,128]{2,1,0:T(8,128)(2,1)S(1)}, u32[]{:S(2)}, u32[]{:S(2)}) %all-to-all-start.1) | async-done | bytes 262176 | tf_op jit(solution)/shard_map/all_to_all | solution.py:38
  50.2 1.1 shard_map.55
  51.3 4.3 %all-to-all-start.2 = ((bf16[4,1024,128]{2,1,0:T(8,128)(2,1)}), bf16[4,1024,128]{2,1,0:T(8,128)(2,1)}, u32[]{:S(2)}, u32[]{:S(2)}) async-start(bf16[4,1024,128]{2,1,0:T(8,128)(2,1)} %shard_map.55), calls=%async_computation.2 | async-start | bytes 2097152 | tf_op jit(solution)/shard_map/all_to_all | solution.py:38
  55.9 0.8 slice.21
  57.2 3.4 %collective-permute-start.3 = (bf16[64,4096]{1,0:T(8,128)(2,1)S(1)}, bf16[64,4096]{1,0:T(8,128)(2,1)S(1)}, u32[]{:S(2)}, u32[]{:S(2)}) collective-permute-start(bf16[64,4096]{1,0:T(8,128)(2,1)S(1)} %slice.16), channel_id=1, source_target_pairs={{0,2},{2,4},{4,6},{6,0},{1,3},{3,5},{5,7},{7,1},{8,10},{10,12},{12... | collective-permute-start | bytes 1572872 | tf_op jit(solution)/shard_map/ppermute | solution.py:299
  60.6 2.5 %collective-permute-start.4 = (bf16[64,4096]{1,0:T(8,128)(2,1)S(1)}, bf16[64,4096]{1,0:T(8,128)(2,1)S(1)}, u32[]{:S(2)}, u32[]{:S(2)}) collective-permute-start(bf16[64,4096]{1,0:T(8,128)(2,1)S(1)} %slice.17), channel_id=1, source_target_pairs={{0,6},{2,0},{4,2},{6,4},{1,7},{3,1},{5,3},{7,5},{8,14},{10,8},{12,... | collective-permute-start | bytes 1572872 | tf_op jit(solution)/shard_map/ppermute | solution.py:300
  63.2 1.8 multiply_sine_fusion
  65.0 5.0 %collective-permute-done.3.refs_2_.refs_3_ = bf16[64,4096]{1,0:T(8,128)(2,1)S(1)} collective-permute-done((bf16[64,4096]{1,0:T(8,128)(2,1)S(1)}, bf16[64,4096]{1,0:T(8,128)(2,1)S(1)}, u32[]{:S(2)}, u32[]{:S(2)}) %collective-permute-start.3) | collective-permute-done | bytes 524320 | tf_op jit(solution)/shard_map/ppermute | solution.py:299
  70.0 0.8 copy-done.1
  70.7 2.5 %collective-permute-done.4.refs_3_.refs_4_ = bf16[64,4096]{1,0:T(8,128)(2,1)S(1)} collective-permute-done((bf16[64,4096]{1,0:T(8,128)(2,1)S(1)}, bf16[64,4096]{1,0:T(8,128)(2,1)S(1)}, u32[]{:S(2)}, u32[]{:S(2)}) %collective-permute-start.4) | collective-permute-done | bytes 524320 | tf_op jit(solution)/shard_map/ppermute | solution.py:300
  73.2 0.8 copy-done.3
  74.0 1.9 %collective-permute-start.5 = (bf16[32,128,128]{2,1,0:T(8,128)(2,1)}, bf16[32,128,128]{2,1,0:T(8,128)(2,1)}, u32[]{:S(2)}, u32[]{:S(2)}) collective-permute-start(bf16[32,128,128]{2,1,0:T(8,128)(2,1)} %bitcast.8.refs_5_), channel_id=1, source_target_pairs={{0,1},{1,0},{2,3},{3,2},{4,5},{5,4},{6,7},{7,6},{8,9},{9,8},{10,11... | collective-permute-start | bytes 3145736 | tf_op jit(solution)/shard_map/ppermute | solution.py:318
  76.0 1.0 copy-done.2
  77.1 1.0 copy-done.4
  78.1 2.5 %shard_map.56.refs_7_ = f32[512,128]{1,0:T(8,128)S(1)} custom-call(bf16[128,4096]{1,0:T(8,128)(2,1)S(1)} %bitcast.37, bf16[128,4096]{1,0:T(8,128)(2,1)S(1)} %collective-permute-done.1.refs_1_.refs_2_, bf16[64,4096]{1,0:T(8,128)(2,1)S(1)} %copy-done.2, bf16[64,4096]{1,0:T(8,128)(2,1)S(1)} %copy-done.4, ...), custom_call_target="tpu_custom_call" | custom-call | flops 536870912 | bytes 5242880 | tf_op jit(solution)/shard_map/pallas_call | solution.py:121
  80.6 2.6 %shard_map.57 = bf16[4,2,128,128]{3,2,1,0:T(8,128)(2,1)S(1)} custom-call(s32[2]{0:T(128)S(1)} %pad_add_fusion.1.refs_0_, bf16[128,4096]{1,0:T(8,128)(2,1)S(1)} %bitcast.38, bf16[128,4096]{1,0:T(8,128)(2,1)S(1)} %collective-permute-done.1.refs_1_.refs_2_, bf16[64,4096]{1,0:T(8,128)(2,1)S(1)} %copy-done.2, bf16[64,4096]{1,0:T(8,128)(2,1)S(1)} %copy-done.4, ...), custom_call_target="tpu_custom_call" | custom-call | flops 536870912 | bytes 5242880 | tf_op jit(solution)/shard_map/pallas_call | solution.py:147
  83.3 11.1 %all_to_all.35 = bf16[4,2,128,128]{3,2,1,0:T(8,128)(2,1)S(1)} all-to-all(bf16[4,2,128,128]{3,2,1,0:T(8,128)(2,1)S(1)} %shard_map.57), channel_id=1, replica_groups=mesh['z1'=2,'z0'=2,'y1'=4,'y0'=2,'zh'=2,'x'=4,'c'=2] {'x'}, dimensions={0} | all-to-all | bytes 524288 | tf_op jit(solution)/shard_map/all_to_all | solution.py:38
  94.4 11.6 %all_to_all.36.refs_0_ = bf16[4,2,128,128]{3,2,1,0:T(8,128)(2,1)S(1)} all-to-all(bf16[4,2,128,128]{3,2,1,0:T(8,128)(2,1)S(1)} %all_to_all.35), channel_id=1, replica_groups=mesh['z1'=2,'z0'=2,'y1'=4,'y0'=2,'zh'=2,'x'=4,'c'=2] {'z1','z0'}, dimensions={0} | all-to-all | bytes 524288 | tf_op jit(solution)/shard_map/all_to_all | solution.py:38
  105.9 3.5 %all-to-all-start.5 = ((bf16[4,128,1024]{2,1,0:T(8,128)(2,1)}), bf16[4,128,1024]{2,1,0:T(8,128)(2,1)S(1)}, u32[]{:S(2)}, u32[]{:S(2)}) async-start(bf16[4,128,1024]{2,1,0:T(8,128)(2,1)} %bitcast.45), calls=%async_computation.5 | async-start | bytes 2097152 | tf_op jit(solution)/shard_map/all_to_all | solution.py:38
  109.4 3.4 %collective-permute-start.6 = (bf16[4,2,128,128]{3,2,1,0:T(8,128)(2,1)S(1)}, bf16[4,2,128,128]{3,2,1,0:T(8,128)(2,1)S(1)}, u32[]{:S(2)}, u32[]{:S(2)}) collective-permute-start(bf16[4,2,128,128]{3,2,1,0:T(8,128)(2,1)S(1)} %all_to_all.36.refs_0_), channel_id=1, source_target_pairs={{0,16},{16,32},{32,48},{48,64},{64,80},{80,96},{96,112},{112,0},{1... | collective-permute-start | bytes 786440 | tf_op jit(solution)/shard_map/ppermute | solution.py:333
  112.8 3.7 %collective-permute-start.10 = (bf16[4,2,128,128]{3,2,1,0:T(8,128)(2,1)S(1)}, bf16[4,2,128,128]{3,2,1,0:T(8,128)(2,1)S(1)}, u32[]{:S(2)}, u32[]{:S(2)}) collective-permute-start(bf16[4,2,128,128]{3,2,1,0:T(8,128)(2,1)S(1)} %all_to_all.36.refs_0_), channel_id=1, source_target_pairs={{0,112},{16,0},{32,16},{48,32},{64,48},{80,64},{96,80},{112,96},{1... | collective-permute-start | bytes 786440 | tf_op jit(solution)/shard_map/ppermute | solution.py:334
  116.7 2.3 %collective-permute-done.6.refs_1_ = bf16[4,2,128,128]{3,2,1,0:T(8,128)(2,1)S(1)} collective-permute-done((bf16[4,2,128,128]{3,2,1,0:T(8,128)(2,1)S(1)}, bf16[4,2,128,128]{3,2,1,0:T(8,128)(2,1)S(1)}, u32[]{:S(2)}, u32[]{:S(2)}) %collective-permute-start.6) | collective-permute-done | bytes 262176 | tf_op jit(solution)/shard_map/ppermute | solution.py:333
  119.1 2.2 %collective-permute-start.7 = (bf16[4,2,128,128]{3,2,1,0:T(8,128)(2,1)S(1)}, bf16[4,2,128,128]{3,2,1,0:T(8,128)(2,1)S(1)}, u32[]{:S(2)}, u32[]{:S(2)}) collective-permute-start(bf16[4,2,128,128]{3,2,1,0:T(8,128)(2,1)S(1)} %collective-permute-done.6.refs_1_), channel_id=1, source_target_pairs={{0,16},{16,32},{32,48},{48,64},{64,80},{80,96},{96,112},{112,0},{1... | collective-permute-start | bytes 786440 | tf_op jit(solution)/shard_map/ppermute | solution.py:333
  121.2 4.9 %collective-permute-start.11 = (bf16[4,2,128,128]{3,2,1,0:T(8,128)(2,1)S(1)}, bf16[4,2,128,128]{3,2,1,0:T(8,128)(2,1)S(1)}, u32[]{:S(2)}, u32[]{:S(2)}) collective-permute-start(bf16[4,2,128,128]{3,2,1,0:T(8,128)(2,1)S(1)} %collective-permute-done.10.refs_0_), channel_id=1, source_target_pairs={{0,112},{16,0},{32,16},{48,32},{64,48},{80,64},{96,80},{112,96},{1... | collective-permute-start | bytes 786440 | tf_op jit(solution)/shard_map/ppermute | solution.py:334
  126.7 1.8 collective-permute-done.7.refs_2_
  128.5 1.9 %collective-permute-start.8 = (bf16[4,2,128,128]{3,2,1,0:T(8,128)(2,1)S(1)}, bf16[4,2,128,128]{3,2,1,0:T(8,128)(2,1)S(1)}, u32[]{:S(2)}, u32[]{:S(2)}) collective-permute-start(bf16[4,2,128,128]{3,2,1,0:T(8,128)(2,1)S(1)} %collective-permute-done.7.refs_2_), channel_id=1, source_target_pairs={{0,16},{16,32},{32,48},{48,64},{64,80},{80,96},{96,112},{112,0},{1... | collective-permute-start | bytes 786440 | tf_op jit(solution)/shard_map/ppermute | solution.py:333
  130.4 5.1 %collective-permute-start.12 = (bf16[4,2,128,128]{3,2,1,0:T(8,128)(2,1)S(1)}, bf16[4,2,128,128]{3,2,1,0:T(8,128)(2,1)S(1)}, u32[]{:S(2)}, u32[]{:S(2)}) collective-permute-start(bf16[4,2,128,128]{3,2,1,0:T(8,128)(2,1)S(1)} %collective-permute-done.11.refs_1_), channel_id=1, source_target_pairs={{0,112},{16,0},{32,16},{48,32},{64,48},{80,64},{96,80},{112,96},{1... | collective-permute-start | bytes 786440 | tf_op jit(solution)/shard_map/ppermute | solution.py:334
  136.3 4.4 %shard_map.59 = (f32[4,128,1024]{2,1,0:T(8,128)S(1)}, f32[4,1,1024]{2,1,0:T(1,128)S(1)}, f32[4,1,1024]{2,1,0:T(1,128)S(1)}) custom-call(s32[5]{0:T(128)S(1)} %pad_add_fusion.where_ref, bf16[4,128,1024]{2,1,0:T(8,128)(2,1)S(1)} %shard_map.58.q_ref, s32[4,1,128]{2,1,0:T(1,128)S(1)} %bitcast.42, bf16[4,2,128,128]{3,2,1,0:T(8,128)(2,1)S(1)} %all_to_all.36.refs_0_, ...), custom_call_target="tpu_custom_call" | custom-call | flops 3221225472 | bytes 4194304 | tf_op jit(solution)/shard_map/pallas_call | solution.py:235
  140.7 4.3 %collective-permute-start.9 = (bf16[4,2,128,128]{3,2,1,0:T(8,128)(2,1)S(1)}, bf16[4,2,128,128]{3,2,1,0:T(8,128)(2,1)S(1)}, u32[]{:S(2)}, u32[]{:S(2)}) collective-permute-start(bf16[4,2,128,128]{3,2,1,0:T(8,128)(2,1)S(1)} %collective-permute-done.8.refs_2_), channel_id=1, source_target_pairs={{0,16},{16,32},{32,48},{48,64},{64,80},{80,96},{96,112},{112,0},{1... | collective-permute-start | bytes 786440 | tf_op jit(solution)/shard_map/ppermute | solution.py:337
  145.0 2.6 %shard_map.60 = (f32[4,128,1024]{2,1,0:T(8,128)S(1)}, f32[4,1,1024]{2,1,0:T(1,128)S(1)}, f32[4,1,1024]{2,1,0:T(1,128)S(1)}) custom-call(s32[5]{0:T(128)S(1)} %pad_add_fusion.where_ref, bf16[4,128,1024]{2,1,0:T(8,128)(2,1)S(1)} %shard_map.58.q_ref, s32[4,1,128]{2,1,0:T(1,128)S(1)} %bitcast.43, bf16[4,2,128,128]{3,2,1,0:T(8,128)(2,1)S(1)} %collective-permute-done.10.refs_0_, ...), custom_call_target="tpu_custom_call" | custom-call | flops 4294967296 | bytes 4194304 | tf_op jit(solution)/shard_map/pallas_call | solution.py:235
  147.6 3.5 %collective-permute-done.9.refs_0_ = bf16[4,2,128,128]{3,2,1,0:T(8,128)(2,1)S(1)} collective-permute-done((bf16[4,2,128,128]{3,2,1,0:T(8,128)(2,1)S(1)}, bf16[4,2,128,128]{3,2,1,0:T(8,128)(2,1)S(1)}, u32[]{:S(2)}, u32[]{:S(2)}) %collective-permute-start.9) | collective-permute-done | bytes 262176 | tf_op jit(solution)/shard_map/ppermute | solution.py:337
  151.1 1.8 shard_map.61
  152.9 30.0 %all_to_all.37.heads_ref = bf16[4,128,1024]{2,1,0:T(8,128)(2,1)S(1)} all-to-all(bf16[4,128,1024]{2,1,0:T(8,128)(2,1)S(1)} %shard_map.61), channel_id=1, replica_groups=mesh['z1'=2,'z0'=2,'y1'=4,'y0'=2,'zh'=2,'x'=4,'c'=2] {'z1','z0'}, dimensions={0} | all-to-all | bytes 2097152 | tf_op jit(solution)/shard_map/all_to_all | solution.py:38
  182.9 1.0 shard_map.62
  (49 shorter events, 3.0 us)
Async XLA Ops:
  0.0 12.5 %copy-start = (bf16[1,128,4096]{2,1,0:T(8,128)(2,1)S(1)}, bf16[1,128,4096]{2,1,0:T(8,128)(2,1)}, u32[]{:S(2)}) copy-start(bf16[1,128,4096]{2,1,0:T(8,128)(2,1)} %param.5) | copy-start | bytes 3145732
  3.2 16.1 %all-to-all-start = ((bf16[8,160,128]{2,1,0:T(8,128)(2,1)}), bf16[8,160,128]{2,1,0:T(8,128)(2,1)S(1)}, u32[]{:S(2)}, u32[]{:S(2)}) async-start(bf16[8,160,128]{2,1,0:T(8,128)(2,1)} %bitcast.4), calls=%async_computation | async-start | bytes 655360 | tf_op jit(solution)/shard_map/all_to_all | solution.py:38
  12.5 37.8 %collective-permute-start.1 = (bf16[128,4096]{1,0:T(8,128)(2,1)S(1)}, bf16[128,4096]{1,0:T(8,128)(2,1)S(1)}, u32[]{:S(2)}, u32[]{:S(2)}) collective-permute-start(bf16[128,4096]{1,0:T(8,128)(2,1)S(1)} %bitcast.35), channel_id=1, source_target_pairs={{0,2},{2,4},{4,6},{6,0},{1,3},{3,5},{5,7},{7,1},{8,10},{10,12},{12... | collective-permute-start | bytes 3145736 | tf_op jit(solution)/shard_map/ppermute | solution.py:294
  15.8 34.4 %collective-permute-start.2 = (bf16[128,4096]{1,0:T(8,128)(2,1)S(1)}, bf16[128,4096]{1,0:T(8,128)(2,1)S(1)}, u32[]{:S(2)}, u32[]{:S(2)}) collective-permute-start(bf16[128,4096]{1,0:T(8,128)(2,1)S(1)} %bitcast.36), channel_id=1, source_target_pairs={{0,6},{2,0},{4,2},{6,4},{1,7},{3,1},{5,3},{7,5},{8,14},{10,8},{12,... | collective-permute-start | bytes 3145736 | tf_op jit(solution)/shard_map/ppermute | solution.py:295
  19.3 12.0 %copy-start.6 = (bf16[8,160,128]{2,1,0:T(8,128)(2,1)}, bf16[8,160,128]{2,1,0:T(8,128)(2,1)S(1)}, u32[]{:S(2)}) copy-start(bf16[8,160,128]{2,1,0:T(8,128)(2,1)S(1)} %all-to-all-done) | copy-start | bytes 983044
  19.3 0.7 copy-start.7
  20.0 9.7 %collective-permute-start = (bf16[128,128]{1,0:T(8,128)(2,1)S(1)}, bf16[128,128]{1,0:T(8,128)(2,1)S(1)}, u32[]{:S(2)}, u32[]{:S(2)}) collective-permute-start(bf16[128,128]{1,0:T(8,128)(2,1)S(1)} %dynamic-slice_bitcast_fusion), channel_id=1, source_target_pairs={{0,8},{8,0},{1,9},{9,1},{2,10},{10,2},{3,11},{11,3},{4,12},{12,4},... | collective-permute-start | bytes 98312 | tf_op jit(solution)/shard_map/ppermute | solution.py:291
  31.3 18.9 %all-to-all-start.1 = ((bf16[8,128,128]{2,1,0:T(8,128)(2,1)}), bf16[8,128,128]{2,1,0:T(8,128)(2,1)S(1)}, u32[]{:S(2)}, u32[]{:S(2)}) async-start(bf16[8,128,128]{2,1,0:T(8,128)(2,1)} %broadcast_in_dim.36), calls=%async_computation.1 | async-start | bytes 524288 | tf_op jit(solution)/shard_map/all_to_all | solution.py:38
  43.7 11.9 %copy-start.8 = (s32[1,4096]{1,0:T(1,128)S(1)}, s32[1,4096]{1,0:T(1,128)}, u32[]{:S(2)}) copy-start(s32[1,4096]{1,0:T(1,128)} %param.8) | copy-start | bytes 49156
  51.3 22.7 %all-to-all-start.2 = ((bf16[4,1024,128]{2,1,0:T(8,128)(2,1)}), bf16[4,1024,128]{2,1,0:T(8,128)(2,1)}, u32[]{:S(2)}, u32[]{:S(2)}) async-start(bf16[4,1024,128]{2,1,0:T(8,128)(2,1)} %shard_map.55), calls=%async_computation.2 | async-start | bytes 2097152 | tf_op jit(solution)/shard_map/all_to_all | solution.py:38
  57.2 12.7 %collective-permute-start.3 = (bf16[64,4096]{1,0:T(8,128)(2,1)S(1)}, bf16[64,4096]{1,0:T(8,128)(2,1)S(1)}, u32[]{:S(2)}, u32[]{:S(2)}) collective-permute-start(bf16[64,4096]{1,0:T(8,128)(2,1)S(1)} %slice.16), channel_id=1, source_target_pairs={{0,2},{2,4},{4,6},{6,0},{1,3},{3,5},{5,7},{7,1},{8,10},{10,12},{12... | collective-permute-start | bytes 1572872 | tf_op jit(solution)/shard_map/ppermute | solution.py:299
  60.6 12.6 %collective-permute-start.4 = (bf16[64,4096]{1,0:T(8,128)(2,1)S(1)}, bf16[64,4096]{1,0:T(8,128)(2,1)S(1)}, u32[]{:S(2)}, u32[]{:S(2)}) collective-permute-start(bf16[64,4096]{1,0:T(8,128)(2,1)S(1)} %slice.17), channel_id=1, source_target_pairs={{0,6},{2,0},{4,2},{6,4},{1,7},{3,1},{5,3},{7,5},{8,14},{10,8},{12,... | collective-permute-start | bytes 1572872 | tf_op jit(solution)/shard_map/ppermute | solution.py:300
  69.9 0.8 copy-start.1
  73.2 0.8 copy-start.3
  74.0 6.6 %collective-permute-start.5 = (bf16[32,128,128]{2,1,0:T(8,128)(2,1)}, bf16[32,128,128]{2,1,0:T(8,128)(2,1)}, u32[]{:S(2)}, u32[]{:S(2)}) collective-permute-start(bf16[32,128,128]{2,1,0:T(8,128)(2,1)} %bitcast.8.refs_5_), channel_id=1, source_target_pairs={{0,1},{1,0},{2,3},{3,2},{4,5},{5,4},{6,7},{7,6},{8,9},{9,8},{10,11... | collective-permute-start | bytes 3145736 | tf_op jit(solution)/shard_map/ppermute | solution.py:318
  76.0 1.0 copy-start.2
  77.1 1.0 copy-start.4
  78.1 2.5 %copy-start.5 = (f32[4,128,64]{2,1,0:T(8,128)S(1)}, f32[4,128,64]{2,1,0:T(8,128)}, u32[]{:S(2)}) copy-start(f32[4,128,64]{2,1,0:T(8,128)} %get-tuple-element.34.refs_8_) | copy-start | bytes 393220
  105.9 29.7 %all-to-all-start.5 = ((bf16[4,128,1024]{2,1,0:T(8,128)(2,1)}), bf16[4,128,1024]{2,1,0:T(8,128)(2,1)S(1)}, u32[]{:S(2)}, u32[]{:S(2)}) async-start(bf16[4,128,1024]{2,1,0:T(8,128)(2,1)} %bitcast.45), calls=%async_computation.5 | async-start | bytes 2097152 | tf_op jit(solution)/shard_map/all_to_all | solution.py:38
  109.4 9.6 %collective-permute-start.6 = (bf16[4,2,128,128]{3,2,1,0:T(8,128)(2,1)S(1)}, bf16[4,2,128,128]{3,2,1,0:T(8,128)(2,1)S(1)}, u32[]{:S(2)}, u32[]{:S(2)}) collective-permute-start(bf16[4,2,128,128]{3,2,1,0:T(8,128)(2,1)S(1)} %all_to_all.36.refs_0_), channel_id=1, source_target_pairs={{0,16},{16,32},{32,48},{48,64},{64,80},{80,96},{96,112},{112,0},{1... | collective-permute-start | bytes 786440 | tf_op jit(solution)/shard_map/ppermute | solution.py:333
  112.8 8.4 %collective-permute-start.10 = (bf16[4,2,128,128]{3,2,1,0:T(8,128)(2,1)S(1)}, bf16[4,2,128,128]{3,2,1,0:T(8,128)(2,1)S(1)}, u32[]{:S(2)}, u32[]{:S(2)}) collective-permute-start(bf16[4,2,128,128]{3,2,1,0:T(8,128)(2,1)S(1)} %all_to_all.36.refs_0_), channel_id=1, source_target_pairs={{0,112},{16,0},{32,16},{48,32},{64,48},{80,64},{96,80},{112,96},{1... | collective-permute-start | bytes 786440 | tf_op jit(solution)/shard_map/ppermute | solution.py:334
  119.1 9.5 %collective-permute-start.7 = (bf16[4,2,128,128]{3,2,1,0:T(8,128)(2,1)S(1)}, bf16[4,2,128,128]{3,2,1,0:T(8,128)(2,1)S(1)}, u32[]{:S(2)}, u32[]{:S(2)}) collective-permute-start(bf16[4,2,128,128]{3,2,1,0:T(8,128)(2,1)S(1)} %collective-permute-done.6.refs_1_), channel_id=1, source_target_pairs={{0,16},{16,32},{32,48},{48,64},{64,80},{80,96},{96,112},{112,0},{1... | collective-permute-start | bytes 786440 | tf_op jit(solution)/shard_map/ppermute | solution.py:333
  121.2 9.2 %collective-permute-start.11 = (bf16[4,2,128,128]{3,2,1,0:T(8,128)(2,1)S(1)}, bf16[4,2,128,128]{3,2,1,0:T(8,128)(2,1)S(1)}, u32[]{:S(2)}, u32[]{:S(2)}) collective-permute-start(bf16[4,2,128,128]{3,2,1,0:T(8,128)(2,1)S(1)} %collective-permute-done.10.refs_0_), channel_id=1, source_target_pairs={{0,112},{16,0},{32,16},{48,32},{64,48},{80,64},{96,80},{112,96},{1... | collective-permute-start | bytes 786440 | tf_op jit(solution)/shard_map/ppermute | solution.py:334
  128.5 12.2 %collective-permute-start.8 = (bf16[4,2,128,128]{3,2,1,0:T(8,128)(2,1)S(1)}, bf16[4,2,128,128]{3,2,1,0:T(8,128)(2,1)S(1)}, u32[]{:S(2)}, u32[]{:S(2)}) collective-permute-start(bf16[4,2,128,128]{3,2,1,0:T(8,128)(2,1)S(1)} %collective-permute-done.7.refs_2_), channel_id=1, source_target_pairs={{0,16},{16,32},{32,48},{48,64},{64,80},{80,96},{96,112},{112,0},{1... | collective-permute-start | bytes 786440 | tf_op jit(solution)/shard_map/ppermute | solution.py:333
  130.4 14.6 %collective-permute-start.12 = (bf16[4,2,128,128]{3,2,1,0:T(8,128)(2,1)S(1)}, bf16[4,2,128,128]{3,2,1,0:T(8,128)(2,1)S(1)}, u32[]{:S(2)}, u32[]{:S(2)}) collective-permute-start(bf16[4,2,128,128]{3,2,1,0:T(8,128)(2,1)S(1)} %collective-permute-done.11.refs_1_), channel_id=1, source_target_pairs={{0,112},{16,0},{32,16},{48,32},{64,48},{80,64},{96,80},{112,96},{1... | collective-permute-start | bytes 786440 | tf_op jit(solution)/shard_map/ppermute | solution.py:334
  140.7 10.3 %collective-permute-start.9 = (bf16[4,2,128,128]{3,2,1,0:T(8,128)(2,1)S(1)}, bf16[4,2,128,128]{3,2,1,0:T(8,128)(2,1)S(1)}, u32[]{:S(2)}, u32[]{:S(2)}) collective-permute-start(bf16[4,2,128,128]{3,2,1,0:T(8,128)(2,1)S(1)} %collective-permute-done.8.refs_2_), channel_id=1, source_target_pairs={{0,16},{16,32},{32,48},{48,64},{64,80},{80,96},{96,112},{112,0},{1... | collective-permute-start | bytes 786440 | tf_op jit(solution)/shard_map/ppermute | solution.py:337

commit v15 on v14

--- a/solution.py
+++ b/solution.py
@@ -251,6 +251,17 @@
     return call(repeat_kernel, out, [VMEM], (0, 5 * 2**18))(rows)
 
 
+def choose_kernel(held_ref, own_ref, other_ref, out_ref):
+    chosen = jnp.where(held_ref[0] == 1, own_ref[...], other_ref[...])
+    for j in range(8):
+        out_ref[j] = chosen
+
+
+def choose_rows(held, own, other):
+    out = jax.ShapeDtypeStruct((8,) + own.shape, own.dtype)
+    return call(choose_kernel, out, [SMEM, VMEM, VMEM], (0, 2**18))(held, own, other)
+
+
 def lay_out_kernel(heads_ref, out_ref, done):
     width = GROUP * HEAD_DIM
     copies = [
@@ -288,12 +299,13 @@
     got = exchange(pieces.reshape(8, 160, 128), ("x", "c"))
     piece = pick(got[:, :BLOCK], origin % 8)
     rows_along = pick(got.reshape(4, 2, 160, 128)[:, :, BLOCK:], c, 1)
-    piece = jnp.where(zh == origin // 8, piece, lax.ppermute(piece, "zh", ring(2, 1)))
+    held = (zh == origin // 8).astype(jnp.int32)[None]
+    pieces = choose_rows(held, piece, lax.ppermute(piece, "zh", ring(2, 1)))
 
     own = hidden[0]
     left = lax.ppermute(own, "x", ring(4, 1))
     right = lax.ppermute(own, "x", ring(4, -1))
-    part = spread(piece, ("z1", "y1"), 8).reshape(8 * BLOCK, 128)
+    part = exchange(pieces, ("z1", "y1")).reshape(8 * BLOCK, 128)
     part, left, right = lax.optimization_barrier((part, left, right))
     mine = exchange(repeat_rows(part), ("z0", "y0")).reshape(32, BLOCK, 128)
     far_low = lax.ppermute(left[:64], "x", ring(4, 1))

time: 186 us -> 202 us (1.086)
  the two profiles are of different devices: /device:TPU:2 before, /device:TPU:14 now
where the time goes in v15:
time: 202 us; the launch traced here: 201 us
  starting transfers between devices  66.2 us (33%)
  blocking collectives  50.2 us (25%)
  waiting for transfers between devices  48.3 us (24%)
  Pallas kernels  20.1 us (10%)
  local copies, waits for them, and re-layouts  10.4 us (5%)
  other arithmetic  4.22 us (2%)
    all_to_all x3, blocking collectives, exchange(): return lax.all_to_all(value, axes, split_axis=0, concat_axis=0, tiled=True)  50.2 us
    all_to_all x4, waiting for transfers between devices, exchange(): return lax.all_to_all(value, axes, split_axis=0, concat_axis=0, tiled=True)  29.5 us
    all_to_all x4, starting transfers between devices, exchange(): return lax.all_to_all(value, axes, split_axis=0, concat_axis=0, tiled=True)  21.3 us
    pallas_call x3, Pallas kernels, attend(): call(functools.partial(attend_kernel, tiles, state is None, closing), out...  11.4 us
    ppermute x1, starting transfers between devices, on_device(): pieces = choose_rows(held, piece, lax.ppermute(piece, 'zh', ring(2, 1)))  10.9 us
    ppermute x3, starting transfers between devices, on_device(): kv[-step] = lax.ppermute(kv[1 - step], Y, ring(8, -1))  10.7 us
    ppermute x3, starting transfers between devices, on_device(): kv[step] = lax.ppermute(kv[step - 1], Y, ring(8, 1))  7.72 us
    unnamed x18, local copies, waits for them, and re-layouts  6.09 us
  transfers between devices with their start and end apart: 17, of which 9 were waited for; matrix products, arithmetic and copies ran while one was open for 5% of the time, Pallas kernels for 7%

profile of v15, /device:TPU:14, one launch (start us, length us, event | category | flops | bytes accessed | tf_op | source)
XLA Modules:
  0.0 200.5 jit_solution(17306430879170092598)
XLA Ops:
  0.0 2.4 %collective-permute-start.1 = (bf16[128,4096]{1,0:T(8,128)(2,1)}, bf16[128,4096]{1,0:T(8,128)(2,1)S(1)}, u32[]{:S(2)}, u32[]{:S(2)}) collective-permute-start(bf16[128,4096]{1,0:T(8,128)(2,1)} %bitcast.32), channel_id=1, source_target_pairs={{0,2},{2,4},{4,6},{6,0},{1,3},{3,5},{5,7},{7,1},{8,10},{10,12},{12... | collective-permute-start | bytes 3145736 | tf_op jit(solution)/shard_map/ppermute | solution.py:306
  2.4 3.5 %collective-permute-start.2 = (bf16[128,4096]{1,0:T(8,128)(2,1)}, bf16[128,4096]{1,0:T(8,128)(2,1)S(1)}, u32[]{:S(2)}, u32[]{:S(2)}) collective-permute-start(bf16[128,4096]{1,0:T(8,128)(2,1)} %bitcast.33), channel_id=1, source_target_pairs={{0,6},{2,0},{4,2},{6,4},{1,7},{3,1},{5,3},{7,5},{8,14},{10,8},{12,... | collective-permute-start | bytes 3145736 | tf_op jit(solution)/shard_map/ppermute | solution.py:307
  5.9 0.8 convert_reduce_fusion.2
  6.6 1.1 reshape_squeeze.9
  8.0 0.8 copy.10
  8.8 5.1 %all-to-all-start = ((bf16[8,160,128]{2,1,0:T(8,128)(2,1)}), bf16[8,160,128]{2,1,0:T(8,128)(2,1)S(1)}, u32[]{:S(2)}, u32[]{:S(2)}) async-start(bf16[8,160,128]{2,1,0:T(8,128)(2,1)} %bitcast.4), calls=%async_computation | async-start | bytes 655360 | tf_op jit(solution)/shard_map/all_to_all | solution.py:38
  14.5 19.3 %all-to-all-done = bf16[8,160,128]{2,1,0:T(8,128)(2,1)S(1)} async-done(((bf16[8,160,128]{2,1,0:T(8,128)(2,1)}), bf16[8,160,128]{2,1,0:T(8,128)(2,1)S(1)}, u32[]{:S(2)}, u32[]{:S(2)}) %all-to-all-start) | async-done | bytes 327712 | tf_op jit(solution)/shard_map/all_to_all | solution.py:38
  34.6 10.9 %collective-permute-start = (bf16[128,128]{1,0:T(8,128)(2,1)S(1)}, bf16[128,128]{1,0:T(8,128)(2,1)S(1)}, u32[]{:S(2)}, u32[]{:S(2)}) collective-permute-start(bf16[128,128]{1,0:T(8,128)(2,1)S(1)} %dynamic-slice_bitcast_fusion.own_ref), channel_id=1, source_target_pairs={{0,8},{8,0},{1,9},{9,1},{2,10},{10,2},{3,11},{11,3},{4,12},{12,4},... | collective-permute-start | bytes 98312 | tf_op jit(solution)/shard_map/ppermute | solution.py:303
  45.5 1.9 collective-permute-done.other_ref
  47.4 0.7 shard_map.55
  48.2 8.3 %all-to-all-start.1 = ((bf16[8,128,128]{2,1,0:T(8,128)(2,1)}), bf16[8,128,128]{2,1,0:T(8,128)(2,1)S(1)}, u32[]{:S(2)}, u32[]{:S(2)}) async-start(bf16[8,128,128]{2,1,0:T(8,128)(2,1)} %shard_map.55), calls=%async_computation.1 | async-start | bytes 524288 | tf_op jit(solution)/shard_map/all_to_all | solution.py:38
  56.5 1.6 copy.11
  58.1 1.3 copy.12
  59.4 9.1 %all-to-all-done.1 = bf16[8,128,128]{2,1,0:T(8,128)(2,1)S(1)} async-done(((bf16[8,128,128]{2,1,0:T(8,128)(2,1)}), bf16[8,128,128]{2,1,0:T(8,128)(2,1)S(1)}, u32[]{:S(2)}, u32[]{:S(2)}) %all-to-all-start.1) | async-done | bytes 262176 | tf_op jit(solution)/shard_map/all_to_all | solution.py:38
  68.6 1.1 shard_map.56
  69.7 4.3 %all-to-all-start.2 = ((bf16[4,1024,128]{2,1,0:T(8,128)(2,1)}), bf16[4,1024,128]{2,1,0:T(8,128)(2,1)}, u32[]{:S(2)}, u32[]{:S(2)}) async-start(bf16[4,1024,128]{2,1,0:T(8,128)(2,1)} %shard_map.56), calls=%async_computation.2 | async-start | bytes 2097152 | tf_op jit(solution)/shard_map/all_to_all | solution.py:38
  74.4 0.8 slice.21
  75.7 1.9 collective-permute-start.3
  77.6 3.9 %collective-permute-start.4 = (bf16[64,4096]{1,0:T(8,128)(2,1)S(1)}, bf16[64,4096]{1,0:T(8,128)(2,1)S(1)}, u32[]{:S(2)}, u32[]{:S(2)}) collective-permute-start(bf16[64,4096]{1,0:T(8,128)(2,1)S(1)} %slice.17), channel_id=1, source_target_pairs={{0,6},{2,0},{4,2},{6,4},{1,7},{3,1},{5,3},{7,5},{8,14},{10,8},{12,... | collective-permute-start | bytes 1572872 | tf_op jit(solution)/shard_map/ppermute | solution.py:312
  81.7 1.8 multiply_sine_fusion
  83.4 4.6 %collective-permute-done.3.refs_2_.refs_3_ = bf16[64,4096]{1,0:T(8,128)(2,1)S(1)} collective-permute-done((bf16[64,4096]{1,0:T(8,128)(2,1)S(1)}, bf16[64,4096]{1,0:T(8,128)(2,1)S(1)}, u32[]{:S(2)}, u32[]{:S(2)}) %collective-permute-start.3) | collective-permute-done | bytes 524320 | tf_op jit(solution)/shard_map/ppermute | solution.py:311
  88.0 0.8 copy-done.1
  88.8 2.4 %collective-permute-done.4.refs_3_.refs_4_ = bf16[64,4096]{1,0:T(8,128)(2,1)S(1)} collective-permute-done((bf16[64,4096]{1,0:T(8,128)(2,1)S(1)}, bf16[64,4096]{1,0:T(8,128)(2,1)S(1)}, u32[]{:S(2)}, u32[]{:S(2)}) %collective-permute-start.4) | collective-permute-done | bytes 524320 | tf_op jit(solution)/shard_map/ppermute | solution.py:312
  91.2 0.8 copy-done.3
  92.0 1.9 collective-permute-start.5
  94.0 1.0 copy-done.2
  95.0 1.0 copy-done.4
  96.1 2.5 %shard_map.57.refs_7_ = f32[512,128]{1,0:T(8,128)S(1)} custom-call(bf16[128,4096]{1,0:T(8,128)(2,1)S(1)} %bitcast.34, bf16[128,4096]{1,0:T(8,128)(2,1)S(1)} %collective-permute-done.1.refs_1_.refs_2_, bf16[64,4096]{1,0:T(8,128)(2,1)S(1)} %copy-done.2, bf16[64,4096]{1,0:T(8,128)(2,1)S(1)} %copy-done.4, ...), custom_call_target="tpu_custom_call" | custom-call | flops 536870912 | bytes 5242880 | tf_op jit(solution)/shard_map/pallas_call | solution.py:121
  98.6 2.6 %shard_map.58 = bf16[4,2,128,128]{3,2,1,0:T(8,128)(2,1)S(1)} custom-call(s32[2]{0:T(128)S(1)} %pad_add_fusion.1.refs_0_, bf16[128,4096]{1,0:T(8,128)(2,1)S(1)} %bitcast.35, bf16[128,4096]{1,0:T(8,128)(2,1)S(1)} %collective-permute-done.1.refs_1_.refs_2_, bf16[64,4096]{1,0:T(8,128)(2,1)S(1)} %copy-done.2, bf16[64,4096]{1,0:T(8,128)(2,1)S(1)} %copy-done.4, ...), custom_call_target="tpu_custom_call" | custom-call | flops 536870912 | bytes 5242880 | tf_op jit(solution)/shard_map/pallas_call | solution.py:147
  101.3 9.6 %all_to_all.35 = bf16[4,2,128,128]{3,2,1,0:T(8,128)(2,1)S(1)} all-to-all(bf16[4,2,128,128]{3,2,1,0:T(8,128)(2,1)S(1)} %shard_map.58), channel_id=1, replica_groups=mesh['z1'=2,'z0'=2,'y1'=4,'y0'=2,'zh'=2,'x'=4,'c'=2] {'x'}, dimensions={0} | all-to-all | bytes 524288 | tf_op jit(solution)/shard_map/all_to_all | solution.py:38
  110.8 11.2 %all_to_all.36.refs_0_ = bf16[4,2,128,128]{3,2,1,0:T(8,128)(2,1)S(1)} all-to-all(bf16[4,2,128,128]{3,2,1,0:T(8,128)(2,1)S(1)} %all_to_all.35), channel_id=1, replica_groups=mesh['z1'=2,'z0'=2,'y1'=4,'y0'=2,'zh'=2,'x'=4,'c'=2] {'z1','z0'}, dimensions={0} | all-to-all | bytes 524288 | tf_op jit(solution)/shard_map/all_to_all | solution.py:38
  122.0 3.5 %all-to-all-start.5 = ((bf16[4,128,1024]{2,1,0:T(8,128)(2,1)}), bf16[4,128,1024]{2,1,0:T(8,128)(2,1)S(1)}, u32[]{:S(2)}, u32[]{:S(2)}) async-start(bf16[4,128,1024]{2,1,0:T(8,128)(2,1)} %bitcast.42), calls=%async_computation.5 | async-start | bytes 2097152 | tf_op jit(solution)/shard_map/all_to_all | solution.py:38
  125.6 2.6 %collective-permute-start.6 = (bf16[4,2,128,128]{3,2,1,0:T(8,128)(2,1)S(1)}, bf16[4,2,128,128]{3,2,1,0:T(8,128)(2,1)S(1)}, u32[]{:S(2)}, u32[]{:S(2)}) collective-permute-start(bf16[4,2,128,128]{3,2,1,0:T(8,128)(2,1)S(1)} %all_to_all.36.refs_0_), channel_id=1, source_target_pairs={{0,16},{16,32},{32,48},{48,64},{64,80},{80,96},{96,112},{112,0},{1... | collective-permute-start | bytes 786440 | tf_op jit(solution)/shard_map/ppermute | solution.py:345
  128.1 3.3 %collective-permute-start.10 = (bf16[4,2,128,128]{3,2,1,0:T(8,128)(2,1)S(1)}, bf16[4,2,128,128]{3,2,1,0:T(8,128)(2,1)S(1)}, u32[]{:S(2)}, u32[]{:S(2)}) collective-permute-start(bf16[4,2,128,128]{3,2,1,0:T(8,128)(2,1)S(1)} %all_to_all.36.refs_0_), channel_id=1, source_target_pairs={{0,112},{16,0},{32,16},{48,32},{64,48},{80,64},{96,80},{112,96},{1... | collective-permute-start | bytes 786440 | tf_op jit(solution)/shard_map/ppermute | solution.py:346
  131.6 2.3 %collective-permute-done.6.refs_1_ = bf16[4,2,128,128]{3,2,1,0:T(8,128)(2,1)S(1)} collective-permute-done((bf16[4,2,128,128]{3,2,1,0:T(8,128)(2,1)S(1)}, bf16[4,2,128,128]{3,2,1,0:T(8,128)(2,1)S(1)}, u32[]{:S(2)}, u32[]{:S(2)}) %collective-permute-start.6) | collective-permute-done | bytes 262176 | tf_op jit(solution)/shard_map/ppermute | solution.py:345
  133.9 2.6 %collective-permute-start.7 = (bf16[4,2,128,128]{3,2,1,0:T(8,128)(2,1)S(1)}, bf16[4,2,128,128]{3,2,1,0:T(8,128)(2,1)S(1)}, u32[]{:S(2)}, u32[]{:S(2)}) collective-permute-start(bf16[4,2,128,128]{3,2,1,0:T(8,128)(2,1)S(1)} %collective-permute-done.6.refs_1_), channel_id=1, source_target_pairs={{0,16},{16,32},{32,48},{48,64},{64,80},{80,96},{96,112},{112,0},{1... | collective-permute-start | bytes 786440 | tf_op jit(solution)/shard_map/ppermute | solution.py:345
  136.5 3.3 %collective-permute-start.11 = (bf16[4,2,128,128]{3,2,1,0:T(8,128)(2,1)S(1)}, bf16[4,2,128,128]{3,2,1,0:T(8,128)(2,1)S(1)}, u32[]{:S(2)}, u32[]{:S(2)}) collective-permute-start(bf16[4,2,128,128]{3,2,1,0:T(8,128)(2,1)S(1)} %collective-permute-done.10.refs_0_), channel_id=1, source_target_pairs={{0,112},{16,0},{32,16},{48,32},{64,48},{80,64},{96,80},{112,96},{1... | collective-permute-start | bytes 786440 | tf_op jit(solution)/shard_map/ppermute | solution.py:346
  140.4 1.8 collective-permute-done.7.refs_2_
  142.2 2.6 %collective-permute-start.8 = (bf16[4,2,128,128]{3,2,1,0:T(8,128)(2,1)S(1)}, bf16[4,2,128,128]{3,2,1,0:T(8,128)(2,1)S(1)}, u32[]{:S(2)}, u32[]{:S(2)}) collective-permute-start(bf16[4,2,128,128]{3,2,1,0:T(8,128)(2,1)S(1)} %collective-permute-done.7.refs_2_), channel_id=1, source_target_pairs={{0,16},{16,32},{32,48},{48,64},{64,80},{80,96},{96,112},{112,0},{1... | collective-permute-start | bytes 786440 | tf_op jit(solution)/shard_map/ppermute | solution.py:345
  144.8 4.2 %collective-permute-start.12 = (bf16[4,2,128,128]{3,2,1,0:T(8,128)(2,1)S(1)}, bf16[4,2,128,128]{3,2,1,0:T(8,128)(2,1)S(1)}, u32[]{:S(2)}, u32[]{:S(2)}) collective-permute-start(bf16[4,2,128,128]{3,2,1,0:T(8,128)(2,1)S(1)} %collective-permute-done.11.refs_1_), channel_id=1, source_target_pairs={{0,112},{16,0},{32,16},{48,32},{64,48},{80,64},{96,80},{112,96},{1... | collective-permute-start | bytes 786440 | tf_op jit(solution)/shard_map/ppermute | solution.py:346
  149.0 1.0 all-to-all-done.5.q_ref
  150.7 7.0 %shard_map.60 = (f32[4,128,1024]{2,1,0:T(8,128)S(1)}, f32[4,1,1024]{2,1,0:T(1,128)S(1)}, f32[4,1,1024]{2,1,0:T(1,128)S(1)}) custom-call(s32[5]{0:T(128)S(1)} %pad_add_fusion.where_ref, bf16[4,128,1024]{2,1,0:T(8,128)(2,1)S(1)} %shard_map.59.q_ref, s32[4,1,128]{2,1,0:T(1,128)S(1)} %bitcast.39, bf16[4,2,128,128]{3,2,1,0:T(8,128)(2,1)S(1)} %all_to_all.36.refs_0_, ...), custom_call_target="tpu_custom_call" | custom-call | flops 3221225472 | bytes 4194304 | tf_op jit(solution)/shard_map/pallas_call | solution.py:235
  157.7 1.9 collective-permute-start.9
  159.7 2.6 %shard_map.61 = (f32[4,128,1024]{2,1,0:T(8,128)S(1)}, f32[4,1,1024]{2,1,0:T(1,128)S(1)}, f32[4,1,1024]{2,1,0:T(1,128)S(1)}) custom-call(s32[5]{0:T(128)S(1)} %pad_add_fusion.where_ref, bf16[4,128,1024]{2,1,0:T(8,128)(2,1)S(1)} %shard_map.59.q_ref, s32[4,1,128]{2,1,0:T(1,128)S(1)} %bitcast.40, bf16[4,2,128,128]{3,2,1,0:T(8,128)(2,1)S(1)} %collective-permute-done.10.refs_0_, ...), custom_call_target="tpu_custom_call" | custom-call | flops 4294967296 | bytes 4194304 | tf_op jit(solution)/shard_map/pallas_call | solution.py:235
  162.3 5.9 %collective-permute-done.9.refs_0_ = bf16[4,2,128,128]{3,2,1,0:T(8,128)(2,1)S(1)} collective-permute-done((bf16[4,2,128,128]{3,2,1,0:T(8,128)(2,1)S(1)}, bf16[4,2,128,128]{3,2,1,0:T(8,128)(2,1)S(1)}, u32[]{:S(2)}, u32[]{:S(2)}) %collective-permute-start.9) | collective-permute-done | bytes 262176 | tf_op jit(solution)/shard_map/ppermute | solution.py:349
  168.2 1.8 shard_map.62
  170.0 29.5 %all_to_all.37.heads_ref = bf16[4,128,1024]{2,1,0:T(8,128)(2,1)S(1)} all-to-all(bf16[4,128,1024]{2,1,0:T(8,128)(2,1)S(1)} %shard_map.62), channel_id=1, replica_groups=mesh['z1'=2,'z0'=2,'y1'=4,'y0'=2,'zh'=2,'x'=4,'c'=2] {'z1','z0'}, dimensions={0} | all-to-all | bytes 2097152 | tf_op jit(solution)/shard_map/all_to_all | solution.py:38
  199.5 1.0 shard_map.63
  (45 shorter events, 3.4 us)
Async XLA Ops:
  0.0 68.6 %collective-permute-start.1 = (bf16[128,4096]{1,0:T(8,128)(2,1)}, bf16[128,4096]{1,0:T(8,128)(2,1)S(1)}, u32[]{:S(2)}, u32[]{:S(2)}) collective-permute-start(bf16[128,4096]{1,0:T(8,128)(2,1)} %bitcast.32), channel_id=1, source_target_pairs={{0,2},{2,4},{4,6},{6,0},{1,3},{3,5},{5,7},{7,1},{8,10},{10,12},{12... | collective-permute-start | bytes 3145736 | tf_op jit(solution)/shard_map/ppermute | solution.py:306
  2.4 66.2 %collective-permute-start.2 = (bf16[128,4096]{1,0:T(8,128)(2,1)}, bf16[128,4096]{1,0:T(8,128)(2,1)S(1)}, u32[]{:S(2)}, u32[]{:S(2)}) collective-permute-start(bf16[128,4096]{1,0:T(8,128)(2,1)} %bitcast.33), channel_id=1, source_target_pairs={{0,6},{2,0},{4,2},{6,4},{1,7},{3,1},{5,3},{7,5},{8,14},{10,8},{12,... | collective-permute-start | bytes 3145736 | tf_op jit(solution)/shard_map/ppermute | solution.py:307
  8.8 25.1 %all-to-all-start = ((bf16[8,160,128]{2,1,0:T(8,128)(2,1)}), bf16[8,160,128]{2,1,0:T(8,128)(2,1)S(1)}, u32[]{:S(2)}, u32[]{:S(2)}) async-start(bf16[8,160,128]{2,1,0:T(8,128)(2,1)} %bitcast.4), calls=%async_computation | async-start | bytes 655360 | tf_op jit(solution)/shard_map/all_to_all | solution.py:38
  33.8 0.7 copy-start.6
  34.6 12.8 %collective-permute-start = (bf16[128,128]{1,0:T(8,128)(2,1)S(1)}, bf16[128,128]{1,0:T(8,128)(2,1)S(1)}, u32[]{:S(2)}, u32[]{:S(2)}) collective-permute-start(bf16[128,128]{1,0:T(8,128)(2,1)S(1)} %dynamic-slice_bitcast_fusion.own_ref), channel_id=1, source_target_pairs={{0,8},{8,0},{1,9},{9,1},{2,10},{10,2},{3,11},{11,3},{4,12},{12,4},... | collective-permute-start | bytes 98312 | tf_op jit(solution)/shard_map/ppermute | solution.py:303
  48.2 20.4 %all-to-all-start.1 = ((bf16[8,128,128]{2,1,0:T(8,128)(2,1)}), bf16[8,128,128]{2,1,0:T(8,128)(2,1)S(1)}, u32[]{:S(2)}, u32[]{:S(2)}) async-start(bf16[8,128,128]{2,1,0:T(8,128)(2,1)} %shard_map.55), calls=%async_computation.1 | async-start | bytes 524288 | tf_op jit(solution)/shard_map/all_to_all | solution.py:38
  59.4 14.6 %copy-start.7 = (s32[1,4096]{1,0:T(1,128)S(1)}, s32[1,4096]{1,0:T(1,128)}, u32[]{:S(2)}) copy-start(s32[1,4096]{1,0:T(1,128)} %param.8) | copy-start | bytes 49156
  69.7 22.3 %all-to-all-start.2 = ((bf16[4,1024,128]{2,1,0:T(8,128)(2,1)}), bf16[4,1024,128]{2,1,0:T(8,128)(2,1)}, u32[]{:S(2)}, u32[]{:S(2)}) async-start(bf16[4,1024,128]{2,1,0:T(8,128)(2,1)} %shard_map.56), calls=%async_computation.2 | async-start | bytes 2097152 | tf_op jit(solution)/shard_map/all_to_all | solution.py:38
  74.0 20.0 %copy-start = (bf16[1,128,4096]{2,1,0:T(8,128)(2,1)S(1)}, bf16[1,128,4096]{2,1,0:T(8,128)(2,1)}, u32[]{:S(2)}) copy-start(bf16[1,128,4096]{2,1,0:T(8,128)(2,1)} %param.5) | copy-start | bytes 3145732
  75.7 12.3 %collective-permute-start.3 = (bf16[64,4096]{1,0:T(8,128)(2,1)S(1)}, bf16[64,4096]{1,0:T(8,128)(2,1)S(1)}, u32[]{:S(2)}, u32[]{:S(2)}) collective-permute-start(bf16[64,4096]{1,0:T(8,128)(2,1)S(1)} %slice.16), channel_id=1, source_target_pairs={{0,2},{2,4},{4,6},{6,0},{1,3},{3,5},{5,7},{7,1},{8,10},{10,12},{12... | collective-permute-start | bytes 1572872 | tf_op jit(solution)/shard_map/ppermute | solution.py:311
  77.6 13.5 %collective-permute-start.4 = (bf16[64,4096]{1,0:T(8,128)(2,1)S(1)}, bf16[64,4096]{1,0:T(8,128)(2,1)S(1)}, u32[]{:S(2)}, u32[]{:S(2)}) collective-permute-start(bf16[64,4096]{1,0:T(8,128)(2,1)S(1)} %slice.17), channel_id=1, source_target_pairs={{0,6},{2,0},{4,2},{6,4},{1,7},{3,1},{5,3},{7,5},{8,14},{10,8},{12,... | collective-permute-start | bytes 1572872 | tf_op jit(solution)/shard_map/ppermute | solution.py:312
  88.0 0.8 copy-start.1
  91.2 0.8 copy-start.3
  92.0 6.6 %collective-permute-start.5 = (bf16[32,128,128]{2,1,0:T(8,128)(2,1)}, bf16[32,128,128]{2,1,0:T(8,128)(2,1)}, u32[]{:S(2)}, u32[]{:S(2)}) collective-permute-start(bf16[32,128,128]{2,1,0:T(8,128)(2,1)} %bitcast.8.refs_5_), channel_id=1, source_target_pairs={{0,1},{1,0},{2,3},{3,2},{4,5},{5,4},{6,7},{7,6},{8,9},{9,8},{10,11... | collective-permute-start | bytes 3145736 | tf_op jit(solution)/shard_map/ppermute | solution.py:330
  94.0 1.0 copy-start.2
  95.0 1.0 copy-start.4
  96.1 2.5 %copy-start.5 = (f32[4,128,64]{2,1,0:T(8,128)S(1)}, f32[4,128,64]{2,1,0:T(8,128)}, u32[]{:S(2)}) copy-start(f32[4,128,64]{2,1,0:T(8,128)} %get-tuple-element.34.refs_8_) | copy-start | bytes 393220
  122.0 28.0 %all-to-all-start.5 = ((bf16[4,128,1024]{2,1,0:T(8,128)(2,1)}), bf16[4,128,1024]{2,1,0:T(8,128)(2,1)S(1)}, u32[]{:S(2)}, u32[]{:S(2)}) async-start(bf16[4,128,1024]{2,1,0:T(8,128)(2,1)} %bitcast.42), calls=%async_computation.5 | async-start | bytes 2097152 | tf_op jit(solution)/shard_map/all_to_all | solution.py:38
  125.6 8.4 %collective-permute-start.6 = (bf16[4,2,128,128]{3,2,1,0:T(8,128)(2,1)S(1)}, bf16[4,2,128,128]{3,2,1,0:T(8,128)(2,1)S(1)}, u32[]{:S(2)}, u32[]{:S(2)}) collective-permute-start(bf16[4,2,128,128]{3,2,1,0:T(8,128)(2,1)S(1)} %all_to_all.36.refs_0_), channel_id=1, source_target_pairs={{0,16},{16,32},{32,48},{48,64},{64,80},{80,96},{96,112},{112,0},{1... | collective-permute-start | bytes 786440 | tf_op jit(solution)/shard_map/ppermute | solution.py:345
  128.1 8.4 %collective-permute-start.10 = (bf16[4,2,128,128]{3,2,1,0:T(8,128)(2,1)S(1)}, bf16[4,2,128,128]{3,2,1,0:T(8,128)(2,1)S(1)}, u32[]{:S(2)}, u32[]{:S(2)}) collective-permute-start(bf16[4,2,128,128]{3,2,1,0:T(8,128)(2,1)S(1)} %all_to_all.36.refs_0_), channel_id=1, source_target_pairs={{0,112},{16,0},{32,16},{48,32},{64,48},{80,64},{96,80},{112,96},{1... | collective-permute-start | bytes 786440 | tf_op jit(solution)/shard_map/ppermute | solution.py:346
  133.9 8.3 %collective-permute-start.7 = (bf16[4,2,128,128]{3,2,1,0:T(8,128)(2,1)S(1)}, bf16[4,2,128,128]{3,2,1,0:T(8,128)(2,1)S(1)}, u32[]{:S(2)}, u32[]{:S(2)}) collective-permute-start(bf16[4,2,128,128]{3,2,1,0:T(8,128)(2,1)S(1)} %collective-permute-done.6.refs_1_), channel_id=1, source_target_pairs={{0,16},{16,32},{32,48},{48,64},{64,80},{80,96},{96,112},{112,0},{1... | collective-permute-start | bytes 786440 | tf_op jit(solution)/shard_map/ppermute | solution.py:345
  136.5 8.3 %collective-permute-start.11 = (bf16[4,2,128,128]{3,2,1,0:T(8,128)(2,1)S(1)}, bf16[4,2,128,128]{3,2,1,0:T(8,128)(2,1)S(1)}, u32[]{:S(2)}, u32[]{:S(2)}) collective-permute-start(bf16[4,2,128,128]{3,2,1,0:T(8,128)(2,1)S(1)} %collective-permute-done.10.refs_0_), channel_id=1, source_target_pairs={{0,112},{16,0},{32,16},{48,32},{64,48},{80,64},{96,80},{112,96},{1... | collective-permute-start | bytes 786440 | tf_op jit(solution)/shard_map/ppermute | solution.py:346
  142.2 15.5 %collective-permute-start.8 = (bf16[4,2,128,128]{3,2,1,0:T(8,128)(2,1)S(1)}, bf16[4,2,128,128]{3,2,1,0:T(8,128)(2,1)S(1)}, u32[]{:S(2)}, u32[]{:S(2)}) collective-permute-start(bf16[4,2,128,128]{3,2,1,0:T(8,128)(2,1)S(1)} %collective-permute-done.7.refs_2_), channel_id=1, source_target_pairs={{0,16},{16,32},{32,48},{48,64},{64,80},{80,96},{96,112},{112,0},{1... | collective-permute-start | bytes 786440 | tf_op jit(solution)/shard_map/ppermute | solution.py:345
  144.8 14.9 %collective-permute-start.12 = (bf16[4,2,128,128]{3,2,1,0:T(8,128)(2,1)S(1)}, bf16[4,2,128,128]{3,2,1,0:T(8,128)(2,1)S(1)}, u32[]{:S(2)}, u32[]{:S(2)}) collective-permute-start(bf16[4,2,128,128]{3,2,1,0:T(8,128)(2,1)S(1)} %collective-permute-done.11.refs_1_), channel_id=1, source_target_pairs={{0,112},{16,0},{32,16},{48,32},{64,48},{80,64},{96,80},{112,96},{1... | collective-permute-start | bytes 786440 | tf_op jit(solution)/shard_map/ppermute | solution.py:346
  157.7 10.4 %collective-permute-start.9 = (bf16[4,2,128,128]{3,2,1,0:T(8,128)(2,1)S(1)}, bf16[4,2,128,128]{3,2,1,0:T(8,128)(2,1)S(1)}, u32[]{:S(2)}, u32[]{:S(2)}) collective-permute-start(bf16[4,2,128,128]{3,2,1,0:T(8,128)(2,1)S(1)} %collective-permute-done.8.refs_2_), channel_id=1, source_target_pairs={{0,16},{16,32},{32,48},{48,64},{64,80},{80,96},{96,112},{112,0},{1... | collective-permute-start | bytes 786440 | tf_op jit(solution)/shard_map/ppermute | solution.py:349
